TPU v7x, 32 devices: a whole 2x2x4 slice. The times are simulated.
32 devices in a mesh: dp: 16 (over z, y, x), tensor: 2 (over core).
Axes of the slice: x: 2, y: 2, z: 4, core: 2. Of those that a mesh axis runs over, the one named last changes fastest.
Arguments:
- hidden_in: bfloat16 [4096, 2560], P(('dp', 'tensor')), may hold values from -6 to 6
- prefix_len: int32 [16], P('dp'), may hold values from 25 to 128
- attn_gain: bfloat16 [2560], P(('dp', 'tensor')), may hold values from 0.25 to 1.75
- q_down: bfloat16 [2560, 768], P(('dp', 'tensor')), may hold values from -0.125 to 0.125
- q_gain: bfloat16 [768], P(('dp', 'tensor')), may hold values from 0.25 to 1.75
- kv_down: bfloat16 [2560, 288], P(('dp', 'tensor')), may hold values from -0.125 to 0.125
- kv_gain: bfloat16 [256], P(('dp', 'tensor')), may hold values from 0.25 to 1.75
- q_up: bfloat16 [768, 3840], P('dp', 'tensor'), may hold values from -0.21875 to 0.21875
- kv_up: bfloat16 [256, 5120], P('dp', 'tensor'), may hold values from -0.375 to 0.375
- o_proj: bfloat16 [2560, 2560], P('tensor', 'dp'), may hold values from -1.25 to 1.25
- mlp_gain: bfloat16 [2560], P(('dp', 'tensor')), may hold values from 0.25 to 1.75
- w_gate: bfloat16 [2560, 6400], P('dp', 'tensor'), may hold values from -0.125 to 0.125
- w_up: bfloat16 [2560, 6400], P('dp', 'tensor'), may hold values from -0.125 to 0.125
- w_down: bfloat16 [6400, 2560], P('tensor', 'dp'), may hold values from -0.4375 to 0.4375
- cotangent: bfloat16 [4096, 2560], P(('dp', 'tensor')), may hold values from -6 to 6
Outputs:
- layer_out: bfloat16 [4096, 2560], P(('dp', 'tensor'))
- grad_input: float32 [4096, 2560], P(('dp', 'tensor'))
- grad_attn_gain: float32 [2560], P(('dp', 'tensor'))
- grad_q_down: float32 [2560, 768], P(('dp', 'tensor'))
- grad_q_gain: float32 [768], P(('dp', 'tensor'))
- grad_kv_down: float32 [2560, 288], P(('dp', 'tensor'))
- grad_kv_gain: float32 [256], P(('dp', 'tensor'))
- grad_q_up: float32 [768, 3840], P('dp', 'tensor')
- grad_kv_up: float32 [256, 5120], P('dp', 'tensor')
- grad_o_proj: float32 [2560, 2560], P('tensor', 'dp')
- grad_mlp_gain: float32 [2560], P(('dp', 'tensor'))
- grad_w_gate: float32 [2560, 6400], P('dp', 'tensor')
- grad_w_up: float32 [2560, 6400], P('dp', 'tensor')
- grad_w_down: float32 [6400, 2560], P('tensor', 'dp')
Inputs may be any that keep to these rules, and one draw needn't show every extreme that they name: prefix_len of a sequence is the number of its leading tokens that see one another in both directions.
All inputs are finite; a program needn't handle non-finite values.
Results may differ from a plain program's by a relative error of at most 0.022.
Values may be sent and summed in bfloat16 or wider, within the bound.
No kernel may reach another device: no remote copies, remote signals or barrier semaphores. Data moves between devices by JAX's collectives and lax.ppermute only.
A program may use at most 320 MiB of HBM per device.

v0:
```python
from functools import partial
import math

import jax
import jax.numpy as jnp
from jax import lax
from jax.sharding import PartitionSpec as P

NOPE = 64
ROPE = 32
VD = 64
KR = 256


EPS = 1e-05
RESID = 1.4 / math.sqrt(62.0)
THETA = 10000.0
NEG_FILL = -1e30


def norm_apply(values, gain):
    inverse = lax.rsqrt(jnp.mean(values * values, axis=-1, keepdims=True) + EPS)
    return values * inverse * gain


def rotate(values, positions):
    width_half = values.shape[-1] // 2
    frequency = THETA ** (-2.0 * jnp.arange(width_half, dtype=jnp.float32) / values.shape[-1])
    angles = positions.astype(jnp.float32)[:, None] * frequency[None, :]
    extra_dims = (1,) * (values.ndim - 2)
    cosine = jnp.cos(angles).reshape(angles.shape[:1] + extra_dims + angles.shape[1:])
    sine = jnp.sin(angles).reshape(angles.shape[:1] + extra_dims + angles.shape[1:])
    lower_part = values[..., :width_half]
    upper_part = values[..., width_half:]
    return jnp.concatenate(
        [lower_part * cosine - upper_part * sine, upper_part * cosine + lower_part * sine], axis=-1
    )


def rotate_back(values, positions, grads):
    _, pullback = jax.vjp(partial(rotate, positions=positions), values)
    return pullback(grads)[0]


def swish(values):
    return values / (1.0 + jnp.exp(-values))


def gated(gate_in, upper_in):
    return swish(gate_in) * upper_in


def plain_mul(left, right):
    return jnp.dot(left, right, preferred_element_type=jnp.float32)


def mul_trans(left, right):
    return lax.dot_general(
        left, right, (((1,), (1,)), ((), ())), preferred_element_type=jnp.float32
    )


def trans_mul(left, right):
    return lax.dot_general(
        left, right, (((0,), (0,)), ((), ())), preferred_element_type=jnp.float32
    )


def split_heads(values, groups):
    seq_length, heads_local, width = values.shape
    return jnp.moveaxis(values.reshape(seq_length, groups, heads_local // groups, width), 1, 0)


def join_heads(values):
    groups, seq_length, group_heads, width = values.shape
    return jnp.moveaxis(values, 0, 1).reshape(seq_length, groups * group_heads, width)


def masked_scores(query_part, key_part, visible, scale):
    scores = (
        jnp.einsum("qhd,khd->hqk", query_part, key_part, preferred_element_type=jnp.float32) * scale
    )
    return jnp.where(visible[None], scores, NEG_FILL)


def attend_forward(pieces, visible, scale):
    query_part, key_part, value_part = pieces
    masked = masked_scores(query_part, key_part, visible, scale)
    row_peak = jnp.max(masked, axis=-1, keepdims=True)
    exp_scores = jnp.exp(masked - row_peak)
    row_total = jnp.sum(exp_scores, axis=-1, keepdims=True)
    attn_probs = exp_scores / row_total
    heads_part = jnp.einsum(
        "hqk,khd->qhd",
        attn_probs.astype(jnp.bfloat16),
        value_part,
        preferred_element_type=jnp.float32,
    )
    return (heads_part, row_peak + jnp.log(row_total))


def attend_backward(pieces, visible, scale):
    query_part, key_part, value_part, log_total, d_heads_part = pieces
    masked = masked_scores(query_part, key_part, visible, scale)
    attn_probs = jnp.exp(masked - log_total)
    probs_low = attn_probs.astype(jnp.bfloat16)
    d_probs = jnp.einsum(
        "qhd,khd->hqk", d_heads_part, value_part, preferred_element_type=jnp.float32
    )
    d_values = jnp.einsum(
        "hqk,qhd->khd", probs_low, d_heads_part, preferred_element_type=jnp.float32
    )
    row_dot = jnp.sum(attn_probs * d_probs, axis=-1, keepdims=True)
    d_scores = (attn_probs * (d_probs - row_dot) * scale).astype(jnp.bfloat16)
    d_query = jnp.einsum("hqk,khd->qhd", d_scores, key_part, preferred_element_type=jnp.float32)
    d_key = jnp.einsum("hqk,qhd->khd", d_scores, query_part, preferred_element_type=jnp.float32)
    return (d_query, d_key, d_values)


def body(
    hidden_in,
    prefix_len,
    attn_gain,
    q_down,
    q_gain,
    kv_down,
    kv_gain,
    q_up,
    kv_up,
    o_proj,
    mlp_gain,
    w_gate,
    w_up,
    w_down,
    cotangent,
):
    tensor_count = lax.axis_size("tensor")
    tensor_rank = lax.axis_index("tensor")
    own_rows = hidden_in.shape[0]
    seq_length = own_rows * tensor_count
    head_qk = NOPE + ROPE
    heads_local = q_up.shape[1] // head_qk
    groups = heads_local // math.gcd(heads_local, 4)
    scale = head_qk ** (-0.5)
    small_params = (
        lax.all_gather(attn_gain, ("dp", "tensor"), axis=0, tiled=True),
        lax.all_gather(q_down, ("dp", "tensor"), axis=0, tiled=True),
        lax.all_gather(q_gain, ("dp", "tensor"), axis=0, tiled=True),
        lax.all_gather(kv_down, ("dp", "tensor"), axis=0, tiled=True),
        lax.all_gather(kv_gain, ("dp", "tensor"), axis=0, tiled=True),
        lax.all_gather(mlp_gain, ("dp", "tensor"), axis=0, tiled=True),
    )
    gain_attn = small_params[0].astype(jnp.float32)
    qdown_weight = small_params[1]
    gain_q = small_params[2].astype(jnp.float32)
    kvdown_weight = small_params[3]
    gain_kv = small_params[4].astype(jnp.float32)
    gain_mlp = small_params[5].astype(jnp.float32)
    q_weight, kv_weight, out_weight, gate_weight, upper_weight, down_weight = (
        lax.all_gather(q_up, "dp", axis=0, tiled=True),
        lax.all_gather(kv_up, "dp", axis=0, tiled=True),
        lax.all_gather(o_proj, "dp", axis=1, tiled=True),
        lax.all_gather(w_gate, "dp", axis=0, tiled=True),
        lax.all_gather(w_up, "dp", axis=0, tiled=True),
        lax.all_gather(w_down, "dp", axis=1, tiled=True),
    )
    resid_in = hidden_in.astype(jnp.float32)
    x_normed = norm_apply(resid_in, gain_attn).astype(jnp.bfloat16)
    q_latent = plain_mul(x_normed, qdown_weight)
    q_normed = norm_apply(q_latent, gain_q).astype(jnp.bfloat16)
    kv_latent = plain_mul(x_normed, kvdown_weight)
    own_pos = tensor_rank * own_rows + jnp.arange(own_rows, dtype=jnp.int32)
    kv_normed = norm_apply(kv_latent[:, :KR], gain_kv).astype(jnp.bfloat16)
    k_rotary = rotate(kv_latent[:, KR:], own_pos).astype(jnp.bfloat16)
    q_seq, kv_seq, rot_seq = (
        lax.all_gather(q_normed, "tensor", axis=0, tiled=True),
        lax.all_gather(kv_normed, "tensor", axis=0, tiled=True),
        lax.all_gather(k_rotary, "tensor", axis=0, tiled=True),
    )
    positions = jnp.arange(seq_length, dtype=jnp.int32)
    query = plain_mul(q_seq, q_weight).reshape(seq_length, heads_local, head_qk)
    q_rot_in = query[..., NOPE:]
    query_full = jnp.concatenate([query[..., :NOPE], rotate(q_rot_in, positions)], axis=-1).astype(
        jnp.bfloat16
    )
    key_value = plain_mul(kv_seq, kv_weight).reshape(seq_length, heads_local, NOPE + VD)
    rotary_heads = jnp.broadcast_to(
        rot_seq.astype(jnp.float32)[:, None, :], (seq_length, heads_local, ROPE)
    )
    key_full = jnp.concatenate([key_value[..., :NOPE], rotary_heads], axis=-1).astype(jnp.bfloat16)
    values_low = key_value[..., NOPE:].astype(jnp.bfloat16)
    row_pos = positions[:, None]
    col_pos = positions[None, :]
    visible = (col_pos <= row_pos) | (col_pos < prefix_len[0])
    query_groups = split_heads(query_full, groups)
    key_groups = split_heads(key_full, groups)
    value_groups = split_heads(values_low, groups)
    heads_groups, log_totals = lax.map(
        partial(attend_forward, visible=visible, scale=scale),
        (query_groups, key_groups, value_groups),
    )
    heads_low = join_heads(heads_groups).astype(jnp.bfloat16).reshape(seq_length, heads_local * VD)
    attn_own = lax.psum_scatter(
        plain_mul(heads_low, out_weight).astype(jnp.bfloat16),
        "tensor",
        scatter_dimension=0,
        tiled=True,
    ).astype(jnp.float32)
    mid_resid = resid_in + RESID * attn_own
    mlp_normed = norm_apply(mid_resid, gain_mlp).astype(jnp.bfloat16)
    mlp_seq = lax.all_gather(mlp_normed, "tensor", axis=0, tiled=True)
    gate_proj = plain_mul(mlp_seq, gate_weight)
    up_proj = plain_mul(mlp_seq, upper_weight)
    act_low = gated(gate_proj, up_proj).astype(jnp.bfloat16)
    mlp_own = lax.psum_scatter(
        plain_mul(act_low, down_weight).astype(jnp.bfloat16),
        "tensor",
        scatter_dimension=0,
        tiled=True,
    ).astype(jnp.float32)
    layer_out = (mid_resid + RESID * mlp_own).astype(jnp.bfloat16)
    q_back, kv_back, out_back, gate_back, upper_back, down_back = (
        lax.all_gather(q_up, "dp", axis=0, tiled=True),
        lax.all_gather(kv_up, "dp", axis=0, tiled=True),
        lax.all_gather(o_proj, "dp", axis=1, tiled=True),
        lax.all_gather(w_gate, "dp", axis=0, tiled=True),
        lax.all_gather(w_up, "dp", axis=0, tiled=True),
        lax.all_gather(w_down, "dp", axis=1, tiled=True),
    )
    grad_out = cotangent.astype(jnp.float32)
    mlp_back = lax.all_gather((RESID * grad_out).astype(jnp.bfloat16), "tensor", axis=0, tiled=True)
    d_act = mul_trans(mlp_back, down_back)
    grad_down = trans_mul(act_low, mlp_back)
    _, act_pullback = jax.vjp(gated, gate_proj, up_proj)
    d_gate, d_upper = act_pullback(d_act)
    d_gate_low = d_gate.astype(jnp.bfloat16)
    d_upper_low = d_upper.astype(jnp.bfloat16)
    d_mlp_terms = mul_trans(d_gate_low, gate_back) + mul_trans(d_upper_low, upper_back)
    grad_gate = trans_mul(mlp_seq, d_gate_low)
    grad_upper = trans_mul(mlp_seq, d_upper_low)
    d_mlp_own = lax.psum_scatter(
        d_mlp_terms.astype(jnp.bfloat16), "tensor", scatter_dimension=0, tiled=True
    ).astype(jnp.float32)
    _, mlp_norm_back = jax.vjp(norm_apply, mid_resid, gain_mlp)
    d_mid_norm, d_gain_mlp = mlp_norm_back(d_mlp_own)
    d_mid = grad_out + d_mid_norm
    gate_shard, upper_shard, down_shard = (
        lax.psum_scatter(grad_gate, "dp", scatter_dimension=0, tiled=True),
        lax.psum_scatter(grad_upper, "dp", scatter_dimension=0, tiled=True),
        lax.psum_scatter(grad_down, "dp", scatter_dimension=1, tiled=True),
    )
    attn_back = lax.all_gather((RESID * d_mid).astype(jnp.bfloat16), "tensor", axis=0, tiled=True)
    d_heads = (
        mul_trans(attn_back, out_back).astype(jnp.bfloat16).reshape(seq_length, heads_local, VD)
    )
    grad_out_proj = trans_mul(heads_low, attn_back)
    d_query_groups, d_key_groups, d_value_groups = lax.map(
        partial(attend_backward, visible=visible, scale=scale),
        (query_groups, key_groups, value_groups, log_totals, split_heads(d_heads, groups)),
    )
    d_query = join_heads(d_query_groups)
    d_key = join_heads(d_key_groups)
    d_values = join_heads(d_value_groups)
    d_query_rot = rotate_back(q_rot_in, positions, d_query[..., NOPE:])
    d_query_low = (
        jnp.concatenate([d_query[..., :NOPE], d_query_rot], axis=-1)
        .astype(jnp.bfloat16)
        .reshape(seq_length, heads_local * head_qk)
    )
    d_kv_low = (
        jnp.concatenate([d_key[..., :NOPE], d_values], axis=-1)
        .astype(jnp.bfloat16)
        .reshape(seq_length, heads_local * (NOPE + VD))
    )
    d_rot_terms = jnp.sum(d_key[..., NOPE:], axis=1)
    d_q_terms = mul_trans(d_query_low, q_back)
    d_kv_terms = mul_trans(d_kv_low, kv_back)
    grad_q_up = trans_mul(q_seq, d_query_low)
    grad_kv_up = trans_mul(kv_seq, d_kv_low)
    d_q_own, d_kv_own, d_rot_own = (
        lax.psum_scatter(
            d_q_terms.astype(jnp.bfloat16), "tensor", scatter_dimension=0, tiled=True
        ).astype(jnp.float32),
        lax.psum_scatter(
            d_kv_terms.astype(jnp.bfloat16), "tensor", scatter_dimension=0, tiled=True
        ).astype(jnp.float32),
        lax.psum_scatter(
            d_rot_terms.astype(jnp.bfloat16), "tensor", scatter_dimension=0, tiled=True
        ).astype(jnp.float32),
    )
    qup_shard, kvup_shard, out_shard = (
        lax.psum_scatter(grad_q_up, "dp", scatter_dimension=0, tiled=True),
        lax.psum_scatter(grad_kv_up, "dp", scatter_dimension=0, tiled=True),
        lax.psum_scatter(grad_out_proj, "dp", scatter_dimension=1, tiled=True),
    )
    _, q_norm_back = jax.vjp(norm_apply, q_latent, gain_q)
    d_q_latent, d_gain_q = q_norm_back(d_q_own)
    _, kv_norm_back = jax.vjp(norm_apply, kv_latent[:, :KR], gain_kv)
    d_kv_latent, d_gain_kv = kv_norm_back(d_kv_own)
    d_rot_raw = rotate_back(kv_latent[:, KR:], own_pos, d_rot_own)
    d_q_low = d_q_latent.astype(jnp.bfloat16)
    d_kvall_low = jnp.concatenate([d_kv_latent, d_rot_raw], axis=-1).astype(jnp.bfloat16)
    d_x_normed = mul_trans(d_q_low, qdown_weight) + mul_trans(d_kvall_low, kvdown_weight)
    grad_qdown = trans_mul(x_normed, d_q_low)
    grad_kvdown = trans_mul(x_normed, d_kvall_low)
    _, x_norm_back = jax.vjp(norm_apply, resid_in, gain_attn)
    d_x_norm, d_gain_attn = x_norm_back(d_x_normed)
    grad_input = d_mid + d_x_norm
    small_shards = (
        lax.psum_scatter(d_gain_attn, ("dp", "tensor"), scatter_dimension=0, tiled=True),
        lax.psum_scatter(grad_qdown, ("dp", "tensor"), scatter_dimension=0, tiled=True),
        lax.psum_scatter(d_gain_q, ("dp", "tensor"), scatter_dimension=0, tiled=True),
        lax.psum_scatter(grad_kvdown, ("dp", "tensor"), scatter_dimension=0, tiled=True),
        lax.psum_scatter(d_gain_kv, ("dp", "tensor"), scatter_dimension=0, tiled=True),
        lax.psum_scatter(d_gain_mlp, ("dp", "tensor"), scatter_dimension=0, tiled=True),
    )
    return (
        layer_out,
        grad_input,
        small_shards[0],
        small_shards[1],
        small_shards[2],
        small_shards[3],
        small_shards[4],
        qup_shard,
        kvup_shard,
        out_shard,
        small_shards[5],
        gate_shard,
        upper_shard,
        down_shard,
    )


def solution(mesh):
    return jax.shard_map(
        body,
        mesh=mesh,
        in_specs=(
            P(("dp", "tensor"), None),
            P("dp"),
            P(("dp", "tensor")),
            P(("dp", "tensor"), None),
            P(("dp", "tensor")),
            P(("dp", "tensor"), None),
            P(("dp", "tensor")),
            P("dp", "tensor"),
            P("dp", "tensor"),
            P("tensor", "dp"),
            P(("dp", "tensor")),
            P("dp", "tensor"),
            P("dp", "tensor"),
            P("tensor", "dp"),
            P(("dp", "tensor"), None),
        ),
        out_specs=(
            P(("dp", "tensor"), None),
            P(("dp", "tensor"), None),
            P(("dp", "tensor")),
            P(("dp", "tensor"), None),
            P(("dp", "tensor")),
            P(("dp", "tensor"), None),
            P(("dp", "tensor")),
            P("dp", "tensor"),
            P("dp", "tensor"),
            P("tensor", "dp"),
            P(("dp", "tensor")),
            P("dp", "tensor"),
            P("dp", "tensor"),
            P("tensor", "dp"),
        ),
        check_vma=False,
    )
```

profile of v0, /device:TPU:0, one launch (start us, length us, event | category | flops | bytes accessed | tf_op | source)
XLA Modules:
  0.0 3912.9 jit_solution(11193796481516179937)
XLA Ops:
  14.0 42.3 %all-reduce.13 = (bf16[2560]{0:T(1024)(128)(2,1)S(1)}, bf16[2560]{0:T(1024)(128)(2,1)S(1)}, bf16[256]{0:T(256)(128)(2,1)S(1)}, bf16[768]{0:T(1024)(128)(2,1)S(1)}) all-reduce(bf16[2560]{0:T(1024)(128)(2,1)S(1)} %dynamic-update-slice.3, bf16[2560]{0:T(1024)(128)(2,1)S(1)} %dynamic-update-slice, ...), channel_id=1, replica_groups=mesh['dp'=16,'tensor'=2] {'dp','tensor'}, use_global_device_ids=true, to_apply=%add.7 | all-reduce | flops 6144 | bytes 24576
  57.6 12.2 all-gather.12.cloned.1.call-done
  69.8 2.4 fusion.110
  74.3 54.0 %all-gather.14.cloned.1.call-done = bf16[256,2560]{1,0:T(8,128)(2,1)} async-done(((bf16[16,2560]{1,0:T(8,128)(2,1)}), bf16[256,2560]{1,0:T(8,128)(2,1)}) %all-gather.14.cloned.1.call-update) | async-done | bytes 1310736 | tf_op jit(solution)/shard_map/all_gather | solution.py:161
  128.2 2.9 convolution_convert_fusion.2
  135.8 55.5 %all-gather.16.cloned.1.call-done = bf16[2560,768]{1,0:T(8,128)(2,1)} async-done(((bf16[80,768]{1,0:T(8,128)(2,1)}), bf16[2560,768]{1,0:T(8,128)(2,1)}) %all-gather.16.cloned.1.call-update) | async-done | bytes 3932176 | tf_op jit(solution)/shard_map/all_gather | solution.py:147
  191.3 2.9 multiply_reduce_fusion.2
  194.3 2.1 all_gather.67
  196.4 62.4 %all-gather.18.cloned.1.call-done = bf16[768,1920]{1,0:T(8,128)(2,1)} async-done(((bf16[48,1920]{1,0:T(8,128)(2,1)}), bf16[768,1920]{1,0:T(8,128)(2,1)}) %all-gather.18.cloned.1.call-update) | async-done | bytes 2949136 | tf_op jit(solution)/shard_map/all_gather | solution.py:160
  258.9 3.1 fusion.114
  263.4 17.1 while.28
  280.5 76.7 %all-gather.20.cloned.1.call-done = bf16[1280,2560]{0,1:T(8,128)(2,1)} async-done(((bf16[1280,160]{0,1:T(8,128)(2,1)}), bf16[1280,2560]{0,1:T(8,128)(2,1)}) %all-gather.20.cloned.1.call-update) | async-done | bytes 6553616 | tf_op jit(solution)/shard_map/all_gather | solution.py:162
  357.2 5.8 convolution_convert_fusion.1
  363.1 7.1 reduce-scatter.19.cloned.1.call-done
  376.5 7.2 all-gather.22.cloned.1.call-done
  383.7 192.2 %all-gather.24.cloned.1.call-done = bf16[2560,3200]{1,0:T(8,128)(2,1)} async-done(((bf16[160,3200]{1,0:T(8,128)(2,1)}), bf16[2560,3200]{1,0:T(8,128)(2,1)}) %all-gather.24.cloned.1.call-update) | async-done | bytes 16384016 | tf_op jit(solution)/shard_map/all_gather | solution.py:163
  575.9 12.3 fusion.115
  588.2 176.9 %all-gather.26.cloned.1.call-done = bf16[2560,3200]{1,0:T(8,128)(2,1)} async-done(((bf16[160,3200]{1,0:T(8,128)(2,1)}), bf16[2560,3200]{1,0:T(8,128)(2,1)}) %all-gather.26.cloned.1.call-update) | async-done | bytes 16384016 | tf_op jit(solution)/shard_map/all_gather | solution.py:164
  765.1 10.0 fusion.116
  775.1 191.9 %all-gather.28.cloned.1.call-done = bf16[3200,2560]{0,1:T(8,128)(2,1)} async-done(((bf16[3200,160]{0,1:T(8,128)(2,1)}), bf16[3200,2560]{0,1:T(8,128)(2,1)}) %all-gather.28.cloned.1.call-update) | async-done | bytes 16384016 | tf_op jit(solution)/shard_map/all_gather | solution.py:165
  967.0 15.9 multiply_convert_fusion
  982.8 12.3 fusion.117
  995.1 12.5 fusion.61
  1007.7 8.6 all-gather.32.cloned.1.call-start
  1016.3 2.4 fusion.70
  1020.2 9.2 all-gather.32.cloned.1.call-done
  1029.4 5.1 convolution_convert_fusion.3
  1036.5 48.0 %while.29 = (s32[]{:T(128)}, f32[5,256,4,96]{1,3,2,0:T(8,128)}, f32[5,256,4,96]{1,3,2,0:T(8,128)}, bf16[5,256,4,64]{1,3,2,0:T(8,128)(2,1)}, bf16[5,256,4,96]{1,3...) while((s32[]{:T(128)}, f32[5,256,4,96]{1,3,2,0:T(8,128)}, ...), condition=%wide.region_14.15_spmd.clone, body=%wide.region_12.14_spmd.clone.sunk | while | flops 221907456 | bytes 13913521 | solution.py:257
  1085.9 2.3 slice.88
  1094.6 3.9 convolution_convert_fusion.4
  1098.7 11.9 convolution_convert_fusion
  1113.0 2.6 fusion.84
  1123.0 4.4 fusion.106
  1128.7 3.6 fusion.119
  1133.4 8.0 fusion.121
  1142.7 15.0 fusion.122
  1157.7 15.0 fusion.123
  1174.2 14.9 fusion.124
  1189.2 3.6 fusion.118
  1194.8 41.1 %all-reduce.12 = (f32[2560]{0:T(1024)S(1)}, f32[768]{0:T(1024)S(1)}, f32[256]{0:T(256)S(1)}, f32[2560]{0:T(1024)S(1)}) all-reduce(f32[2560]{0:T(1024)S(1)} %get-tuple-element.153, f32[768]{0:T(1024)S(1)} %get-tuple-element.155, f32[256]{0:T(256)S(1)} %get-tuple-element.157, ...), channel_id=8, replica_groups=mesh['dp'=16,'tensor'=2] {'dp','tensor'}, use_global_device_ids=true, to_apply=%region_23.24.clone | all-reduce | flops 6144 | bytes 49152
  1238.4 3.8 fusion.71
  1244.0 83.9 %reduce-scatter.33.cloned.1.call-done = f32[16,2560]{1,0:T(8,128)} async-done(((f32[256,2560]{1,0:T(8,128)}), f32[16,2560]{1,0:T(8,128)}) %reduce-scatter.33.cloned.1.call-update) | async-done | bytes 163856 | tf_op jit(solution)/shard_map/reduce_scatter | solution.py:293
  1327.9 126.2 %reduce-scatter.27.cloned.1.call-done = f32[80,768]{1,0:T(8,128)} async-done(((f32[2560,768]{1,0:T(8,128)}), f32[80,768]{1,0:T(8,128)}) %reduce-scatter.27.cloned.1.call-update) | async-done | bytes 245776 | tf_op jit(solution)/shard_map/reduce_scatter | solution.py:311
  1454.1 149.5 %reduce-scatter.31.cloned.1.call-done = f32[48,1920]{1,0:T(8,128)} async-done(((f32[768,1920]{1,0:T(8,128)}), f32[48,1920]{1,0:T(8,128)}) %reduce-scatter.31.cloned.1.call-update) | async-done | bytes 368656 | tf_op jit(solution)/shard_map/reduce_scatter | solution.py:292
  1603.6 274.4 %reduce-scatter.35.cloned.1.call-done = f32[1280,160]{0,1:T(8,128)} async-done(((f32[1280,2560]{0,1:T(8,128)}), f32[1280,160]{0,1:T(8,128)}) %reduce-scatter.35.cloned.1.call-update) | async-done | bytes 819216 | tf_op jit(solution)/shard_map/reduce_scatter | solution.py:294
  1878.0 675.7 %reduce-scatter.37.cloned.1.call-done = f32[160,3200]{1,0:T(8,128)} async-done(((f32[2560,3200]{1,0:T(8,128)}), f32[160,3200]{1,0:T(8,128)}) %reduce-scatter.37.cloned.1.call-update) | async-done | bytes 2048016 | tf_op jit(solution)/shard_map/reduce_scatter | solution.py:248
  2553.7 676.0 %reduce-scatter.39.cloned.1.call-done = f32[160,3200]{1,0:T(8,128)} async-done(((f32[2560,3200]{1,0:T(8,128)}), f32[160,3200]{1,0:T(8,128)}) %reduce-scatter.39.cloned.1.call-update) | async-done | bytes 2048016 | tf_op jit(solution)/shard_map/reduce_scatter | solution.py:249
  3229.7 676.3 %reduce-scatter.41.cloned.1.call-done = f32[3200,160]{0,1:T(8,128)} async-done(((f32[3200,2560]{0,1:T(8,128)}), f32[3200,160]{0,1:T(8,128)}) %reduce-scatter.41.cloned.1.call-update) | async-done | bytes 2048016 | tf_op jit(solution)/shard_map/reduce_scatter | solution.py:250
  (317 shorter events, 118.8 us)
Async XLA Ops:
  7.2 50.0 %copy-start = (bf16[128,2560]{1,0:T(8,128)(2,1)S(1)}, bf16[128,2560]{1,0:T(8,128)(2,1)}, u32[]{:S(2)}) copy-start(bf16[128,2560]{1,0:T(8,128)(2,1)} %param.19) | copy-start | bytes 1966084
  7.2 62.6 %all-gather.12.cloned.1.call-start = ((), (), s32[]{:S(2)}) async-start(), calls=%async_computation.14 | async-start | bytes 2027520 | tf_op jit(solution)/shard_map/all_gather | solution.py:149
  7.9 120.3 %all-gather.14.cloned.1.call-start = ((), (), s32[]{:S(2)}) async-start(), calls=%async_computation.15 | async-start | bytes 1392640 | tf_op jit(solution)/shard_map/all_gather | solution.py:161
  8.7 182.6 %all-gather.16.cloned.1.call-start = ((), (), s32[]{:S(2)}) async-start(), calls=%async_computation.16 | async-start | bytes 4055040 | tf_op jit(solution)/shard_map/all_gather | solution.py:147
  9.4 249.4 %all-gather.18.cloned.1.call-start = ((), (), s32[]{:S(2)}) async-start(), calls=%async_computation.17 | async-start | bytes 3133440 | tf_op jit(solution)/shard_map/all_gather | solution.py:160
  10.0 347.2 %all-gather.20.cloned.1.call-start = ((), (), s32[]{:S(2)}) async-start(), calls=%async_computation.18 | async-start | bytes 6963200 | tf_op jit(solution)/shard_map/all_gather | solution.py:162
  10.6 359.7 %reduce-scatter.19.cloned.1.call-start = ((), (), s32[]{:S(2)}) async-start(), calls=%async_computation.19 | async-start | bytes 1966080 | tf_op jit(solution)/shard_map/reduce_scatter | solution.py:203
  56.4 134.9 %copy-start.23 = (f32[2560]{0:T(1024)}, f32[2560]{0:T(1024)S(1)}, u32[]{:S(2)}) copy-start(f32[2560]{0:T(1024)S(1)} %convert_element_type.158) | copy-start | bytes 30724
  56.4 137.8 %copy-start.29 = (f32[768]{0:T(1024)}, f32[768]{0:T(1024)S(1)}, u32[]{:S(2)}) copy-start(f32[768]{0:T(1024)S(1)} %convert_element_type.162) | copy-start | bytes 9220
  57.1 75.7 %copy-start.42 = (f32[16]{0:T(128)}, f32[16]{0:T(128)S(1)}, u32[]{:S(2)}) copy-start(f32[16]{0:T(128)S(1)} %multiply_power_fusion) | copy-start | bytes 196
  57.1 75.7 %copy-start.48 = (f32[128]{0:T(128)}, f32[128]{0:T(128)S(1)}, u32[]{:S(2)}) copy-start(f32[128]{0:T(128)S(1)} %add_convert_fusion.5) | copy-start | bytes 1540
  57.4 133.9 %copy-start.34 = (f32[128]{0:T(128)}, f32[128]{0:T(128)S(1)}, u32[]{:S(2)}) copy-start(f32[128]{0:T(128)S(1)} %fusion.99) | copy-start | bytes 1540
  57.5 204.6 %copy-start.27 = (f32[256,16]{0,1:T(8,128)}, f32[256,16]{0,1:T(8,128)S(1)}, u32[]{:S(2)}) copy-start(f32[256,16]{0,1:T(8,128)S(1)} %get-tuple-element.218) | copy-start | bytes 49156
  57.6 204.6 %copy-start.28 = (f32[256,16]{0,1:T(8,128)}, f32[256,16]{0,1:T(8,128)S(1)}, u32[]{:S(2)}) copy-start(f32[256,16]{0,1:T(8,128)S(1)} %get-tuple-element.219) | copy-start | bytes 49156
  72.2 58.9 %copy-start.52 = (f32[128]{0:T(128)}, f32[128]{0:T(128)S(1)}, u32[]{:S(2)}) copy-start(f32[128]{0:T(128)S(1)} %multiply_reduce_fusion.3) | copy-start | bytes 1540
  72.3 58.9 %copy-start.40 = (f32[128]{0:T(128)}, f32[128]{0:T(128)S(1)}, u32[]{:S(2)}) copy-start(f32[128]{0:T(128)S(1)} %fusion.100) | copy-start | bytes 1540
  74.3 56.9 %copy-start.20 = (bf16[256,256]{0,1:T(8,128)(2,1)}, bf16[256,256]{0,1:T(8,128)(2,1)S(1)}, u32[]{:S(2)}) copy-start(bf16[256,256]{0,1:T(8,128)(2,1)S(1)} %all_gather.63) | copy-start | bytes 393220
  194.2 67.8 %copy-start.5 = (f32[128,768]{1,0:T(8,128)}, f32[128,768]{1,0:T(8,128)S(1)}, u32[]{:S(2)}) copy-start(f32[128,768]{1,0:T(8,128)S(1)} %get-tuple-element.221) | copy-start | bytes 1179652
  194.2 67.8 %copy-start.50 = (f32[128]{0:T(128)}, f32[128]{0:T(128)S(1)}, u32[]{:S(2)}) copy-start(f32[128]{0:T(128)S(1)} %get-tuple-element.220) | copy-start | bytes 1540
  194.2 67.8 %copy-start.44 = (f32[128]{0:T(128)}, f32[128]{0:T(128)S(1)}, u32[]{:S(2)}) copy-start(f32[128]{0:T(128)S(1)} %fusion.101) | copy-start | bytes 1540
  196.4 65.6 %copy-start.11 = (bf16[256,768]{1,0:T(8,128)(2,1)}, bf16[256,768]{1,0:T(8,128)(2,1)S(1)}, u32[]{:S(2)}) copy-start(bf16[256,768]{1,0:T(8,128)(2,1)S(1)} %all_gather.67) | copy-start | bytes 1179652
  280.5 82.5 %copy-start.13 = (bf16[5,256,4,96]{1,3,2,0:T(8,128)(2,1)}, bf16[5,256,4,96]{1,3,2,0:T(8,128)(2,1)S(1)}, u32[]{:S(2)}) copy-start(bf16[5,256,4,96]{1,3,2,0:T(8,128)(2,1)S(1)} %get-tuple-element.434) | copy-start | bytes 2949124
  280.5 82.5 %copy-start.15 = (bf16[5,256,4,64]{1,3,2,0:T(8,128)(2,1)}, bf16[5,256,4,64]{1,3,2,0:T(8,128)(2,1)S(1)}, u32[]{:S(2)}) copy-start(bf16[5,256,4,64]{1,3,2,0:T(8,128)(2,1)S(1)} %get-tuple-element.106) | copy-start | bytes 1966084
  363.1 20.6 all-gather.22.cloned.1.call-start
  363.1 655.5 %copy-start.25 = (f32[2560]{0:T(1024)}, f32[2560]{0:T(1024)S(1)}, u32[]{:S(2)}) copy-start(f32[2560]{0:T(1024)S(1)} %convert_element_type.171) | copy-start | bytes 30724
  371.8 646.9 %copy-start.38 = (f32[128]{0:T(128)}, f32[128]{0:T(128)S(1)}, u32[]{:S(2)}) copy-start(f32[128]{0:T(128)S(1)} %fusion.102) | copy-start | bytes 1540
  372.9 203.0 %all-gather.24.cloned.1.call-start = ((), (), s32[]{:S(2)}) async-start(), calls=%async_computation.21 | async-start | bytes 17408000 | tf_op jit(solution)/shard_map/all_gather | solution.py:163
  373.7 391.4 %all-gather.26.cloned.1.call-start = ((), (), s32[]{:S(2)}) async-start(), calls=%async_computation.22 | async-start | bytes 17408000 | tf_op jit(solution)/shard_map/all_gather | solution.py:164
  374.4 400.7 %all-gather.30.cloned.1.call-start = ((), (), s32[]{:S(2)}) async-start(), calls=%async_computation.25 | async-start | bytes 1966080 | tf_op jit(solution)/shard_map/all_gather | solution.py:231
  375.4 591.6 %all-gather.28.cloned.1.call-start = ((), (), s32[]{:S(2)}) async-start(), calls=%async_computation.23 | async-start | bytes 17408000 | tf_op jit(solution)/shard_map/all_gather | solution.py:165
  376.2 640.1 %reduce-scatter.23.cloned.1.call-start = ((), (), s32[]{:S(2)}) async-start(), calls=%async_computation.26 | async-start | bytes 1966080 | tf_op jit(solution)/shard_map/reduce_scatter | solution.py:241
  383.7 381.4 %copy-start.3 = (bf16[256,2560]{1,0:T(8,128)(2,1)S(1)}, bf16[256,2560]{1,0:T(8,128)(2,1)}, u32[]{:S(2)}) copy-start(bf16[256,2560]{1,0:T(8,128)(2,1)} %all-gather.22.cloned.1.call-done) | copy-start | bytes 3932164
  1007.7 21.7 all-gather.32.cloned.1.call-start
  1020.1 90.5 %reduce-scatter.45.cloned.1.call-start = ((), (), s32[]{:S(2)}) async-start(), calls=%async_computation.38 | async-start | bytes 98304
  1089.0 22.6 reduce-scatter.43.cloned.1.call-start
  1094.6 26.2 reduce-scatter.25.cloned.1.call-start
  1098.6 139.7 %reduce-scatter.21.cloned.1.call-start = ((), (), s32[]{:S(2)}) async-start(), calls=%async_computation.24 | async-start | bytes 1966080 | tf_op jit(solution)/shard_map/reduce_scatter | solution.py:215
  1110.6 133.4 %reduce-scatter.29.cloned.1.call-start = ((), (), s32[]{:S(2)}) async-start(), calls=%async_computation.30 | async-start | bytes 4055040 | tf_op jit(solution)/shard_map/reduce_scatter | solution.py:313
  1115.6 212.3 %reduce-scatter.33.cloned.1.call-start = ((), (), s32[]{:S(2)}) async-start(), calls=%async_computation.32 | async-start | bytes 2785280 | tf_op jit(solution)/shard_map/reduce_scatter | solution.py:293
  1118.6 335.5 %reduce-scatter.27.cloned.1.call-start = ((), (), s32[]{:S(2)}) async-start(), calls=%async_computation.29 | async-start | bytes 8110080 | tf_op jit(solution)/shard_map/reduce_scatter | solution.py:311
  1127.4 476.2 %reduce-scatter.31.cloned.1.call-start = ((), (), s32[]{:S(2)}) async-start(), calls=%async_computation.31 | async-start | bytes 6266880 | tf_op jit(solution)/shard_map/reduce_scatter | solution.py:292
  1132.3 745.7 %reduce-scatter.35.cloned.1.call-start = ((), (), s32[]{:S(2)}) async-start(), calls=%async_computation.33 | async-start | bytes 13926400 | tf_op jit(solution)/shard_map/reduce_scatter | solution.py:294
  1141.4 1412.3 %reduce-scatter.37.cloned.1.call-start = ((), (), s32[]{:S(2)}) async-start(), calls=%async_computation.34 | async-start | bytes 34816000 | tf_op jit(solution)/shard_map/reduce_scatter | solution.py:248
  1157.7 2072.0 %reduce-scatter.39.cloned.1.call-start = ((), (), s32[]{:S(2)}) async-start(), calls=%async_computation.35 | async-start | bytes 34816000 | tf_op jit(solution)/shard_map/reduce_scatter | solution.py:249
  1172.8 2733.2 %reduce-scatter.41.cloned.1.call-start = ((), (), s32[]{:S(2)}) async-start(), calls=%async_computation.36 | async-start | bytes 34816000 | tf_op jit(solution)/shard_map/reduce_scatter | solution.py:250
  1192.8 45.5 %copy-start.8 = (bf16[128,2560]{1,0:T(8,128)(2,1)S(1)}, bf16[128,2560]{1,0:T(8,128)(2,1)}, u32[]{:S(2)}) copy-start(bf16[128,2560]{1,0:T(8,128)(2,1)} %reduce-scatter.23.cloned.1.call-done) | copy-start | bytes 1966084
  1192.9 45.5 %copy-start.10 = (bf16[128,2560]{1,0:T(8,128)(2,1)S(1)}, bf16[128,2560]{1,0:T(8,128)(2,1)}, u32[]{:S(2)}) copy-start(bf16[128,2560]{1,0:T(8,128)(2,1)} %param.33) | copy-start | bytes 1966084
  1192.9 45.5 %copy-start.26 = (f32[2560]{0:T(1024)S(1)}, f32[2560]{0:T(1024)}, u32[]{:S(2)}) copy-start(f32[2560]{0:T(1024)} %copy-done.25) | copy-start | bytes 30724
  (41 other events, 235.0 us)
Sparse Core Ops, SparseCore 0:
  10.9 58.8 all-gather.11
  72.5 55.6 all-gather.13
  131.2 60.0 all-gather.15
  193.9 64.9 all-gather.17
  261.4 95.7 all-gather.19
  363.2 6.9 reduce-scatter.18
  373.0 10.6 all-gather.21
  386.7 189.0 all-gather.23
  578.9 186.1 all-gather.25
  767.1 7.5 all-gather.29
  777.8 189.0 all-gather.27
  1007.8 6.9 reduce-scatter.22
  1020.2 9.1 all-gather.31
  1089.2 8.6 reduce-scatter.44
  1100.5 8.6 reduce-scatter.42
  1111.8 8.9 reduce-scatter.24
  1123.0 9.9 reduce-scatter.20
  1138.8 105.1 reduce-scatter.28
  1246.8 81.0 reduce-scatter.32
  1334.0 120.0 reduce-scatter.26
  1460.8 142.7 reduce-scatter.30
  1606.6 271.3 reduce-scatter.34
  1881.1 672.5 reduce-scatter.36
  2556.5 673.1 reduce-scatter.38
  3232.7 673.1 reduce-scatter.40
where the time goes:
time: 3930 us; the launch traced here: 3910 us
  waiting for transfers between devices  3520 us (90%)
  matrix products  230 us (6%)
  blocking collectives  89.3 us (2%)
    reduce_scatter x1, waiting for transfers between devices, body(): lax.psum_scatter(grad_down, 'dp', scatter_dimension=1, tiled=True)  676 us
    reduce_scatter x1, waiting for transfers between devices, body(): lax.psum_scatter(grad_upper, 'dp', scatter_dimension=0, tiled=True)  676 us
    reduce_scatter x1, waiting for transfers between devices, body(): lax.psum_scatter(grad_gate, 'dp', scatter_dimension=0, tiled=True)  676 us
    reduce_scatter x1, waiting for transfers between devices, body(): lax.psum_scatter(grad_out_proj, 'dp', scatter_dimension=1, tiled=True)  274 us
    all_gather x1, waiting for transfers between devices, body(): lax.all_gather(w_gate, 'dp', axis=0, tiled=True)  192 us
    all_gather x1, waiting for transfers between devices, body(): lax.all_gather(w_down, 'dp', axis=1, tiled=True)  192 us
    all_gather x1, waiting for transfers between devices, body(): lax.all_gather(w_up, 'dp', axis=0, tiled=True)  177 us
    reduce_scatter x1, waiting for transfers between devices, body(): lax.psum_scatter(grad_q_up, 'dp', scatter_dimension=0, tiled=True)  150 us
  transfers between devices with their start and end apart: 25, of which 20 were waited for; matrix products, arithmetic and copies ran while one was open for 4% of the time, Pallas kernels for 0%

commit v1 on v0

v1 whole, which is shorter than its diff:
```python
from functools import partial
import math

import jax
import jax.numpy as jnp
from jax import lax
from jax.sharding import PartitionSpec as P

NOPE = 64
ROPE = 32
VD = 64
KR = 256
COLUMN = 4


EPS = 1e-05
RESID = 1.4 / math.sqrt(62.0)
THETA = 10000.0
NEG_FILL = -1e30


def norm_apply(values, gain):
    inverse = lax.rsqrt(jnp.mean(values * values, axis=-1, keepdims=True) + EPS)
    return values * inverse * gain


def rotate(values, positions):
    width_half = values.shape[-1] // 2
    frequency = THETA ** (-2.0 * jnp.arange(width_half, dtype=jnp.float32) / values.shape[-1])
    angles = positions.astype(jnp.float32)[:, None] * frequency[None, :]
    extra_dims = (1,) * (values.ndim - 2)
    cosine = jnp.cos(angles).reshape(angles.shape[:1] + extra_dims + angles.shape[1:])
    sine = jnp.sin(angles).reshape(angles.shape[:1] + extra_dims + angles.shape[1:])
    lower_part = values[..., :width_half]
    upper_part = values[..., width_half:]
    return jnp.concatenate(
        [lower_part * cosine - upper_part * sine, upper_part * cosine + lower_part * sine], axis=-1
    )


def rotate_back(values, positions, grads):
    _, pullback = jax.vjp(partial(rotate, positions=positions), values)
    return pullback(grads)[0]


def swish(values):
    return values / (1.0 + jnp.exp(-values))


def gated(gate_in, upper_in):
    return swish(gate_in) * upper_in


def plain_mul(left, right):
    return jnp.dot(left, right, preferred_element_type=jnp.float32)


def mul_trans(left, right):
    return lax.dot_general(
        left, right, (((1,), (1,)), ((), ())), preferred_element_type=jnp.float32
    )


def trans_mul(left, right):
    return lax.dot_general(
        left, right, (((0,), (0,)), ((), ())), preferred_element_type=jnp.float32
    )


def split_heads(values, groups):
    seq_length, heads_local, width = values.shape
    return jnp.moveaxis(values.reshape(seq_length, groups, heads_local // groups, width), 1, 0)


def join_heads(values):
    groups, seq_length, group_heads, width = values.shape
    return jnp.moveaxis(values, 0, 1).reshape(seq_length, groups * group_heads, width)


def masked_scores(query_part, key_part, visible, scale):
    scores = (
        jnp.einsum("qhd,khd->hqk", query_part, key_part, preferred_element_type=jnp.float32) * scale
    )
    return jnp.where(visible[None], scores, NEG_FILL)


def attend_forward(pieces, visible, scale):
    query_part, key_part, value_part = pieces
    masked = masked_scores(query_part, key_part, visible, scale)
    row_peak = jnp.max(masked, axis=-1, keepdims=True)
    exp_scores = jnp.exp(masked - row_peak)
    row_total = jnp.sum(exp_scores, axis=-1, keepdims=True)
    attn_probs = exp_scores / row_total
    heads_part = jnp.einsum(
        "hqk,khd->qhd",
        attn_probs.astype(jnp.bfloat16),
        value_part,
        preferred_element_type=jnp.float32,
    )
    return (heads_part, row_peak + jnp.log(row_total))


def attend_backward(pieces, visible, scale):
    query_part, key_part, value_part, log_total, d_heads_part = pieces
    masked = masked_scores(query_part, key_part, visible, scale)
    attn_probs = jnp.exp(masked - log_total)
    probs_low = attn_probs.astype(jnp.bfloat16)
    d_probs = jnp.einsum(
        "qhd,khd->hqk", d_heads_part, value_part, preferred_element_type=jnp.float32
    )
    d_values = jnp.einsum(
        "hqk,qhd->khd", probs_low, d_heads_part, preferred_element_type=jnp.float32
    )
    row_dot = jnp.sum(attn_probs * d_probs, axis=-1, keepdims=True)
    d_scores = (attn_probs * (d_probs - row_dot) * scale).astype(jnp.bfloat16)
    d_query = jnp.einsum("hqk,khd->qhd", d_scores, key_part, preferred_element_type=jnp.float32)
    d_key = jnp.einsum("hqk,qhd->khd", d_scores, query_part, preferred_element_type=jnp.float32)
    return (d_query, d_key, d_values)


def low(values):
    return values.astype(jnp.bfloat16)


def wide(values):
    return values.astype(jnp.float32)


def core_swap(values):
    return lax.ppermute(values, "tensor", [(0, 1), (1, 0)])


def hop(values, place_of):
    count = lax.axis_size("dp")
    return lax.ppermute(values, "dp", [(place, place_of(place)) for place in range(count)])


def turn(values, steps):
    count = lax.axis_size("dp")
    rest = count // COLUMN
    return hop(values, lambda place: (place + steps * rest) % count)


def flip(values, mask):
    return hop(values, lambda place: place ^ mask)


def places():
    rest = lax.axis_size("dp") // COLUMN
    place = lax.axis_index("dp")
    return place // rest, place % rest, rest


def top_bit(mask):
    return 1 << (mask.bit_length() - 1)


def low_bit(mask):
    return mask & -mask


def by_count(rest):
    return sorted(range(1, rest), key=lambda mask: bin(mask).count("1"))


def spread_rest(values):
    _, rest_place, rest = places()
    half = COLUMN // 2
    known = {0: (values[:half], values[half:])}
    for mask in by_count(rest):
        if mask == low_bit(mask):
            got = flip(values, mask)
            known[mask] = (got[:half], got[half:])
        else:
            first, last = top_bit(mask), low_bit(mask)
            known[mask] = (
                flip(known[mask ^ first][0], first),
                flip(known[mask ^ last][1], last),
            )
    whole = jnp.zeros((COLUMN, rest) + values.shape[1:], values.dtype)
    for mask, parts in known.items():
        for start, part in zip((0, half), parts):
            whole = lax.dynamic_update_slice(
                whole,
                part[:, None],
                (start, rest_place ^ mask) + (0,) * (values.ndim - 1),
            )
    return whole


def reduce_rest(values):
    _, rest_place, rest = places()
    half = COLUMN // 2
    parts = {}
    for mask in range(rest):
        block = lax.dynamic_index_in_dim(values, rest_place ^ mask, axis=1, keepdims=False)
        parts[mask] = [block[:half], block[half:]]
    for mask in reversed(by_count(rest)):
        if mask == low_bit(mask):
            got = flip(low(jnp.concatenate(parts[mask])), mask)
            parts[0][0] += wide(got[:half])
            parts[0][1] += wide(got[half:])
        else:
            first, last = top_bit(mask), low_bit(mask)
            parts[mask ^ first][0] += wide(flip(low(parts[mask][0]), first))
            parts[mask ^ last][1] += wide(flip(low(parts[mask][1]), last))
    return jnp.concatenate(parts[0])


def place_column(blocks):
    column_place, _, _ = places()
    stacked = jnp.zeros((COLUMN,) + blocks[0].shape, blocks[0].dtype)
    for step, block in enumerate(blocks):
        stacked = lax.dynamic_update_slice(
            stacked, block[None], ((column_place - step) % COLUMN,) + (0,) * block.ndim
        )
    return stacked


def exchange_column(values):
    column_place, _, _ = places()
    blocks = []
    for step in range(COLUMN):
        block = lax.dynamic_index_in_dim(
            values, (column_place + step) % COLUMN, axis=0, keepdims=False
        )
        blocks.append(turn(block, step) if step else block)
    return blocks


def gather_dp(values):
    blocks = [values] + [turn(values, step) for step in range(1, COLUMN)]
    whole = spread_rest(place_column(blocks))
    return whole.reshape((-1,) + values.shape)


def reduce_dp(values):
    rest = lax.axis_size("dp") // COLUMN
    values = values.reshape((COLUMN, rest, -1) + values.shape[1:])
    partial_sum = reduce_rest(values)
    column_place, _, _ = places()
    total = lax.dynamic_index_in_dim(partial_sum, column_place, axis=0, keepdims=False)
    moving = low(partial_sum)
    for step in range(1, COLUMN):
        block = lax.dynamic_index_in_dim(
            moving, (column_place + step) % COLUMN, axis=0, keepdims=False
        )
        total = total + wide(turn(block, step))
    return total


def gather_units(weight):
    rows, units = weight.shape
    pieces = jnp.moveaxis(weight.reshape(rows, COLUMN, units // COLUMN), 1, 0)
    whole = spread_rest(place_column(exchange_column(pieces)))
    return whole.reshape(-1, units // COLUMN)


def reduce_units(grad):
    rest = lax.axis_size("dp") // COLUMN
    units = grad.shape[1]
    partial_sum = low(reduce_rest(grad.reshape(COLUMN, rest, -1, units)))
    pieces = place_column(exchange_column(partial_sum))
    return wide(jnp.moveaxis(pieces, 0, 1).reshape(-1, COLUMN * units))


def gather_tokens(values):
    own = jnp.stack([values] + [turn(values, step) for step in range(1, COLUMN)])
    return jnp.stack([own, core_swap(own)], axis=1).reshape(-1, values.shape[1])


def return_tokens(values, rows):
    values = values.reshape(COLUMN, 2, rows, -1)
    chip_sum = values[:, 0] + wide(core_swap(low(values[:, 1])))
    total = chip_sum[0]
    moving = low(chip_sum)
    for step in range(1, COLUMN):
        total = total + wide(turn(moving[step], -step))
    return total


def pair_tokens(values):
    return jnp.concatenate([values, core_swap(values)], axis=0)


def split_pair(values):
    rows = values.shape[0] // 2
    return values[:rows] + wide(core_swap(low(values[rows:])))


def body(
    hidden_in,
    prefix_len,
    attn_gain,
    q_down,
    q_gain,
    kv_down,
    kv_gain,
    q_up,
    kv_up,
    o_proj,
    mlp_gain,
    w_gate,
    w_up,
    w_down,
    cotangent,
):
    tensor_count = lax.axis_size("tensor")
    tensor_rank = lax.axis_index("tensor")
    dp_count = lax.axis_size("dp")
    own_rows, width = hidden_in.shape
    seq_length = own_rows * tensor_count
    q_rank = q_down.shape[1]
    down_rows = q_down.shape[0]
    q_share = q_gain.shape[0]
    kv_share = kv_gain.shape[0]
    head_qk = NOPE + ROPE
    heads_local = q_up.shape[1] // head_qk
    groups = heads_local // math.gcd(heads_local, 4)
    scale = head_qk ** (-0.5)

    def column_of(gain):
        return jnp.pad(gain, (0, down_rows - gain.shape[0]))[:, None]

    down_columns = q_rank + kv_down.shape[1]
    packed = jnp.concatenate(
        [q_down, kv_down, column_of(attn_gain), column_of(mlp_gain), column_of(q_gain), column_of(kv_gain)],
        axis=1,
    )
    core_packed = gather_dp(packed)
    other_packed = core_swap(core_packed)
    is_first = tensor_rank == 0
    all_packed = jnp.stack(
        [
            jnp.where(is_first, core_packed, other_packed),
            jnp.where(is_first, other_packed, core_packed),
        ],
        axis=1,
    )
    down_weight = all_packed.reshape(width, -1)[:, :down_columns]
    gains = wide(jnp.moveaxis(all_packed[..., down_columns:], -1, 0))
    gain_attn = gains[0].reshape(width)
    gain_mlp = gains[1].reshape(width)
    gain_q = gains[2][..., :q_share].reshape(q_rank)
    gain_kv = gains[3][..., :kv_share].reshape(KR)

    q_weight = gather_dp(q_up).reshape(q_rank, -1)
    kv_weight = gather_dp(kv_up).reshape(KR, -1)
    out_trans = gather_dp(o_proj.T).reshape(width, -1)
    gate_weight = gather_units(w_gate)
    upper_weight = gather_units(w_up)
    down_trans = gather_units(w_down.T)

    resid_in = hidden_in.astype(jnp.float32)
    x_normed = norm_apply(resid_in, gain_attn).astype(jnp.bfloat16)
    latents = plain_mul(x_normed, down_weight)
    q_latent = latents[:, :q_rank]
    kv_latent = latents[:, q_rank:]
    q_normed = norm_apply(q_latent, gain_q).astype(jnp.bfloat16)
    own_pos = tensor_rank * own_rows + jnp.arange(own_rows, dtype=jnp.int32)
    other_pos = (1 - tensor_rank) * own_rows + jnp.arange(own_rows, dtype=jnp.int32)
    kv_normed = norm_apply(kv_latent[:, :KR], gain_kv).astype(jnp.bfloat16)
    k_rotary = rotate(kv_latent[:, KR:], own_pos).astype(jnp.bfloat16)
    q_seq = pair_tokens(q_normed)
    kv_seq = pair_tokens(kv_normed)
    rot_seq = pair_tokens(k_rotary)
    positions = jnp.concatenate([own_pos, other_pos])
    query = plain_mul(q_seq, q_weight).reshape(seq_length, heads_local, head_qk)
    q_rot_in = query[..., NOPE:]
    query_full = jnp.concatenate([query[..., :NOPE], rotate(q_rot_in, positions)], axis=-1).astype(
        jnp.bfloat16
    )
    key_value = plain_mul(kv_seq, kv_weight).reshape(seq_length, heads_local, NOPE + VD)
    rotary_heads = jnp.broadcast_to(
        rot_seq.astype(jnp.float32)[:, None, :], (seq_length, heads_local, ROPE)
    )
    key_full = jnp.concatenate([key_value[..., :NOPE], rotary_heads], axis=-1).astype(jnp.bfloat16)
    values_low = key_value[..., NOPE:].astype(jnp.bfloat16)
    row_pos = positions[:, None]
    col_pos = positions[None, :]
    visible = (col_pos <= row_pos) | (col_pos < prefix_len[0])
    query_groups = split_heads(query_full, groups)
    key_groups = split_heads(key_full, groups)
    value_groups = split_heads(values_low, groups)
    heads_groups, log_totals = lax.map(
        partial(attend_forward, visible=visible, scale=scale),
        (query_groups, key_groups, value_groups),
    )
    heads_low = join_heads(heads_groups).astype(jnp.bfloat16).reshape(seq_length, heads_local * VD)
    attn_own = split_pair(mul_trans(heads_low, out_trans))
    mid_resid = resid_in + RESID * attn_own
    mlp_normed = norm_apply(mid_resid, gain_mlp).astype(jnp.bfloat16)

    grad_out = cotangent.astype(jnp.float32)
    mlp_back = gather_tokens((RESID * grad_out).astype(jnp.bfloat16))
    mlp_seq = gather_tokens(mlp_normed)
    gate_proj = plain_mul(mlp_seq, gate_weight)
    up_proj = plain_mul(mlp_seq, upper_weight)
    act_low = gated(gate_proj, up_proj).astype(jnp.bfloat16)
    d_act = plain_mul(mlp_back, down_trans)
    _, act_pullback = jax.vjp(gated, gate_proj, up_proj)
    d_gate, d_upper = act_pullback(d_act)
    d_gate_low = d_gate.astype(jnp.bfloat16)
    d_upper_low = d_upper.astype(jnp.bfloat16)
    d_mlp_terms = mul_trans(d_gate_low, gate_weight) + mul_trans(d_upper_low, upper_weight)
    d_mlp_own = return_tokens(d_mlp_terms, own_rows)
    mlp_own = return_tokens(mul_trans(act_low, down_trans), own_rows)
    layer_out = (mid_resid + RESID * mlp_own).astype(jnp.bfloat16)
    gate_shard = reduce_units(trans_mul(mlp_seq, d_gate_low))
    upper_shard = reduce_units(trans_mul(mlp_seq, d_upper_low))
    down_shard = reduce_units(trans_mul(mlp_back, act_low)).T

    _, mlp_norm_back = jax.vjp(norm_apply, mid_resid, gain_mlp)
    d_mid_norm, d_gain_mlp = mlp_norm_back(d_mlp_own)
    d_mid = grad_out + d_mid_norm
    attn_back = pair_tokens((RESID * d_mid).astype(jnp.bfloat16))
    d_heads = plain_mul(attn_back, out_trans).astype(jnp.bfloat16).reshape(
        seq_length, heads_local, VD
    )
    out_shard = reduce_dp(trans_mul(attn_back, heads_low)).T
    d_query_groups, d_key_groups, d_value_groups = lax.map(
        partial(attend_backward, visible=visible, scale=scale),
        (query_groups, key_groups, value_groups, log_totals, split_heads(d_heads, groups)),
    )
    d_query = join_heads(d_query_groups)
    d_key = join_heads(d_key_groups)
    d_values = join_heads(d_value_groups)
    d_query_rot = rotate_back(q_rot_in, positions, d_query[..., NOPE:])
    d_query_low = (
        jnp.concatenate([d_query[..., :NOPE], d_query_rot], axis=-1)
        .astype(jnp.bfloat16)
        .reshape(seq_length, heads_local * head_qk)
    )
    d_kv_low = (
        jnp.concatenate([d_key[..., :NOPE], d_values], axis=-1)
        .astype(jnp.bfloat16)
        .reshape(seq_length, heads_local * (NOPE + VD))
    )
    d_q_own = split_pair(mul_trans(d_query_low, q_weight))
    d_kv_own = split_pair(mul_trans(d_kv_low, kv_weight))
    d_rot_own = split_pair(jnp.sum(d_key[..., NOPE:], axis=1))
    qup_shard = reduce_dp(trans_mul(q_seq, d_query_low))
    kvup_shard = reduce_dp(trans_mul(kv_seq, d_kv_low))

    _, q_norm_back = jax.vjp(norm_apply, q_latent, gain_q)
    d_q_latent, d_gain_q = q_norm_back(d_q_own)
    _, kv_norm_back = jax.vjp(norm_apply, kv_latent[:, :KR], gain_kv)
    d_kv_latent, d_gain_kv = kv_norm_back(d_kv_own)
    d_rot_raw = rotate_back(kv_latent[:, KR:], own_pos, d_rot_own)
    d_latents = jnp.concatenate([d_q_latent, d_kv_latent, d_rot_raw], axis=-1).astype(jnp.bfloat16)
    d_x_normed = mul_trans(d_latents, down_weight)
    _, x_norm_back = jax.vjp(norm_apply, resid_in, gain_attn)
    d_x_norm, d_gain_attn = x_norm_back(d_x_normed)
    grad_input = d_mid + d_x_norm

    def columns_of(gain, share):
        gain = gain.reshape(-1, share)
        return jnp.pad(gain, ((0, 0), (0, down_rows - share))).reshape(width, 1)

    grad_packed = jnp.concatenate(
        [
            trans_mul(x_normed, d_latents),
            columns_of(d_gain_attn, down_rows),
            columns_of(d_gain_mlp, down_rows),
            columns_of(d_gain_q, q_share),
            columns_of(d_gain_kv, kv_share),
        ],
        axis=1,
    ).reshape(dp_count, tensor_count, down_rows, -1)
    keep = lax.dynamic_index_in_dim(grad_packed, tensor_rank, axis=1, keepdims=False)
    give = lax.dynamic_index_in_dim(grad_packed, 1 - tensor_rank, axis=1, keepdims=False)
    keep = keep + wide(core_swap(low(give)))
    packed_shard = reduce_dp(keep.reshape(dp_count * down_rows, -1))
    gain_shards = packed_shard[:, down_columns:].T

    return (
        layer_out,
        grad_input,
        gain_shards[0],
        packed_shard[:, :q_rank],
        gain_shards[2, :q_share],
        packed_shard[:, q_rank:down_columns],
        gain_shards[3, :kv_share],
        qup_shard,
        kvup_shard,
        out_shard,
        gain_shards[1],
        gate_shard,
        upper_shard,
        down_shard,
    )


def solution(mesh):
    return jax.shard_map(
        body,
        mesh=mesh,
        in_specs=(
            P(("dp", "tensor"), None),
            P("dp"),
            P(("dp", "tensor")),
            P(("dp", "tensor"), None),
            P(("dp", "tensor")),
            P(("dp", "tensor"), None),
            P(("dp", "tensor")),
            P("dp", "tensor"),
            P("dp", "tensor"),
            P("tensor", "dp"),
            P(("dp", "tensor")),
            P("dp", "tensor"),
            P("dp", "tensor"),
            P("tensor", "dp"),
            P(("dp", "tensor"), None),
        ),
        out_specs=(
            P(("dp", "tensor"), None),
            P(("dp", "tensor"), None),
            P(("dp", "tensor")),
            P(("dp", "tensor"), None),
            P(("dp", "tensor")),
            P(("dp", "tensor"), None),
            P(("dp", "tensor")),
            P("dp", "tensor"),
            P("dp", "tensor"),
            P("tensor", "dp"),
            P(("dp", "tensor")),
            P("dp", "tensor"),
            P("dp", "tensor"),
            P("tensor", "dp"),
        ),
        check_vma=False,
    )
```

time: 3930 us -> 1250 us (0.32)
  waiting for transfers between devices: 3520 us -> 448 us
  local copies, waits for them, and re-layouts: 24.7 us -> 287 us
  starting transfers between devices: 10.3 us -> 248 us
  blocking collectives: 89.3 us -> 0 us
  matrix products: 230 us -> 161 us
  other arithmetic: 26.1 us -> 89.6 us
    reduce_scatter x12 -> x0, waiting for transfers between devices: 2670 us -> none  [the longest x1 676 us: body(): lax.psum_scatter(grad_down, 'dp', scatter_dimension=1, tiled=True)]
    all_gather x11 -> x0, waiting for transfers between devices: 838 us -> none  [the longest x1 192 us: body(): lax.all_gather(w_gate, 'dp', axis=0, tiled=True)]
    ppermute x0 -> x124, waiting for transfers between devices: none -> 448 us  [the longest x110 445 us: hop(): lax.ppermute(values, 'dp', [(place, place_of(place)) for place in range(c...]
    ppermute x0 -> x124, starting transfers between devices: none -> 248 us  [the longest x110 246 us: hop(): lax.ppermute(values, 'dp', [(place, place_of(place)) for place in range(c...]
    unnamed x2 -> x0, blocking collectives: 83.5 us -> none
    dynamic_update_slice x0 -> x92, local copies, waits for them, and re-layouts: none -> 74.1 us  [the longest x55 54.2 us: spread_rest(): lax.dynamic_update_slice(whole, part[:, None], (start, rest_place ^ mask)...]
  transfers between devices with their start and end apart: 25 -> 124, of which waited for: 20 -> 51; matrix products, arithmetic and copies ran while one was open for 4% -> 35% of each run, Pallas kernels for 0% -> 0%
where the time goes in v1:
time: 1250 us; the launch traced here: 1240 us
  waiting for transfers between devices  448 us (36%)
  local copies, waits for them, and re-layouts  287 us (23%)
  starting transfers between devices  248 us (20%)
  matrix products  161 us (13%)
  other arithmetic  89.6 us (7%)
    ppermute x110, waiting for transfers between devices, hop(): lax.ppermute(values, 'dp', [(place, place_of(place)) for place in range(c...  445 us
    ppermute x110, starting transfers between devices, hop(): lax.ppermute(values, 'dp', [(place, place_of(place)) for place in range(c...  246 us
    dynamic_update_slice x55, local copies, waits for them, and re-layouts, spread_rest(): lax.dynamic_update_slice(whole, part[:, None], (start, rest_place ^ mask)...  54.2 us
    unnamed x312, local copies, waits for them, and re-layouts  48.1 us
    dot_general x7, matrix products, mul_trans(): lax.dot_general(left, right, (((1,), (1,)), ((), ())), preferred_element_...  37.4 us
    dot_general x7, matrix products, plain_mul(): return jnp.dot(left, right, preferred_element_type=jnp.float32)  37.3 us
    dot_general x7, matrix products, trans_mul(): lax.dot_general(left, right, (((0,), (0,)), ((), ())), preferred_element_...  28.8 us
  transfers between devices with their start and end apart: 124, of which 51 were waited for; matrix products, arithmetic and copies ran while one was open for 35% of the time, Pallas kernels for 0%

profile of v1, /device:TPU:0, one launch (start us, length us, event | category | flops | bytes accessed | tf_op | source)
XLA Modules:
  0.0 1237.7 jit_solution(14463154049968256874)
XLA Ops:
  99.5 9.9 collective-permute-done.38
  112.9 12.5 %collective-permute-start.52 = (bf16[160,800]{1,0:T(8,128)(2,1)S(1)}, bf16[160,800]{1,0:T(8,128)(2,1)S(1)}, u32[]{:S(2)}, u32[]{:S(2)}) collective-permute-start(bf16[160,800]{1,0:T(8,128)(2,1)S(1)} %bitcast.1157), channel_id=1, source_target_pairs={{0,16},{2,18},{4,20},{6,22},{8,24},{10,26},{12,28},{14,30},{16,0},... | collective-permute-start | bytes 768008 | tf_op jit(solution)/shard_map/ppermute | solution.py:135
  129.6 9.5 collective-permute-done.52
  170.5 15.9 %collective-permute-start.63 = (bf16[128,2560]{1,0:T(8,128)(2,1)}, bf16[128,2560]{1,0:T(8,128)(2,1)}, u32[]{:S(2)}, u32[]{:S(2)}) collective-permute-start(bf16[128,2560]{1,0:T(8,128)(2,1)} %get-tuple-element.315), channel_id=1, source_target_pairs={{0,16},{2,18},{4,20},{6,22},{8,24},{10,26},{12,28},{14,30},{16,0},... | collective-permute-start | bytes 1966088 | tf_op jit(solution)/shard_map/ppermute | solution.py:135
  206.2 7.4 collective-permute-done.15
  241.3 7.6 collective-permute-done.21
  251.0 49.8 %collective-permute-done.5 = bf16[2,80,1060]{2,1,0:T(8,128)(2,1)S(1)} collective-permute-done((bf16[2,80,1060]{2,1,0:T(8,128)(2,1)S(1)}, bf16[2,80,1060]{2,1,0:T(8,128)(2,1)S(1)}, u32[]{:S(2)}, u32[]{:S(2)}) %collective-permute-start.5) | collective-permute-done | bytes 339232 | tf_op jit(solution)/shard_map/ppermute | solution.py:135
  303.0 8.7 collective-permute-done.6
  323.6 16.6 %collective-permute-done.54 = bf16[4,160,800]{2,1,0:T(8,128)(2,1)S(1)} collective-permute-done((bf16[4,160,800]{2,1,0:T(8,128)(2,1)}, bf16[4,160,800]{2,1,0:T(8,128)(2,1)S(1)}, u32[]{:S(2)}, u32[]{:S(2)}) %collective-permute-start.54) | collective-permute-done | bytes 1024032 | tf_op jit(solution)/shard_map/ppermute | solution.py:135
  350.0 24.5 %collective-permute-done.22 = bf16[2,48,1920]{2,1,0:T(8,128)(2,1)S(1)} collective-permute-done((bf16[2,48,1920]{2,1,0:T(8,128)(2,1)S(1)}, bf16[2,48,1920]{2,1,0:T(8,128)(2,1)S(1)}, u32[]{:S(2)}, u32[]{:S(2)}) %collective-permute-start.22) | collective-permute-done | bytes 368672 | tf_op jit(solution)/shard_map/ppermute | solution.py:135
  394.8 13.6 %collective-permute-done.30 = bf16[2,160,1280]{2,1,0:T(8,128)(2,1)S(1)} collective-permute-done((bf16[2,160,1280]{2,1,0:T(8,128)(2,1)S(1)}, bf16[2,160,1280]{2,1,0:T(8,128)(2,1)S(1)}, u32[]{:S(2)}, u32[]{:S(2)}) %collective-permute-start.30) | collective-permute-done | bytes 819232 | tf_op jit(solution)/shard_map/ppermute | solution.py:135
  424.2 5.3 fusion.63
  441.5 17.7 %while.28 = (s32[]{:T(128)}, bf16[5,256,4,64]{1,3,2,0:T(8,128)(2,1)S(1)}, f32[5,4,256,1]{2,1,3,0:T(4,128)}, bf16[5,256,4,64]{1,3,2,0:T(8,128)(2,1)}, bf16[5,256,...) while((s32[]{:T(128)}, ...), condition=%wide.region_6.7_spmd.clone, body=%wide.region_3.6_spmd.clone.sunk | while | flops 86113280 | bytes 4099933 | solution.py:385
  473.7 9.8 collective-permute-start.33
  487.2 14.9 %collective-permute-done.33 = bf16[128,2560]{1,0:T(8,128)(2,1)S(1)} collective-permute-done((bf16[128,2560]{1,0:T(8,128)(2,1)S(1)}, bf16[128,2560]{1,0:T(8,128)(2,1)S(1)}, u32[]{:S(2)}, u32[]{:S(2)}) %collective-permute-start.33) | collective-permute-done | bytes 655392 | tf_op jit(solution)/shard_map/ppermute | solution.py:135
  503.6 26.1 %collective-permute-done.34 = bf16[128,2560]{1,0:T(8,128)(2,1)S(1)} collective-permute-done((bf16[128,2560]{1,0:T(8,128)(2,1)S(1)}, bf16[128,2560]{1,0:T(8,128)(2,1)S(1)}, u32[]{:S(2)}, u32[]{:S(2)}) %collective-permute-start.34) | collective-permute-done | bytes 655392 | tf_op jit(solution)/shard_map/ppermute | solution.py:135
  536.6 7.8 collective-permute-done.56
  551.3 7.9 copy.327
  559.2 10.0 fusion.292
  574.3 6.2 fusion.291
  580.5 11.2 add_convert_fusion
  591.7 5.8 fusion.77
  603.5 8.1 copy.316
  611.6 7.9 fusion.79
  628.9 5.7 fusion.81
  640.3 8.3 fusion.293
  667.2 10.0 convolution_add_fusion
  682.0 5.7 fusion.83
  709.6 23.4 %collective-permute-done.118 = bf16[4,160,800]{2,1,0:T(8,128)(2,1)S(1)} collective-permute-done((bf16[4,160,800]{2,1,0:T(8,128)(2,1)S(1)}, bf16[4,160,800]{2,1,0:T(8,128)(2,1)S(1)}, u32[]{:S(2)}, u32[]{:S(2)}) %collective-permute-start.118) | collective-permute-done | bytes 1024032 | tf_op jit(solution)/shard_map/ppermute | solution.py:135
  738.0 19.5 %collective-permute-done.111 = bf16[4,160,800]{2,1,0:T(8,128)(2,1)S(1)} collective-permute-done((bf16[4,160,800]{2,1,0:T(8,128)(2,1)S(1)}, bf16[4,160,800]{2,1,0:T(8,128)(2,1)S(1)}, u32[]{:S(2)}, u32[]{:S(2)}) %collective-permute-start.111) | collective-permute-done | bytes 1024032 | tf_op jit(solution)/shard_map/ppermute | solution.py:135
  757.6 13.7 %collective-permute-start.121 = (bf16[160,800]{1,0:T(8,128)(2,1)S(1)}, bf16[160,800]{1,0:T(8,128)(2,1)S(1)}, u32[]{:S(2)}, u32[]{:S(2)}) collective-permute-start(bf16[160,800]{1,0:T(8,128)(2,1)S(1)} %get-tuple-element.276), channel_id=1, source_target_pairs={{0,8},{2,10},{4,12},{6,14},{8,16},{10,18},{12,20},{14,22},{16,24},... | collective-permute-start | bytes 768008 | tf_op jit(solution)/shard_map/ppermute | solution.py:135
  773.4 5.4 collective-permute-done.104
  778.8 12.8 %collective-permute-start.122 = (bf16[160,800]{1,0:T(8,128)(2,1)S(1)}, bf16[160,800]{1,0:T(8,128)(2,1)S(1)}, u32[]{:S(2)}, u32[]{:S(2)}) collective-permute-start(bf16[160,800]{1,0:T(8,128)(2,1)S(1)} %get-tuple-element.277), channel_id=1, source_target_pairs={{0,16},{2,18},{4,20},{6,22},{8,24},{10,26},{12,28},{14,30},{16,0},... | collective-permute-start | bytes 768008 | tf_op jit(solution)/shard_map/ppermute | solution.py:135
  799.4 8.5 collective-permute-done.122
  808.0 6.7 collective-permute-start.116
  814.8 12.4 %collective-permute-start.107 = (bf16[160,800]{1,0:T(8,128)(2,1)S(1)}, bf16[160,800]{1,0:T(8,128)(2,1)S(1)}, u32[]{:S(2)}, u32[]{:S(2)}) collective-permute-start(bf16[160,800]{1,0:T(8,128)(2,1)S(1)} %get-tuple-element.288), channel_id=1, source_target_pairs={{0,8},{2,10},{4,12},{6,14},{8,16},{10,18},{12,20},{14,22},{16,24},... | collective-permute-start | bytes 768008 | tf_op jit(solution)/shard_map/ppermute | solution.py:135
  827.2 8.5 collective-permute-done.115
  864.6 7.7 collective-permute-start.67
  878.9 6.7 fusion.286
  889.1 44.2 %collective-permute-done.68 = bf16[128,2560]{1,0:T(8,128)(2,1)S(1)} collective-permute-done((bf16[128,2560]{1,0:T(8,128)(2,1)S(1)}, bf16[128,2560]{1,0:T(8,128)(2,1)S(1)}, u32[]{:S(2)}, u32[]{:S(2)}) %collective-permute-start.68) | collective-permute-done | bytes 655392 | tf_op jit(solution)/shard_map/ppermute | solution.py:135
  959.1 48.5 %while.29 = (s32[]{:T(128)}, f32[5,256,4,96]{1,3,2,0:T(8,128)}, f32[5,256,4,96]{1,3,2,0:T(8,128)}, bf16[5,256,4,64]{1,3,2,0:T(8,128)(2,1)}, bf16[5,256,4,96]{1,3...) while((s32[]{:T(128)}, f32[5,256,4,96]{1,3,2,0:T(8,128)}, ...), condition=%wide.region_11.12_spmd.clone, body=%wide.region_9.11_spmd.clone.sunk | while | flops 221907456 | bytes 13912441 | solution.py:421
  1040.1 5.8 collective-permute-done.89
  1066.2 6.0 fusion.241
  1075.1 14.7 %concatenate.181 = f32[16,2,80,1060]{3,2,1,0:T(8,128)} concatenate(f32[16,2,80,1056]{3,2,1,0:T(8,128)} %bitcast.1084, f32[16,2,80,1]{3,2,1,0:T(8,128)S(1)} %concatenate.203, f32[16,2,80,1]{3,2,1,0:T(8,128)S(1)} %copy-done.30, f32[16,2,80,1]{3,2,1,0:T(8,128)} %copy.294, f32[16,2,80,1]{3,2,1,0:T(8,128)} %copy.295), dimensions={3} | concatenate | bytes 21708800 | tf_op jit(solution)/shard_map/concatenate | solution.py:460
  1120.6 10.6 collective-permute-done.83
  1150.7 35.2 %collective-permute-done.75 = bf16[2,80,1060]{2,1,0:T(8,128)(2,1)S(1)} collective-permute-done((bf16[2,80,1060]{2,1,0:T(8,128)(2,1)S(1)}, bf16[2,80,1060]{2,1,0:T(8,128)(2,1)S(1)}, u32[]{:S(2)}, u32[]{:S(2)}) %collective-permute-start.75) | collective-permute-done | bytes 339232 | tf_op jit(solution)/shard_map/ppermute | solution.py:135
  1210.7 13.1 %collective-permute-done.101 = bf16[160,1280]{1,0:T(8,128)(2,1)S(1)} collective-permute-done((bf16[160,1280]{1,0:T(8,128)(2,1)S(1)}, bf16[160,1280]{1,0:T(8,128)(2,1)S(1)}, u32[]{:S(2)}, u32[]{:S(2)}) %collective-permute-start.101) | collective-permute-done | bytes 409632 | tf_op jit(solution)/shard_map/ppermute | solution.py:135
  1224.9 9.0 collective-permute-done.80
  (934 shorter events, 642.4 us)
Async XLA Ops:
  0.6 185.8 %collective-permute-start.25 = (bf16[160,1280]{1,0:T(8,128)(2,1)}, bf16[160,1280]{1,0:T(8,128)(2,1)}, u32[]{:S(2)}, u32[]{:S(2)}) collective-permute-start(bf16[160,1280]{1,0:T(8,128)(2,1)} %bitcast.1150), channel_id=1, source_target_pairs={{0,8},{2,10},{4,12},{6,14},{8,16},{10,18},{12,20},{14,22},{16,24},... | collective-permute-start | bytes 1228808 | tf_op jit(solution)/shard_map/ppermute | solution.py:135
  3.7 188.0 %collective-permute-start.26 = (bf16[160,1280]{1,0:T(8,128)(2,1)}, bf16[160,1280]{1,0:T(8,128)(2,1)}, u32[]{:S(2)}, u32[]{:S(2)}) collective-permute-start(bf16[160,1280]{1,0:T(8,128)(2,1)} %bitcast.1151), channel_id=1, source_target_pairs={{0,16},{2,18},{4,20},{6,22},{8,24},{10,26},{12,28},{14,30},{16,0},... | collective-permute-start | bytes 1228808 | tf_op jit(solution)/shard_map/ppermute | solution.py:135
  6.3 188.7 %collective-permute-start.27 = (bf16[160,1280]{1,0:T(8,128)(2,1)}, bf16[160,1280]{1,0:T(8,128)(2,1)}, u32[]{:S(2)}, u32[]{:S(2)}) collective-permute-start(bf16[160,1280]{1,0:T(8,128)(2,1)} %bitcast.1152), channel_id=1, source_target_pairs={{0,24},{2,26},{4,28},{6,30},{8,0},{10,2},{12,4},{14,6},{16,8},{18,... | collective-permute-start | bytes 1228808 | tf_op jit(solution)/shard_map/ppermute | solution.py:135
  12.4 48.7 %collective-permute-start = (bf16[80,1060]{1,0:T(8,128)(2,1)}, bf16[80,1060]{1,0:T(8,128)(2,1)}, u32[]{:S(2)}, u32[]{:S(2)}) collective-permute-start(bf16[80,1060]{1,0:T(8,128)(2,1)} %concatenate.160), channel_id=1, source_target_pairs={{0,8},{2,10},{4,12},{6,14},{8,16},{10,18},{12,20},{14,22},{16,24},... | collective-permute-start | bytes 508808 | tf_op jit(solution)/shard_map/ppermute | solution.py:135
  160.2 55.5 %collective-permute-start.62 = (bf16[128,2560]{1,0:T(8,128)(2,1)}, bf16[128,2560]{1,0:T(8,128)(2,1)}, u32[]{:S(2)}, u32[]{:S(2)}) collective-permute-start(bf16[128,2560]{1,0:T(8,128)(2,1)} %get-tuple-element.315), channel_id=1, source_target_pairs={{0,8},{2,10},{4,12},{6,14},{8,16},{10,18},{12,20},{14,22},{16,24},... | collective-permute-start | bytes 1966088 | tf_op jit(solution)/shard_map/ppermute | solution.py:135
  170.5 46.7 %collective-permute-start.63 = (bf16[128,2560]{1,0:T(8,128)(2,1)}, bf16[128,2560]{1,0:T(8,128)(2,1)}, u32[]{:S(2)}, u32[]{:S(2)}) collective-permute-start(bf16[128,2560]{1,0:T(8,128)(2,1)} %get-tuple-element.315), channel_id=1, source_target_pairs={{0,16},{2,18},{4,20},{6,22},{8,24},{10,26},{12,28},{14,30},{16,0},... | collective-permute-start | bytes 1966088 | tf_op jit(solution)/shard_map/ppermute | solution.py:135
  218.7 95.3 %collective-permute-start.40 = (bf16[4,160,800]{2,1,0:T(8,128)(2,1)S(1)}, bf16[4,160,800]{2,1,0:T(8,128)(2,1)S(1)}, u32[]{:S(2)}, u32[]{:S(2)}) collective-permute-start(bf16[4,160,800]{2,1,0:T(8,128)(2,1)S(1)} %bitcast_dynamic-update-slice_fusion.47), channel_id=1, source_target_pairs={{0,2},{2,0},{4,6},{6,4},{8,10},{10,8},{12,14},{14,12},{16,18},{18,... | collective-permute-start | bytes 3072008 | tf_op jit(solution)/shard_map/ppermute | solution.py:135
  223.2 93.0 %collective-permute-start.41 = (bf16[4,160,800]{2,1,0:T(8,128)(2,1)S(1)}, bf16[4,160,800]{2,1,0:T(8,128)(2,1)S(1)}, u32[]{:S(2)}, u32[]{:S(2)}) collective-permute-start(bf16[4,160,800]{2,1,0:T(8,128)(2,1)S(1)} %bitcast_dynamic-update-slice_fusion.47), channel_id=1, source_target_pairs={{0,4},{2,6},{4,0},{6,2},{8,12},{10,14},{12,8},{14,10},{16,20},{18,... | collective-permute-start | bytes 3072008 | tf_op jit(solution)/shard_map/ppermute | solution.py:135
  233.2 85.4 %collective-permute-start.47 = (bf16[4,160,800]{2,1,0:T(8,128)(2,1)}, bf16[4,160,800]{2,1,0:T(8,128)(2,1)S(1)}, u32[]{:S(2)}, u32[]{:S(2)}) collective-permute-start(bf16[4,160,800]{2,1,0:T(8,128)(2,1)} %bitcast_dynamic-update-slice_fusion.44), channel_id=1, source_target_pairs={{0,2},{2,0},{4,6},{6,4},{8,10},{10,8},{12,14},{14,12},{16,18},{18,... | collective-permute-start | bytes 3072008 | tf_op jit(solution)/shard_map/ppermute | solution.py:135
  239.2 82.6 %collective-permute-start.48 = (bf16[4,160,800]{2,1,0:T(8,128)(2,1)}, bf16[4,160,800]{2,1,0:T(8,128)(2,1)S(1)}, u32[]{:S(2)}, u32[]{:S(2)}) collective-permute-start(bf16[4,160,800]{2,1,0:T(8,128)(2,1)} %bitcast_dynamic-update-slice_fusion.44), channel_id=1, source_target_pairs={{0,4},{2,6},{4,0},{6,2},{8,12},{10,14},{12,8},{14,10},{16,20},{18,... | collective-permute-start | bytes 3072008 | tf_op jit(solution)/shard_map/ppermute | solution.py:135
  248.8 51.9 %collective-permute-start.5 = (bf16[2,80,1060]{2,1,0:T(8,128)(2,1)S(1)}, bf16[2,80,1060]{2,1,0:T(8,128)(2,1)S(1)}, u32[]{:S(2)}, u32[]{:S(2)}) collective-permute-start(bf16[2,80,1060]{2,1,0:T(8,128)(2,1)S(1)} %slice.928), channel_id=1, source_target_pairs={{0,4},{2,6},{4,0},{6,2},{8,12},{10,14},{12,8},{14,10},{16,20},{18,... | collective-permute-start | bytes 1017608 | tf_op jit(solution)/shard_map/ppermute | solution.py:135
  316.2 64.6 %collective-permute-start.28 = (bf16[4,160,1280]{2,1,0:T(8,128)(2,1)}, bf16[4,160,1280]{2,1,0:T(8,128)(2,1)}, u32[]{:S(2)}, u32[]{:S(2)}) collective-permute-start(bf16[4,160,1280]{2,1,0:T(8,128)(2,1)} %bitcast_dynamic-update-slice_fusion.18), channel_id=1, source_target_pairs={{0,2},{2,0},{4,6},{6,4},{8,10},{10,8},{12,14},{14,12},{16,18},{18,... | collective-permute-start | bytes 4915208 | tf_op jit(solution)/shard_map/ppermute | solution.py:135
  318.5 65.1 %collective-permute-start.29 = (bf16[4,160,1280]{2,1,0:T(8,128)(2,1)}, bf16[4,160,1280]{2,1,0:T(8,128)(2,1)}, u32[]{:S(2)}, u32[]{:S(2)}) collective-permute-start(bf16[4,160,1280]{2,1,0:T(8,128)(2,1)} %bitcast_dynamic-update-slice_fusion.18), channel_id=1, source_target_pairs={{0,4},{2,6},{4,0},{6,2},{8,12},{10,14},{12,8},{14,10},{16,20},{18,... | collective-permute-start | bytes 4915208 | tf_op jit(solution)/shard_map/ppermute | solution.py:135
  321.8 224.4 %collective-permute-start.65 = (bf16[4,128,2560]{2,1,0:T(8,128)(2,1)}, bf16[4,128,2560]{2,1,0:T(8,128)(2,1)}, u32[]{:S(2)}, u32[]{:S(2)}) collective-permute-start(bf16[4,128,2560]{2,1,0:T(8,128)(2,1)} %get-tuple-element.253), channel_id=1, source_target_pairs={{0,1},{1,0},{2,3},{3,2},{4,5},{5,4},{6,7},{7,6},{8,9},{9,8},{10,11... | collective-permute-start | bytes 7864328 | tf_op jit(solution)/shard_map/ppermute | solution.py:130
  374.5 36.9 %collective-permute-start.7 = (bf16[16,80,1060]{2,1,0:T(8,128)(2,1)}, bf16[16,80,1060]{2,1,0:T(8,128)(2,1)}, u32[]{:S(2)}, u32[]{:S(2)}) collective-permute-start(bf16[16,80,1060]{2,1,0:T(8,128)(2,1)} %bitcast.23), channel_id=1, source_target_pairs={{0,1},{1,0},{2,3},{3,2},{4,5},{5,4},{6,7},{7,6},{8,9},{9,8},{10,11... | collective-permute-start | bytes 8140808 | tf_op jit(solution)/shard_map/ppermute | solution.py:130
  375.9 91.4 %collective-permute-start.42 = (bf16[2,160,800]{2,1,0:T(8,128)(2,1)}, bf16[2,160,800]{2,1,0:T(8,128)(2,1)}, u32[]{:S(2)}, u32[]{:S(2)}) collective-permute-start(bf16[2,160,800]{2,1,0:T(8,128)(2,1)} %slice.972), channel_id=1, source_target_pairs={{0,4},{2,6},{4,0},{6,2},{8,12},{10,14},{12,8},{14,10},{16,20},{18,... | collective-permute-start | bytes 1536008 | tf_op jit(solution)/shard_map/ppermute | solution.py:135
  408.4 60.8 %collective-permute-start.43 = (bf16[2,160,800]{2,1,0:T(8,128)(2,1)}, bf16[2,160,800]{2,1,0:T(8,128)(2,1)}, u32[]{:S(2)}, u32[]{:S(2)}) collective-permute-start(bf16[2,160,800]{2,1,0:T(8,128)(2,1)} %slice.975), channel_id=1, source_target_pairs={{0,2},{2,0},{4,6},{6,4},{8,10},{10,8},{12,14},{14,12},{16,18},{18,... | collective-permute-start | bytes 1536008 | tf_op jit(solution)/shard_map/ppermute | solution.py:135
  409.9 123.9 %collective-permute-start.49 = (bf16[2,160,800]{2,1,0:T(8,128)(2,1)}, bf16[2,160,800]{2,1,0:T(8,128)(2,1)}, u32[]{:S(2)}, u32[]{:S(2)}) collective-permute-start(bf16[2,160,800]{2,1,0:T(8,128)(2,1)} %slice.978), channel_id=1, source_target_pairs={{0,4},{2,6},{4,0},{6,2},{8,12},{10,14},{12,8},{14,10},{16,20},{18,... | collective-permute-start | bytes 1536008 | tf_op jit(solution)/shard_map/ppermute | solution.py:135
  483.6 46.1 %collective-permute-start.34 = (bf16[128,2560]{1,0:T(8,128)(2,1)S(1)}, bf16[128,2560]{1,0:T(8,128)(2,1)S(1)}, u32[]{:S(2)}, u32[]{:S(2)}) collective-permute-start(bf16[128,2560]{1,0:T(8,128)(2,1)S(1)} %multiply_convert_fusion.3), channel_id=1, source_target_pairs={{0,16},{2,18},{4,20},{6,22},{8,24},{10,26},{12,28},{14,30},{16,0},... | collective-permute-start | bytes 1966088 | tf_op jit(solution)/shard_map/ppermute | solution.py:135
  486.9 43.2 %collective-permute-start.35 = (bf16[128,2560]{1,0:T(8,128)(2,1)S(1)}, bf16[128,2560]{1,0:T(8,128)(2,1)S(1)}, u32[]{:S(2)}, u32[]{:S(2)}) collective-permute-start(bf16[128,2560]{1,0:T(8,128)(2,1)S(1)} %multiply_convert_fusion.3), channel_id=1, source_target_pairs={{0,24},{2,26},{4,28},{6,30},{8,0},{10,2},{12,4},{14,6},{16,8},{18,... | collective-permute-start | bytes 1966088 | tf_op jit(solution)/shard_map/ppermute | solution.py:135
  533.8 37.0 %collective-permute-start.36 = (bf16[4,128,2560]{2,1,0:T(8,128)(2,1)}, bf16[4,128,2560]{2,1,0:T(8,128)(2,1)}, u32[]{:S(2)}, u32[]{:S(2)}) collective-permute-start(bf16[4,128,2560]{2,1,0:T(8,128)(2,1)} %get-tuple-element.258), channel_id=1, source_target_pairs={{0,1},{1,0},{2,3},{3,2},{4,5},{5,4},{6,7},{7,6},{8,9},{9,8},{10,11... | collective-permute-start | bytes 7864328 | tf_op jit(solution)/shard_map/ppermute | solution.py:130
  656.2 36.2 %collective-permute-start.117 = (bf16[2,160,800]{2,1,0:T(8,128)(2,1)}, bf16[2,160,800]{2,1,0:T(8,128)(2,1)}, u32[]{:S(2)}, u32[]{:S(2)}) collective-permute-start(bf16[2,160,800]{2,1,0:T(8,128)(2,1)} %get-tuple-element.278), channel_id=1, source_target_pairs={{0,2},{2,0},{4,6},{6,4},{8,10},{10,8},{12,14},{14,12},{16,18},{18,... | collective-permute-start | bytes 1536008 | tf_op jit(solution)/shard_map/ppermute | solution.py:135
  658.6 36.1 %collective-permute-start.119 = (bf16[2,160,800]{2,1,0:T(8,128)(2,1)}, bf16[2,160,800]{2,1,0:T(8,128)(2,1)}, u32[]{:S(2)}, u32[]{:S(2)}) collective-permute-start(bf16[2,160,800]{2,1,0:T(8,128)(2,1)} %get-tuple-element.279), channel_id=1, source_target_pairs={{0,4},{2,6},{4,0},{6,2},{8,12},{10,14},{12,8},{14,10},{16,20},{18,... | collective-permute-start | bytes 1536008 | tf_op jit(solution)/shard_map/ppermute | solution.py:135
  663.3 36.2 %collective-permute-start.112 = (bf16[2,160,800]{2,1,0:T(8,128)(2,1)}, bf16[2,160,800]{2,1,0:T(8,128)(2,1)}, u32[]{:S(2)}, u32[]{:S(2)}) collective-permute-start(bf16[2,160,800]{2,1,0:T(8,128)(2,1)} %get-tuple-element.285), channel_id=1, source_target_pairs={{0,4},{2,6},{4,0},{6,2},{8,12},{10,14},{12,8},{14,10},{16,20},{18,... | collective-permute-start | bytes 1536008 | tf_op jit(solution)/shard_map/ppermute | solution.py:135
  665.6 36.7 %collective-permute-start.103 = (bf16[2,160,800]{2,1,0:T(8,128)(2,1)}, bf16[2,160,800]{2,1,0:T(8,128)(2,1)S(1)}, u32[]{:S(2)}, u32[]{:S(2)}) collective-permute-start(bf16[2,160,800]{2,1,0:T(8,128)(2,1)} %get-tuple-element.290), channel_id=1, source_target_pairs={{0,2},{2,0},{4,6},{6,4},{8,10},{10,8},{12,14},{14,12},{16,18},{18,... | collective-permute-start | bytes 1536008 | tf_op jit(solution)/shard_map/ppermute | solution.py:135
  694.8 38.2 %collective-permute-start.118 = (bf16[4,160,800]{2,1,0:T(8,128)(2,1)S(1)}, bf16[4,160,800]{2,1,0:T(8,128)(2,1)S(1)}, u32[]{:S(2)}, u32[]{:S(2)}) collective-permute-start(bf16[4,160,800]{2,1,0:T(8,128)(2,1)S(1)} %pad_maximum_fusion.16), channel_id=1, source_target_pairs={{0,4},{2,6},{4,0},{6,2},{8,12},{10,14},{12,8},{14,10},{16,20},{18,... | collective-permute-start | bytes 3072008 | tf_op jit(solution)/shard_map/ppermute | solution.py:135
  697.6 37.6 %collective-permute-start.120 = (bf16[4,160,800]{2,1,0:T(8,128)(2,1)S(1)}, bf16[4,160,800]{2,1,0:T(8,128)(2,1)S(1)}, u32[]{:S(2)}, u32[]{:S(2)}) collective-permute-start(bf16[4,160,800]{2,1,0:T(8,128)(2,1)S(1)} %pad_maximum_fusion.17), channel_id=1, source_target_pairs={{0,2},{2,0},{4,6},{6,4},{8,10},{10,8},{12,14},{14,12},{16,18},{18,... | collective-permute-start | bytes 3072008 | tf_op jit(solution)/shard_map/ppermute | solution.py:135
  699.5 58.1 %collective-permute-start.111 = (bf16[4,160,800]{2,1,0:T(8,128)(2,1)S(1)}, bf16[4,160,800]{2,1,0:T(8,128)(2,1)S(1)}, u32[]{:S(2)}, u32[]{:S(2)}) collective-permute-start(bf16[4,160,800]{2,1,0:T(8,128)(2,1)S(1)} %pad_maximum_fusion.14), channel_id=1, source_target_pairs={{0,4},{2,6},{4,0},{6,2},{8,12},{10,14},{12,8},{14,10},{16,20},{18,... | collective-permute-start | bytes 3072008 | tf_op jit(solution)/shard_map/ppermute | solution.py:135
  702.3 55.2 %collective-permute-start.113 = (bf16[4,160,800]{2,1,0:T(8,128)(2,1)S(1)}, bf16[4,160,800]{2,1,0:T(8,128)(2,1)S(1)}, u32[]{:S(2)}, u32[]{:S(2)}) collective-permute-start(bf16[4,160,800]{2,1,0:T(8,128)(2,1)S(1)} %pad_maximum_fusion.15), channel_id=1, source_target_pairs={{0,2},{2,0},{4,6},{6,4},{8,10},{10,8},{12,14},{14,12},{16,18},{18,... | collective-permute-start | bytes 3072008 | tf_op jit(solution)/shard_map/ppermute | solution.py:135
  708.4 70.4 %collective-permute-start.104 = (bf16[4,160,800]{2,1,0:T(8,128)(2,1)S(1)}, bf16[4,160,800]{2,1,0:T(8,128)(2,1)S(1)}, u32[]{:S(2)}, u32[]{:S(2)}) collective-permute-start(bf16[4,160,800]{2,1,0:T(8,128)(2,1)S(1)} %pad_maximum_fusion.12), channel_id=1, source_target_pairs={{0,4},{2,6},{4,0},{6,2},{8,12},{10,14},{12,8},{14,10},{16,20},{18,... | collective-permute-start | bytes 3072008 | tf_op jit(solution)/shard_map/ppermute | solution.py:135
  733.0 58.6 %collective-permute-start.106 = (bf16[4,160,800]{2,1,0:T(8,128)(2,1)S(1)}, bf16[4,160,800]{2,1,0:T(8,128)(2,1)S(1)}, u32[]{:S(2)}, u32[]{:S(2)}) collective-permute-start(bf16[4,160,800]{2,1,0:T(8,128)(2,1)S(1)} %pad_maximum_fusion.13), channel_id=1, source_target_pairs={{0,2},{2,0},{4,6},{6,4},{8,10},{10,8},{12,14},{14,12},{16,18},{18,... | collective-permute-start | bytes 3072008 | tf_op jit(solution)/shard_map/ppermute | solution.py:135
  735.2 124.8 %collective-permute-start.66 = (bf16[4,128,2560]{2,1,0:T(8,128)(2,1)}, bf16[4,128,2560]{2,1,0:T(8,128)(2,1)}, u32[]{:S(2)}, u32[]{:S(2)}) collective-permute-start(bf16[4,128,2560]{2,1,0:T(8,128)(2,1)} %fusion.68), channel_id=1, source_target_pairs={{0,1},{1,0},{2,3},{3,2},{4,5},{5,4},{6,7},{7,6},{8,9},{9,8},{10,11... | collective-permute-start | bytes 7864328 | tf_op jit(solution)/shard_map/ppermute | solution.py:130
  757.6 121.4 %collective-permute-start.58 = (bf16[4,128,2560]{2,1,0:T(8,128)(2,1)}, bf16[4,128,2560]{2,1,0:T(8,128)(2,1)}, u32[]{:S(2)}, u32[]{:S(2)}) collective-permute-start(bf16[4,128,2560]{2,1,0:T(8,128)(2,1)} %fusion.67), channel_id=1, source_target_pairs={{0,1},{1,0},{2,3},{3,2},{4,5},{5,4},{6,7},{7,6},{8,9},{9,8},{10,11... | collective-permute-start | bytes 7864328 | tf_op jit(solution)/shard_map/ppermute | solution.py:130
  757.6 41.8 %collective-permute-start.121 = (bf16[160,800]{1,0:T(8,128)(2,1)S(1)}, bf16[160,800]{1,0:T(8,128)(2,1)S(1)}, u32[]{:S(2)}, u32[]{:S(2)}) collective-permute-start(bf16[160,800]{1,0:T(8,128)(2,1)S(1)} %get-tuple-element.276), channel_id=1, source_target_pairs={{0,8},{2,10},{4,12},{6,14},{8,16},{10,18},{12,20},{14,22},{16,24},... | collective-permute-start | bytes 768008 | tf_op jit(solution)/shard_map/ppermute | solution.py:135
  872.3 61.0 %collective-permute-start.68 = (bf16[128,2560]{1,0:T(8,128)(2,1)S(1)}, bf16[128,2560]{1,0:T(8,128)(2,1)S(1)}, u32[]{:S(2)}, u32[]{:S(2)}) collective-permute-start(bf16[128,2560]{1,0:T(8,128)(2,1)S(1)} %get-tuple-element.251), channel_id=1, source_target_pairs={{0,16},{2,18},{4,20},{6,22},{8,24},{10,26},{12,28},{14,30},{16,0},... | collective-permute-start | bytes 1966088 | tf_op jit(solution)/shard_map/ppermute | solution.py:135
  876.8 56.5 %collective-permute-start.69 = (bf16[128,2560]{1,0:T(8,128)(2,1)S(1)}, bf16[128,2560]{1,0:T(8,128)(2,1)S(1)}, u32[]{:S(2)}, u32[]{:S(2)}) collective-permute-start(bf16[128,2560]{1,0:T(8,128)(2,1)S(1)} %get-tuple-element.250), channel_id=1, source_target_pairs={{0,8},{2,10},{4,12},{6,14},{8,16},{10,18},{12,20},{14,22},{16,24},... | collective-permute-start | bytes 1966088 | tf_op jit(solution)/shard_map/ppermute | solution.py:135
  936.5 122.8 %collective-permute-start.59 = (bf16[128,2560]{1,0:T(8,128)(2,1)}, bf16[128,2560]{1,0:T(8,128)(2,1)}, u32[]{:S(2)}, u32[]{:S(2)}) collective-permute-start(bf16[128,2560]{1,0:T(8,128)(2,1)} %get-tuple-element.254), channel_id=1, source_target_pairs={{0,24},{2,26},{4,28},{6,30},{8,0},{10,2},{12,4},{14,6},{16,8},{18,... | collective-permute-start | bytes 1966088 | tf_op jit(solution)/shard_map/ppermute | solution.py:135
  936.5 123.3 %collective-permute-start.60 = (bf16[128,2560]{1,0:T(8,128)(2,1)}, bf16[128,2560]{1,0:T(8,128)(2,1)}, u32[]{:S(2)}, u32[]{:S(2)}) collective-permute-start(bf16[128,2560]{1,0:T(8,128)(2,1)} %get-tuple-element.256), channel_id=1, source_target_pairs={{0,16},{2,18},{4,20},{6,22},{8,24},{10,26},{12,28},{14,30},{16,0},... | collective-permute-start | bytes 1966088 | tf_op jit(solution)/shard_map/ppermute | solution.py:135
  936.5 124.8 %collective-permute-start.61 = (bf16[128,2560]{1,0:T(8,128)(2,1)}, bf16[128,2560]{1,0:T(8,128)(2,1)}, u32[]{:S(2)}, u32[]{:S(2)}) collective-permute-start(bf16[128,2560]{1,0:T(8,128)(2,1)} %get-tuple-element.255), channel_id=1, source_target_pairs={{0,8},{2,10},{4,12},{6,14},{8,16},{10,18},{12,20},{14,22},{16,24},... | collective-permute-start | bytes 1966088 | tf_op jit(solution)/shard_map/ppermute | solution.py:135
  1022.0 93.6 %collective-permute-start.96 = (bf16[2,160,1280]{2,1,0:T(8,128)(2,1)}, bf16[2,160,1280]{2,1,0:T(8,128)(2,1)}, u32[]{:S(2)}, u32[]{:S(2)}) collective-permute-start(bf16[2,160,1280]{2,1,0:T(8,128)(2,1)} %get-tuple-element.266), channel_id=1, source_target_pairs={{0,2},{2,0},{4,6},{6,4},{8,10},{10,8},{12,14},{14,12},{16,18},{18,... | collective-permute-start | bytes 2457608 | tf_op jit(solution)/shard_map/ppermute | solution.py:135
  1053.1 66.0 %collective-permute-start.98 = (bf16[2,160,1280]{2,1,0:T(8,128)(2,1)}, bf16[2,160,1280]{2,1,0:T(8,128)(2,1)}, u32[]{:S(2)}, u32[]{:S(2)}) collective-permute-start(bf16[2,160,1280]{2,1,0:T(8,128)(2,1)} %get-tuple-element.267), channel_id=1, source_target_pairs={{0,4},{2,6},{4,0},{6,2},{8,12},{10,14},{12,8},{14,10},{16,20},{18,... | collective-permute-start | bytes 2457608 | tf_op jit(solution)/shard_map/ppermute | solution.py:135
  1059.8 35.9 %collective-permute-start.84 = (bf16[2,48,1920]{2,1,0:T(8,128)(2,1)}, bf16[2,48,1920]{2,1,0:T(8,128)(2,1)}, u32[]{:S(2)}, u32[]{:S(2)}) collective-permute-start(bf16[2,48,1920]{2,1,0:T(8,128)(2,1)} %get-tuple-element.308), channel_id=1, source_target_pairs={{0,4},{2,6},{4,0},{6,2},{8,12},{10,14},{12,8},{14,10},{16,20},{18,... | collective-permute-start | bytes 1105928 | tf_op jit(solution)/shard_map/ppermute | solution.py:135
  1061.3 35.6 %collective-permute-start.90 = (bf16[4,16,2560]{2,1,0:T(8,128)(2,1)}, bf16[4,16,2560]{2,1,0:T(8,128)(2,1)}, u32[]{:S(2)}, u32[]{:S(2)}) collective-permute-start(bf16[4,16,2560]{2,1,0:T(8,128)(2,1)} %pad_maximum_fusion.26), channel_id=1, source_target_pairs={{0,4},{2,6},{4,0},{6,2},{8,12},{10,14},{12,8},{14,10},{16,20},{18,... | collective-permute-start | bytes 983048 | tf_op jit(solution)/shard_map/ppermute | solution.py:135
  1109.8 37.6 %collective-permute-start.74 = (bf16[16,80,1060]{2,1,0:T(8,128)(2,1)S(1)}, bf16[16,80,1060]{2,1,0:T(8,128)(2,1)S(1)}, u32[]{:S(2)}, u32[]{:S(2)}) collective-permute-start(bf16[16,80,1060]{2,1,0:T(8,128)(2,1)S(1)} %fusion.66), channel_id=1, source_target_pairs={{0,1},{1,0},{2,3},{3,2},{4,5},{5,4},{6,7},{7,6},{8,9},{9,8},{10,11... | collective-permute-start | bytes 8140808 | tf_op jit(solution)/shard_map/ppermute | solution.py:130
  1118.6 69.4 %collective-permute-start.97 = (bf16[4,160,1280]{2,1,0:T(8,128)(2,1)}, bf16[4,160,1280]{2,1,0:T(8,128)(2,1)S(1)}, u32[]{:S(2)}, u32[]{:S(2)}) collective-permute-start(bf16[4,160,1280]{2,1,0:T(8,128)(2,1)} %pad_maximum_fusion.8), channel_id=1, source_target_pairs={{0,4},{2,6},{4,0},{6,2},{8,12},{10,14},{12,8},{14,10},{16,20},{18,... | collective-permute-start | bytes 4915208 | tf_op jit(solution)/shard_map/ppermute | solution.py:135
  1142.4 45.6 %collective-permute-start.99 = (bf16[4,160,1280]{2,1,0:T(8,128)(2,1)}, bf16[4,160,1280]{2,1,0:T(8,128)(2,1)S(1)}, u32[]{:S(2)}, u32[]{:S(2)}) collective-permute-start(bf16[4,160,1280]{2,1,0:T(8,128)(2,1)} %pad_maximum_fusion.9), channel_id=1, source_target_pairs={{0,2},{2,0},{4,6},{6,4},{8,10},{10,8},{12,14},{14,12},{16,18},{18,... | collective-permute-start | bytes 4915208 | tf_op jit(solution)/shard_map/ppermute | solution.py:135
  1148.4 37.5 %collective-permute-start.75 = (bf16[2,80,1060]{2,1,0:T(8,128)(2,1)S(1)}, bf16[2,80,1060]{2,1,0:T(8,128)(2,1)S(1)}, u32[]{:S(2)}, u32[]{:S(2)}) collective-permute-start(bf16[2,80,1060]{2,1,0:T(8,128)(2,1)S(1)} %get-tuple-element.312), channel_id=1, source_target_pairs={{0,2},{2,0},{4,6},{6,4},{8,10},{10,8},{12,14},{14,12},{16,18},{18,... | collective-permute-start | bytes 1017608 | tf_op jit(solution)/shard_map/ppermute | solution.py:135
  1150.1 36.0 %collective-permute-start.77 = (bf16[2,80,1060]{2,1,0:T(8,128)(2,1)S(1)}, bf16[2,80,1060]{2,1,0:T(8,128)(2,1)S(1)}, u32[]{:S(2)}, u32[]{:S(2)}) collective-permute-start(bf16[2,80,1060]{2,1,0:T(8,128)(2,1)S(1)} %get-tuple-element.313), channel_id=1, source_target_pairs={{0,4},{2,6},{4,0},{6,2},{8,12},{10,14},{12,8},{14,10},{16,20},{18,... | collective-permute-start | bytes 1017608 | tf_op jit(solution)/shard_map/ppermute | solution.py:135
  (224 other events, 3529.6 us)

commit v2 on v0

v2 whole, which is shorter than its diff:
```python
from functools import partial
import math

import jax
import jax.numpy as jnp
from jax import lax
from jax.experimental import pallas as pl
from jax.experimental.pallas import tpu as pltpu
from jax.sharding import PartitionSpec as P

NOPE = 64
ROPE = 32
VD = 64
KR = 256
LANES = 128
GROUP_BITS = (2, 8)
LAST_BITS = (1, 2)
NEAR, FAR = 4, 8
GROUP = 4


EPS = 1e-05
RESID = 1.4 / math.sqrt(62.0)
THETA = 10000.0
NEG_FILL = -1e30


def norm_apply(values, gain):
    inverse = lax.rsqrt(jnp.mean(values * values, axis=-1, keepdims=True) + EPS)
    return values * inverse * gain


def rotate(values, positions):
    width_half = values.shape[-1] // 2
    frequency = THETA ** (-2.0 * jnp.arange(width_half, dtype=jnp.float32) / values.shape[-1])
    angles = positions.astype(jnp.float32)[:, None] * frequency[None, :]
    extra_dims = (1,) * (values.ndim - 2)
    cosine = jnp.cos(angles).reshape(angles.shape[:1] + extra_dims + angles.shape[1:])
    sine = jnp.sin(angles).reshape(angles.shape[:1] + extra_dims + angles.shape[1:])
    lower_part = values[..., :width_half]
    upper_part = values[..., width_half:]
    return jnp.concatenate(
        [lower_part * cosine - upper_part * sine, upper_part * cosine + lower_part * sine], axis=-1
    )


def rotate_back(values, positions, grads):
    _, pullback = jax.vjp(partial(rotate, positions=positions), values)
    return pullback(grads)[0]


def plain_mul(left, right):
    return jnp.dot(left, right, preferred_element_type=jnp.float32)


def mul_trans(left, right):
    return lax.dot_general(
        left, right, (((1,), (1,)), ((), ())), preferred_element_type=jnp.float32
    )


def trans_mul(left, right):
    return lax.dot_general(
        left, right, (((0,), (0,)), ((), ())), preferred_element_type=jnp.float32
    )


def low(values):
    return values.astype(jnp.bfloat16)


def wide(values):
    return values.astype(jnp.float32)


def core_swap(values):
    return lax.ppermute(values, "tensor", [(0, 1), (1, 0)])


def all_bits():
    count = lax.axis_size("dp")
    return tuple(1 << at for at in range(count.bit_length() - 1))


def other_bits(bits):
    return tuple(bit for bit in all_bits() if bit not in bits)


def masks_of(bits):
    masks = [0]
    for bit in bits:
        masks += [mask | bit for mask in masks]
    return masks


def by_count(bits):
    return sorted(masks_of(bits)[1:], key=lambda mask: (bin(mask).count("1"), mask))


def group_place():
    place = lax.axis_index("dp")
    return sum(((place // bit) % 2) << at for at, bit in enumerate(GROUP_BITS))


class Links:
    def __init__(self):
        self.last = {}
        self.ties = {}

    def tie(self, bit, other):
        self.ties[bit] = self.last[other]

    def flip(self, values, mask):
        bits = [bit for bit in all_bits() if bit & mask]
        before = [self.last[bit] for bit in bits if bit in self.last]
        before += [self.ties.pop(bit) for bit in bits if bit in self.ties]
        if before:
            values, _ = lax.optimization_barrier((values, before))
        count = lax.axis_size("dp")
        got = lax.ppermute(values, "dp", [(place, place ^ mask) for place in range(count)])
        for bit in bits:
            self.last[bit] = got
        return got


def routes(mask, bits, split):
    ordered = [bit for bit in bits if bit & mask]
    if len(ordered) == 1 or not split:
        return [(ordered[0], slice(None))]
    return [(ordered[0], 0), (ordered[-1], 1)]


def halves(values):
    half = values.shape[0] // 2
    return values[:half], values[half:]


def gather_bits(links, values, bits, split, known=None, most=None):
    known = dict(known or {0: [values]})
    for mask in by_count(bits):
        if mask in known or (most and bin(mask).count("1") > most):
            continue
        pieces = []
        for bit, part in routes(mask, bits, split):
            source = known[mask ^ bit]
            whole = source[0] if len(source) == 1 else None
            if part == slice(None):
                moving = whole if whole is not None else jnp.concatenate(source)
            else:
                moving = halves(whole)[part] if whole is not None else source[part]
            pieces.append(links.flip(moving, bit))
        known[mask] = pieces
    return known


def reduce_bits(links, block_of, bits, split, arrive=lambda values, bit: values):
    added = {mask: [] for mask in masks_of(bits)}

    def summed(mask, part):
        values = block_of(mask)
        if part != slice(None):
            values = halves(values)[part]
        if added[mask]:
            values = wide(values)
        for held, extra in added[mask]:
            if part == slice(None) and held != slice(None):
                rest = [jnp.zeros_like(extra)] * 2
                rest[held] = extra
                values = values + jnp.concatenate([wide(item) for item in rest])
            elif part == held:
                values = values + wide(extra)
            elif held == slice(None):
                values = values + wide(halves(extra)[part])
        return values

    for mask in reversed(by_count(bits)):
        for bit, part in routes(mask, bits, split):
            if part == slice(None) and any(held != slice(None) for held, _ in added[mask]):
                moving = jnp.concatenate([low(summed(mask, 0)), low(summed(mask, 1))])
            else:
                moving = low(summed(mask, part))
            added[mask ^ bit].append((part, arrive(links.flip(moving, bit), bit)))
    if any(held != slice(None) for held, _ in added[0]):
        return jnp.concatenate([summed(0, 0), summed(0, 1)])
    return summed(0, slice(None))


def row_order():
    return [
        other | group for other in masks_of(other_bits(GROUP_BITS)) for group in masks_of(GROUP_BITS)
    ]


def first_bits():
    return other_bits(LAST_BITS)


def start_gather(links, values):
    known = gather_bits(links, values, first_bits(), False)
    return jnp.stack([known[mask][0] for mask in masks_of(first_bits())])


def end_gather(links, column, split=True):
    known = gather_bits(links, column, LAST_BITS, split)
    first = masks_of(first_bits())
    half = column.shape[0] // 2

    def block(mask):
        at = first.index(mask & ~sum(LAST_BITS))
        pieces = known[mask & sum(LAST_BITS)]
        return pieces[0][at] if len(pieces) == 1 else pieces[at // half][at % half]

    return jnp.concatenate([block(mask) for mask in row_order()], axis=0)


def reduce_dp(links, grad, split=True):
    order = row_order()
    blocks = grad.reshape(len(order), -1, grad.shape[1])
    first = masks_of(first_bits())

    def column(last):
        return jnp.stack([blocks[order.index(last | mask)] for mask in first])

    partial_sum = reduce_bits(links, column, LAST_BITS, split)
    return reduce_bits(links, lambda mask: partial_sum[first.index(mask)], first_bits(), False)


def place_kernel(place_ref, *refs):
    out_ref = refs[-1]
    for step, ref in enumerate(refs[:-1]):

        @pl.when(pl.program_id(0) == step)
        def _():
            out_ref[0] = ref[...]


def pick_kernel(place_ref, values_ref, *out_refs):
    for step, ref in enumerate(out_refs):

        @pl.when(pl.program_id(0) == step)
        def _():
            ref[...] = values_ref[0]


def place_index():
    return group_place().reshape(1).astype(jnp.int32)


def place_group(blocks):
    rows, width = blocks[0].shape
    return pl.pallas_call(
        place_kernel,
        grid_spec=pltpu.PrefetchScalarGridSpec(
            num_scalar_prefetch=1,
            grid=(GROUP,),
            in_specs=[pl.BlockSpec((rows, width), lambda step, place: (0, 0))] * GROUP,
            out_specs=pl.BlockSpec(
                (1, rows, width), lambda step, place: (lax.bitwise_xor(place[0], step), 0, 0)
            ),
        ),
        out_shape=jax.ShapeDtypeStruct((GROUP, rows, width), blocks[0].dtype),
        compiler_params=pltpu.CompilerParams(vmem_limit_bytes=32 * 2**20),
        name="place_group",
    )(place_index(), *blocks)


def pick_group(values):
    _, rows, width = values.shape
    blocks = pl.pallas_call(
        pick_kernel,
        grid_spec=pltpu.PrefetchScalarGridSpec(
            num_scalar_prefetch=1,
            grid=(GROUP,),
            in_specs=[
                pl.BlockSpec(
                    (1, rows, width), lambda step, place: (lax.bitwise_xor(place[0], step), 0, 0)
                )
            ],
            out_specs=[pl.BlockSpec((rows, width), lambda step, place: (0, 0))] * GROUP,
        ),
        out_shape=[jax.ShapeDtypeStruct((rows, width), values.dtype)] * GROUP,
        compiler_params=pltpu.CompilerParams(vmem_limit_bytes=32 * 2**20),
        name="pick_group",
    )(place_index(), values)
    return list(blocks)


def exchange_group(links, blocks):
    near, far = GROUP_BITS
    there = links.flip(jnp.stack([blocks[1], blocks[3]]), near)
    across = links.flip(blocks[2], far)
    return [blocks[0], there[0], across, links.flip(there[1], far)]


def cut_units(weight, share):
    rows, units = weight.shape
    cut = jnp.moveaxis(weight.reshape(rows, GROUP, units // GROUP), 1, 0)
    return jnp.pad(cut, ((0, 0), (0, 0), (0, share - units // GROUP)))


def join_units(pieces, units):
    rows = pieces.shape[1]
    return wide(jnp.moveaxis(pieces[..., : units // GROUP], 0, 1)).reshape(rows, units)


CHUNKS = 4


def reorder_kernel(steps, block, *refs):
    width = refs[0].shape[-1]
    chunk = width // CHUNKS
    for at, step in enumerate(steps):
        source, target = refs[at], refs[-1].at[at]
        if not step:
            target[...] = source[...]
            continue
        row = lax.broadcasted_iota(jnp.int32, (chunk, chunk), 0)
        column = lax.broadcasted_iota(jnp.int32, (chunk, chunk), 1)
        index = lax.rem(lax.div(column, block), GROUP)
        origin = column + (lax.bitwise_xor(index, step) - index) * block
        moved = jnp.where(row == origin, 1.0, 0.0).astype(jnp.bfloat16)
        for part in range(CHUNKS):
            columns = slice(part * chunk, (part + 1) * chunk)
            target[:, columns] = low(plain_mul(source[:, columns], moved))


def reorder(arrays, steps):
    rows, width = arrays[0].shape
    return pl.pallas_call(
        partial(reorder_kernel, tuple(steps), width // lax.axis_size("dp")),
        out_shape=jax.ShapeDtypeStruct((len(steps), rows, width), arrays[0].dtype),
        compiler_params=pltpu.CompilerParams(vmem_limit_bytes=32 * 2**20),
        name="reorder",
    )(*arrays)


def gather_tokens(links, values):
    known = gather_bits(links, values, GROUP_BITS, False)
    own = reorder([known[mask][0] for mask in masks_of(GROUP_BITS)], range(GROUP))
    own = own.reshape(-1, values.shape[1])
    return own, core_swap(own)


def return_tokens(links, values, rows):
    mine = values.shape[0] // 2
    chip_sum = wide(values[:mine]) + wide(core_swap(values[mine:]))
    chip_sum = chip_sum.reshape(GROUP, rows, -1)
    masks = masks_of(GROUP_BITS)
    return reduce_bits(
        links,
        lambda mask: chip_sum[masks.index(mask)],
        GROUP_BITS,
        False,
        lambda got, bit: reorder([got], [masks.index(bit)])[0],
    )


def units_kernel(
    share, count, own_ref, other_ref, own_back_ref, other_back_ref, *refs
):
    pieces, (act_ref, d_units_ref, d_in_ref, out_ref, weight_ref, sems) = refs[:count], refs[count:]
    step = pl.program_id(0)

    @pl.when(step == 0)
    def _():
        copies, start = [], 0
        for at, piece in enumerate(pieces):
            rows = piece.shape[0]
            copies.append(
                pltpu.make_async_copy(piece, weight_ref.at[pl.ds(start, rows)], sems.at[at])
            )
            start += rows
        for copy in copies:
            copy.start()
        for copy in copies:
            copy.wait()

    is_own = step < pl.num_programs(0) // 2
    tokens = jnp.where(is_own, own_ref[...], other_ref[...])
    back = jnp.where(is_own, own_back_ref[...], other_back_ref[...])
    gate_cut, up_cut = slice(0, share), slice(share, 2 * share)
    down_cut = slice(2 * share, 3 * share)
    gate = plain_mul(tokens, weight_ref[:, gate_cut])
    upper = plain_mul(tokens, weight_ref[:, up_cut])
    d_act = plain_mul(back, weight_ref[:, down_cut])
    slope = 1.0 / (1.0 + jnp.exp(-gate))
    swished = gate * slope
    act = low(swished * upper)
    act_ref[...] = act
    d_units_ref[:, gate_cut] = low(d_act * upper * (slope + swished * (1.0 - slope)))
    d_units_ref[:, up_cut] = low(d_act * swished)
    d_in_ref[...] = low(mul_trans(d_units_ref[...], weight_ref[:, : 2 * share]))
    out_ref[...] = low(mul_trans(act, weight_ref[:, down_cut]))


def run_units(tokens, back, pieces, share):
    own, other = tokens
    rows, width = own.shape
    steps = 4
    block = 2 * rows // steps
    half = steps // 2
    in_own = pl.BlockSpec((block, width), lambda step: (jnp.minimum(step, half - 1), 0))
    in_other = pl.BlockSpec((block, width), lambda step: (jnp.maximum(step - half, 0), 0))
    many = pl.BlockSpec(memory_space=pl.ANY)

    def out_spec(columns):
        return pl.BlockSpec((block, columns), lambda step: (step, 0))

    columns = (share, 2 * share, width, width)
    return pl.pallas_call(
        partial(units_kernel, share, len(pieces)),
        grid=(steps,),
        in_specs=[in_own, in_other, in_own, in_other] + [many] * len(pieces),
        out_specs=[out_spec(item) for item in columns],
        out_shape=[jax.ShapeDtypeStruct((2 * rows, item), jnp.bfloat16) for item in columns],
        scratch_shapes=[
            pltpu.VMEM((width, 3 * share), jnp.bfloat16),
            pltpu.SemaphoreType.DMA((len(pieces),)),
        ],
        compiler_params=pltpu.CompilerParams(vmem_limit_bytes=56 * 2**20),
        name="run_units",
    )(own, other, *back, *pieces)


def unit_grads_kernel(share, own_ref, other_ref, own_back_ref, other_back_ref, act_ref, d_units_ref, out_ref):
    tokens = jnp.concatenate([own_ref[...], other_ref[...]], axis=0)
    out_ref[:, : 2 * share] = low(trans_mul(tokens, d_units_ref[...]))
    back = jnp.concatenate([own_back_ref[...], other_back_ref[...]], axis=0)
    out_ref[:, 2 * share :] = low(trans_mul(back, act_ref[...]))


def unit_grads(tokens, back, act, d_units, share):
    rows, width = tokens[0].shape
    chunk = width // CHUNKS
    part = pl.BlockSpec((rows, chunk), lambda step: (0, step))
    return pl.pallas_call(
        partial(unit_grads_kernel, share),
        grid=(CHUNKS,),
        in_specs=[part] * 4
        + [pl.BlockSpec(act.shape, lambda step: (0, 0)), pl.BlockSpec(d_units.shape, lambda step: (0, 0))],
        out_specs=pl.BlockSpec((chunk, 3 * share), lambda step: (step, 0)),
        out_shape=jax.ShapeDtypeStruct((width, 3 * share), jnp.bfloat16),
        compiler_params=pltpu.CompilerParams(vmem_limit_bytes=56 * 2**20),
        name="unit_grads",
    )(*tokens, *back, act, d_units)


def pair_tokens(values):
    return jnp.concatenate([values, core_swap(values)], axis=0)


def split_pair(values):
    rows = values.shape[0] // 2
    return values[:rows] + wide(core_swap(low(values[rows:])))


def block_origins(total):
    order = row_order()
    block = total // len(order)
    place = jnp.arange(total, dtype=jnp.int32)
    index = place // block
    mask = jnp.zeros_like(index)
    for at, bit in enumerate(GROUP_BITS + other_bits(GROUP_BITS)):
        mask = mask + ((index >> at) % 2) * bit
    return (lax.axis_index("dp") ^ mask) * block + place % block


def one_hot(origins, size):
    return (jnp.arange(size, dtype=jnp.int32)[:, None] == origins[None, :]).astype(jnp.bfloat16)


def in_parts(values, count):
    parts = []
    for _ in range(count):
        part = low(values)
        parts.append(part)
        values = values - wide(part)
    return parts


def move_columns(values, selector, transpose, count):
    rows = values.shape[0]
    stacked = jnp.concatenate(in_parts(values, count), axis=0)
    moved = mul_trans(stacked, selector) if transpose else plain_mul(stacked, selector)
    return sum(moved[at * rows : (at + 1) * rows] for at in range(count))


def round_up(size, step):
    return -(-size // step) * step


def turn_tables(positions):
    lane = jnp.arange(LANES, dtype=jnp.int32)[None, :]
    half = ROPE // 2
    frequency = THETA ** (-2.0 * ((lane - NOPE) % half).astype(jnp.float32) / ROPE)
    angles = positions.astype(jnp.float32)[:, None] * frequency
    in_first = (lane >= NOPE) & (lane < NOPE + half)
    in_last = (lane >= NOPE + half) & (lane < NOPE + ROPE)
    cosine, sine = jnp.cos(angles), jnp.sin(angles)
    keep = jnp.where(in_first | in_last, cosine, jnp.where(lane < NOPE, 1.0, 0.0))
    return keep, jnp.where(in_first, -sine, 0.0), jnp.where(in_last, sine, 0.0)


def lanes_on(values, step):
    return pltpu.roll(values, (-step) % LANES, 1)


def key_of(tile, k_rotary):
    lane = lax.broadcasted_iota(jnp.int32, tile.shape, 1)
    return jnp.where(lane < NOPE, tile, k_rotary)


def probs_of(query, key, visible, scale):
    scores = jnp.where(visible, mul_trans(query, key) * scale, NEG_FILL)
    exp_scores = jnp.exp(scores - jnp.max(scores, axis=-1, keepdims=True))
    return exp_scores / jnp.sum(exp_scores, axis=-1, keepdims=True)


def attend_kernel(scale, q_ref, kv_ref, rot_ref, seen_ref, keep_ref, up_ref, down_ref, out_ref, query_ref):
    visible = seen_ref[...] > 0.0
    outs = []
    for head in range(2):
        lanes = slice(head * LANES, (head + 1) * LANES)
        raw = q_ref[:, lanes]
        query = (
            raw * keep_ref[...]
            + lanes_on(raw, ROPE // 2) * up_ref[...]
            + lanes_on(raw, -(ROPE // 2)) * down_ref[...]
        ).astype(jnp.bfloat16)
        query_ref[:, lanes] = query
        tile = kv_ref[:, lanes]
        probs = probs_of(query, key_of(tile, rot_ref[...]), visible, scale)
        outs.append(plain_mul(probs.astype(jnp.bfloat16), tile))
    lane = lax.broadcasted_iota(jnp.int32, outs[0].shape, 1)
    out_ref[...] = jnp.where(lane < VD, pltpu.roll(outs[0], VD, 1), outs[1]).astype(jnp.bfloat16)


def attend_back_kernel(
    scale, query_ref, kv_ref, rot_ref, seen_ref, keep_ref, up_ref, down_ref, d_out_ref,
    d_q_ref, d_kv_ref, d_rot_ref,
):
    @pl.when(pl.program_id(0) == 0)
    def _():
        d_rot_ref[...] = jnp.zeros_like(d_rot_ref)

    visible = seen_ref[...] > 0.0
    d_pair = wide(d_out_ref[...])
    lane = lax.broadcasted_iota(jnp.int32, d_pair.shape, 1)
    d_rot = d_rot_ref[...]
    for head in range(2):
        lanes = slice(head * LANES, (head + 1) * LANES)
        query = query_ref[:, lanes]
        tile = kv_ref[:, lanes]
        key = key_of(tile, rot_ref[...])
        probs = probs_of(query, key, visible, scale)
        d_head = d_pair if head else pltpu.roll(d_pair, VD, 1)
        d_head = low(jnp.where(lane < NOPE, 0.0, d_head))
        d_probs = mul_trans(d_head, tile)
        d_values = trans_mul(low(probs), d_head)
        row_dot = jnp.sum(probs * d_probs, axis=-1, keepdims=True)
        d_scores = low(probs * (d_probs - row_dot) * scale)
        d_query = plain_mul(d_scores, key)
        d_key = trans_mul(d_scores, query)
        d_q_ref[:, lanes] = low(
            d_query * keep_ref[...]
            - lanes_on(d_query, ROPE // 2) * up_ref[...]
            - lanes_on(d_query, -(ROPE // 2)) * down_ref[...]
        )
        d_kv_ref[:, lanes] = low(jnp.where(lane < NOPE, d_key, d_values))
        d_rot += d_key
    d_rot_ref[...] = d_rot


def attend_specs(length):
    pair = pl.BlockSpec((length, 2 * LANES), lambda step: (0, step))
    single = pl.BlockSpec((length, LANES), lambda step: (0, step))
    table = pl.BlockSpec((length, LANES), lambda step: (0, 0))
    seen = pl.BlockSpec((length, length), lambda step: (0, 0))
    return pair, single, table, seen


def attend(query, key_value, rot_pad, seen, tables, scale):
    length, columns = query.shape
    pair, single, table, whole = attend_specs(length)
    return pl.pallas_call(
        partial(attend_kernel, scale),
        grid=(columns // (2 * LANES),),
        in_specs=[pair, pair, table, whole, table, table, table],
        out_specs=[single, pair],
        out_shape=[
            jax.ShapeDtypeStruct((length, columns // 2), jnp.bfloat16),
            jax.ShapeDtypeStruct((length, columns), jnp.bfloat16),
        ],
        compiler_params=pltpu.CompilerParams(vmem_limit_bytes=32 * 2**20),
        name="attend",
    )(query, key_value, rot_pad, seen, *tables)


def attend_back(query_full, key_value, rot_pad, seen, tables, d_heads, scale):
    length, columns = query_full.shape
    pair, single, table, whole = attend_specs(length)
    return pl.pallas_call(
        partial(attend_back_kernel, scale),
        grid=(columns // (2 * LANES),),
        in_specs=[pair, pair, table, whole, table, table, table, single],
        out_specs=[pair, pair, table],
        out_shape=[
            jax.ShapeDtypeStruct((length, columns), jnp.bfloat16),
            jax.ShapeDtypeStruct((length, columns), jnp.bfloat16),
            jax.ShapeDtypeStruct((length, LANES), jnp.float32),
        ],
        compiler_params=pltpu.CompilerParams(vmem_limit_bytes=32 * 2**20),
        name="attend_back",
    )(query_full, key_value, rot_pad, seen, *tables, d_heads)


def body(
    hidden_in,
    prefix_len,
    attn_gain,
    q_down,
    q_gain,
    kv_down,
    kv_gain,
    q_up,
    kv_up,
    o_proj,
    mlp_gain,
    w_gate,
    w_up,
    w_down,
    cotangent,
):
    tensor_count = lax.axis_size("tensor")
    tensor_rank = lax.axis_index("tensor")
    dp_count = lax.axis_size("dp")
    own_rows, width = hidden_in.shape
    q_rank = q_down.shape[1]
    rank = q_rank + KR
    down_rows = q_down.shape[0]
    q_share, kv_share = q_gain.shape[0], kv_gain.shape[0]
    q_rows, kv_rows = q_up.shape[0], kv_up.shape[0]
    head_qk = NOPE + ROPE
    heads_local = q_up.shape[1] // head_qk
    scale = head_qk ** (-0.5)
    links = Links()
    heads_width = heads_local * LANES
    q_padded = jnp.pad(
        q_up.reshape(q_rows, heads_local, head_qk), ((0, 0), (0, 0), (0, LANES - head_qk))
    ).reshape(q_rows, heads_width)
    units = w_gate.shape[1]
    share = round_up(units // GROUP, LANES)

    down_columns = rank + ROPE
    packed_columns = round_up(down_columns + 3, LANES)

    def column_of(gain):
        return jnp.pad(gain, (0, down_rows - gain.shape[0]))[:, None]

    packed = jnp.concatenate(
        [
            q_down,
            kv_down,
            column_of(attn_gain),
            column_of(mlp_gain),
            column_of(jnp.concatenate([q_gain, kv_gain])),
            jnp.zeros((down_rows, packed_columns - down_columns - 3), jnp.bfloat16),
        ],
        axis=1,
    )
    down_column = start_gather(links, packed)
    up_column = start_gather(links, jnp.concatenate([q_padded, kv_up], axis=0))
    out_column = start_gather(links, o_proj.T)
    core_packed = end_gather(links, down_column).reshape(dp_count, down_rows, packed_columns)
    unit_column = jnp.stack(
        exchange_group(
            links,
            pick_group(
                jnp.concatenate([cut_units(item, share) for item in (w_gate, w_up, w_down.T)], axis=-1)
            ),
        )
    )
    up_weight = end_gather(links, up_column)
    out_trans = end_gather(links, out_column)
    other_packed = core_swap(core_packed)
    is_first = tensor_rank == 0
    all_packed = jnp.stack(
        [
            jnp.where(is_first, core_packed, other_packed),
            jnp.where(is_first, other_packed, core_packed),
        ],
        axis=1,
    ).reshape(width, packed_columns)

    width_origins = block_origins(width)
    to_order = one_hot(width_origins, width)
    rank_block = q_rows + kv_rows
    place = jnp.arange(rank, dtype=jnp.int32)
    device_of = block_origins(rank) // rank_block
    in_block = place % rank_block
    is_query = in_block < q_rows
    rank_order = one_hot(
        jnp.where(
            is_query,
            device_of * q_rows + in_block,
            q_rank + device_of * kv_rows + in_block - q_rows,
        ),
        rank,
    )
    device_place = width_origins // down_rows
    in_share = width_origins % down_rows
    gain_order = one_hot(
        jnp.where(
            in_share < q_share,
            device_place * q_share + in_share,
            jnp.where(
                in_share < q_share + kv_share,
                q_rank + device_place * kv_share + in_share - q_share,
                -1,
            ),
        ),
        rank,
    )
    gains = all_packed[:, down_columns : down_columns + 3].T
    gain_attn = wide(gains[0])
    gain_mlp = wide(gains[1])
    gain_rank = mul_trans(gains[2:3], gain_order)[0]
    gain_q, gain_kv = gain_rank[:q_rank], gain_rank[q_rank:]

    moved_in = plain_mul(jnp.concatenate([hidden_in, cotangent], axis=0), to_order)
    resid_in, grad_out = moved_in[:own_rows], moved_in[own_rows:]
    mlp_back = gather_tokens(links, (RESID * grad_out).astype(jnp.bfloat16))
    others = other_bits(GROUP_BITS)
    links.tie(NEAR, FAR)
    known_units = gather_bits(links, unit_column, others, True, most=1)
    x_normed = norm_apply(resid_in, gain_attn).astype(jnp.bfloat16)
    latents = plain_mul(x_normed, all_packed)
    q_latent = latents[:, :q_rank]
    kv_latent = latents[:, q_rank:rank]
    rot_latent = latents[:, rank:down_columns]
    q_normed = norm_apply(q_latent, gain_q).astype(jnp.bfloat16)
    kv_normed = norm_apply(kv_latent, gain_kv).astype(jnp.bfloat16)
    own_pos = tensor_rank * own_rows + jnp.arange(own_rows, dtype=jnp.int32)
    other_pos = (1 - tensor_rank) * own_rows + jnp.arange(own_rows, dtype=jnp.int32)
    positions = jnp.concatenate([own_pos, other_pos])
    k_rotary = rotate(rot_latent, own_pos).astype(jnp.bfloat16)
    ranks_normed = low(plain_mul(jnp.concatenate([q_normed, kv_normed], axis=-1), rank_order))
    rot_pad = jnp.pad(k_rotary, ((0, 0), (NOPE, LANES - head_qk)))
    latent_seq = pair_tokens(jnp.concatenate([ranks_normed, rot_pad], axis=-1))
    rank_seq = latent_seq[:, :rank]
    rot_seq = latent_seq[:, rank:]
    zero = jnp.zeros((), jnp.bfloat16)
    q_seq = jnp.where(is_query[None, :], rank_seq, zero)
    kv_seq = jnp.where(is_query[None, :], zero, rank_seq)
    query = plain_mul(q_seq, up_weight)
    key_value = low(plain_mul(kv_seq, up_weight))
    visible = (positions[None, :] <= positions[:, None]) | (positions[None, :] < prefix_len[0])
    seen = visible.astype(jnp.float32)
    tables = turn_tables(positions)
    heads_low, query_full = attend(query, key_value, rot_seq, seen, tables, scale)
    attn_own = split_pair(mul_trans(heads_low, out_trans))
    mid_resid = resid_in + RESID * attn_own
    mlp_normed = norm_apply(mid_resid, gain_mlp).astype(jnp.bfloat16)

    links.tie(FAR, NEAR)
    mlp_seq = gather_tokens(links, mlp_normed)
    links.tie(NEAR, FAR)
    known_units = gather_bits(links, unit_column, others, True, known=known_units)
    unit_pieces = [
        piece.reshape(-1, 3 * share) for mask in masks_of(others) for piece in known_units[mask]
    ]
    act_low, d_units, d_mlp_terms, mlp_terms = run_units(mlp_seq, mlp_back, unit_pieces, share)
    d_mlp_own = return_tokens(links, d_mlp_terms, own_rows)
    unit_grad = unit_grads(mlp_seq, mlp_back, act_low, d_units, share).reshape(
        len(masks_of(others)), GROUP, -1, 3 * share
    )
    links.tie(NEAR, FAR)
    unit_sum = reduce_bits(
        links, lambda mask: unit_grad[masks_of(others).index(mask)], others, True
    )
    mlp_own = return_tokens(links, mlp_terms, own_rows)
    layer_out = low(mul_trans(low(mid_resid + RESID * mlp_own), to_order))
    unit_shards = place_group(exchange_group(links, [low(unit_sum[at]) for at in range(GROUP)]))
    gate_shard = join_units(unit_shards[..., :share], units)
    upper_shard = join_units(unit_shards[..., share : 2 * share], units)
    down_shard = join_units(unit_shards[..., 2 * share :], units).T

    _, mlp_norm_back = jax.vjp(norm_apply, mid_resid, gain_mlp)
    d_mid_norm, _ = mlp_norm_back(d_mlp_own)
    mid_inverse = lax.rsqrt(jnp.mean(mid_resid * mid_resid, axis=-1, keepdims=True) + EPS)
    gain_mlp_terms = d_mlp_own * mid_resid * mid_inverse
    d_mid = grad_out + d_mid_norm
    attn_back = pair_tokens((RESID * d_mid).astype(jnp.bfloat16))
    d_heads = low(plain_mul(attn_back, out_trans))
    out_shard = reduce_dp(links, trans_mul(attn_back, heads_low)).T
    d_query, d_key_value, d_rot = attend_back(
        query_full, key_value, rot_seq, seen, tables, d_heads, scale
    )
    d_rank = jnp.where(
        is_query[None, :], mul_trans(d_query, up_weight), mul_trans(d_key_value, up_weight)
    )
    d_latent_own = split_pair(jnp.concatenate([d_rank, d_rot], axis=-1))
    d_rank_own = move_columns(d_latent_own[:, :rank], rank_order, True, 2)
    d_q_own, d_kv_own = d_rank_own[:, :q_rank], d_rank_own[:, q_rank:]
    d_rot_own = d_latent_own[:, rank + NOPE : rank + head_qk]
    up_shard = reduce_dp(
        links,
        trans_mul(
            jnp.concatenate([q_seq, kv_seq], axis=0),
            jnp.concatenate([d_query, d_key_value], axis=0),
        ),
    )
    qup_shard = up_shard[:q_rows].reshape(q_rows, heads_local, LANES)[..., :head_qk]
    kvup_shard = up_shard[q_rows:]

    _, q_norm_back = jax.vjp(norm_apply, q_latent, gain_q)
    d_q_latent, _ = q_norm_back(d_q_own)
    _, kv_norm_back = jax.vjp(norm_apply, kv_latent, gain_kv)
    d_kv_latent, _ = kv_norm_back(d_kv_own)
    q_inverse = lax.rsqrt(jnp.mean(q_latent * q_latent, axis=-1, keepdims=True) + EPS)
    kv_inverse = lax.rsqrt(jnp.mean(kv_latent * kv_latent, axis=-1, keepdims=True) + EPS)
    gain_rank_terms = low(
        jnp.concatenate(
            [d_q_own * q_latent * q_inverse, d_kv_own * kv_latent * kv_inverse], axis=-1
        )
    )
    d_rot_raw = rotate_back(rot_latent, own_pos, d_rot_own)
    d_latents = low(
        jnp.concatenate(
            [
                d_q_latent,
                d_kv_latent,
                d_rot_raw,
                jnp.zeros((own_rows, packed_columns - down_columns), jnp.float32),
            ],
            axis=-1,
        )
    )
    d_x_normed = mul_trans(d_latents, all_packed)
    _, x_norm_back = jax.vjp(norm_apply, resid_in, gain_attn)
    d_x_norm, _ = x_norm_back(d_x_normed)
    x_inverse = lax.rsqrt(jnp.mean(resid_in * resid_in, axis=-1, keepdims=True) + EPS)
    gain_attn_terms = d_x_normed * resid_in * x_inverse
    grad_input = move_columns(d_mid + d_x_norm, to_order, True, 3)

    kind = jnp.arange(3 * own_rows, dtype=jnp.int32)[:, None] // own_rows + down_columns
    markers = (jnp.arange(packed_columns, dtype=jnp.int32)[None, :] == kind).astype(jnp.bfloat16)
    grad_packed = trans_mul(
        jnp.concatenate(
            [
                x_normed,
                low(gain_attn_terms),
                low(gain_mlp_terms),
                low(plain_mul(gain_rank_terms, gain_order)),
            ],
            axis=0,
        ),
        jnp.concatenate([d_latents, markers], axis=0),
    ).reshape(dp_count, tensor_count, down_rows, packed_columns)
    keep = jnp.where(is_first, grad_packed[:, 0], grad_packed[:, 1])
    give = jnp.where(is_first, grad_packed[:, 1], grad_packed[:, 0])
    keep = keep + wide(core_swap(low(give)))
    packed_shard = reduce_dp(links, keep.reshape(dp_count * down_rows, packed_columns))
    gain_shards = packed_shard[:, down_columns : down_columns + 3].T

    return (
        layer_out,
        grad_input,
        gain_shards[0],
        packed_shard[:, :q_rank],
        gain_shards[2, :q_share],
        packed_shard[:, q_rank:down_columns],
        gain_shards[2, q_share : q_share + kv_share],
        qup_shard.reshape(q_up.shape),
        kvup_shard,
        out_shard,
        gain_shards[1],
        gate_shard,
        upper_shard,
        down_shard,
    )


def solution(mesh):
    return jax.shard_map(
        body,
        mesh=mesh,
        in_specs=(
            P(("dp", "tensor"), None),
            P("dp"),
            P(("dp", "tensor")),
            P(("dp", "tensor"), None),
            P(("dp", "tensor")),
            P(("dp", "tensor"), None),
            P(("dp", "tensor")),
            P("dp", "tensor"),
            P("dp", "tensor"),
            P("tensor", "dp"),
            P(("dp", "tensor")),
            P("dp", "tensor"),
            P("dp", "tensor"),
            P("tensor", "dp"),
            P(("dp", "tensor"), None),
        ),
        out_specs=(
            P(("dp", "tensor"), None),
            P(("dp", "tensor"), None),
            P(("dp", "tensor")),
            P(("dp", "tensor"), None),
            P(("dp", "tensor")),
            P(("dp", "tensor"), None),
            P(("dp", "tensor")),
            P("dp", "tensor"),
            P("dp", "tensor"),
            P("tensor", "dp"),
            P(("dp", "tensor")),
            P("dp", "tensor"),
            P("dp", "tensor"),
            P("tensor", "dp"),
        ),
        check_vma=False,
    )
```

time: 3930 us -> 942 us (0.24)
  waiting for transfers between devices: 3520 us -> 532 us
  matrix products: 230 us -> 56.4 us
  Pallas kernels: 0 us -> 99.1 us
  blocking collectives: 89.3 us -> 0 us
  local copies, waits for them, and re-layouts: 24.7 us -> 105 us
  starting transfers between devices: 10.3 us -> 67 us
  other arithmetic: 26.1 us -> 68.7 us
    reduce_scatter x12 -> x0, waiting for transfers between devices: 2670 us -> none  [the longest x1 676 us: body(): lax.psum_scatter(grad_down, 'dp', scatter_dimension=1, tiled=True)]
    all_gather x11 -> x0, waiting for transfers between devices: 838 us -> none  [the longest x1 192 us: body(): lax.all_gather(w_gate, 'dp', axis=0, tiled=True)]
    ppermute x0 -> x78, waiting for transfers between devices: none -> 532 us  [the longest x68 532 us: flip(): lax.ppermute(values, 'dp', [(place, place ^ mask) for place in range(coun...]
    pallas_call x0 -> x14, Pallas kernels: none -> 99.1 us  [the longest x1 41.6 us: run_units(): pl.pallas_call(partial(units_kernel, share, len(pieces)), grid=(steps,),...]
    unnamed x2 -> x0, blocking collectives: 83.5 us -> none
    ppermute x0 -> x78, starting transfers between devices: none -> 67 us  [the longest x68 65.8 us: flip(): lax.ppermute(values, 'dp', [(place, place ^ mask) for place in range(coun...]
    dot_general x8 -> x3, matrix products: 65.5 us -> 8.46 us  [trans_mul(): lax.dot_general(left, right, (((0,), (0,)), ((), ())), preferred_element_...]
    dot_general x35 -> x0, matrix products: 56.6 us -> none  [the longest x10 13.9 us: masked_scores(): jnp.einsum('qhd,khd->hqk', query_part, key_part, preferred_element_type=j...]
  transfers between devices with their start and end apart: 25 -> 78, of which waited for: 20 -> 46; matrix products, arithmetic and copies ran while one was open for 4% -> 22% of each run, Pallas kernels for 0% -> 4%
where the time goes in v2:
time: 942 us; the launch traced here: 932 us
  waiting for transfers between devices  532 us (56%)
  local copies, waits for them, and re-layouts  105 us (11%)
  Pallas kernels  99.1 us (11%)
  other arithmetic  68.7 us (7%)
  starting transfers between devices  67 us (7%)
  matrix products  56.4 us (6%)
    ppermute x68, waiting for transfers between devices, flip(): lax.ppermute(values, 'dp', [(place, place ^ mask) for place in range(coun...  532 us
    ppermute x68, starting transfers between devices, flip(): lax.ppermute(values, 'dp', [(place, place ^ mask) for place in range(coun...  65.8 us
    pallas_call x1, Pallas kernels, run_units(): pl.pallas_call(partial(units_kernel, share, len(pieces)), grid=(steps,),...  41.6 us
    unnamed x259, local copies, waits for them, and re-layouts  40.1 us
    dot_general x8, matrix products, mul_trans(): lax.dot_general(left, right, (((1,), (1,)), ((), ())), preferred_element_...  31 us
    pallas_call x1, Pallas kernels, unit_grads(): pl.pallas_call(partial(unit_grads_kernel, share), grid=(CHUNKS,), in_spec...  21.1 us
  transfers between devices with their start and end apart: 78, of which 46 were waited for; matrix products, arithmetic and copies ran while one was open for 22% of the time, Pallas kernels for 4%

profile of v2, /device:TPU:0, one launch (start us, length us, event | category | flops | bytes accessed | tf_op | source)
XLA Modules:
  0.0 932.2 jit_solution(4696898938418970800)
XLA Ops:
  4.9 4.0 collective-permute-start.1
  21.2 5.0 fusion.2
  28.4 5.6 collective-permute-done.2
  42.4 11.4 %collective-permute-done.3 = bf16[4,80,1152]{2,1,0:T(8,128)(2,1)} collective-permute-done((bf16[4,80,1152]{2,1,0:T(8,128)(2,1)}, bf16[4,80,1152]{2,1,0:T(8,128)(2,1)}, u32[]{:S(2)}, u32[]{:S(2)}) %collective-permute-start.3) | collective-permute-done | bytes 737312 | tf_op jit(solution)/shard_map/ppermute | solution.py:120
  75.2 20.0 %collective-permute-done.18 = bf16[160,1280]{1,0:T(8,128)(2,1)S(1)} collective-permute-done((bf16[160,1280]{1,0:T(8,128)(2,1)S(1)}, bf16[160,1280]{1,0:T(8,128)(2,1)S(1)}, u32[]{:S(2)}, u32[]{:S(2)}) %collective-permute-start.18) | collective-permute-done | bytes 409632 | tf_op jit(solution)/shard_map/ppermute | solution.py:120
  97.9 4.1 collective-permute-done.12
  102.2 30.8 %collective-permute-done.25 = bf16[160,2688]{1,0:T(8,128)(2,1)S(1)} collective-permute-done((bf16[160,2688]{1,0:T(8,128)(2,1)S(1)}, bf16[160,2688]{1,0:T(8,128)(2,1)S(1)}, u32[]{:S(2)}, u32[]{:S(2)}) %collective-permute-start.25) | collective-permute-done | bytes 860192 | tf_op jit(solution)/shard_map/ppermute | solution.py:120
  137.0 23.6 %collective-permute-done.19 = bf16[160,1280]{1,0:T(8,128)(2,1)S(1)} collective-permute-done((bf16[160,1280]{1,0:T(8,128)(2,1)S(1)}, bf16[160,1280]{1,0:T(8,128)(2,1)S(1)}, u32[]{:S(2)}, u32[]{:S(2)}) %collective-permute-start.19) | collective-permute-done | bytes 409632 | tf_op jit(solution)/shard_map/ppermute | solution.py:120
  163.5 8.6 collective-permute-done.26
  184.8 8.6 collective-permute-done.13
  201.5 15.1 %collective-permute-done.27.refs_2_ = bf16[128,2560]{1,0:T(8,128)(2,1)S(1)} collective-permute-done((bf16[128,2560]{1,0:T(8,128)(2,1)S(1)}, bf16[128,2560]{1,0:T(8,128)(2,1)S(1)}, u32[]{:S(2)}, u32[]{:S(2)}) %collective-permute-start.27) | collective-permute-done | bytes 655392 | tf_op jit(solution)/shard_map/ppermute | solution.py:120
  228.2 4.1 fusion.258.q_ref
  233.9 11.0 %attend.1 = (bf16[256,1280]{1,0:T(8,128)(2,1)S(1)}, bf16[256,2560]{1,0:T(8,128)(2,1)S(1)}) custom-call(f32[256,2560]{1,0:T(8,128)S(1)} %fusion.258.q_ref, bf16[256,2560]{1,0:T(8,128)(2,1)S(1)} %convolution_convert_fusion.kv_ref, bf16[256,128]{1,0:T(8,128)(2,1)S(1)} %pad_maximum_fusion.27.rot_ref, f32[256,256]{1,0:T(8,128)S(1)} %copy-done.2, ...), custom_call_target="tpu_custom_call" | custom-call | tf_op jit(solution)/shard_map/attend/pallas_call | solution.py:585
  244.9 9.5 %collective-permute-done.20 = bf16[4,160,1280]{2,1,0:T(8,128)(2,1)S(1)} collective-permute-done((bf16[4,160,1280]{2,1,0:T(8,128)(2,1)S(1)}, bf16[4,160,1280]{2,1,0:T(8,128)(2,1)S(1)}, u32[]{:S(2)}, u32[]{:S(2)}) %collective-permute-start.20) | collective-permute-done | bytes 1638432 | tf_op jit(solution)/shard_map/ppermute | solution.py:120
  257.1 17.3 %collective-permute-done.23 = bf16[2,160,1280]{2,1,0:T(8,128)(2,1)S(1)} collective-permute-done((bf16[2,160,1280]{2,1,0:T(8,128)(2,1)S(1)}, bf16[2,160,1280]{2,1,0:T(8,128)(2,1)S(1)}, u32[]{:S(2)}, u32[]{:S(2)}) %collective-permute-start.23) | collective-permute-done | bytes 819232 | tf_op jit(solution)/shard_map/ppermute | solution.py:120
  280.9 8.4 collective-permute-done.28.refs_1_
  293.2 10.9 %collective-permute-done.29.refs_3_ = bf16[128,2560]{1,0:T(8,128)(2,1)S(1)} collective-permute-done((bf16[128,2560]{1,0:T(8,128)(2,1)S(1)}, bf16[128,2560]{1,0:T(8,128)(2,1)S(1)}, u32[]{:S(2)}, u32[]{:S(2)}) %collective-permute-start.29) | collective-permute-done | bytes 655392 | tf_op jit(solution)/shard_map/ppermute | solution.py:120
  305.4 18.3 %collective-permute-done.32.refs_2_ = bf16[128,2560]{1,0:T(8,128)(2,1)S(1)} collective-permute-done((bf16[128,2560]{1,0:T(8,128)(2,1)S(1)}, bf16[128,2560]{1,0:T(8,128)(2,1)S(1)}, u32[]{:S(2)}, u32[]{:S(2)}) %collective-permute-start.32) | collective-permute-done | bytes 655392 | tf_op jit(solution)/shard_map/ppermute | solution.py:120
  326.6 13.8 %collective-permute-done.33.refs_3_ = bf16[128,2560]{1,0:T(8,128)(2,1)S(1)} collective-permute-done((bf16[128,2560]{1,0:T(8,128)(2,1)S(1)}, bf16[128,2560]{1,0:T(8,128)(2,1)S(1)}, u32[]{:S(2)}, u32[]{:S(2)}) %collective-permute-start.33) | collective-permute-done | bytes 655392 | tf_op jit(solution)/shard_map/ppermute | solution.py:120
  342.8 13.4 %collective-permute-done.36 = bf16[4,160,2688]{2,1,0:T(8,128)(2,1)S(1)} collective-permute-done((bf16[4,160,2688]{2,1,0:T(8,128)(2,1)S(1)}, bf16[4,160,2688]{2,1,0:T(8,128)(2,1)S(1)}, u32[]{:S(2)}, u32[]{:S(2)}) %collective-permute-start.36) | collective-permute-done | bytes 3440672 | tf_op jit(solution)/shard_map/ppermute | solution.py:120
  359.2 36.1 %collective-permute-done.37 = bf16[2,160,2688]{2,1,0:T(8,128)(2,1)S(1)} collective-permute-done((bf16[2,160,2688]{2,1,0:T(8,128)(2,1)S(1)}, bf16[2,160,2688]{2,1,0:T(8,128)(2,1)S(1)}, u32[]{:S(2)}, u32[]{:S(2)}) %collective-permute-start.37) | collective-permute-done | bytes 1720352 | tf_op jit(solution)/shard_map/ppermute | solution.py:120
  398.8 41.6 %run_units.1 = (bf16[1024,896]{1,0:T(8,128)(2,1)}, bf16[1024,1792]{1,0:T(8,128)(2,1)}, bf16[1024,2560]{1,0:T(8,128)(2,1)}, bf16[1024,2560]{1,0:T(8,128)(2,1)}) custom-call(bf16[512,2560]{1,0:T(8,128)(2,1)} %bitcast.431, bf16[512,2560]{1,0:T(8,128)(2,1)} %copy-done.16, bf16[512,2560]{1,0:T(8,128)(2,1)} %bitcast.428, bf16[512,2560]{1,0:T(8,128)(2,1)} %copy-done.15, ...), custom_call_target="tpu_custom_call" | custom-call | tf_op jit(solution)/shard_map/run_units/pallas_call | solution.py:410
  440.4 21.1 %unit_grads.1 = bf16[2560,2688]{1,0:T(8,128)(2,1)} custom-call(bf16[512,2560]{1,0:T(8,128)(2,1)} %bitcast.432, bf16[512,2560]{1,0:T(8,128)(2,1)} %copy-done.16, bf16[512,2560]{1,0:T(8,128)(2,1)} %bitcast.429, bf16[512,2560]{1,0:T(8,128)(2,1)} %copy-done.15, bf16[1024,896]{1,0:T(8,128)(2,1)} %get-tuple-element.138.act_ref, ...), custom_call_target="tpu_custom_call" | custom-call | tf_op jit(solution)/shard_map/unit_grads/pallas_call | solution.py:436
  461.5 6.8 fusion.249
  473.6 32.7 %collective-permute-done.51 = bf16[2,160,2688]{2,1,0:T(8,128)(2,1)S(1)} collective-permute-done((bf16[2,160,2688]{2,1,0:T(8,128)(2,1)S(1)}, bf16[2,160,2688]{2,1,0:T(8,128)(2,1)S(1)}, u32[]{:S(2)}, u32[]{:S(2)}) %collective-permute-start.51) | collective-permute-done | bytes 1720352 | tf_op jit(solution)/shard_map/ppermute | solution.py:120
  513.4 13.2 %collective-permute-done.41.refs_0_ = bf16[128,2560]{1,0:T(8,128)(2,1)S(1)} collective-permute-done((bf16[128,2560]{1,0:T(8,128)(2,1)S(1)}, bf16[128,2560]{1,0:T(8,128)(2,1)S(1)}, u32[]{:S(2)}, u32[]{:S(2)}) %collective-permute-start.41) | collective-permute-done | bytes 655392 | tf_op jit(solution)/shard_map/ppermute | solution.py:120
  530.6 10.9 %collective-permute-done.42.refs_0_ = bf16[128,2560]{1,0:T(8,128)(2,1)S(1)} collective-permute-done((bf16[128,2560]{1,0:T(8,128)(2,1)S(1)}, bf16[128,2560]{1,0:T(8,128)(2,1)S(1)}, u32[]{:S(2)}, u32[]{:S(2)}) %collective-permute-start.42) | collective-permute-done | bytes 655392 | tf_op jit(solution)/shard_map/ppermute | solution.py:120
  543.1 12.5 %collective-permute-done.44.refs_0_ = bf16[128,2560]{1,0:T(8,128)(2,1)S(1)} collective-permute-done((bf16[128,2560]{1,0:T(8,128)(2,1)S(1)}, bf16[128,2560]{1,0:T(8,128)(2,1)S(1)}, u32[]{:S(2)}, u32[]{:S(2)}) %collective-permute-start.44) | collective-permute-done | bytes 655392 | tf_op jit(solution)/shard_map/ppermute | solution.py:120
  565.9 14.0 %attend_back.1 = (bf16[256,2560]{1,0:T(8,128)(2,1)S(1)}, bf16[256,2560]{1,0:T(8,128)(2,1)S(1)}, f32[256,128]{1,0:T(8,128)S(1)}) custom-call(bf16[256,2560]{1,0:T(8,128)(2,1)S(1)} %copy-done.4, bf16[256,2560]{1,0:T(8,128)(2,1)S(1)} %convolution_convert_fusion.kv_ref, bf16[256,128]{1,0:T(8,128)(2,1)S(1)} %pad_maximum_fusion.27.rot_ref, ...), custom_call_target="tpu_custom_call" | custom-call | tf_op jit(solution)/shard_map/attend_back/pallas_call | solution.py:602
  584.4 4.0 convolution_select_fusion
  604.4 5.1 multiply_reduce_fusion
  626.1 7.6 fusion
  639.9 54.8 %collective-permute-done.52 = bf16[4,160,2688]{2,1,0:T(8,128)(2,1)} collective-permute-done((bf16[4,160,2688]{2,1,0:T(8,128)(2,1)}, bf16[4,160,2688]{2,1,0:T(8,128)(2,1)}, u32[]{:S(2)}, u32[]{:S(2)}) %collective-permute-start.52) | collective-permute-done | bytes 3440672 | tf_op jit(solution)/shard_map/ppermute | solution.py:120
  696.0 4.3 fusion.9
  703.5 8.0 fusion.19
  712.0 6.4 fusion.244
  718.4 23.5 %collective-permute-done.55 = bf16[2,160,2688]{2,1,0:T(8,128)(2,1)} collective-permute-done((bf16[2,160,2688]{2,1,0:T(8,128)(2,1)}, bf16[2,160,2688]{2,1,0:T(8,128)(2,1)}, u32[]{:S(2)}, u32[]{:S(2)}) %collective-permute-start.55) | collective-permute-done | bytes 1720352 | tf_op jit(solution)/shard_map/ppermute | solution.py:120
  746.7 14.0 %collective-permute-done.56 = bf16[2,160,1280]{2,1,0:T(8,128)(2,1)S(1)} collective-permute-done((bf16[2,160,1280]{2,1,0:T(8,128)(2,1)}, bf16[2,160,1280]{2,1,0:T(8,128)(2,1)S(1)}, u32[]{:S(2)}, u32[]{:S(2)}) %collective-permute-start.56) | collective-permute-done | bytes 819232 | tf_op jit(solution)/shard_map/ppermute | solution.py:120
  763.8 17.8 %collective-permute-done.72.refs_2_ = bf16[160,2688]{1,0:T(8,128)(2,1)S(1)} collective-permute-done((bf16[160,2688]{1,0:T(8,128)(2,1)S(1)}, bf16[160,2688]{1,0:T(8,128)(2,1)S(1)}, u32[]{:S(2)}, u32[]{:S(2)}) %collective-permute-start.72) | collective-permute-done | bytes 860192 | tf_op jit(solution)/shard_map/ppermute | solution.py:120
  784.8 36.9 %collective-permute-done.73.refs_3_ = bf16[160,2688]{1,0:T(8,128)(2,1)S(1)} collective-permute-done((bf16[160,2688]{1,0:T(8,128)(2,1)S(1)}, bf16[160,2688]{1,0:T(8,128)(2,1)S(1)}, u32[]{:S(2)}, u32[]{:S(2)}) %collective-permute-start.73) | collective-permute-done | bytes 860192 | tf_op jit(solution)/shard_map/ppermute | solution.py:120
  827.6 11.4 %collective-permute-done.60 = bf16[2,64,2560]{2,1,0:T(8,128)(2,1)S(1)} collective-permute-done((bf16[2,64,2560]{2,1,0:T(8,128)(2,1)S(1)}, bf16[2,64,2560]{2,1,0:T(8,128)(2,1)S(1)}, u32[]{:S(2)}, u32[]{:S(2)}) %collective-permute-start.60) | collective-permute-done | bytes 655392 | tf_op jit(solution)/shard_map/ppermute | solution.py:120
  854.0 4.6 copy.75
  864.9 3.7 reshape.668
  886.4 4.5 collective-permute-done.74
  899.1 3.8 collective-permute-done.70
  905.0 4.8 collective-permute-done.71
  912.1 8.4 collective-permute-done.75
  922.3 6.2 collective-permute-done.76
  (574 shorter events, 266.5 us)
Async XLA Ops:
  4.9 23.0 %collective-permute-start.1 = (bf16[80,1152]{1,0:T(8,128)(2,1)}, bf16[80,1152]{1,0:T(8,128)(2,1)}, u32[]{:S(2)}, u32[]{:S(2)}) collective-permute-start(bf16[80,1152]{1,0:T(8,128)(2,1)} %concatenate.113), channel_id=1, source_target_pairs={{0,16},{2,18},{4,20},{6,22},{8,24},{10,26},{12,28},{14,30},{16,0},... | collective-permute-start | bytes 552968 | tf_op jit(solution)/shard_map/ppermute | solution.py:120
  8.9 19.0 %collective-permute-start = (bf16[80,1152]{1,0:T(8,128)(2,1)}, bf16[80,1152]{1,0:T(8,128)(2,1)}, u32[]{:S(2)}, u32[]{:S(2)}) collective-permute-start(bf16[80,1152]{1,0:T(8,128)(2,1)} %concatenate.113), channel_id=1, source_target_pairs={{0,8},{2,10},{4,12},{6,14},{8,0},{10,2},{12,4},{14,6},{16,24},{18,... | collective-permute-start | bytes 552968 | tf_op jit(solution)/shard_map/ppermute | solution.py:120
  41.6 32.1 %collective-permute-start.10 = (bf16[64,2560]{1,0:T(8,128)(2,1)S(1)}, bf16[64,2560]{1,0:T(8,128)(2,1)S(1)}, u32[]{:S(2)}, u32[]{:S(2)}) collective-permute-start(bf16[64,2560]{1,0:T(8,128)(2,1)S(1)} %get-tuple-element.94), channel_id=1, source_target_pairs={{0,16},{2,18},{4,20},{6,22},{8,24},{10,26},{12,28},{14,30},{16,0},... | collective-permute-start | bytes 983048 | tf_op jit(solution)/shard_map/ppermute | solution.py:120
  42.0 32.1 %collective-permute-start.9 = (bf16[64,2560]{1,0:T(8,128)(2,1)S(1)}, bf16[64,2560]{1,0:T(8,128)(2,1)S(1)}, u32[]{:S(2)}, u32[]{:S(2)}) collective-permute-start(bf16[64,2560]{1,0:T(8,128)(2,1)S(1)} %get-tuple-element.94), channel_id=1, source_target_pairs={{0,8},{2,10},{4,12},{6,14},{8,0},{10,2},{12,4},{14,6},{16,24},{18,... | collective-permute-start | bytes 983048 | tf_op jit(solution)/shard_map/ppermute | solution.py:120
  66.3 35.7 %collective-permute-start.12 = (bf16[2,160,2688]{2,1,0:T(8,128)(2,1)S(1)}, bf16[2,160,2688]{2,1,0:T(8,128)(2,1)S(1)}, u32[]{:S(2)}, u32[]{:S(2)}) collective-permute-start(bf16[2,160,2688]{2,1,0:T(8,128)(2,1)S(1)} %pad_maximum_fusion.4), channel_id=1, source_target_pairs={{0,4},{2,6},{4,0},{6,2},{8,12},{10,14},{12,8},{14,10},{16,20},{18,... | collective-permute-start | bytes 5160968 | tf_op jit(solution)/shard_map/ppermute | solution.py:120
  73.6 100.9 %collective-permute-start.7 = (bf16[16,80,1152]{2,1,0:T(8,128)(2,1)S(1)}, bf16[16,80,1152]{2,1,0:T(8,128)(2,1)S(1)}, u32[]{:S(2)}, u32[]{:S(2)}) collective-permute-start(bf16[16,80,1152]{2,1,0:T(8,128)(2,1)S(1)} %bitcast.450), channel_id=1, source_target_pairs={{0,1},{1,0},{2,3},{3,2},{4,5},{5,4},{6,7},{7,6},{8,9},{9,8},{10,11... | collective-permute-start | bytes 8847368 | tf_op jit(solution)/shard_map/ppermute | solution.py:77
  73.7 21.5 %collective-permute-start.18 = (bf16[160,1280]{1,0:T(8,128)(2,1)S(1)}, bf16[160,1280]{1,0:T(8,128)(2,1)S(1)}, u32[]{:S(2)}, u32[]{:S(2)}) collective-permute-start(bf16[160,1280]{1,0:T(8,128)(2,1)S(1)} %bitcast.457), channel_id=1, source_target_pairs={{0,16},{2,18},{4,20},{6,22},{8,24},{10,26},{12,28},{14,30},{16,0},... | collective-permute-start | bytes 1228808 | tf_op jit(solution)/shard_map/ppermute | solution.py:120
  74.1 21.1 %collective-permute-start.11 = (bf16[64,2560]{1,0:T(8,128)(2,1)S(1)}, bf16[64,2560]{1,0:T(8,128)(2,1)S(1)}, u32[]{:S(2)}, u32[]{:S(2)}) collective-permute-start(bf16[64,2560]{1,0:T(8,128)(2,1)S(1)} %collective-permute-done.10), channel_id=1, source_target_pairs={{0,8},{2,10},{4,12},{6,14},{8,0},{10,2},{12,4},{14,6},{16,24},{18,... | collective-permute-start | bytes 983048 | tf_op jit(solution)/shard_map/ppermute | solution.py:120
  95.2 37.8 %collective-permute-start.25 = (bf16[160,2688]{1,0:T(8,128)(2,1)S(1)}, bf16[160,2688]{1,0:T(8,128)(2,1)S(1)}, u32[]{:S(2)}, u32[]{:S(2)}) collective-permute-start(bf16[160,2688]{1,0:T(8,128)(2,1)S(1)} %get-tuple-element.113), channel_id=1, source_target_pairs={{0,16},{2,18},{4,20},{6,22},{8,24},{10,26},{12,28},{14,30},{16,0},... | collective-permute-start | bytes 2580488 | tf_op jit(solution)/shard_map/ppermute | solution.py:120
  95.2 37.8 %collective-permute-start.17 = (bf16[160,1280]{1,0:T(8,128)(2,1)S(1)}, bf16[160,1280]{1,0:T(8,128)(2,1)S(1)}, u32[]{:S(2)}, u32[]{:S(2)}) collective-permute-start(bf16[160,1280]{1,0:T(8,128)(2,1)S(1)} %bitcast.458), channel_id=1, source_target_pairs={{0,8},{2,10},{4,12},{6,14},{8,0},{10,2},{12,4},{14,6},{16,24},{18,... | collective-permute-start | bytes 1228808 | tf_op jit(solution)/shard_map/ppermute | solution.py:120
  97.3 64.7 %collective-permute-start.14 = (bf16[4,64,2560]{2,1,0:T(8,128)(2,1)}, bf16[4,64,2560]{2,1,0:T(8,128)(2,1)S(1)}, u32[]{:S(2)}, u32[]{:S(2)}) collective-permute-start(bf16[4,64,2560]{2,1,0:T(8,128)(2,1)} %pad_maximum_fusion.9), channel_id=1, source_target_pairs={{0,2},{2,0},{4,6},{6,4},{8,10},{10,8},{12,14},{14,12},{16,18},{18,... | collective-permute-start | bytes 3932168 | tf_op jit(solution)/shard_map/ppermute | solution.py:120
  132.9 39.2 %collective-permute-start.26 = (bf16[160,2688]{1,0:T(8,128)(2,1)S(1)}, bf16[160,2688]{1,0:T(8,128)(2,1)S(1)}, u32[]{:S(2)}, u32[]{:S(2)}) collective-permute-start(bf16[160,2688]{1,0:T(8,128)(2,1)S(1)} %get-tuple-element.114), channel_id=1, source_target_pairs={{0,16},{2,18},{4,20},{6,22},{8,24},{10,26},{12,28},{14,30},{16,0},... | collective-permute-start | bytes 2580488 | tf_op jit(solution)/shard_map/ppermute | solution.py:120
  133.0 27.6 %collective-permute-start.19 = (bf16[160,1280]{1,0:T(8,128)(2,1)S(1)}, bf16[160,1280]{1,0:T(8,128)(2,1)S(1)}, u32[]{:S(2)}, u32[]{:S(2)}) collective-permute-start(bf16[160,1280]{1,0:T(8,128)(2,1)S(1)} %collective-permute-done.18), channel_id=1, source_target_pairs={{0,8},{2,10},{4,12},{6,14},{8,0},{10,2},{12,4},{14,6},{16,24},{18,... | collective-permute-start | bytes 1228808 | tf_op jit(solution)/shard_map/ppermute | solution.py:120
  162.9 30.5 %collective-permute-start.13 = (bf16[4,64,2560]{2,1,0:T(8,128)(2,1)}, bf16[4,64,2560]{2,1,0:T(8,128)(2,1)}, u32[]{:S(2)}, u32[]{:S(2)}) collective-permute-start(bf16[4,64,2560]{2,1,0:T(8,128)(2,1)} %pad_maximum_fusion.9), channel_id=1, source_target_pairs={{0,4},{2,6},{4,0},{6,2},{8,12},{10,14},{12,8},{14,10},{16,20},{18,... | collective-permute-start | bytes 3932168 | tf_op jit(solution)/shard_map/ppermute | solution.py:120
  184.8 31.8 %collective-permute-start.27 = (bf16[128,2560]{1,0:T(8,128)(2,1)S(1)}, bf16[128,2560]{1,0:T(8,128)(2,1)S(1)}, u32[]{:S(2)}, u32[]{:S(2)}) collective-permute-start(bf16[128,2560]{1,0:T(8,128)(2,1)S(1)} %get-tuple-element.116.refs_0_), channel_id=1, source_target_pairs={{0,16},{2,18},{4,20},{6,22},{8,24},{10,26},{12,28},{14,30},{16,0},... | collective-permute-start | bytes 1966088 | tf_op jit(solution)/shard_map/ppermute | solution.py:120
  194.5 22.8 %collective-permute-start.15 = (bf16[2,64,2560]{2,1,0:T(8,128)(2,1)S(1)}, bf16[2,64,2560]{2,1,0:T(8,128)(2,1)S(1)}, u32[]{:S(2)}, u32[]{:S(2)}) collective-permute-start(bf16[2,64,2560]{2,1,0:T(8,128)(2,1)S(1)} %slice.939), channel_id=1, source_target_pairs={{0,2},{2,0},{4,6},{6,4},{8,10},{10,8},{12,14},{14,12},{16,18},{18,... | collective-permute-start | bytes 1966088 | tf_op jit(solution)/shard_map/ppermute | solution.py:120
  195.2 21.4 %collective-permute-start.16 = (bf16[2,64,2560]{2,1,0:T(8,128)(2,1)S(1)}, bf16[2,64,2560]{2,1,0:T(8,128)(2,1)S(1)}, u32[]{:S(2)}, u32[]{:S(2)}) collective-permute-start(bf16[2,64,2560]{2,1,0:T(8,128)(2,1)S(1)} %copy-done.87), channel_id=1, source_target_pairs={{0,4},{2,6},{4,0},{6,2},{8,12},{10,14},{12,8},{14,10},{16,20},{18,... | collective-permute-start | bytes 1966088 | tf_op jit(solution)/shard_map/ppermute | solution.py:120
  216.6 76.4 %collective-permute-start.31 = (bf16[4,160,2688]{2,1,0:T(8,128)(2,1)S(1)}, bf16[4,160,2688]{2,1,0:T(8,128)(2,1)S(1)}, u32[]{:S(2)}, u32[]{:S(2)}) collective-permute-start(bf16[4,160,2688]{2,1,0:T(8,128)(2,1)S(1)} %copy-done.14), channel_id=1, source_target_pairs={{0,8},{2,10},{4,12},{6,14},{8,0},{10,2},{12,4},{14,6},{16,24},{18,... | collective-permute-start | bytes 10321928 | tf_op jit(solution)/shard_map/ppermute | solution.py:120
  216.6 37.8 %collective-permute-start.20 = (bf16[4,160,1280]{2,1,0:T(8,128)(2,1)S(1)}, bf16[4,160,1280]{2,1,0:T(8,128)(2,1)S(1)}, u32[]{:S(2)}, u32[]{:S(2)}) collective-permute-start(bf16[4,160,1280]{2,1,0:T(8,128)(2,1)S(1)} %copy-done.57), channel_id=1, source_target_pairs={{0,4},{2,6},{4,0},{6,2},{8,12},{10,14},{12,8},{14,10},{16,20},{18,... | collective-permute-start | bytes 4915208 | tf_op jit(solution)/shard_map/ppermute | solution.py:120
  217.3 37.5 %collective-permute-start.21 = (bf16[4,160,1280]{2,1,0:T(8,128)(2,1)S(1)}, bf16[4,160,1280]{2,1,0:T(8,128)(2,1)S(1)}, u32[]{:S(2)}, u32[]{:S(2)}) collective-permute-start(bf16[4,160,1280]{2,1,0:T(8,128)(2,1)S(1)} %copy-done.57), channel_id=1, source_target_pairs={{0,2},{2,0},{4,6},{6,4},{8,10},{10,8},{12,14},{14,12},{16,18},{18,... | collective-permute-start | bytes 4915208 | tf_op jit(solution)/shard_map/ppermute | solution.py:120
  254.8 20.9 %collective-permute-start.22 = (bf16[2,160,1280]{2,1,0:T(8,128)(2,1)S(1)}, bf16[2,160,1280]{2,1,0:T(8,128)(2,1)S(1)}, u32[]{:S(2)}, u32[]{:S(2)}) collective-permute-start(bf16[2,160,1280]{2,1,0:T(8,128)(2,1)S(1)} %slice.953), channel_id=1, source_target_pairs={{0,2},{2,0},{4,6},{6,4},{8,10},{10,8},{12,14},{14,12},{16,18},{18,... | collective-permute-start | bytes 2457608 | tf_op jit(solution)/shard_map/ppermute | solution.py:120
  279.4 76.8 %collective-permute-start.36 = (bf16[4,160,2688]{2,1,0:T(8,128)(2,1)S(1)}, bf16[4,160,2688]{2,1,0:T(8,128)(2,1)S(1)}, u32[]{:S(2)}, u32[]{:S(2)}) collective-permute-start(bf16[4,160,2688]{2,1,0:T(8,128)(2,1)S(1)} %copy-done.14), channel_id=1, source_target_pairs={{0,2},{2,0},{4,6},{6,4},{8,10},{10,8},{12,14},{14,12},{16,18},{18,... | collective-permute-start | bytes 10321928 | tf_op jit(solution)/shard_map/ppermute | solution.py:120
  293.0 30.8 %collective-permute-start.32 = (bf16[128,2560]{1,0:T(8,128)(2,1)S(1)}, bf16[128,2560]{1,0:T(8,128)(2,1)S(1)}, u32[]{:S(2)}, u32[]{:S(2)}) collective-permute-start(bf16[128,2560]{1,0:T(8,128)(2,1)S(1)} %multiply_convert_fusion.4.refs_0_), channel_id=1, source_target_pairs={{0,16},{2,18},{4,20},{6,22},{8,24},{10,26},{12,28},{14,30},{16,0},... | collective-permute-start | bytes 1966088 | tf_op jit(solution)/shard_map/ppermute | solution.py:120
  304.1 19.6 %collective-permute-start.30 = (bf16[128,2560]{1,0:T(8,128)(2,1)S(1)}, bf16[128,2560]{1,0:T(8,128)(2,1)S(1)}, u32[]{:S(2)}, u32[]{:S(2)}) collective-permute-start(bf16[128,2560]{1,0:T(8,128)(2,1)S(1)} %multiply_convert_fusion.4.refs_0_), channel_id=1, source_target_pairs={{0,4},{2,6},{4,0},{6,2},{8,12},{10,14},{12,8},{14,10},{16,20},{18,... | collective-permute-start | bytes 1966088 | tf_op jit(solution)/shard_map/ppermute | solution.py:120
  326.6 32.7 %collective-permute-start.35 = (bf16[512,2560]{1,0:T(8,128)(2,1)S(1)}, bf16[512,2560]{1,0:T(8,128)(2,1)S(1)}, u32[]{:S(2)}, u32[]{:S(2)}) collective-permute-start(bf16[512,2560]{1,0:T(8,128)(2,1)S(1)} %bitcast.427), channel_id=1, source_target_pairs={{0,1},{1,0},{2,3},{3,2},{4,5},{5,4},{6,7},{7,6},{8,9},{9,8},{10,11... | collective-permute-start | bytes 7864328 | tf_op jit(solution)/shard_map/ppermute | solution.py:77
  342.6 54.1 %collective-permute-start.34 = (bf16[512,2560]{1,0:T(8,128)(2,1)S(1)}, bf16[512,2560]{1,0:T(8,128)(2,1)S(1)}, u32[]{:S(2)}, u32[]{:S(2)}) collective-permute-start(bf16[512,2560]{1,0:T(8,128)(2,1)S(1)} %bitcast.430), channel_id=1, source_target_pairs={{0,1},{1,0},{2,3},{3,2},{4,5},{5,4},{6,7},{7,6},{8,9},{9,8},{10,11... | collective-permute-start | bytes 7864328 | tf_op jit(solution)/shard_map/ppermute | solution.py:77
  356.2 39.1 %collective-permute-start.37 = (bf16[2,160,2688]{2,1,0:T(8,128)(2,1)S(1)}, bf16[2,160,2688]{2,1,0:T(8,128)(2,1)S(1)}, u32[]{:S(2)}, u32[]{:S(2)}) collective-permute-start(bf16[2,160,2688]{2,1,0:T(8,128)(2,1)S(1)} %slice.970), channel_id=1, source_target_pairs={{0,2},{2,0},{4,6},{6,4},{8,10},{10,8},{12,14},{14,12},{16,18},{18,... | collective-permute-start | bytes 5160968 | tf_op jit(solution)/shard_map/ppermute | solution.py:120
  357.8 38.9 %collective-permute-start.38 = (bf16[2,160,2688]{2,1,0:T(8,128)(2,1)S(1)}, bf16[2,160,2688]{2,1,0:T(8,128)(2,1)S(1)}, u32[]{:S(2)}, u32[]{:S(2)}) collective-permute-start(bf16[2,160,2688]{2,1,0:T(8,128)(2,1)S(1)} %slice.971), channel_id=1, source_target_pairs={{0,8},{2,10},{4,12},{6,14},{8,0},{10,2},{12,4},{14,6},{16,24},{18,... | collective-permute-start | bytes 5160968 | tf_op jit(solution)/shard_map/ppermute | solution.py:120
  468.3 38.0 %collective-permute-start.51 = (bf16[2,160,2688]{2,1,0:T(8,128)(2,1)S(1)}, bf16[2,160,2688]{2,1,0:T(8,128)(2,1)S(1)}, u32[]{:S(2)}, u32[]{:S(2)}) collective-permute-start(bf16[2,160,2688]{2,1,0:T(8,128)(2,1)S(1)} %bitcast.454), channel_id=1, source_target_pairs={{0,2},{2,0},{4,6},{6,4},{8,10},{10,8},{12,14},{14,12},{16,18},{18,... | collective-permute-start | bytes 5160968 | tf_op jit(solution)/shard_map/ppermute | solution.py:120
  469.2 39.7 %collective-permute-start.40 = (bf16[512,2560]{1,0:T(8,128)(2,1)S(1)}, bf16[512,2560]{1,0:T(8,128)(2,1)}, u32[]{:S(2)}, u32[]{:S(2)}) collective-permute-start(bf16[512,2560]{1,0:T(8,128)(2,1)S(1)} %slice.773), channel_id=1, source_target_pairs={{0,1},{1,0},{2,3},{3,2},{4,5},{5,4},{6,7},{7,6},{8,9},{9,8},{10,11... | collective-permute-start | bytes 7864328 | tf_op jit(solution)/shard_map/ppermute | solution.py:77
  473.1 39.3 %collective-permute-start.39 = (bf16[512,2560]{1,0:T(8,128)(2,1)S(1)}, bf16[512,2560]{1,0:T(8,128)(2,1)S(1)}, u32[]{:S(2)}, u32[]{:S(2)}) collective-permute-start(bf16[512,2560]{1,0:T(8,128)(2,1)S(1)} %slice.768), channel_id=1, source_target_pairs={{0,1},{1,0},{2,3},{3,2},{4,5},{5,4},{6,7},{7,6},{8,9},{9,8},{10,11... | collective-permute-start | bytes 7864328 | tf_op jit(solution)/shard_map/ppermute | solution.py:77
  528.3 27.3 %collective-permute-start.44 = (bf16[128,2560]{1,0:T(8,128)(2,1)S(1)}, bf16[128,2560]{1,0:T(8,128)(2,1)S(1)}, u32[]{:S(2)}, u32[]{:S(2)}) collective-permute-start(bf16[128,2560]{1,0:T(8,128)(2,1)S(1)} %fusion.53), channel_id=1, source_target_pairs={{0,16},{2,18},{4,20},{6,22},{8,24},{10,26},{12,28},{14,30},{16,0},... | collective-permute-start | bytes 1966088 | tf_op jit(solution)/shard_map/ppermute | solution.py:120
  558.8 54.3 %collective-permute-start.50 = (bf16[2,160,2688]{2,1,0:T(8,128)(2,1)}, bf16[2,160,2688]{2,1,0:T(8,128)(2,1)}, u32[]{:S(2)}, u32[]{:S(2)}) collective-permute-start(bf16[2,160,2688]{2,1,0:T(8,128)(2,1)} %bitcast.99), channel_id=1, source_target_pairs={{0,8},{2,10},{4,12},{6,14},{8,0},{10,2},{12,4},{14,6},{16,24},{18,... | collective-permute-start | bytes 5160968 | tf_op jit(solution)/shard_map/ppermute | solution.py:120
  558.8 78.3 %collective-permute-start.46 = (bf16[128,2560]{1,0:T(8,128)(2,1)}, bf16[128,2560]{1,0:T(8,128)(2,1)S(1)}, u32[]{:S(2)}, u32[]{:S(2)}) collective-permute-start(bf16[128,2560]{1,0:T(8,128)(2,1)} %get-tuple-element.133), channel_id=1, source_target_pairs={{0,4},{2,6},{4,0},{6,2},{8,12},{10,14},{12,8},{14,10},{16,20},{18,... | collective-permute-start | bytes 1966088 | tf_op jit(solution)/shard_map/ppermute | solution.py:120
  562.1 75.9 %collective-permute-start.45 = (bf16[128,2560]{1,0:T(8,128)(2,1)}, bf16[128,2560]{1,0:T(8,128)(2,1)}, u32[]{:S(2)}, u32[]{:S(2)}) collective-permute-start(bf16[128,2560]{1,0:T(8,128)(2,1)} %fusion.54), channel_id=1, source_target_pairs={{0,16},{2,18},{4,20},{6,22},{8,24},{10,26},{12,28},{14,30},{16,0},... | collective-permute-start | bytes 1966088 | tf_op jit(solution)/shard_map/ppermute | solution.py:120
  617.6 77.1 %collective-permute-start.52 = (bf16[4,160,2688]{2,1,0:T(8,128)(2,1)}, bf16[4,160,2688]{2,1,0:T(8,128)(2,1)}, u32[]{:S(2)}, u32[]{:S(2)}) collective-permute-start(bf16[4,160,2688]{2,1,0:T(8,128)(2,1)} %pad_maximum_fusion.2), channel_id=1, source_target_pairs={{0,2},{2,0},{4,6},{6,4},{8,10},{10,8},{12,14},{14,12},{16,18},{18,... | collective-permute-start | bytes 10321928 | tf_op jit(solution)/shard_map/ppermute | solution.py:120
  619.2 76.8 %collective-permute-start.54 = (bf16[4,160,2688]{2,1,0:T(8,128)(2,1)}, bf16[4,160,2688]{2,1,0:T(8,128)(2,1)}, u32[]{:S(2)}, u32[]{:S(2)}) collective-permute-start(bf16[4,160,2688]{2,1,0:T(8,128)(2,1)} %pad_maximum_fusion.3), channel_id=1, source_target_pairs={{0,8},{2,10},{4,12},{6,14},{8,0},{10,2},{12,4},{14,6},{16,24},{18,... | collective-permute-start | bytes 10321928 | tf_op jit(solution)/shard_map/ppermute | solution.py:120
  625.3 86.7 %collective-permute-start.49 = (bf16[16,80,1152]{2,1,0:T(8,128)(2,1)}, bf16[16,80,1152]{2,1,0:T(8,128)(2,1)}, u32[]{:S(2)}, u32[]{:S(2)}) collective-permute-start(bf16[16,80,1152]{2,1,0:T(8,128)(2,1)} %fusion.25), channel_id=1, source_target_pairs={{0,1},{1,0},{2,3},{3,2},{4,5},{5,4},{6,7},{7,6},{8,9},{9,8},{10,11... | collective-permute-start | bytes 8847368 | tf_op jit(solution)/shard_map/ppermute | solution.py:77
  702.8 39.1 %collective-permute-start.55 = (bf16[2,160,2688]{2,1,0:T(8,128)(2,1)}, bf16[2,160,2688]{2,1,0:T(8,128)(2,1)}, u32[]{:S(2)}, u32[]{:S(2)}) collective-permute-start(bf16[2,160,2688]{2,1,0:T(8,128)(2,1)} %pad_maximum_fusion.5), channel_id=1, source_target_pairs={{0,4},{2,6},{4,0},{6,2},{8,12},{10,14},{12,8},{14,10},{16,20},{18,... | collective-permute-start | bytes 5160968 | tf_op jit(solution)/shard_map/ppermute | solution.py:120
  711.5 33.4 %collective-permute-start.53 = (bf16[2,160,1280]{2,1,0:T(8,128)(2,1)}, bf16[2,160,1280]{2,1,0:T(8,128)(2,1)}, u32[]{:S(2)}, u32[]{:S(2)}) collective-permute-start(bf16[2,160,1280]{2,1,0:T(8,128)(2,1)} %pad_maximum_fusion.15), channel_id=1, source_target_pairs={{0,2},{2,0},{4,6},{6,4},{8,10},{10,8},{12,14},{14,12},{16,18},{18,... | collective-permute-start | bytes 2457608 | tf_op jit(solution)/shard_map/ppermute | solution.py:120
  743.3 38.3 %collective-permute-start.72 = (bf16[160,2688]{1,0:T(8,128)(2,1)S(1)}, bf16[160,2688]{1,0:T(8,128)(2,1)S(1)}, u32[]{:S(2)}, u32[]{:S(2)}) collective-permute-start(bf16[160,2688]{1,0:T(8,128)(2,1)S(1)} %copy-done.78), channel_id=1, source_target_pairs={{0,16},{2,18},{4,20},{6,22},{8,24},{10,26},{12,28},{14,30},{16,0},... | collective-permute-start | bytes 2580488 | tf_op jit(solution)/shard_map/ppermute | solution.py:120
  761.1 61.3 %collective-permute-start.59 = (bf16[4,160,1280]{2,1,0:T(8,128)(2,1)S(1)}, bf16[4,160,1280]{2,1,0:T(8,128)(2,1)S(1)}, u32[]{:S(2)}, u32[]{:S(2)}) collective-permute-start(bf16[4,160,1280]{2,1,0:T(8,128)(2,1)S(1)} %pad_maximum_fusion.8), channel_id=1, source_target_pairs={{0,2},{2,0},{4,6},{6,4},{8,10},{10,8},{12,14},{14,12},{16,18},{18,... | collective-permute-start | bytes 4915208 | tf_op jit(solution)/shard_map/ppermute | solution.py:120
  762.0 61.7 %collective-permute-start.57 = (bf16[4,160,1280]{2,1,0:T(8,128)(2,1)S(1)}, bf16[4,160,1280]{2,1,0:T(8,128)(2,1)S(1)}, u32[]{:S(2)}, u32[]{:S(2)}) collective-permute-start(bf16[4,160,1280]{2,1,0:T(8,128)(2,1)S(1)} %pad_maximum_fusion.7), channel_id=1, source_target_pairs={{0,4},{2,6},{4,0},{6,2},{8,12},{10,14},{12,8},{14,10},{16,20},{18,... | collective-permute-start | bytes 4915208 | tf_op jit(solution)/shard_map/ppermute | solution.py:120
  781.6 40.0 %collective-permute-start.73 = (bf16[160,2688]{1,0:T(8,128)(2,1)S(1)}, bf16[160,2688]{1,0:T(8,128)(2,1)S(1)}, u32[]{:S(2)}, u32[]{:S(2)}) collective-permute-start(bf16[160,2688]{1,0:T(8,128)(2,1)S(1)} %get-tuple-element.163), channel_id=1, source_target_pairs={{0,16},{2,18},{4,20},{6,22},{8,24},{10,26},{12,28},{14,30},{16,0},... | collective-permute-start | bytes 2580488 | tf_op jit(solution)/shard_map/ppermute | solution.py:120
  840.5 31.4 %collective-permute-start.63 = (bf16[4,64,2560]{2,1,0:T(8,128)(2,1)}, bf16[4,64,2560]{2,1,0:T(8,128)(2,1)}, u32[]{:S(2)}, u32[]{:S(2)}) collective-permute-start(bf16[4,64,2560]{2,1,0:T(8,128)(2,1)} %pad_maximum_fusion.12), channel_id=1, source_target_pairs={{0,4},{2,6},{4,0},{6,2},{8,12},{10,14},{12,8},{14,10},{16,20},{18,... | collective-permute-start | bytes 3932168 | tf_op jit(solution)/shard_map/ppermute | solution.py:120
  843.8 29.9 %collective-permute-start.61 = (bf16[4,64,2560]{2,1,0:T(8,128)(2,1)}, bf16[4,64,2560]{2,1,0:T(8,128)(2,1)}, u32[]{:S(2)}, u32[]{:S(2)}) collective-permute-start(bf16[4,64,2560]{2,1,0:T(8,128)(2,1)} %pad_maximum_fusion.11), channel_id=1, source_target_pairs={{0,2},{2,0},{4,6},{6,4},{8,10},{10,8},{12,14},{14,12},{16,18},{18,... | collective-permute-start | bytes 3932168 | tf_op jit(solution)/shard_map/ppermute | solution.py:120
  845.6 23.0 %collective-permute-start.67 = (bf16[160,1280]{1,0:T(8,128)(2,1)}, bf16[160,1280]{1,0:T(8,128)(2,1)}, u32[]{:S(2)}, u32[]{:S(2)}) collective-permute-start(bf16[160,1280]{1,0:T(8,128)(2,1)} %get-tuple-element.157), channel_id=1, source_target_pairs={{0,8},{2,10},{4,12},{6,14},{8,0},{10,2},{12,4},{14,6},{16,24},{18,... | collective-permute-start | bytes 1228808 | tf_op jit(solution)/shard_map/ppermute | solution.py:120
  871.8 19.1 %collective-permute-start.74 = (bf16[160,1280]{1,0:T(8,128)(2,1)S(1)}, bf16[160,1280]{1,0:T(8,128)(2,1)S(1)}, u32[]{:S(2)}, u32[]{:S(2)}) collective-permute-start(bf16[160,1280]{1,0:T(8,128)(2,1)S(1)} %fusion.79), channel_id=1, source_target_pairs={{0,16},{2,18},{4,20},{6,22},{8,24},{10,26},{12,28},{14,30},{16,0},... | collective-permute-start | bytes 1228808 | tf_op jit(solution)/shard_map/ppermute | solution.py:120
  (138 other events, 1716.6 us)

commit v3 on v2

--- a/solution.py
+++ b/solution.py
@@ -94,7 +94,7 @@
 
 
 def by_count(bits):
-    return sorted(masks_of(bits)[1:], key=lambda mask: (bin(mask).count("1"), mask))
+    return sorted(masks_of(bits)[1:], key=lambda mask: bin(mask).count("1"))
 
 
 def group_place():
@@ -102,32 +102,100 @@
     return sum(((place // bit) % 2) << at for at, bit in enumerate(GROUP_BITS))
 
 
+def tied(values, others):
+    return lax.optimization_barrier((values, others))[0] if others else values
+
+
+AFTER = {
+    "A1": ("B0", "B1"),
+    "C1": ("B0",),
+    "U0": ("B2", "C0", "C1"),
+    "B3": ("C0", "C1"),
+    "B4": ("C2",),
+    "B5": ("latents", "V1"),
+    "B6": ("latents",),
+    "G1": ("B4",),
+    "G2": ("B5", "B6"),
+    "C5": ("G1", "V2"),
+    "C6": ("G1", "V2"),
+    "M0": ("G2",),
+    "M1": ("G2",),
+    "M2": ("W1", "W0"),
+    "W2": ("M1",),
+    "W3": ("M1",),
+    "R1": ("D1",),
+    "R2": ("D2", "D1"),
+    "R3": ("D2", "D1"),
+    "P0": ("D2", "D1"),
+    "P1": ("R0",),
+    "P2": ("R1",),
+    "O0": ("R1",),
+    "Q0": ("P2", "R2"),
+    "Q1": ("R2",),
+    "T0": ("Q3",),
+}
+
+
+class Flow:
+    def __init__(self, links, name, routine):
+        self.links, self.name, self.routine = links, name, routine
+        self.count, self.result, self.given = 0, None, None
+        self.wanted = self.resume(None)
+
+    def resume(self, given):
+        try:
+            return self.routine.send(given)
+        except StopIteration as end:
+            self.result = end.value
+            return None
+
+    def step(self, hold=()):
+        if self.wanted is None:
+            return self
+        name = self.name + str(self.count)
+        got = self.links.send(*self.wanted, AFTER.get(name, ()))
+        self.links.done[name] = got
+        self.count += 1
+        self.wanted = self.resume(tied(got, self.links.named(hold)))
+        return self
+
+    def end(self):
+        while self.wanted is not None:
+            self.step()
+        return self.result
+
+
 class Links:
     def __init__(self):
         self.last = {}
-        self.ties = {}
-
-    def tie(self, bit, other):
-        self.ties[bit] = self.last[other]
-
-    def flip(self, values, mask):
-        bits = [bit for bit in all_bits() if bit & mask]
-        before = [self.last[bit] for bit in bits if bit in self.last]
-        before += [self.ties.pop(bit) for bit in bits if bit in self.ties]
-        if before:
-            values, _ = lax.optimization_barrier((values, before))
+        self.done = {}
+
+    def named(self, names):
+        return [self.done[name] for name in names if name in self.done]
+
+    def send(self, values, mask, after=()):
+        masks = mask if isinstance(mask, list) else [mask]
+        bits = sorted({bit for item in masks for bit in all_bits() if bit & item})
+        before = self.named(after) + [self.last[bit] for bit in bits if bit in self.last]
+        values = tied(values, before)
         count = lax.axis_size("dp")
-        got = lax.ppermute(values, "dp", [(place, place ^ mask) for place in range(count)])
-        for bit in bits:
-            self.last[bit] = got
+        got = [
+            lax.ppermute(item, "dp", [(place, place ^ to) for place in range(count)])
+            for item, to in zip(values if mask is masks else [values], masks)
+        ]
+        got = got if mask is masks else got[0]
+        self.last.update({bit: got for bit in bits})
         return got
+
+    def flow(self, name, routine):
+        return Flow(self, name, routine)
 
 
 def routes(mask, bits, split):
     ordered = [bit for bit in bits if bit & mask]
-    if len(ordered) == 1 or not split:
-        return [(ordered[0], slice(None))]
-    return [(ordered[0], 0), (ordered[-1], 1)]
+    if len(ordered) > 1 and split == "both":
+        return [(ordered[0], 0), (ordered[-1], 1)]
+    return [(ordered[-1 if split == "last" else 0], None)]
 
 
 def halves(values):
@@ -135,54 +203,53 @@
     return values[:half], values[half:]
 
 
-def gather_bits(links, values, bits, split, known=None, most=None):
-    known = dict(known or {0: [values]})
+def gather_bits(values, bits, split):
+    known = {0: [values]}
     for mask in by_count(bits):
-        if mask in known or (most and bin(mask).count("1") > most):
-            continue
         pieces = []
         for bit, part in routes(mask, bits, split):
             source = known[mask ^ bit]
-            whole = source[0] if len(source) == 1 else None
-            if part == slice(None):
-                moving = whole if whole is not None else jnp.concatenate(source)
+            if part is None:
+                moving = source[0] if len(source) == 1 else jnp.concatenate(source)
             else:
-                moving = halves(whole)[part] if whole is not None else source[part]
-            pieces.append(links.flip(moving, bit))
+                moving = halves(source[0])[part] if len(source) == 1 else source[part]
+            pieces.append((yield moving, bit))
         known[mask] = pieces
     return known
 
 
-def reduce_bits(links, block_of, bits, split, arrive=lambda values, bit: values):
+def reduce_bits(block_of, bits, split, arrive=lambda values, bit: values):
     added = {mask: [] for mask in masks_of(bits)}
 
     def summed(mask, part):
         values = block_of(mask)
-        if part != slice(None):
+        if part is not None:
             values = halves(values)[part]
         if added[mask]:
             values = wide(values)
         for held, extra in added[mask]:
-            if part == slice(None) and held != slice(None):
-                rest = [jnp.zeros_like(extra)] * 2
-                rest[held] = extra
-                values = values + jnp.concatenate([wide(item) for item in rest])
-            elif part == held:
+            if part is None or part == held:
                 values = values + wide(extra)
-            elif held == slice(None):
+            elif held is None:
                 values = values + wide(halves(extra)[part])
         return values
 
+    def whole(mask):
+        if any(held is not None for held, _ in added[mask]):
+            return [summed(mask, 0), summed(mask, 1)]
+        return [summed(mask, None)]
+
     for mask in reversed(by_count(bits)):
         for bit, part in routes(mask, bits, split):
-            if part == slice(None) and any(held != slice(None) for held, _ in added[mask]):
-                moving = jnp.concatenate([low(summed(mask, 0)), low(summed(mask, 1))])
+            if part is None:
+                parts = [low(item) for item in whole(mask)]
+                moving = parts[0] if len(parts) == 1 else jnp.concatenate(parts)
             else:
                 moving = low(summed(mask, part))
-            added[mask ^ bit].append((part, arrive(links.flip(moving, bit), bit)))
-    if any(held != slice(None) for held, _ in added[0]):
-        return jnp.concatenate([summed(0, 0), summed(0, 1)])
-    return summed(0, slice(None))
+            got = yield moving, bit
+            added[mask ^ bit].append((part, arrive(got, bit)))
+    parts = whole(0)
+    return parts[0] if len(parts) == 1 else jnp.concatenate(parts)
 
 
 def row_order():
@@ -195,15 +262,12 @@
     return other_bits(LAST_BITS)
 
 
-def start_gather(links, values):
-    known = gather_bits(links, values, first_bits(), False)
-    return jnp.stack([known[mask][0] for mask in masks_of(first_bits())])
-
-
-def end_gather(links, column, split=True):
-    known = gather_bits(links, column, LAST_BITS, split)
+def gather_dp(values):
     first = masks_of(first_bits())
-    half = column.shape[0] // 2
+    known = yield from gather_bits(values, first_bits(), "first")
+    column = jnp.stack([known[mask][0] for mask in first])
+    known = yield from gather_bits(column, LAST_BITS, "both")
+    half = len(first) // 2
 
     def block(mask):
         at = first.index(mask & ~sum(LAST_BITS))
@@ -213,7 +277,29 @@
     return jnp.concatenate([block(mask) for mask in row_order()], axis=0)
 
 
-def reduce_dp(links, grad, split=True):
+def gather_dp_direct(values):
+    first, last = masks_of(first_bits()), masks_of(LAST_BITS)
+    got = yield [values] * (len(first) - 1), first[1:]
+    column = jnp.stack([values] + got)
+    got = yield [column] * (len(last) - 1), last[1:]
+    known = dict(zip(last, [column] + got))
+    return jnp.concatenate(
+        [known[mask & sum(LAST_BITS)][first.index(mask & ~sum(LAST_BITS))] for mask in row_order()],
+        axis=0,
+    )
+
+
+def reduce_dp_direct(grad):
+    order, first, last = row_order(), masks_of(first_bits()), masks_of(LAST_BITS)
+    blocks = grad.reshape(len(order), -1, grad.shape[1])
+    columns = [jnp.stack([blocks[order.index(mask | item)] for item in first]) for mask in last]
+    got = yield [low(column) for column in columns[1:]], last[1:]
+    column = columns[0] + sum(wide(item) for item in got)
+    got = yield [low(column[at]) for at in range(1, len(first))], first[1:]
+    return column[0] + sum(wide(item) for item in got)
+
+
+def reduce_dp(grad):
     order = row_order()
     blocks = grad.reshape(len(order), -1, grad.shape[1])
     first = masks_of(first_bits())
@@ -221,8 +307,10 @@
     def column(last):
         return jnp.stack([blocks[order.index(last | mask)] for mask in first])
 
-    partial_sum = reduce_bits(links, column, LAST_BITS, split)
-    return reduce_bits(links, lambda mask: partial_sum[first.index(mask)], first_bits(), False)
+    partial_sum = yield from reduce_bits(column, LAST_BITS, "both")
+    return (
+        yield from reduce_bits(lambda mask: partial_sum[first.index(mask)], first_bits(), "first")
+    )
 
 
 def place_kernel(place_ref, *refs):
@@ -285,11 +373,13 @@
     return list(blocks)
 
 
-def exchange_group(links, blocks):
+def exchange_group(blocks, arrived):
     near, far = GROUP_BITS
-    there = links.flip(jnp.stack([blocks[1], blocks[3]]), near)
-    across = links.flip(blocks[2], far)
-    return [blocks[0], there[0], across, links.flip(there[1], far)]
+    there = yield jnp.stack([blocks[1], blocks[3]]), near
+    arrived.append(jnp.stack([blocks[0], there[0]]))
+    across = yield blocks[2], far
+    relayed = yield there[1], far
+    arrived.append(jnp.stack([across, relayed]))
 
 
 def cut_units(weight, share):
@@ -334,23 +424,27 @@
     )(*arrays)
 
 
-def gather_tokens(links, values):
-    known = gather_bits(links, values, GROUP_BITS, False)
+def gather_tokens(values):
+    known = yield from gather_bits(values, GROUP_BITS, "first")
     own = reorder([known[mask][0] for mask in masks_of(GROUP_BITS)], range(GROUP))
     own = own.reshape(-1, values.shape[1])
     return own, core_swap(own)
 
 
-def return_tokens(links, values, rows):
-    mine = values.shape[0] // 2
-    chip_sum = wide(values[:mine]) + wide(core_swap(values[mine:]))
-    chip_sum = chip_sum.reshape(GROUP, rows, -1)
+def gather_whole_tokens(values, to_order):
+    known = yield from gather_bits(values, GROUP_BITS, "last")
+    own = jnp.concatenate([known[mask][0] for mask in masks_of(GROUP_BITS)], axis=0)
+    own = low(plain_mul(own, to_order))
+    return own, core_swap(own)
+
+
+def return_tokens(mine, others, rows):
+    chip_sum = (wide(mine) + wide(others)).reshape(GROUP, rows, -1)
     masks = masks_of(GROUP_BITS)
     return reduce_bits(
-        links,
         lambda mask: chip_sum[masks.index(mask)],
         GROUP_BITS,
-        False,
+        "first",
         lambda got, bit: reorder([got], [masks.index(bit)])[0],
     )
 
@@ -467,6 +561,12 @@
 
 def one_hot(origins, size):
     return (jnp.arange(size, dtype=jnp.int32)[:, None] == origins[None, :]).astype(jnp.bfloat16)
+
+
+def pad_heads(columns, head):
+    column = jnp.arange(columns // head * LANES, dtype=jnp.int32)
+    within = column % LANES
+    return one_hot(jnp.where(within < head, column // LANES * head + within, -1), columns)
 
 
 def in_parts(values, count):
@@ -644,10 +744,8 @@
     heads_local = q_up.shape[1] // head_qk
     scale = head_qk ** (-0.5)
     links = Links()
-    heads_width = heads_local * LANES
-    q_padded = jnp.pad(
-        q_up.reshape(q_rows, heads_local, head_qk), ((0, 0), (0, 0), (0, LANES - head_qk))
-    ).reshape(q_rows, heads_width)
+    width_origins = block_origins(width)
+    to_order = one_hot(width_origins, width)
     units = w_gate.shape[1]
     share = round_up(units // GROUP, LANES)
 
@@ -668,20 +766,37 @@
         ],
         axis=1,
     )
-    down_column = start_gather(links, packed)
-    up_column = start_gather(links, jnp.concatenate([q_padded, kv_up], axis=0))
-    out_column = start_gather(links, o_proj.T)
-    core_packed = end_gather(links, down_column).reshape(dp_count, down_rows, packed_columns)
-    unit_column = jnp.stack(
-        exchange_group(
-            links,
-            pick_group(
-                jnp.concatenate([cut_units(item, share) for item in (w_gate, w_up, w_down.T)], axis=-1)
-            ),
+    others = other_bits(GROUP_BITS)
+    near_first = (NEAR,) + tuple(bit for bit in others if bit != NEAR)
+    back_flow = links.flow(
+        "G",
+        gather_whole_tokens(
+            (RESID * cotangent.astype(jnp.float32)).astype(jnp.bfloat16), to_order
+        ),
+    )
+    down_flow = links.flow("A", gather_dp_direct(packed)).step()
+    back_flow.step()
+    q_padded = low(plain_mul(q_up, pad_heads(q_up.shape[1], head_qk)))
+    up_flow = links.flow("B", gather_dp(jnp.concatenate([q_padded, kv_up], axis=0))).step().step()
+    down_flow.step()
+    up_flow.step()
+    out_flow = links.flow("C", gather_dp(o_proj.T)).step().step().step()
+    core_packed = down_flow.end().reshape(dp_count, down_rows, packed_columns)
+    unit_parts = []
+    unit_picks = pick_group(
+        jnp.concatenate(
+            [
+                cut_units(item, share)
+                for item in tied((w_gate, w_up, w_down.T), links.named(["B0"]))
+            ],
+            axis=-1,
         )
     )
-    up_weight = end_gather(links, up_column)
-    out_trans = end_gather(links, out_column)
+    exchange_flow = links.flow("U", exchange_group(unit_picks, unit_parts))
+    exchange_flow.step().step().step()
+    first_flow = links.flow("V", gather_bits(unit_parts[0], near_first, "first")).step()
+    up_flow.step()
+    up_flow.step()
     other_packed = core_swap(core_packed)
     is_first = tensor_rank == 0
     all_packed = jnp.stack(
@@ -692,8 +807,6 @@
         axis=1,
     ).reshape(width, packed_columns)
 
-    width_origins = block_origins(width)
-    to_order = one_hot(width_origins, width)
     rank_block = q_rows + kv_rows
     place = jnp.arange(rank, dtype=jnp.int32)
     device_of = block_origins(rank) // rank_block
@@ -707,6 +820,9 @@
         ),
         rank,
     )
+    hidden_low, cotangent_low = tied((hidden_in, cotangent), links.named(["A0"]))
+    moved_in = plain_mul(jnp.concatenate([hidden_low, cotangent_low], axis=0), to_order)
+    resid_in, grad_out = moved_in[:own_rows], moved_in[own_rows:]
     device_place = width_origins // down_rows
     in_share = width_origins % down_rows
     gain_order = one_hot(
@@ -727,12 +843,6 @@
     gain_rank = mul_trans(gains[2:3], gain_order)[0]
     gain_q, gain_kv = gain_rank[:q_rank], gain_rank[q_rank:]
 
-    moved_in = plain_mul(jnp.concatenate([hidden_in, cotangent], axis=0), to_order)
-    resid_in, grad_out = moved_in[:own_rows], moved_in[own_rows:]
-    mlp_back = gather_tokens(links, (RESID * grad_out).astype(jnp.bfloat16))
-    others = other_bits(GROUP_BITS)
-    links.tie(NEAR, FAR)
-    known_units = gather_bits(links, unit_column, others, True, most=1)
     x_normed = norm_apply(resid_in, gain_attn).astype(jnp.bfloat16)
     latents = plain_mul(x_normed, all_packed)
     q_latent = latents[:, :q_rank]
@@ -747,6 +857,18 @@
     ranks_normed = low(plain_mul(jnp.concatenate([q_normed, kv_normed], axis=-1), rank_order))
     rot_pad = jnp.pad(k_rotary, ((0, 0), (NOPE, LANES - head_qk)))
     latent_seq = pair_tokens(jnp.concatenate([ranks_normed, rot_pad], axis=-1))
+    links.done["latents"] = latent_seq
+    first_flow.step()
+    up_flow.step().step()
+    up_weight = up_flow.end()
+    first_flow.step()
+    out_flow.step().step()
+    last_flow = links.flow("W", gather_bits(unit_parts[1], near_first, "both")).step()
+    back_flow.step().step()
+    mlp_back = back_flow.end()
+    out_flow.step().step()
+    out_trans = out_flow.end()
+    last_flow.step()
     rank_seq = latent_seq[:, :rank]
     rot_seq = latent_seq[:, rank:]
     zero = jnp.zeros((), jnp.bfloat16)
@@ -758,32 +880,42 @@
     seen = visible.astype(jnp.float32)
     tables = turn_tables(positions)
     heads_low, query_full = attend(query, key_value, rot_seq, seen, tables, scale)
-    attn_own = split_pair(mul_trans(heads_low, out_trans))
+    attn_own = split_pair(mul_trans(heads_low, tied(out_trans, links.named(["G2"]))))
     mid_resid = resid_in + RESID * attn_own
     mlp_normed = norm_apply(mid_resid, gain_mlp).astype(jnp.bfloat16)
 
-    links.tie(FAR, NEAR)
-    mlp_seq = gather_tokens(links, mlp_normed)
-    links.tie(NEAR, FAR)
-    known_units = gather_bits(links, unit_column, others, True, known=known_units)
+    mlp_flow = links.flow("M", gather_tokens(mlp_normed)).step().step()
+    mlp_seq = mlp_flow.end()
+    last_flow.step().step()
+    first_units, last_units = first_flow.end(), last_flow.end()
     unit_pieces = [
-        piece.reshape(-1, 3 * share) for mask in masks_of(others) for piece in known_units[mask]
+        piece.reshape(-1, 3 * share)
+        for mask in masks_of(others)
+        for piece in first_units[mask] + last_units[mask]
     ]
+    if any(piece.shape[0] % 16 for piece in unit_pieces):
+        unit_pieces = [jnp.concatenate(unit_pieces)]
     act_low, d_units, d_mlp_terms, mlp_terms = run_units(mlp_seq, mlp_back, unit_pieces, share)
-    d_mlp_own = return_tokens(links, d_mlp_terms, own_rows)
-    unit_grad = unit_grads(mlp_seq, mlp_back, act_low, d_units, share).reshape(
-        len(masks_of(others)), GROUP, -1, 3 * share
-    )
-    links.tie(NEAR, FAR)
-    unit_sum = reduce_bits(
-        links, lambda mask: unit_grad[masks_of(others).index(mask)], others, True
-    )
-    mlp_own = return_tokens(links, mlp_terms, own_rows)
-    layer_out = low(mul_trans(low(mid_resid + RESID * mlp_own), to_order))
-    unit_shards = place_group(exchange_group(links, [low(unit_sum[at]) for at in range(GROUP)]))
-    gate_shard = join_units(unit_shards[..., :share], units)
-    upper_shard = join_units(unit_shards[..., share : 2 * share], units)
-    down_shard = join_units(unit_shards[..., 2 * share :], units).T
+    chip_rows = GROUP * own_rows
+    d_mlp_other = core_swap(d_mlp_terms[chip_rows:])
+    d_mlp_flow = links.flow("D", return_tokens(d_mlp_terms[:chip_rows], d_mlp_other, own_rows))
+    d_mlp_flow.step().step().step()
+    d_mlp_own = d_mlp_flow.end()
+    unit_grad = unit_grads(
+        mlp_seq, mlp_back, tied(act_low, [d_mlp_other]), d_units, share
+    ).reshape(len(masks_of(others)), GROUP, -1, 3 * share)
+    unit_flow = links.flow(
+        "R", reduce_bits(lambda mask: unit_grad[masks_of(others).index(mask)], others, "both")
+    )
+    unit_flow.step(["D1", "D2"]).step()
+    mlp_flow = links.flow(
+        "O",
+        return_tokens(
+            mlp_terms[:chip_rows],
+            core_swap(tied(mlp_terms, [d_mlp_other])[chip_rows:]),
+            own_rows,
+        ),
+    )
 
     _, mlp_norm_back = jax.vjp(norm_apply, mid_resid, gain_mlp)
     d_mid_norm, _ = mlp_norm_back(d_mlp_own)
@@ -792,10 +924,15 @@
     d_mid = grad_out + d_mid_norm
     attn_back = pair_tokens((RESID * d_mid).astype(jnp.bfloat16))
     d_heads = low(plain_mul(attn_back, out_trans))
-    out_shard = reduce_dp(links, trans_mul(attn_back, heads_low)).T
+    out_grad = trans_mul(attn_back, heads_low)
+    out_flow = links.flow("P", reduce_dp(out_grad)).step().step()
+    unit_flow.step().step()
+    out_flow.step()
+    mlp_flow.step().step().step()
     d_query, d_key_value, d_rot = attend_back(
-        query_full, key_value, rot_seq, seen, tables, d_heads, scale
-    )
+        query_full, key_value, rot_seq, seen, tables, tied(d_heads, links.named(["R0"]) + [out_grad]), scale
+    )
+    d_query, d_key_value, d_rot = tied((d_query, d_key_value, d_rot), links.named(["R1"]))
     d_rank = jnp.where(
         is_query[None, :], mul_trans(d_query, up_weight), mul_trans(d_key_value, up_weight)
     )
@@ -803,15 +940,26 @@
     d_rank_own = move_columns(d_latent_own[:, :rank], rank_order, True, 2)
     d_q_own, d_kv_own = d_rank_own[:, :q_rank], d_rank_own[:, q_rank:]
     d_rot_own = d_latent_own[:, rank + NOPE : rank + head_qk]
-    up_shard = reduce_dp(
-        links,
-        trans_mul(
-            jnp.concatenate([q_seq, kv_seq], axis=0),
-            jnp.concatenate([d_query, d_key_value], axis=0),
+    up_flow = links.flow(
+        "Q",
+        reduce_dp(
+            trans_mul(
+                jnp.concatenate([q_seq, kv_seq], axis=0),
+                jnp.concatenate([d_query, d_key_value], axis=0),
+            )
         ),
     )
-    qup_shard = up_shard[:q_rows].reshape(q_rows, heads_local, LANES)[..., :head_qk]
-    kvup_shard = up_shard[q_rows:]
+    unit_sum = unit_flow.end()
+    unit_parts = []
+    exchange_flow = links.flow(
+        "S", exchange_group([low(unit_sum[at]) for at in range(GROUP)], unit_parts)
+    )
+    exchange_flow.step().step()
+    out_flow.step()
+    exchange_flow.step()
+    up_flow.step().step().step().step()
+    out_flow.step().step()
+    out_shard = out_flow.end().T
 
     _, q_norm_back = jax.vjp(norm_apply, q_latent, gain_q)
     d_q_latent, _ = q_norm_back(d_q_own)
@@ -860,7 +1008,22 @@
     keep = jnp.where(is_first, grad_packed[:, 0], grad_packed[:, 1])
     give = jnp.where(is_first, grad_packed[:, 1], grad_packed[:, 0])
     keep = keep + wide(core_swap(low(give)))
-    packed_shard = reduce_dp(links, keep.reshape(dp_count * down_rows, packed_columns))
+    up_flow.step()
+    down_flow = links.flow("T", reduce_dp_direct(keep.reshape(dp_count * down_rows, packed_columns)))
+    down_flow.step()
+    up_flow.step().step()
+    up_shard = up_flow.end()
+    packed_shard = down_flow.end()
+    qup_shard = up_shard[:q_rows].reshape(q_rows, heads_local, LANES)[..., :head_qk]
+    kvup_shard = up_shard[q_rows:]
+    exchange_flow.end()
+    unit_parts = tied(unit_parts, links.named(["Q3"]))
+    unit_shards = place_group([part[at] for part in unit_parts for at in range(GROUP // 2)])
+    gate_shard = join_units(unit_shards[..., :share], units)
+    upper_shard = join_units(unit_shards[..., share : 2 * share], units)
+    down_shard = join_units(unit_shards[..., 2 * share :], units).T
+    mlp_own = mlp_flow.end()
+    layer_out = low(mul_trans(low(mid_resid + RESID * mlp_own), to_order))
     gain_shards = packed_shard[:, down_columns : down_columns + 3].T
 
     return (

time: 942 us -> 860 us (0.913)
  waiting for transfers between devices: 532 us -> 435 us
  matrix products: 56.4 us -> 70.5 us
  other arithmetic: 68.7 us -> 81.9 us
  local copies, waits for them, and re-layouts: 105 us -> 93.6 us
    ppermute x68 -> x69, waiting for transfers between devices: 532 us -> 430 us  [send(): lax.ppermute(item, 'dp', [(place, place ^ to) for place in range(count)])]
    dot_general x7 -> x9, matrix products: 17 us -> 37.2 us  [plain_mul(): return jnp.dot(left, right, preferred_element_type=jnp.float32)]
    another operation x16 -> x24, other arithmetic: 26.2 us -> 40.3 us
    unnamed x259 -> x263, local copies, waits for them, and re-layouts: 40.1 us -> 28.2 us
    ppermute x68 -> x69, starting transfers between devices: 65.8 us -> 70.3 us  [send(): lax.ppermute(item, 'dp', [(place, place ^ to) for place in range(count)])]
  transfers between devices with their start and end apart: 78 -> 79, of which waited for: 46 -> 38; matrix products, arithmetic and copies ran while one was open for 22% -> 26% of each run, Pallas kernels for 4% -> 6%
where the time goes in v3:
time: 860 us; the launch traced here: 852 us
  waiting for transfers between devices  435 us (51%)
  Pallas kernels  95.9 us (11%)
  local copies, waits for them, and re-layouts  93.6 us (11%)
  other arithmetic  81.9 us (10%)
  starting transfers between devices  70.9 us (8%)
  matrix products  70.5 us (8%)
    ppermute x69, waiting for transfers between devices, send(): lax.ppermute(item, 'dp', [(place, place ^ to) for place in range(count)])  430 us
    ppermute x69, starting transfers between devices, send(): lax.ppermute(item, 'dp', [(place, place ^ to) for place in range(count)])  70.3 us
    pallas_call x1, Pallas kernels, run_units(): pl.pallas_call(partial(units_kernel, share, len(pieces)), grid=(steps,),...  41.7 us
    dot_general x9, matrix products, plain_mul(): return jnp.dot(left, right, preferred_element_type=jnp.float32)  37.2 us
    unnamed x263, local copies, waits for them, and re-layouts  28.2 us
    another operation x11, other arithmetic  27.3 us
    dot_general x8, matrix products, mul_trans(): lax.dot_general(left, right, (((1,), (1,)), ((), ())), preferred_element_...  24.9 us
    pallas_call x1, Pallas kernels, unit_grads(): pl.pallas_call(partial(unit_grads_kernel, share), grid=(CHUNKS,), in_spec...  21.1 us
  transfers between devices with their start and end apart: 79, of which 38 were waited for; matrix products, arithmetic and copies ran while one was open for 26% of the time, Pallas kernels for 6%

profile of v3, /device:TPU:0, one launch (start us, length us, event | category | flops | bytes accessed | tf_op | source)
XLA Modules:
  0.0 852.2 jit_solution(12237964411562153500)
XLA Ops:
  4.1 5.1 collective-permute-start.2
  15.2 4.1 constant_dynamic-update-slice_fusion.8
  29.0 12.6 %collective-permute-done.3 = bf16[64,2560]{1,0:T(8,128)(2,1)S(1)} collective-permute-done((bf16[64,2560]{1,0:T(8,128)(2,1)S(1)}, bf16[64,2560]{1,0:T(8,128)(2,1)S(1)}, u32[]{:S(2)}, u32[]{:S(2)}) %collective-permute-start.3) | collective-permute-done | bytes 327712 | tf_op jit(solution)/shard_map/ppermute | solution.py:183
  57.6 12.4 %collective-permute-done.6 = bf16[4,80,1152]{2,1,0:T(8,128)(2,1)S(1)} collective-permute-done((bf16[4,80,1152]{2,1,0:T(8,128)(2,1)S(1)}, bf16[4,80,1152]{2,1,0:T(8,128)(2,1)S(1)}, u32[]{:S(2)}, u32[]{:S(2)}) %collective-permute-start.6) | collective-permute-done | bytes 737312 | tf_op jit(solution)/shard_map/ppermute | solution.py:183
  70.0 4.1 collective-permute-done.7
  74.1 13.7 %collective-permute-done.8 = bf16[4,80,1152]{2,1,0:T(8,128)(2,1)S(1)} collective-permute-done((bf16[4,80,1152]{2,1,0:T(8,128)(2,1)S(1)}, bf16[4,80,1152]{2,1,0:T(8,128)(2,1)S(1)}, u32[]{:S(2)}, u32[]{:S(2)}) %collective-permute-start.8) | collective-permute-done | bytes 737312 | tf_op jit(solution)/shard_map/ppermute | solution.py:183
  94.2 5.0 fusion.3
  102.0 4.4 collective-permute-done.14
  108.9 14.6 %collective-permute-done.17 = bf16[4,64,2560]{2,1,0:T(8,128)(2,1)S(1)} collective-permute-done((bf16[4,64,2560]{2,1,0:T(8,128)(2,1)}, bf16[4,64,2560]{2,1,0:T(8,128)(2,1)S(1)}, u32[]{:S(2)}, u32[]{:S(2)}) %collective-permute-start.17) | collective-permute-done | bytes 1310752 | tf_op jit(solution)/shard_map/ppermute | solution.py:183
  124.5 4.1 collective-permute-done.15
  131.1 8.4 collective-permute-done.23
  157.0 23.2 %collective-permute-done.24 = bf16[160,2688]{1,0:T(8,128)(2,1)} collective-permute-done((bf16[160,2688]{1,0:T(8,128)(2,1)}, bf16[160,2688]{1,0:T(8,128)(2,1)}, u32[]{:S(2)}, u32[]{:S(2)}) %collective-permute-start.24) | collective-permute-done | bytes 860192 | tf_op jit(solution)/shard_map/ppermute | solution.py:183
  188.7 24.4 %collective-permute-done.26 = bf16[2,160,2688]{2,1,0:T(8,128)(2,1)} collective-permute-done((bf16[2,160,2688]{2,1,0:T(8,128)(2,1)}, bf16[2,160,2688]{2,1,0:T(8,128)(2,1)}, u32[]{:S(2)}, u32[]{:S(2)}) %collective-permute-start.26) | collective-permute-done | bytes 1720352 | tf_op jit(solution)/shard_map/ppermute | solution.py:183
  228.5 4.2 convolution_convert_fusion.kv_ref
  232.7 4.2 fusion.276.q_ref
  236.8 10.6 %attend.1 = (bf16[256,1280]{1,0:T(8,128)(2,1)S(1)}, bf16[256,2560]{1,0:T(8,128)(2,1)S(1)}) custom-call(f32[256,2560]{1,0:T(8,128)S(1)} %fusion.276.q_ref, bf16[256,2560]{1,0:T(8,128)(2,1)S(1)} %convolution_convert_fusion.kv_ref, bf16[256,128]{1,0:T(8,128)(2,1)S(1)} %slice.962.rot_ref, f32[256,256]{1,0:T(8,128)S(1)} %or_convert_fusion.seen_ref, ...), custom_call_target="tpu_custom_call" | custom-call | tf_op jit(solution)/shard_map/attend/pallas_call | solution.py:685
  249.7 14.8 %collective-permute-done.27 = bf16[2,160,2688]{2,1,0:T(8,128)(2,1)S(1)} collective-permute-done((bf16[2,160,2688]{2,1,0:T(8,128)(2,1)}, bf16[2,160,2688]{2,1,0:T(8,128)(2,1)S(1)}, u32[]{:S(2)}, u32[]{:S(2)}) %collective-permute-start.27) | collective-permute-done | bytes 1720352 | tf_op jit(solution)/shard_map/ppermute | solution.py:183
  266.7 16.6 %collective-permute-done.28 = bf16[2,160,1280]{2,1,0:T(8,128)(2,1)S(1)} collective-permute-done((bf16[2,160,1280]{2,1,0:T(8,128)(2,1)S(1)}, bf16[2,160,1280]{2,1,0:T(8,128)(2,1)S(1)}, u32[]{:S(2)}, u32[]{:S(2)}) %collective-permute-start.28) | collective-permute-done | bytes 819232 | tf_op jit(solution)/shard_map/ppermute | solution.py:183
  293.2 50.3 %collective-permute-done.35 = bf16[2,160,2688]{2,1,0:T(8,128)(2,1)S(1)} collective-permute-done((bf16[2,160,2688]{2,1,0:T(8,128)(2,1)S(1)}, bf16[2,160,2688]{2,1,0:T(8,128)(2,1)S(1)}, u32[]{:S(2)}, u32[]{:S(2)}) %collective-permute-start.35) | collective-permute-done | bytes 1720352 | tf_op jit(solution)/shard_map/ppermute | solution.py:183
  345.9 13.5 %fusion.20.own_back_ref = bf16[512,2560]{1,0:T(8,128)(2,1)S(1)} fusion(s32[2560]{0:T(1024)S(1)} %fusion.188, bf16[128,2560]{1,0:T(8,128)(2,1)} %copy-done.94, bf16[128,2560]{1,0:T(8,128)(2,1)S(1)} %collective-permute-done.25, bf16[128,2560]{1,0:T(8,128)(2,1)} %collective-permute-done.5, bf16[128,2560]{1,0:T(8,128)(2,1)} %multiply_convert_fusion.5), kind=kOutput, calls=%fused_computation.35 | convolution fusion | flops 6729236480 | bytes 5253120 | tf_op jit(solution)/shard_map/dot_general | solution.py:53
  364.4 20.6 %collective-permute-done.39 = bf16[1,160,2688]{2,1,0:T(8,128)(2,1)S(1)} collective-permute-done((bf16[1,160,2688]{2,1,0:T(8,128)(2,1)S(1)}, bf16[1,160,2688]{2,1,0:T(8,128)(2,1)S(1)}, u32[]{:S(2)}, u32[]{:S(2)}) %collective-permute-start.39) | collective-permute-done | bytes 860192 | tf_op jit(solution)/shard_map/ppermute | solution.py:183
  387.1 41.7 %run_units.1 = (bf16[1024,896]{1,0:T(8,128)(2,1)}, bf16[1024,1792]{1,0:T(8,128)(2,1)}, bf16[1024,2560]{1,0:T(8,128)(2,1)}, bf16[1024,2560]{1,0:T(8,128)(2,1)}) custom-call(bf16[512,2560]{1,0:T(8,128)(2,1)} %bitcast.431, bf16[512,2560]{1,0:T(8,128)(2,1)} %copy-done.14, bf16[512,2560]{1,0:T(8,128)(2,1)} %copy-done.12, bf16[512,2560]{1,0:T(8,128)(2,1)} %copy-done.13, ...), custom_call_target="tpu_custom_call" | custom-call | tf_op jit(solution)/shard_map/run_units/pallas_call | solution.py:504
  431.0 4.9 collective-permute-done.41
  440.3 21.1 %unit_grads.1 = bf16[2560,2688]{1,0:T(8,128)(2,1)} custom-call(bf16[512,2560]{1,0:T(8,128)(2,1)} %bitcast.432, bf16[512,2560]{1,0:T(8,128)(2,1)} %copy-done.14, bf16[512,2560]{1,0:T(8,128)(2,1)} %copy-done.12, bf16[512,2560]{1,0:T(8,128)(2,1)} %copy-done.13, bf16[1024,896]{1,0:T(8,128)(2,1)} %get-tuple-element.152.act_ref, ...), custom_call_target="tpu_custom_call" | custom-call | tf_op jit(solution)/shard_map/unit_grads/pallas_call | solution.py:530
  467.3 6.6 fusion.266
  477.4 18.0 %collective-permute-done.44.refs_0_ = bf16[128,2560]{1,0:T(8,128)(2,1)S(1)} collective-permute-done((bf16[128,2560]{1,0:T(8,128)(2,1)S(1)}, bf16[128,2560]{1,0:T(8,128)(2,1)S(1)}, u32[]{:S(2)}, u32[]{:S(2)}) %collective-permute-start.44) | collective-permute-done | bytes 655392 | tf_op jit(solution)/shard_map/ppermute | solution.py:183
  499.9 12.8 %collective-permute-done.48 = bf16[2,160,2688]{2,1,0:T(8,128)(2,1)S(1)} collective-permute-done((bf16[2,160,2688]{2,1,0:T(8,128)(2,1)S(1)}, bf16[2,160,2688]{2,1,0:T(8,128)(2,1)S(1)}, u32[]{:S(2)}, u32[]{:S(2)}) %collective-permute-start.48) | collective-permute-done | bytes 1720352 | tf_op jit(solution)/shard_map/ppermute | solution.py:183
  523.4 14.2 %attend_back.1 = (bf16[256,2560]{1,0:T(8,128)(2,1)S(1)}, bf16[256,2560]{1,0:T(8,128)(2,1)S(1)}, f32[256,128]{1,0:T(8,128)S(1)}) custom-call(bf16[256,2560]{1,0:T(8,128)(2,1)S(1)} %get-tuple-element.165.query_ref, bf16[256,2560]{1,0:T(8,128)(2,1)S(1)} %convolution_convert_fusion.kv_ref, bf16[256,128]{1,0:T(8,128)(2,1)S(1)} %slice.962.rot_ref, ...), custom_call_target="tpu_custom_call" | custom-call | tf_op jit(solution)/shard_map/attend_back/pallas_call | solution.py:702
  539.5 5.0 fusion.254
  573.7 4.8 multiply_reduce_fusion
  582.7 3.6 fusion.40
  587.2 15.3 %collective-permute-done.51 = bf16[4,160,1280]{2,1,0:T(8,128)(2,1)} collective-permute-done((bf16[4,160,1280]{2,1,0:T(8,128)(2,1)}, bf16[4,160,1280]{2,1,0:T(8,128)(2,1)}, u32[]{:S(2)}, u32[]{:S(2)}) %collective-permute-start.51) | collective-permute-done | bytes 1638432 | tf_op jit(solution)/shard_map/ppermute | solution.py:183
  603.4 5.3 fusion
  608.8 9.7 %collective-permute-done.52.refs_0_ = bf16[128,2560]{1,0:T(8,128)(2,1)S(1)} collective-permute-done((bf16[128,2560]{1,0:T(8,128)(2,1)S(1)}, bf16[128,2560]{1,0:T(8,128)(2,1)S(1)}, u32[]{:S(2)}, u32[]{:S(2)}) %collective-permute-start.52) | collective-permute-done | bytes 655392 | tf_op jit(solution)/shard_map/ppermute | solution.py:183
  624.2 25.7 %collective-permute-done.53.refs_0_ = bf16[128,2560]{1,0:T(8,128)(2,1)S(1)} collective-permute-done((bf16[128,2560]{1,0:T(8,128)(2,1)S(1)}, bf16[128,2560]{1,0:T(8,128)(2,1)S(1)}, u32[]{:S(2)}, u32[]{:S(2)}) %collective-permute-start.53) | collective-permute-done | bytes 655392 | tf_op jit(solution)/shard_map/ppermute | solution.py:183
  651.6 6.7 fusion.24
  658.3 6.2 fusion.261
  668.1 4.2 fusion.13
  674.8 28.3 %collective-permute-done.61 = bf16[4,160,1280]{2,1,0:T(8,128)(2,1)S(1)} collective-permute-done((bf16[4,160,1280]{2,1,0:T(8,128)(2,1)}, bf16[4,160,1280]{2,1,0:T(8,128)(2,1)S(1)}, u32[]{:S(2)}, u32[]{:S(2)}) %collective-permute-start.61) | collective-permute-done | bytes 1638432 | tf_op jit(solution)/shard_map/ppermute | solution.py:183
  712.9 8.0 collective-permute-done.68
  721.0 7.7 collective-permute-done.60
  731.1 20.2 %collective-permute-done.73 = bf16[160,2688]{1,0:T(8,128)(2,1)S(1)} collective-permute-done((bf16[160,2688]{1,0:T(8,128)(2,1)S(1)}, bf16[160,2688]{1,0:T(8,128)(2,1)S(1)}, u32[]{:S(2)}, u32[]{:S(2)}) %collective-permute-start.73) | collective-permute-done | bytes 860192 | tf_op jit(solution)/shard_map/ppermute | solution.py:183
  753.1 18.9 %collective-permute-done.74 = bf16[160,1280]{1,0:T(8,128)(2,1)S(1)} collective-permute-done((bf16[160,1280]{1,0:T(8,128)(2,1)S(1)}, bf16[160,1280]{1,0:T(8,128)(2,1)S(1)}, u32[]{:S(2)}, u32[]{:S(2)}) %collective-permute-start.74) | collective-permute-done | bytes 409632 | tf_op jit(solution)/shard_map/ppermute | solution.py:183
  773.2 8.9 %collective-permute-done.64 = bf16[4,64,2560]{2,1,0:T(8,128)(2,1)S(1)} collective-permute-done((bf16[4,64,2560]{2,1,0:T(8,128)(2,1)S(1)}, bf16[4,64,2560]{2,1,0:T(8,128)(2,1)S(1)}, u32[]{:S(2)}, u32[]{:S(2)}) %collective-permute-start.64) | collective-permute-done | bytes 1310752 | tf_op jit(solution)/shard_map/ppermute | solution.py:183
  800.0 4.6 copy.75
  821.5 9.0 %collective-permute-done.75 = bf16[64,2560]{1,0:T(8,128)(2,1)S(1)} collective-permute-done((bf16[64,2560]{1,0:T(8,128)(2,1)S(1)}, bf16[64,2560]{1,0:T(8,128)(2,1)S(1)}, u32[]{:S(2)}, u32[]{:S(2)}) %collective-permute-start.75) | collective-permute-done | bytes 327712 | tf_op jit(solution)/shard_map/ppermute | solution.py:183
  836.7 3.7 collective-permute-done.76
  840.5 6.6 collective-permute-done.77
  (585 shorter events, 255.7 us)
Async XLA Ops:
  11.9 40.2 %collective-permute-start.5 = (bf16[128,2560]{1,0:T(8,128)(2,1)}, bf16[128,2560]{1,0:T(8,128)(2,1)}, u32[]{:S(2)}, u32[]{:S(2)}) collective-permute-start(bf16[128,2560]{1,0:T(8,128)(2,1)} %multiply_convert_fusion.5), channel_id=1, source_target_pairs={{0,4},{2,6},{4,0},{6,2},{8,12},{10,14},{12,8},{14,10},{16,20},{18,... | collective-permute-start | bytes 1966088 | tf_op jit(solution)/shard_map/ppermute | solution.py:183
  41.6 46.9 %collective-permute-start.12 = (bf16[160,1280]{1,0:T(8,128)(2,1)S(1)}, bf16[160,1280]{1,0:T(8,128)(2,1)}, u32[]{:S(2)}, u32[]{:S(2)}) collective-permute-start(bf16[160,1280]{1,0:T(8,128)(2,1)S(1)} %bitcast.465), channel_id=1, source_target_pairs={{0,16},{2,18},{4,20},{6,22},{8,24},{10,26},{12,28},{14,30},{16,0},... | collective-permute-start | bytes 1228808 | tf_op jit(solution)/shard_map/ppermute | solution.py:183
  56.2 31.7 %collective-permute-start.8 = (bf16[4,80,1152]{2,1,0:T(8,128)(2,1)S(1)}, bf16[4,80,1152]{2,1,0:T(8,128)(2,1)S(1)}, u32[]{:S(2)}, u32[]{:S(2)}) collective-permute-start(bf16[4,80,1152]{2,1,0:T(8,128)(2,1)S(1)} %copy-done.71), channel_id=1, source_target_pairs={{0,6},{2,4},{4,2},{6,0},{8,14},{10,12},{12,10},{14,8},{16,22},{18,... | collective-permute-start | bytes 2211848 | tf_op jit(solution)/shard_map/ppermute | solution.py:183
  57.6 30.9 %collective-permute-start.13 = (bf16[160,1280]{1,0:T(8,128)(2,1)S(1)}, bf16[160,1280]{1,0:T(8,128)(2,1)S(1)}, u32[]{:S(2)}, u32[]{:S(2)}) collective-permute-start(bf16[160,1280]{1,0:T(8,128)(2,1)S(1)} %bitcast.466), channel_id=1, source_target_pairs={{0,8},{2,10},{4,12},{6,14},{8,0},{10,2},{12,4},{14,6},{16,24},{18,... | collective-permute-start | bytes 1228808 | tf_op jit(solution)/shard_map/ppermute | solution.py:183
  88.2 56.1 %collective-permute-start.9 = (bf16[16,80,1152]{2,1,0:T(8,128)(2,1)S(1)}, bf16[16,80,1152]{2,1,0:T(8,128)(2,1)S(1)}, u32[]{:S(2)}, u32[]{:S(2)}) collective-permute-start(bf16[16,80,1152]{2,1,0:T(8,128)(2,1)S(1)} %bitcast.458), channel_id=1, source_target_pairs={{0,1},{1,0},{2,3},{3,2},{4,5},{5,4},{6,7},{7,6},{8,9},{9,8},{10,11... | collective-permute-start | bytes 8847368 | tf_op jit(solution)/shard_map/ppermute | solution.py:77
  88.5 40.0 %collective-permute-start.15 = (bf16[2,160,2688]{2,1,0:T(8,128)(2,1)S(1)}, bf16[2,160,2688]{2,1,0:T(8,128)(2,1)S(1)}, u32[]{:S(2)}, u32[]{:S(2)}) collective-permute-start(bf16[2,160,2688]{2,1,0:T(8,128)(2,1)S(1)} %pad_maximum_fusion.3), channel_id=1, source_target_pairs={{0,4},{2,6},{4,0},{6,2},{8,12},{10,14},{12,8},{14,10},{16,20},{18,... | collective-permute-start | bytes 5160968 | tf_op jit(solution)/shard_map/ppermute | solution.py:183
  92.7 30.8 %collective-permute-start.17 = (bf16[4,64,2560]{2,1,0:T(8,128)(2,1)}, bf16[4,64,2560]{2,1,0:T(8,128)(2,1)S(1)}, u32[]{:S(2)}, u32[]{:S(2)}) collective-permute-start(bf16[4,64,2560]{2,1,0:T(8,128)(2,1)} %pad_maximum_fusion.12), channel_id=1, source_target_pairs={{0,2},{2,0},{4,6},{6,4},{8,10},{10,8},{12,14},{14,12},{16,18},{18,... | collective-permute-start | bytes 3932168 | tf_op jit(solution)/shard_map/ppermute | solution.py:183
  99.4 40.1 %collective-permute-start.23 = (bf16[160,2688]{1,0:T(8,128)(2,1)S(1)}, bf16[160,2688]{1,0:T(8,128)(2,1)S(1)}, u32[]{:S(2)}, u32[]{:S(2)}) collective-permute-start(bf16[160,2688]{1,0:T(8,128)(2,1)S(1)} %get-tuple-element.132), channel_id=1, source_target_pairs={{0,16},{2,18},{4,20},{6,22},{8,24},{10,26},{12,28},{14,30},{16,0},... | collective-permute-start | bytes 2580488 | tf_op jit(solution)/shard_map/ppermute | solution.py:183
  128.5 51.7 %collective-permute-start.16 = (bf16[4,64,2560]{2,1,0:T(8,128)(2,1)}, bf16[4,64,2560]{2,1,0:T(8,128)(2,1)}, u32[]{:S(2)}, u32[]{:S(2)}) collective-permute-start(bf16[4,64,2560]{2,1,0:T(8,128)(2,1)} %pad_maximum_fusion.12), channel_id=1, source_target_pairs={{0,4},{2,6},{4,0},{6,2},{8,12},{10,14},{12,8},{14,10},{16,20},{18,... | collective-permute-start | bytes 3932168 | tf_op jit(solution)/shard_map/ppermute | solution.py:183
  141.0 39.2 %collective-permute-start.24 = (bf16[160,2688]{1,0:T(8,128)(2,1)}, bf16[160,2688]{1,0:T(8,128)(2,1)}, u32[]{:S(2)}, u32[]{:S(2)}) collective-permute-start(bf16[160,2688]{1,0:T(8,128)(2,1)} %get-tuple-element.133), channel_id=1, source_target_pairs={{0,16},{2,18},{4,20},{6,22},{8,24},{10,26},{12,28},{14,30},{16,0},... | collective-permute-start | bytes 2580488 | tf_op jit(solution)/shard_map/ppermute | solution.py:183
  141.0 46.4 %collective-permute-start.18 = (bf16[2,160,2688]{2,1,0:T(8,128)(2,1)}, bf16[2,160,2688]{2,1,0:T(8,128)(2,1)}, u32[]{:S(2)}, u32[]{:S(2)}) collective-permute-start(bf16[2,160,2688]{2,1,0:T(8,128)(2,1)} %pad_maximum_fusion.4), channel_id=1, source_target_pairs={{0,2},{2,0},{4,6},{6,4},{8,10},{10,8},{12,14},{14,12},{16,18},{18,... | collective-permute-start | bytes 5160968 | tf_op jit(solution)/shard_map/ppermute | solution.py:183
  141.5 71.6 %collective-permute-start.26 = (bf16[2,160,2688]{2,1,0:T(8,128)(2,1)}, bf16[2,160,2688]{2,1,0:T(8,128)(2,1)}, u32[]{:S(2)}, u32[]{:S(2)}) collective-permute-start(bf16[2,160,2688]{2,1,0:T(8,128)(2,1)} %pad_maximum_fusion.4), channel_id=1, source_target_pairs={{0,8},{2,10},{4,12},{6,14},{8,0},{10,2},{12,4},{14,6},{16,24},{18,... | collective-permute-start | bytes 5160968 | tf_op jit(solution)/shard_map/ppermute | solution.py:183
  156.9 29.7 %collective-permute-start.10 = (bf16[128,1152]{1,0:T(8,128)(2,1)S(1)}, bf16[128,1152]{1,0:T(8,128)(2,1)S(1)}, u32[]{:S(2)}, u32[]{:S(2)}) collective-permute-start(bf16[128,1152]{1,0:T(8,128)(2,1)S(1)} %pad_maximum_fusion.29), channel_id=1, source_target_pairs={{0,1},{1,0},{2,3},{3,2},{4,5},{5,4},{6,7},{7,6},{8,9},{9,8},{10,11... | collective-permute-start | bytes 884744 | tf_op jit(solution)/shard_map/ppermute | solution.py:77
  180.2 33.5 %collective-permute-start.25 = (bf16[128,2560]{1,0:T(8,128)(2,1)}, bf16[128,2560]{1,0:T(8,128)(2,1)S(1)}, u32[]{:S(2)}, u32[]{:S(2)}) collective-permute-start(bf16[128,2560]{1,0:T(8,128)(2,1)} %multiply_convert_fusion.5), channel_id=1, source_target_pairs={{0,16},{2,18},{4,20},{6,22},{8,24},{10,26},{12,28},{14,30},{16,0},... | collective-permute-start | bytes 1966088 | tf_op jit(solution)/shard_map/ppermute | solution.py:183
  186.7 26.4 %collective-permute-start.20 = (bf16[2,64,2560]{2,1,0:T(8,128)(2,1)S(1)}, bf16[2,64,2560]{2,1,0:T(8,128)(2,1)S(1)}, u32[]{:S(2)}, u32[]{:S(2)}) collective-permute-start(bf16[2,64,2560]{2,1,0:T(8,128)(2,1)S(1)} %copy-done.85), channel_id=1, source_target_pairs={{0,4},{2,6},{4,0},{6,2},{8,12},{10,14},{12,8},{14,10},{16,20},{18,... | collective-permute-start | bytes 1966088 | tf_op jit(solution)/shard_map/ppermute | solution.py:183
  187.4 26.4 %collective-permute-start.19 = (bf16[2,64,2560]{2,1,0:T(8,128)(2,1)S(1)}, bf16[2,64,2560]{2,1,0:T(8,128)(2,1)S(1)}, u32[]{:S(2)}, u32[]{:S(2)}) collective-permute-start(bf16[2,64,2560]{2,1,0:T(8,128)(2,1)S(1)} %slice.950), channel_id=1, source_target_pairs={{0,2},{2,0},{4,6},{6,4},{8,10},{10,8},{12,14},{14,12},{16,18},{18,... | collective-permute-start | bytes 1966088 | tf_op jit(solution)/shard_map/ppermute | solution.py:183
  213.1 51.4 %collective-permute-start.27 = (bf16[2,160,2688]{2,1,0:T(8,128)(2,1)}, bf16[2,160,2688]{2,1,0:T(8,128)(2,1)S(1)}, u32[]{:S(2)}, u32[]{:S(2)}) collective-permute-start(bf16[2,160,2688]{2,1,0:T(8,128)(2,1)} %collective-permute-done.18), channel_id=1, source_target_pairs={{0,8},{2,10},{4,12},{6,14},{8,0},{10,2},{12,4},{14,6},{16,24},{18,... | collective-permute-start | bytes 5160968 | tf_op jit(solution)/shard_map/ppermute | solution.py:183
  213.1 35.4 %collective-permute-start.21 = (bf16[4,160,1280]{2,1,0:T(8,128)(2,1)S(1)}, bf16[4,160,1280]{2,1,0:T(8,128)(2,1)S(1)}, u32[]{:S(2)}, u32[]{:S(2)}) collective-permute-start(bf16[4,160,1280]{2,1,0:T(8,128)(2,1)S(1)} %copy-done.57), channel_id=1, source_target_pairs={{0,4},{2,6},{4,0},{6,2},{8,12},{10,14},{12,8},{14,10},{16,20},{18,... | collective-permute-start | bytes 4915208 | tf_op jit(solution)/shard_map/ppermute | solution.py:183
  213.7 71.2 %collective-permute-start.30 = (bf16[128,2560]{1,0:T(8,128)(2,1)}, bf16[128,2560]{1,0:T(8,128)(2,1)S(1)}, u32[]{:S(2)}, u32[]{:S(2)}) collective-permute-start(bf16[128,2560]{1,0:T(8,128)(2,1)} %collective-permute-done.5), channel_id=1, source_target_pairs={{0,16},{2,18},{4,20},{6,22},{8,24},{10,26},{12,28},{14,30},{16,0},... | collective-permute-start | bytes 1966088 | tf_op jit(solution)/shard_map/ppermute | solution.py:183
  215.8 48.7 %collective-permute-start.22 = (bf16[4,160,1280]{2,1,0:T(8,128)(2,1)S(1)}, bf16[4,160,1280]{2,1,0:T(8,128)(2,1)S(1)}, u32[]{:S(2)}, u32[]{:S(2)}) collective-permute-start(bf16[4,160,1280]{2,1,0:T(8,128)(2,1)S(1)} %copy-done.57), channel_id=1, source_target_pairs={{0,2},{2,0},{4,6},{6,4},{8,10},{10,8},{12,14},{14,12},{16,18},{18,... | collective-permute-start | bytes 4915208 | tf_op jit(solution)/shard_map/ppermute | solution.py:183
  289.4 54.1 %collective-permute-start.35 = (bf16[2,160,2688]{2,1,0:T(8,128)(2,1)S(1)}, bf16[2,160,2688]{2,1,0:T(8,128)(2,1)S(1)}, u32[]{:S(2)}, u32[]{:S(2)}) collective-permute-start(bf16[2,160,2688]{2,1,0:T(8,128)(2,1)S(1)} %pad_maximum_fusion.5), channel_id=1, source_target_pairs={{0,8},{2,10},{4,12},{6,14},{8,0},{10,2},{12,4},{14,6},{16,24},{18,... | collective-permute-start | bytes 5160968 | tf_op jit(solution)/shard_map/ppermute | solution.py:183
  289.5 54.0 %collective-permute-start.34 = (bf16[2,160,2688]{2,1,0:T(8,128)(2,1)S(1)}, bf16[2,160,2688]{2,1,0:T(8,128)(2,1)S(1)}, u32[]{:S(2)}, u32[]{:S(2)}) collective-permute-start(bf16[2,160,2688]{2,1,0:T(8,128)(2,1)S(1)} %pad_maximum_fusion.5), channel_id=1, source_target_pairs={{0,2},{2,0},{4,6},{6,4},{8,10},{10,8},{12,14},{14,12},{16,18},{18,... | collective-permute-start | bytes 5160968 | tf_op jit(solution)/shard_map/ppermute | solution.py:183
  290.8 52.7 %collective-permute-start.32 = (bf16[128,2560]{1,0:T(8,128)(2,1)S(1)}, bf16[128,2560]{1,0:T(8,128)(2,1)S(1)}, u32[]{:S(2)}, u32[]{:S(2)}) collective-permute-start(bf16[128,2560]{1,0:T(8,128)(2,1)S(1)} %multiply_convert_fusion.3.refs_0_), channel_id=1, source_target_pairs={{0,4},{2,6},{4,0},{6,2},{8,12},{10,14},{12,8},{14,10},{16,20},{18,... | collective-permute-start | bytes 1966088 | tf_op jit(solution)/shard_map/ppermute | solution.py:183
  291.1 52.4 %collective-permute-start.33 = (bf16[128,2560]{1,0:T(8,128)(2,1)S(1)}, bf16[128,2560]{1,0:T(8,128)(2,1)S(1)}, u32[]{:S(2)}, u32[]{:S(2)}) collective-permute-start(bf16[128,2560]{1,0:T(8,128)(2,1)S(1)} %multiply_convert_fusion.3.refs_0_), channel_id=1, source_target_pairs={{0,16},{2,18},{4,20},{6,22},{8,24},{10,26},{12,28},{14,30},{16,0},... | collective-permute-start | bytes 1966088 | tf_op jit(solution)/shard_map/ppermute | solution.py:183
  463.9 31.5 %collective-permute-start.44 = (bf16[128,2560]{1,0:T(8,128)(2,1)S(1)}, bf16[128,2560]{1,0:T(8,128)(2,1)S(1)}, u32[]{:S(2)}, u32[]{:S(2)}) collective-permute-start(bf16[128,2560]{1,0:T(8,128)(2,1)S(1)} %fusion.66), channel_id=1, source_target_pairs={{0,16},{2,18},{4,20},{6,22},{8,24},{10,26},{12,28},{14,30},{16,0},... | collective-permute-start | bytes 1966088 | tf_op jit(solution)/shard_map/ppermute | solution.py:183
  465.6 30.6 %collective-permute-start.46 = (bf16[128,2560]{1,0:T(8,128)(2,1)}, bf16[128,2560]{1,0:T(8,128)(2,1)S(1)}, u32[]{:S(2)}, u32[]{:S(2)}) collective-permute-start(bf16[128,2560]{1,0:T(8,128)(2,1)} %get-tuple-element.157), channel_id=1, source_target_pairs={{0,4},{2,6},{4,0},{6,2},{8,12},{10,14},{12,8},{14,10},{16,20},{18,... | collective-permute-start | bytes 1966088 | tf_op jit(solution)/shard_map/ppermute | solution.py:183
  474.0 38.8 %collective-permute-start.48 = (bf16[2,160,2688]{2,1,0:T(8,128)(2,1)S(1)}, bf16[2,160,2688]{2,1,0:T(8,128)(2,1)S(1)}, u32[]{:S(2)}, u32[]{:S(2)}) collective-permute-start(bf16[2,160,2688]{2,1,0:T(8,128)(2,1)S(1)} %bitcast.462), channel_id=1, source_target_pairs={{0,2},{2,0},{4,6},{6,4},{8,10},{10,8},{12,14},{14,12},{16,18},{18,... | collective-permute-start | bytes 5160968 | tf_op jit(solution)/shard_map/ppermute | solution.py:183
  477.4 62.1 %collective-permute-start.42 = (bf16[512,2560]{1,0:T(8,128)(2,1)}, bf16[512,2560]{1,0:T(8,128)(2,1)}, u32[]{:S(2)}, u32[]{:S(2)}) collective-permute-start(bf16[512,2560]{1,0:T(8,128)(2,1)} %slice.777), channel_id=1, source_target_pairs={{0,1},{1,0},{2,3},{3,2},{4,5},{5,4},{6,7},{7,6},{8,9},{9,8},{10,11... | collective-permute-start | bytes 7864328 | tf_op jit(solution)/shard_map/ppermute | solution.py:77
  499.9 51.3 %collective-permute-start.45 = (bf16[2,160,2688]{2,1,0:T(8,128)(2,1)}, bf16[2,160,2688]{2,1,0:T(8,128)(2,1)}, u32[]{:S(2)}, u32[]{:S(2)}) collective-permute-start(bf16[2,160,2688]{2,1,0:T(8,128)(2,1)} %bitcast.82), channel_id=1, source_target_pairs={{0,8},{2,10},{4,12},{6,14},{8,0},{10,2},{12,4},{14,6},{16,24},{18,... | collective-permute-start | bytes 5160968 | tf_op jit(solution)/shard_map/ppermute | solution.py:183
  522.9 25.5 %collective-permute-start.50 = (bf16[2,160,1280]{2,1,0:T(8,128)(2,1)}, bf16[2,160,1280]{2,1,0:T(8,128)(2,1)}, u32[]{:S(2)}, u32[]{:S(2)}) collective-permute-start(bf16[2,160,1280]{2,1,0:T(8,128)(2,1)} %pad_maximum_fusion.19), channel_id=1, source_target_pairs={{0,4},{2,6},{4,0},{6,2},{8,12},{10,14},{12,8},{14,10},{16,20},{18,... | collective-permute-start | bytes 2457608 | tf_op jit(solution)/shard_map/ppermute | solution.py:183
  551.2 116.9 %collective-permute-start.57 = (bf16[4,160,2688]{2,1,0:T(8,128)(2,1)}, bf16[4,160,2688]{2,1,0:T(8,128)(2,1)}, u32[]{:S(2)}, u32[]{:S(2)}) collective-permute-start(bf16[4,160,2688]{2,1,0:T(8,128)(2,1)} %pad_maximum_fusion.1), channel_id=1, source_target_pairs={{0,8},{2,10},{4,12},{6,14},{8,0},{10,2},{12,4},{14,6},{16,24},{18,... | collective-permute-start | bytes 10321928 | tf_op jit(solution)/shard_map/ppermute | solution.py:183
  562.7 104.9 %collective-permute-start.58 = (bf16[4,160,2688]{2,1,0:T(8,128)(2,1)}, bf16[4,160,2688]{2,1,0:T(8,128)(2,1)}, u32[]{:S(2)}, u32[]{:S(2)}) collective-permute-start(bf16[4,160,2688]{2,1,0:T(8,128)(2,1)} %pad_maximum_fusion.2), channel_id=1, source_target_pairs={{0,2},{2,0},{4,6},{6,4},{8,10},{10,8},{12,14},{14,12},{16,18},{18,... | collective-permute-start | bytes 10321928 | tf_op jit(solution)/shard_map/ppermute | solution.py:183
  564.3 38.2 %collective-permute-start.51 = (bf16[4,160,1280]{2,1,0:T(8,128)(2,1)}, bf16[4,160,1280]{2,1,0:T(8,128)(2,1)}, u32[]{:S(2)}, u32[]{:S(2)}) collective-permute-start(bf16[4,160,1280]{2,1,0:T(8,128)(2,1)} %pad_maximum_fusion.10), channel_id=1, source_target_pairs={{0,4},{2,6},{4,0},{6,2},{8,12},{10,14},{12,8},{14,10},{16,20},{18,... | collective-permute-start | bytes 4915208 | tf_op jit(solution)/shard_map/ppermute | solution.py:183
  587.0 71.4 %collective-permute-start.56 = (bf16[16,80,1152]{2,1,0:T(8,128)(2,1)S(1)}, bf16[16,80,1152]{2,1,0:T(8,128)(2,1)}, u32[]{:S(2)}, u32[]{:S(2)}) collective-permute-start(bf16[16,80,1152]{2,1,0:T(8,128)(2,1)S(1)} %fusion.32), channel_id=1, source_target_pairs={{0,1},{1,0},{2,3},{3,2},{4,5},{5,4},{6,7},{7,6},{8,9},{9,8},{10,11... | collective-permute-start | bytes 8847368 | tf_op jit(solution)/shard_map/ppermute | solution.py:77
  619.7 30.2 %collective-permute-start.53 = (bf16[128,2560]{1,0:T(8,128)(2,1)S(1)}, bf16[128,2560]{1,0:T(8,128)(2,1)S(1)}, u32[]{:S(2)}, u32[]{:S(2)}) collective-permute-start(bf16[128,2560]{1,0:T(8,128)(2,1)S(1)} %fusion.67), channel_id=1, source_target_pairs={{0,16},{2,18},{4,20},{6,22},{8,24},{10,26},{12,28},{14,30},{16,0},... | collective-permute-start | bytes 1966088 | tf_op jit(solution)/shard_map/ppermute | solution.py:183
  621.2 29.6 %collective-permute-start.54 = (bf16[128,2560]{1,0:T(8,128)(2,1)S(1)}, bf16[128,2560]{1,0:T(8,128)(2,1)S(1)}, u32[]{:S(2)}, u32[]{:S(2)}) collective-permute-start(bf16[128,2560]{1,0:T(8,128)(2,1)S(1)} %copy-done.79), channel_id=1, source_target_pairs={{0,4},{2,6},{4,0},{6,2},{8,12},{10,14},{12,8},{14,10},{16,20},{18,... | collective-permute-start | bytes 1966088 | tf_op jit(solution)/shard_map/ppermute | solution.py:183
  667.6 35.5 %collective-permute-start.61 = (bf16[4,160,1280]{2,1,0:T(8,128)(2,1)}, bf16[4,160,1280]{2,1,0:T(8,128)(2,1)S(1)}, u32[]{:S(2)}, u32[]{:S(2)}) collective-permute-start(bf16[4,160,1280]{2,1,0:T(8,128)(2,1)} %pad_maximum_fusion.11), channel_id=1, source_target_pairs={{0,2},{2,0},{4,6},{6,4},{8,10},{10,8},{12,14},{14,12},{16,18},{18,... | collective-permute-start | bytes 4915208 | tf_op jit(solution)/shard_map/ppermute | solution.py:183
  672.8 36.9 %collective-permute-start.59 = (bf16[2,160,2688]{2,1,0:T(8,128)(2,1)S(1)}, bf16[2,160,2688]{2,1,0:T(8,128)(2,1)S(1)}, u32[]{:S(2)}, u32[]{:S(2)}) collective-permute-start(bf16[2,160,2688]{2,1,0:T(8,128)(2,1)S(1)} %pad_maximum_fusion.6), channel_id=1, source_target_pairs={{0,4},{2,6},{4,0},{6,2},{8,12},{10,14},{12,8},{14,10},{16,20},{18,... | collective-permute-start | bytes 5160968 | tf_op jit(solution)/shard_map/ppermute | solution.py:183
  674.8 37.3 %collective-permute-start.72 = (bf16[160,2688]{1,0:T(8,128)(2,1)S(1)}, bf16[160,2688]{1,0:T(8,128)(2,1)S(1)}, u32[]{:S(2)}, u32[]{:S(2)}) collective-permute-start(bf16[160,2688]{1,0:T(8,128)(2,1)S(1)} %get-tuple-element.189), channel_id=1, source_target_pairs={{0,16},{2,18},{4,20},{6,22},{8,24},{10,26},{12,28},{14,30},{16,0},... | collective-permute-start | bytes 2580488 | tf_op jit(solution)/shard_map/ppermute | solution.py:183
  705.7 23.4 %collective-permute-start.62 = (bf16[2,64,2560]{2,1,0:T(8,128)(2,1)S(1)}, bf16[2,64,2560]{2,1,0:T(8,128)(2,1)S(1)}, u32[]{:S(2)}, u32[]{:S(2)}) collective-permute-start(bf16[2,64,2560]{2,1,0:T(8,128)(2,1)S(1)} %copy-done.83), channel_id=1, source_target_pairs={{0,2},{2,0},{4,6},{6,4},{8,10},{10,8},{12,14},{14,12},{16,18},{18,... | collective-permute-start | bytes 1966088 | tf_op jit(solution)/shard_map/ppermute | solution.py:183
  712.2 39.1 %collective-permute-start.73 = (bf16[160,2688]{1,0:T(8,128)(2,1)S(1)}, bf16[160,2688]{1,0:T(8,128)(2,1)S(1)}, u32[]{:S(2)}, u32[]{:S(2)}) collective-permute-start(bf16[160,2688]{1,0:T(8,128)(2,1)S(1)} %get-tuple-element.190), channel_id=1, source_target_pairs={{0,16},{2,18},{4,20},{6,22},{8,24},{10,26},{12,28},{14,30},{16,0},... | collective-permute-start | bytes 2580488 | tf_op jit(solution)/shard_map/ppermute | solution.py:183
  720.9 32.2 %collective-permute-start.69 = (bf16[160,1280]{1,0:T(8,128)(2,1)S(1)}, bf16[160,1280]{1,0:T(8,128)(2,1)S(1)}, u32[]{:S(2)}, u32[]{:S(2)}) collective-permute-start(bf16[160,1280]{1,0:T(8,128)(2,1)S(1)} %get-tuple-element.186), channel_id=1, source_target_pairs={{0,8},{2,10},{4,12},{6,14},{8,0},{10,2},{12,4},{14,6},{16,24},{18,... | collective-permute-start | bytes 1228808 | tf_op jit(solution)/shard_map/ppermute | solution.py:183
  729.1 44.0 %collective-permute-start.63 = (bf16[4,64,2560]{2,1,0:T(8,128)(2,1)S(1)}, bf16[4,64,2560]{2,1,0:T(8,128)(2,1)S(1)}, u32[]{:S(2)}, u32[]{:S(2)}) collective-permute-start(bf16[4,64,2560]{2,1,0:T(8,128)(2,1)S(1)} %pad_maximum_fusion.14), channel_id=1, source_target_pairs={{0,2},{2,0},{4,6},{6,4},{8,10},{10,8},{12,14},{14,12},{16,18},{18,... | collective-permute-start | bytes 3932168 | tf_op jit(solution)/shard_map/ppermute | solution.py:183
  751.4 30.8 %collective-permute-start.64 = (bf16[4,64,2560]{2,1,0:T(8,128)(2,1)S(1)}, bf16[4,64,2560]{2,1,0:T(8,128)(2,1)S(1)}, u32[]{:S(2)}, u32[]{:S(2)}) collective-permute-start(bf16[4,64,2560]{2,1,0:T(8,128)(2,1)S(1)} %pad_maximum_fusion.15), channel_id=1, source_target_pairs={{0,4},{2,6},{4,0},{6,2},{8,12},{10,14},{12,8},{14,10},{16,20},{18,... | collective-permute-start | bytes 3932168 | tf_op jit(solution)/shard_map/ppermute | solution.py:183
  782.2 35.3 %collective-permute-start.65 = (bf16[4,80,1152]{2,1,0:T(8,128)(2,1)}, bf16[4,80,1152]{2,1,0:T(8,128)(2,1)}, u32[]{:S(2)}, u32[]{:S(2)}) collective-permute-start(bf16[4,80,1152]{2,1,0:T(8,128)(2,1)} %pad_maximum_fusion.21), channel_id=1, source_target_pairs={{0,2},{2,0},{4,6},{6,4},{8,10},{10,8},{12,14},{14,12},{16,18},{18,... | collective-permute-start | bytes 2211848 | tf_op jit(solution)/shard_map/ppermute | solution.py:183
  783.8 33.7 %collective-permute-start.66 = (bf16[4,80,1152]{2,1,0:T(8,128)(2,1)}, bf16[4,80,1152]{2,1,0:T(8,128)(2,1)}, u32[]{:S(2)}, u32[]{:S(2)}) collective-permute-start(bf16[4,80,1152]{2,1,0:T(8,128)(2,1)} %pad_maximum_fusion.22), channel_id=1, source_target_pairs={{0,4},{2,6},{4,0},{6,2},{8,12},{10,14},{12,8},{14,10},{16,20},{18,... | collective-permute-start | bytes 2211848 | tf_op jit(solution)/shard_map/ppermute | solution.py:183
  784.8 32.7 %collective-permute-start.67 = (bf16[4,80,1152]{2,1,0:T(8,128)(2,1)}, bf16[4,80,1152]{2,1,0:T(8,128)(2,1)}, u32[]{:S(2)}, u32[]{:S(2)}) collective-permute-start(bf16[4,80,1152]{2,1,0:T(8,128)(2,1)} %pad_maximum_fusion.23), channel_id=1, source_target_pairs={{0,6},{2,4},{4,2},{6,0},{8,14},{10,12},{12,10},{14,8},{16,22},{18,... | collective-permute-start | bytes 2211848 | tf_op jit(solution)/shard_map/ppermute | solution.py:183
  788.6 25.8 %collective-permute-start.70 = (bf16[64,2560]{1,0:T(8,128)(2,1)}, bf16[64,2560]{1,0:T(8,128)(2,1)}, u32[]{:S(2)}, u32[]{:S(2)}) collective-permute-start(bf16[64,2560]{1,0:T(8,128)(2,1)} %get-tuple-element.187), channel_id=1, source_target_pairs={{0,8},{2,10},{4,12},{6,14},{8,0},{10,2},{12,4},{14,6},{16,24},{18,... | collective-permute-start | bytes 983048 | tf_op jit(solution)/shard_map/ppermute | solution.py:183
  (141 other events, 2214.8 us)

commit v4 on v3

--- a/solution.py
+++ b/solution.py
@@ -114,13 +114,12 @@
     "B4": ("C2",),
     "B5": ("latents", "V1"),
     "B6": ("latents",),
-    "G1": ("B4",),
-    "G2": ("B5", "B6"),
+    "G1": ("B5", "B6"),
     "C5": ("G1", "V2"),
     "C6": ("G1", "V2"),
     "M0": ("G2",),
     "M1": ("G2",),
-    "M2": ("W1", "W0"),
+    "M2": ("W1",),
     "W2": ("M1",),
     "W3": ("M1",),
     "R1": ("D1",),
@@ -136,6 +135,9 @@
 }
 
 
+FREE = ("T1",)
+
+
 class Flow:
     def __init__(self, links, name, routine):
         self.links, self.name, self.routine = links, name, routine
@@ -153,7 +155,8 @@
         if self.wanted is None:
             return self
         name = self.name + str(self.count)
-        got = self.links.send(*self.wanted, AFTER.get(name, ()))
+        got = self.links.send(*self.wanted, AFTER.get(name, ()), name not in FREE)
+        self.links.sent[name] = self.wanted[0]
         self.links.done[name] = got
         self.count += 1
         self.wanted = self.resume(tied(got, self.links.named(hold)))
@@ -169,14 +172,17 @@
     def __init__(self):
         self.last = {}
         self.done = {}
+        self.sent = {}
 
     def named(self, names):
         return [self.done[name] for name in names if name in self.done]
 
-    def send(self, values, mask, after=()):
+    def send(self, values, mask, after=(), in_line=True):
         masks = mask if isinstance(mask, list) else [mask]
         bits = sorted({bit for item in masks for bit in all_bits() if bit & item})
-        before = self.named(after) + [self.last[bit] for bit in bits if bit in self.last]
+        before = self.named(after)
+        if in_line:
+            before += [self.last[bit] for bit in bits if bit in self.last]
         values = tied(values, before)
         count = lax.axis_size("dp")
         got = [
@@ -424,10 +430,10 @@
     )(*arrays)
 
 
-def gather_tokens(values):
+def gather_tokens(values, held):
     known = yield from gather_bits(values, GROUP_BITS, "first")
     own = reorder([known[mask][0] for mask in masks_of(GROUP_BITS)], range(GROUP))
-    own = own.reshape(-1, values.shape[1])
+    own = tied(own.reshape(-1, values.shape[1]), held)
     return own, core_swap(own)
 
 
@@ -884,7 +890,7 @@
     mid_resid = resid_in + RESID * attn_own
     mlp_normed = norm_apply(mid_resid, gain_mlp).astype(jnp.bfloat16)
 
-    mlp_flow = links.flow("M", gather_tokens(mlp_normed)).step().step()
+    mlp_flow = links.flow("M", gather_tokens(mlp_normed, links.named(["W0"]))).step().step()
     mlp_seq = mlp_flow.end()
     last_flow.step().step()
     first_units, last_units = first_flow.end(), last_flow.end()
@@ -928,11 +934,13 @@
     out_flow = links.flow("P", reduce_dp(out_grad)).step().step()
     unit_flow.step().step()
     out_flow.step()
-    mlp_flow.step().step().step()
+    mlp_flow.step().step(["R3"]).step(["R3"])
     d_query, d_key_value, d_rot = attend_back(
-        query_full, key_value, rot_seq, seen, tables, tied(d_heads, links.named(["R0"]) + [out_grad]), scale
-    )
-    d_query, d_key_value, d_rot = tied((d_query, d_key_value, d_rot), links.named(["R1"]))
+        query_full, key_value, rot_seq, seen, tables, tied(d_heads, [links.sent["R0"], out_grad]), scale
+    )
+    d_query, d_key_value, d_rot = tied(
+        (d_query, d_key_value, d_rot), links.named(["R1"]) + [links.sent["R3"]]
+    )
     d_rank = jnp.where(
         is_query[None, :], mul_trans(d_query, up_weight), mul_trans(d_key_value, up_weight)
     )
@@ -996,7 +1004,7 @@
     grad_packed = trans_mul(
         jnp.concatenate(
             [
-                x_normed,
+                tied(x_normed, links.named(["R3"])),
                 low(gain_attn_terms),
                 low(gain_mlp_terms),
                 low(plain_mul(gain_rank_terms, gain_order)),
@@ -1017,7 +1025,7 @@
     qup_shard = up_shard[:q_rows].reshape(q_rows, heads_local, LANES)[..., :head_qk]
     kvup_shard = up_shard[q_rows:]
     exchange_flow.end()
-    unit_parts = tied(unit_parts, links.named(["Q3"]))
+    unit_parts = tied(unit_parts, links.named(["Q4"]))
     unit_shards = place_group([part[at] for part in unit_parts for at in range(GROUP // 2)])
     gate_shard = join_units(unit_shards[..., :share], units)
     upper_shard = join_units(unit_shards[..., share : 2 * share], units)

time: 860 us -> 802 us (0.933)
  waiting for transfers between devices: 435 us -> 356 us
  other arithmetic: 81.9 us -> 94.8 us
  starting transfers between devices: 70.9 us -> 83 us
    ppermute x69, waiting for transfers between devices: 430 us -> 351 us  [send(): lax.ppermute(item, 'dp', [(place, place ^ to) for place in range(count)])]
    ppermute x69, starting transfers between devices: 70.3 us -> 82.5 us  [send(): lax.ppermute(item, 'dp', [(place, place ^ to) for place in range(count)])]
  transfers between devices with their start and end apart: 79 -> 79, of which waited for: 38 -> 42; matrix products, arithmetic and copies ran while one was open for 26% -> 29% of each run, Pallas kernels for 6% -> 7%
where the time goes in v4:
time: 802 us; the launch traced here: 795 us
  waiting for transfers between devices  356 us (44%)
  Pallas kernels  95.9 us (12%)
  local copies, waits for them, and re-layouts  94.8 us (12%)
  other arithmetic  94.8 us (12%)
  starting transfers between devices  83 us (10%)
  matrix products  66.7 us (8%)
    ppermute x69, waiting for transfers between devices, send(): lax.ppermute(item, 'dp', [(place, place ^ to) for place in range(count)])  351 us
    ppermute x69, starting transfers between devices, send(): lax.ppermute(item, 'dp', [(place, place ^ to) for place in range(count)])  82.5 us
    pallas_call x1, Pallas kernels, run_units(): pl.pallas_call(partial(units_kernel, share, len(pieces)), grid=(steps,),...  41.7 us
    dot_general x9, matrix products, plain_mul(): return jnp.dot(left, right, preferred_element_type=jnp.float32)  33 us
    another operation x11, other arithmetic  26.9 us
    dot_general x8, matrix products, mul_trans(): lax.dot_general(left, right, (((1,), (1,)), ((), ())), preferred_element_...  25.3 us
    unnamed x263, local copies, waits for them, and re-layouts  24.8 us
    pallas_call x1, Pallas kernels, unit_grads(): pl.pallas_call(partial(unit_grads_kernel, share), grid=(CHUNKS,), in_spec...  21.1 us
  transfers between devices with their start and end apart: 79, of which 42 were waited for; matrix products, arithmetic and copies ran while one was open for 29% of the time, Pallas kernels for 7%

profile of v4, /device:TPU:0, one launch (start us, length us, event | category | flops | bytes accessed | tf_op | source)
XLA Modules:
  0.0 795.2 jit_solution(6999467023986453375)
XLA Ops:
  4.1 5.1 collective-permute-start.2
  15.2 4.1 constant_dynamic-update-slice_fusion.8
  29.0 12.6 %collective-permute-done.3 = bf16[64,2560]{1,0:T(8,128)(2,1)S(1)} collective-permute-done((bf16[64,2560]{1,0:T(8,128)(2,1)S(1)}, bf16[64,2560]{1,0:T(8,128)(2,1)S(1)}, u32[]{:S(2)}, u32[]{:S(2)}) %collective-permute-start.3) | collective-permute-done | bytes 327712 | tf_op jit(solution)/shard_map/ppermute | solution.py:189
  57.6 12.4 %collective-permute-done.6 = bf16[4,80,1152]{2,1,0:T(8,128)(2,1)S(1)} collective-permute-done((bf16[4,80,1152]{2,1,0:T(8,128)(2,1)S(1)}, bf16[4,80,1152]{2,1,0:T(8,128)(2,1)S(1)}, u32[]{:S(2)}, u32[]{:S(2)}) %collective-permute-start.6) | collective-permute-done | bytes 737312 | tf_op jit(solution)/shard_map/ppermute | solution.py:189
  70.0 4.2 collective-permute-done.7
  74.2 13.7 %collective-permute-done.8 = bf16[4,80,1152]{2,1,0:T(8,128)(2,1)S(1)} collective-permute-done((bf16[4,80,1152]{2,1,0:T(8,128)(2,1)S(1)}, bf16[4,80,1152]{2,1,0:T(8,128)(2,1)S(1)}, u32[]{:S(2)}, u32[]{:S(2)}) %collective-permute-start.8) | collective-permute-done | bytes 737312 | tf_op jit(solution)/shard_map/ppermute | solution.py:189
  94.3 5.0 fusion.3
  102.1 4.4 collective-permute-done.14
  109.0 14.6 %collective-permute-done.17 = bf16[4,64,2560]{2,1,0:T(8,128)(2,1)S(1)} collective-permute-done((bf16[4,64,2560]{2,1,0:T(8,128)(2,1)}, bf16[4,64,2560]{2,1,0:T(8,128)(2,1)S(1)}, u32[]{:S(2)}, u32[]{:S(2)}) %collective-permute-start.17) | collective-permute-done | bytes 1310752 | tf_op jit(solution)/shard_map/ppermute | solution.py:189
  124.5 4.1 collective-permute-done.15
  131.2 8.4 %collective-permute-done.23 = bf16[160,2688]{1,0:T(8,128)(2,1)S(1)} collective-permute-done((bf16[160,2688]{1,0:T(8,128)(2,1)S(1)}, bf16[160,2688]{1,0:T(8,128)(2,1)S(1)}, u32[]{:S(2)}, u32[]{:S(2)}) %collective-permute-start.23) | collective-permute-done | bytes 860192 | tf_op jit(solution)/shard_map/ppermute | solution.py:189
  167.4 12.3 %collective-permute-done.18 = bf16[2,160,2688]{2,1,0:T(8,128)(2,1)} collective-permute-done((bf16[2,160,2688]{2,1,0:T(8,128)(2,1)}, bf16[2,160,2688]{2,1,0:T(8,128)(2,1)}, u32[]{:S(2)}, u32[]{:S(2)}) %collective-permute-start.18) | collective-permute-done | bytes 1720352 | tf_op jit(solution)/shard_map/ppermute | solution.py:189
  181.0 18.2 %collective-permute-done.26 = bf16[2,160,2688]{2,1,0:T(8,128)(2,1)} collective-permute-done((bf16[2,160,2688]{2,1,0:T(8,128)(2,1)}, bf16[2,160,2688]{2,1,0:T(8,128)(2,1)}, u32[]{:S(2)}, u32[]{:S(2)}) %collective-permute-start.26) | collective-permute-done | bytes 1720352 | tf_op jit(solution)/shard_map/ppermute | solution.py:189
  214.5 4.2 convolution_convert_fusion.kv_ref
  218.7 4.2 fusion.276.q_ref
  222.9 10.5 %attend.1 = (bf16[256,1280]{1,0:T(8,128)(2,1)S(1)}, bf16[256,2560]{1,0:T(8,128)(2,1)S(1)}) custom-call(f32[256,2560]{1,0:T(8,128)S(1)} %fusion.276.q_ref, bf16[256,2560]{1,0:T(8,128)(2,1)S(1)} %convolution_convert_fusion.kv_ref, bf16[256,128]{1,0:T(8,128)(2,1)S(1)} %slice.962.rot_ref, f32[256,256]{1,0:T(8,128)S(1)} %or_convert_fusion.seen_ref, ...), custom_call_target="tpu_custom_call" | custom-call | tf_op jit(solution)/shard_map/attend/pallas_call | solution.py:691
  233.4 15.0 %collective-permute-done.25 = bf16[128,2560]{1,0:T(8,128)(2,1)S(1)} collective-permute-done((bf16[128,2560]{1,0:T(8,128)(2,1)}, bf16[128,2560]{1,0:T(8,128)(2,1)S(1)}, u32[]{:S(2)}, u32[]{:S(2)}) %collective-permute-start.25) | collective-permute-done | bytes 655392 | tf_op jit(solution)/shard_map/ppermute | solution.py:189
  255.2 14.7 %collective-permute-done.28 = bf16[2,160,1280]{2,1,0:T(8,128)(2,1)S(1)} collective-permute-done((bf16[2,160,1280]{2,1,0:T(8,128)(2,1)S(1)}, bf16[2,160,1280]{2,1,0:T(8,128)(2,1)S(1)}, u32[]{:S(2)}, u32[]{:S(2)}) %collective-permute-start.28) | collective-permute-done | bytes 819232 | tf_op jit(solution)/shard_map/ppermute | solution.py:189
  271.5 7.2 collective-permute-done.30
  288.4 13.5 %collective-permute-done.32.refs_1_ = bf16[128,2560]{1,0:T(8,128)(2,1)S(1)} collective-permute-done((bf16[128,2560]{1,0:T(8,128)(2,1)S(1)}, bf16[128,2560]{1,0:T(8,128)(2,1)S(1)}, u32[]{:S(2)}, u32[]{:S(2)}) %collective-permute-start.32) | collective-permute-done | bytes 655392 | tf_op jit(solution)/shard_map/ppermute | solution.py:189
  302.0 14.9 %collective-permute-done.33.refs_2_ = bf16[128,2560]{1,0:T(8,128)(2,1)S(1)} collective-permute-done((bf16[128,2560]{1,0:T(8,128)(2,1)S(1)}, bf16[128,2560]{1,0:T(8,128)(2,1)S(1)}, u32[]{:S(2)}, u32[]{:S(2)}) %collective-permute-start.33) | collective-permute-done | bytes 655392 | tf_op jit(solution)/shard_map/ppermute | solution.py:189
  316.8 6.7 collective-permute-done.34
  324.0 8.6 %fusion.20.own_back_ref = bf16[512,2560]{1,0:T(8,128)(2,1)S(1)} fusion(s32[2560]{0:T(1024)S(1)} %fusion.188, bf16[128,2560]{1,0:T(8,128)(2,1)S(1)} %collective-permute-done.30, bf16[128,2560]{1,0:T(8,128)(2,1)S(1)} %collective-permute-done.25, bf16[128,2560]{1,0:T(8,128)(2,1)} %collective-permute-done.5, bf16[128,2560]{1,0:T(8,128)(2,1)} %multiply_convert_fusion.5), kind=kOutput, calls=%fused_computation.35 | convolution fusion | flops 6729236480 | bytes 5253120 | tf_op jit(solution)/shard_map/dot_general | solution.py:53
  332.7 7.1 collective-permute-done.35.refs_3_
  346.6 19.6 %collective-permute-done.39 = bf16[1,160,2688]{2,1,0:T(8,128)(2,1)S(1)} collective-permute-done((bf16[1,160,2688]{2,1,0:T(8,128)(2,1)S(1)}, bf16[1,160,2688]{2,1,0:T(8,128)(2,1)S(1)}, u32[]{:S(2)}, u32[]{:S(2)}) %collective-permute-start.39) | collective-permute-done | bytes 860192 | tf_op jit(solution)/shard_map/ppermute | solution.py:189
  368.3 41.7 %run_units.1 = (bf16[1024,896]{1,0:T(8,128)(2,1)}, bf16[1024,1792]{1,0:T(8,128)(2,1)}, bf16[1024,2560]{1,0:T(8,128)(2,1)}, bf16[1024,2560]{1,0:T(8,128)(2,1)}) custom-call(bf16[512,2560]{1,0:T(8,128)(2,1)} %bitcast.431, bf16[512,2560]{1,0:T(8,128)(2,1)} %copy-done.14, bf16[512,2560]{1,0:T(8,128)(2,1)} %copy-done.12, bf16[512,2560]{1,0:T(8,128)(2,1)} %copy-done.13, ...), custom_call_target="tpu_custom_call" | custom-call | tf_op jit(solution)/shard_map/run_units/pallas_call | solution.py:510
  412.1 4.9 collective-permute-done.41
  421.6 21.1 %unit_grads.1 = bf16[2560,2688]{1,0:T(8,128)(2,1)} custom-call(bf16[512,2560]{1,0:T(8,128)(2,1)} %bitcast.432, bf16[512,2560]{1,0:T(8,128)(2,1)} %copy-done.14, bf16[512,2560]{1,0:T(8,128)(2,1)} %copy-done.12, bf16[512,2560]{1,0:T(8,128)(2,1)} %copy-done.13, bf16[1024,896]{1,0:T(8,128)(2,1)} %get-tuple-element.154.act_ref, ...), custom_call_target="tpu_custom_call" | custom-call | tf_op jit(solution)/shard_map/unit_grads/pallas_call | solution.py:536
  448.9 6.6 fusion.266
  459.8 17.0 %collective-permute-done.44.refs_0_ = bf16[128,2560]{1,0:T(8,128)(2,1)S(1)} collective-permute-done((bf16[128,2560]{1,0:T(8,128)(2,1)S(1)}, bf16[128,2560]{1,0:T(8,128)(2,1)S(1)}, u32[]{:S(2)}, u32[]{:S(2)}) %collective-permute-start.44) | collective-permute-done | bytes 655392 | tf_op jit(solution)/shard_map/ppermute | solution.py:189
  481.3 12.9 %collective-permute-done.48 = bf16[2,160,2688]{2,1,0:T(8,128)(2,1)S(1)} collective-permute-done((bf16[2,160,2688]{2,1,0:T(8,128)(2,1)S(1)}, bf16[2,160,2688]{2,1,0:T(8,128)(2,1)S(1)}, u32[]{:S(2)}, u32[]{:S(2)}) %collective-permute-start.48) | collective-permute-done | bytes 1720352 | tf_op jit(solution)/shard_map/ppermute | solution.py:189
  505.8 14.2 %attend_back.1 = (bf16[256,2560]{1,0:T(8,128)(2,1)S(1)}, bf16[256,2560]{1,0:T(8,128)(2,1)S(1)}, f32[256,128]{1,0:T(8,128)S(1)}) custom-call(bf16[256,2560]{1,0:T(8,128)(2,1)S(1)} %get-tuple-element.170.query_ref, bf16[256,2560]{1,0:T(8,128)(2,1)S(1)} %convolution_convert_fusion.kv_ref, bf16[256,128]{1,0:T(8,128)(2,1)S(1)} %slice.962.rot_ref, ...), custom_call_target="tpu_custom_call" | custom-call | tf_op jit(solution)/shard_map/attend_back/pallas_call | solution.py:708
  521.8 5.0 fusion.254
  555.1 4.9 multiply_reduce_fusion
  564.9 5.3 fusion
  570.2 13.6 %collective-permute-done.51 = bf16[4,160,1280]{2,1,0:T(8,128)(2,1)} collective-permute-done((bf16[4,160,1280]{2,1,0:T(8,128)(2,1)}, bf16[4,160,1280]{2,1,0:T(8,128)(2,1)}, u32[]{:S(2)}, u32[]{:S(2)}) %collective-permute-start.51) | collective-permute-done | bytes 1638432 | tf_op jit(solution)/shard_map/ppermute | solution.py:189
  586.2 13.6 %collective-permute-done.52.refs_0_ = bf16[128,2560]{1,0:T(8,128)(2,1)S(1)} collective-permute-done((bf16[128,2560]{1,0:T(8,128)(2,1)S(1)}, bf16[128,2560]{1,0:T(8,128)(2,1)S(1)}, u32[]{:S(2)}, u32[]{:S(2)}) %collective-permute-start.52) | collective-permute-done | bytes 655392 | tf_op jit(solution)/shard_map/ppermute | solution.py:189
  603.8 11.1 %collective-permute-done.58 = bf16[4,160,2688]{2,1,0:T(8,128)(2,1)} collective-permute-done((bf16[4,160,2688]{2,1,0:T(8,128)(2,1)}, bf16[4,160,2688]{2,1,0:T(8,128)(2,1)}, u32[]{:S(2)}, u32[]{:S(2)}) %collective-permute-start.58) | collective-permute-done | bytes 3440672 | tf_op jit(solution)/shard_map/ppermute | solution.py:189
  614.9 7.1 collective-permute-done.54
  621.9 4.2 fusion.13
  641.5 6.7 fusion.24
  648.2 16.8 %collective-permute-done.61 = bf16[4,160,1280]{2,1,0:T(8,128)(2,1)} collective-permute-done((bf16[4,160,1280]{2,1,0:T(8,128)(2,1)}, bf16[4,160,1280]{2,1,0:T(8,128)(2,1)}, u32[]{:S(2)}, u32[]{:S(2)}) %collective-permute-start.61) | collective-permute-done | bytes 1638432 | tf_op jit(solution)/shard_map/ppermute | solution.py:189
  678.6 6.2 collective-permute-done.71
  693.2 19.4 %collective-permute-done.75 = bf16[160,2688]{1,0:T(8,128)(2,1)S(1)} collective-permute-done((bf16[160,2688]{1,0:T(8,128)(2,1)S(1)}, bf16[160,2688]{1,0:T(8,128)(2,1)S(1)}, u32[]{:S(2)}, u32[]{:S(2)}) %collective-permute-start.75) | collective-permute-done | bytes 860192 | tf_op jit(solution)/shard_map/ppermute | solution.py:189
  715.5 6.2 fusion.261
  750.4 4.6 copy.75
  764.7 4.2 collective-permute-done.66
  784.0 6.4 collective-permute-done.69
  (585 shorter events, 293.0 us)
Async XLA Ops:
  11.9 40.2 %collective-permute-start.5 = (bf16[128,2560]{1,0:T(8,128)(2,1)}, bf16[128,2560]{1,0:T(8,128)(2,1)}, u32[]{:S(2)}, u32[]{:S(2)}) collective-permute-start(bf16[128,2560]{1,0:T(8,128)(2,1)} %multiply_convert_fusion.5), channel_id=1, source_target_pairs={{0,4},{2,6},{4,0},{6,2},{8,12},{10,14},{12,8},{14,10},{16,20},{18,... | collective-permute-start | bytes 1966088 | tf_op jit(solution)/shard_map/ppermute | solution.py:189
  41.6 47.0 %collective-permute-start.12 = (bf16[160,1280]{1,0:T(8,128)(2,1)S(1)}, bf16[160,1280]{1,0:T(8,128)(2,1)}, u32[]{:S(2)}, u32[]{:S(2)}) collective-permute-start(bf16[160,1280]{1,0:T(8,128)(2,1)S(1)} %bitcast.462), channel_id=1, source_target_pairs={{0,16},{2,18},{4,20},{6,22},{8,24},{10,26},{12,28},{14,30},{16,0},... | collective-permute-start | bytes 1228808 | tf_op jit(solution)/shard_map/ppermute | solution.py:189
  56.3 31.7 %collective-permute-start.8 = (bf16[4,80,1152]{2,1,0:T(8,128)(2,1)S(1)}, bf16[4,80,1152]{2,1,0:T(8,128)(2,1)S(1)}, u32[]{:S(2)}, u32[]{:S(2)}) collective-permute-start(bf16[4,80,1152]{2,1,0:T(8,128)(2,1)S(1)} %copy-done.71), channel_id=1, source_target_pairs={{0,6},{2,4},{4,2},{6,0},{8,14},{10,12},{12,10},{14,8},{16,22},{18,... | collective-permute-start | bytes 2211848 | tf_op jit(solution)/shard_map/ppermute | solution.py:189
  57.6 31.0 %collective-permute-start.13 = (bf16[160,1280]{1,0:T(8,128)(2,1)S(1)}, bf16[160,1280]{1,0:T(8,128)(2,1)S(1)}, u32[]{:S(2)}, u32[]{:S(2)}) collective-permute-start(bf16[160,1280]{1,0:T(8,128)(2,1)S(1)} %bitcast.463), channel_id=1, source_target_pairs={{0,8},{2,10},{4,12},{6,14},{8,0},{10,2},{12,4},{14,6},{16,24},{18,... | collective-permute-start | bytes 1228808 | tf_op jit(solution)/shard_map/ppermute | solution.py:189
  88.3 56.1 %collective-permute-start.9 = (bf16[16,80,1152]{2,1,0:T(8,128)(2,1)S(1)}, bf16[16,80,1152]{2,1,0:T(8,128)(2,1)S(1)}, u32[]{:S(2)}, u32[]{:S(2)}) collective-permute-start(bf16[16,80,1152]{2,1,0:T(8,128)(2,1)S(1)} %bitcast.455), channel_id=1, source_target_pairs={{0,1},{1,0},{2,3},{3,2},{4,5},{5,4},{6,7},{7,6},{8,9},{9,8},{10,11... | collective-permute-start | bytes 8847368 | tf_op jit(solution)/shard_map/ppermute | solution.py:77
  88.6 40.0 %collective-permute-start.15 = (bf16[2,160,2688]{2,1,0:T(8,128)(2,1)S(1)}, bf16[2,160,2688]{2,1,0:T(8,128)(2,1)S(1)}, u32[]{:S(2)}, u32[]{:S(2)}) collective-permute-start(bf16[2,160,2688]{2,1,0:T(8,128)(2,1)S(1)} %pad_maximum_fusion.3), channel_id=1, source_target_pairs={{0,4},{2,6},{4,0},{6,2},{8,12},{10,14},{12,8},{14,10},{16,20},{18,... | collective-permute-start | bytes 5160968 | tf_op jit(solution)/shard_map/ppermute | solution.py:189
  92.8 30.8 %collective-permute-start.17 = (bf16[4,64,2560]{2,1,0:T(8,128)(2,1)}, bf16[4,64,2560]{2,1,0:T(8,128)(2,1)S(1)}, u32[]{:S(2)}, u32[]{:S(2)}) collective-permute-start(bf16[4,64,2560]{2,1,0:T(8,128)(2,1)} %pad_maximum_fusion.12), channel_id=1, source_target_pairs={{0,2},{2,0},{4,6},{6,4},{8,10},{10,8},{12,14},{14,12},{16,18},{18,... | collective-permute-start | bytes 3932168 | tf_op jit(solution)/shard_map/ppermute | solution.py:189
  99.5 40.1 %collective-permute-start.23 = (bf16[160,2688]{1,0:T(8,128)(2,1)S(1)}, bf16[160,2688]{1,0:T(8,128)(2,1)S(1)}, u32[]{:S(2)}, u32[]{:S(2)}) collective-permute-start(bf16[160,2688]{1,0:T(8,128)(2,1)S(1)} %get-tuple-element.133), channel_id=1, source_target_pairs={{0,16},{2,18},{4,20},{6,22},{8,24},{10,26},{12,28},{14,30},{16,0},... | collective-permute-start | bytes 2580488 | tf_op jit(solution)/shard_map/ppermute | solution.py:189
  128.6 30.7 %collective-permute-start.16 = (bf16[4,64,2560]{2,1,0:T(8,128)(2,1)}, bf16[4,64,2560]{2,1,0:T(8,128)(2,1)}, u32[]{:S(2)}, u32[]{:S(2)}) collective-permute-start(bf16[4,64,2560]{2,1,0:T(8,128)(2,1)} %pad_maximum_fusion.12), channel_id=1, source_target_pairs={{0,4},{2,6},{4,0},{6,2},{8,12},{10,14},{12,8},{14,10},{16,20},{18,... | collective-permute-start | bytes 3932168 | tf_op jit(solution)/shard_map/ppermute | solution.py:189
  141.1 58.7 %collective-permute-start.24 = (bf16[160,2688]{1,0:T(8,128)(2,1)}, bf16[160,2688]{1,0:T(8,128)(2,1)}, u32[]{:S(2)}, u32[]{:S(2)}) collective-permute-start(bf16[160,2688]{1,0:T(8,128)(2,1)} %get-tuple-element.134), channel_id=1, source_target_pairs={{0,16},{2,18},{4,20},{6,22},{8,24},{10,26},{12,28},{14,30},{16,0},... | collective-permute-start | bytes 2580488 | tf_op jit(solution)/shard_map/ppermute | solution.py:189
  141.1 38.6 %collective-permute-start.18 = (bf16[2,160,2688]{2,1,0:T(8,128)(2,1)}, bf16[2,160,2688]{2,1,0:T(8,128)(2,1)}, u32[]{:S(2)}, u32[]{:S(2)}) collective-permute-start(bf16[2,160,2688]{2,1,0:T(8,128)(2,1)} %pad_maximum_fusion.4), channel_id=1, source_target_pairs={{0,2},{2,0},{4,6},{6,4},{8,10},{10,8},{12,14},{14,12},{16,18},{18,... | collective-permute-start | bytes 5160968 | tf_op jit(solution)/shard_map/ppermute | solution.py:189
  141.6 57.6 %collective-permute-start.26 = (bf16[2,160,2688]{2,1,0:T(8,128)(2,1)}, bf16[2,160,2688]{2,1,0:T(8,128)(2,1)}, u32[]{:S(2)}, u32[]{:S(2)}) collective-permute-start(bf16[2,160,2688]{2,1,0:T(8,128)(2,1)} %pad_maximum_fusion.4), channel_id=1, source_target_pairs={{0,8},{2,10},{4,12},{6,14},{8,0},{10,2},{12,4},{14,6},{16,24},{18,... | collective-permute-start | bytes 5160968 | tf_op jit(solution)/shard_map/ppermute | solution.py:189
  165.8 33.4 %collective-permute-start.20 = (bf16[2,64,2560]{2,1,0:T(8,128)(2,1)S(1)}, bf16[2,64,2560]{2,1,0:T(8,128)(2,1)S(1)}, u32[]{:S(2)}, u32[]{:S(2)}) collective-permute-start(bf16[2,64,2560]{2,1,0:T(8,128)(2,1)S(1)} %copy-done.85), channel_id=1, source_target_pairs={{0,4},{2,6},{4,0},{6,2},{8,12},{10,14},{12,8},{14,10},{16,20},{18,... | collective-permute-start | bytes 1966088 | tf_op jit(solution)/shard_map/ppermute | solution.py:189
  199.2 53.8 %collective-permute-start.27 = (bf16[2,160,2688]{2,1,0:T(8,128)(2,1)}, bf16[2,160,2688]{2,1,0:T(8,128)(2,1)S(1)}, u32[]{:S(2)}, u32[]{:S(2)}) collective-permute-start(bf16[2,160,2688]{2,1,0:T(8,128)(2,1)} %collective-permute-done.18), channel_id=1, source_target_pairs={{0,8},{2,10},{4,12},{6,14},{8,0},{10,2},{12,4},{14,6},{16,24},{18,... | collective-permute-start | bytes 5160968 | tf_op jit(solution)/shard_map/ppermute | solution.py:189
  199.2 52.6 %collective-permute-start.21 = (bf16[4,160,1280]{2,1,0:T(8,128)(2,1)S(1)}, bf16[4,160,1280]{2,1,0:T(8,128)(2,1)S(1)}, u32[]{:S(2)}, u32[]{:S(2)}) collective-permute-start(bf16[4,160,1280]{2,1,0:T(8,128)(2,1)S(1)} %copy-done.54), channel_id=1, source_target_pairs={{0,4},{2,6},{4,0},{6,2},{8,12},{10,14},{12,8},{14,10},{16,20},{18,... | collective-permute-start | bytes 4915208 | tf_op jit(solution)/shard_map/ppermute | solution.py:189
  199.8 48.6 %collective-permute-start.25 = (bf16[128,2560]{1,0:T(8,128)(2,1)}, bf16[128,2560]{1,0:T(8,128)(2,1)S(1)}, u32[]{:S(2)}, u32[]{:S(2)}) collective-permute-start(bf16[128,2560]{1,0:T(8,128)(2,1)} %multiply_convert_fusion.5), channel_id=1, source_target_pairs={{0,16},{2,18},{4,20},{6,22},{8,24},{10,26},{12,28},{14,30},{16,0},... | collective-permute-start | bytes 1966088 | tf_op jit(solution)/shard_map/ppermute | solution.py:189
  201.8 51.2 %collective-permute-start.22 = (bf16[4,160,1280]{2,1,0:T(8,128)(2,1)S(1)}, bf16[4,160,1280]{2,1,0:T(8,128)(2,1)S(1)}, u32[]{:S(2)}, u32[]{:S(2)}) collective-permute-start(bf16[4,160,1280]{2,1,0:T(8,128)(2,1)S(1)} %copy-done.54), channel_id=1, source_target_pairs={{0,2},{2,0},{4,6},{6,4},{8,10},{10,8},{12,14},{14,12},{16,18},{18,... | collective-permute-start | bytes 4915208 | tf_op jit(solution)/shard_map/ppermute | solution.py:189
  248.4 30.2 %collective-permute-start.30 = (bf16[128,2560]{1,0:T(8,128)(2,1)}, bf16[128,2560]{1,0:T(8,128)(2,1)S(1)}, u32[]{:S(2)}, u32[]{:S(2)}) collective-permute-start(bf16[128,2560]{1,0:T(8,128)(2,1)} %collective-permute-done.5), channel_id=1, source_target_pairs={{0,16},{2,18},{4,20},{6,22},{8,24},{10,26},{12,28},{14,30},{16,0},... | collective-permute-start | bytes 1966088 | tf_op jit(solution)/shard_map/ppermute | solution.py:189
  283.2 40.3 %collective-permute-start.34 = (bf16[2,160,2688]{2,1,0:T(8,128)(2,1)}, bf16[2,160,2688]{2,1,0:T(8,128)(2,1)}, u32[]{:S(2)}, u32[]{:S(2)}) collective-permute-start(bf16[2,160,2688]{2,1,0:T(8,128)(2,1)} %pad_maximum_fusion.5), channel_id=1, source_target_pairs={{0,2},{2,0},{4,6},{6,4},{8,10},{10,8},{12,14},{14,12},{16,18},{18,... | collective-permute-start | bytes 5160968 | tf_op jit(solution)/shard_map/ppermute | solution.py:189
  285.7 31.2 %collective-permute-start.33 = (bf16[128,2560]{1,0:T(8,128)(2,1)S(1)}, bf16[128,2560]{1,0:T(8,128)(2,1)S(1)}, u32[]{:S(2)}, u32[]{:S(2)}) collective-permute-start(bf16[128,2560]{1,0:T(8,128)(2,1)S(1)} %multiply_convert_fusion.3.refs_0_), channel_id=1, source_target_pairs={{0,16},{2,18},{4,20},{6,22},{8,24},{10,26},{12,28},{14,30},{16,0},... | collective-permute-start | bytes 1966088 | tf_op jit(solution)/shard_map/ppermute | solution.py:189
  285.7 56.4 %collective-permute-start.36 = (bf16[2,160,2688]{2,1,0:T(8,128)(2,1)}, bf16[2,160,2688]{2,1,0:T(8,128)(2,1)}, u32[]{:S(2)}, u32[]{:S(2)}) collective-permute-start(bf16[2,160,2688]{2,1,0:T(8,128)(2,1)} %pad_maximum_fusion.5), channel_id=1, source_target_pairs={{0,8},{2,10},{4,12},{6,14},{8,0},{10,2},{12,4},{14,6},{16,24},{18,... | collective-permute-start | bytes 5160968 | tf_op jit(solution)/shard_map/ppermute | solution.py:189
  342.1 24.2 %collective-permute-start.37 = (bf16[512,2560]{1,0:T(8,128)(2,1)S(1)}, bf16[512,2560]{1,0:T(8,128)(2,1)S(1)}, u32[]{:S(2)}, u32[]{:S(2)}) collective-permute-start(bf16[512,2560]{1,0:T(8,128)(2,1)S(1)} %bitcast.430), channel_id=1, source_target_pairs={{0,1},{1,0},{2,3},{3,2},{4,5},{5,4},{6,7},{7,6},{8,9},{9,8},{10,11... | collective-permute-start | bytes 7864328 | tf_op jit(solution)/shard_map/ppermute | solution.py:77
  421.1 21.7 %collective-permute-start.43 = (bf16[128,2560]{1,0:T(8,128)(2,1)S(1)}, bf16[128,2560]{1,0:T(8,128)(2,1)S(1)}, u32[]{:S(2)}, u32[]{:S(2)}) collective-permute-start(bf16[128,2560]{1,0:T(8,128)(2,1)S(1)} %get-tuple-element.156), channel_id=1, source_target_pairs={{0,4},{2,6},{4,0},{6,2},{8,12},{10,14},{12,8},{14,10},{16,20},{18,... | collective-permute-start | bytes 1966088 | tf_op jit(solution)/shard_map/ppermute | solution.py:189
  445.3 31.5 %collective-permute-start.44 = (bf16[128,2560]{1,0:T(8,128)(2,1)S(1)}, bf16[128,2560]{1,0:T(8,128)(2,1)S(1)}, u32[]{:S(2)}, u32[]{:S(2)}) collective-permute-start(bf16[128,2560]{1,0:T(8,128)(2,1)S(1)} %fusion.66), channel_id=1, source_target_pairs={{0,16},{2,18},{4,20},{6,22},{8,24},{10,26},{12,28},{14,30},{16,0},... | collective-permute-start | bytes 1966088 | tf_op jit(solution)/shard_map/ppermute | solution.py:189
  447.5 30.2 %collective-permute-start.46 = (bf16[128,2560]{1,0:T(8,128)(2,1)}, bf16[128,2560]{1,0:T(8,128)(2,1)S(1)}, u32[]{:S(2)}, u32[]{:S(2)}) collective-permute-start(bf16[128,2560]{1,0:T(8,128)(2,1)} %get-tuple-element.159), channel_id=1, source_target_pairs={{0,4},{2,6},{4,0},{6,2},{8,12},{10,14},{12,8},{14,10},{16,20},{18,... | collective-permute-start | bytes 1966088 | tf_op jit(solution)/shard_map/ppermute | solution.py:189
  455.5 38.8 %collective-permute-start.48 = (bf16[2,160,2688]{2,1,0:T(8,128)(2,1)S(1)}, bf16[2,160,2688]{2,1,0:T(8,128)(2,1)S(1)}, u32[]{:S(2)}, u32[]{:S(2)}) collective-permute-start(bf16[2,160,2688]{2,1,0:T(8,128)(2,1)S(1)} %bitcast.459), channel_id=1, source_target_pairs={{0,2},{2,0},{4,6},{6,4},{8,10},{10,8},{12,14},{14,12},{16,18},{18,... | collective-permute-start | bytes 5160968 | tf_op jit(solution)/shard_map/ppermute | solution.py:189
  459.8 62.0 %collective-permute-start.42 = (bf16[512,2560]{1,0:T(8,128)(2,1)}, bf16[512,2560]{1,0:T(8,128)(2,1)}, u32[]{:S(2)}, u32[]{:S(2)}) collective-permute-start(bf16[512,2560]{1,0:T(8,128)(2,1)} %slice.777), channel_id=1, source_target_pairs={{0,1},{1,0},{2,3},{3,2},{4,5},{5,4},{6,7},{7,6},{8,9},{9,8},{10,11... | collective-permute-start | bytes 7864328 | tf_op jit(solution)/shard_map/ppermute | solution.py:77
  481.3 52.2 %collective-permute-start.45 = (bf16[2,160,2688]{2,1,0:T(8,128)(2,1)}, bf16[2,160,2688]{2,1,0:T(8,128)(2,1)}, u32[]{:S(2)}, u32[]{:S(2)}) collective-permute-start(bf16[2,160,2688]{2,1,0:T(8,128)(2,1)} %bitcast.82), channel_id=1, source_target_pairs={{0,8},{2,10},{4,12},{6,14},{8,0},{10,2},{12,4},{14,6},{16,24},{18,... | collective-permute-start | bytes 5160968 | tf_op jit(solution)/shard_map/ppermute | solution.py:189
  503.9 24.1 %collective-permute-start.49 = (bf16[2,160,1280]{2,1,0:T(8,128)(2,1)}, bf16[2,160,1280]{2,1,0:T(8,128)(2,1)}, u32[]{:S(2)}, u32[]{:S(2)}) collective-permute-start(bf16[2,160,1280]{2,1,0:T(8,128)(2,1)} %pad_maximum_fusion.18), channel_id=1, source_target_pairs={{0,2},{2,0},{4,6},{6,4},{8,10},{10,8},{12,14},{14,12},{16,18},{18,... | collective-permute-start | bytes 2457608 | tf_op jit(solution)/shard_map/ppermute | solution.py:189
  505.2 25.5 %collective-permute-start.50 = (bf16[2,160,1280]{2,1,0:T(8,128)(2,1)}, bf16[2,160,1280]{2,1,0:T(8,128)(2,1)}, u32[]{:S(2)}, u32[]{:S(2)}) collective-permute-start(bf16[2,160,1280]{2,1,0:T(8,128)(2,1)} %pad_maximum_fusion.19), channel_id=1, source_target_pairs={{0,4},{2,6},{4,0},{6,2},{8,12},{10,14},{12,8},{14,10},{16,20},{18,... | collective-permute-start | bytes 2457608 | tf_op jit(solution)/shard_map/ppermute | solution.py:189
  533.6 81.3 %collective-permute-start.58 = (bf16[4,160,2688]{2,1,0:T(8,128)(2,1)}, bf16[4,160,2688]{2,1,0:T(8,128)(2,1)}, u32[]{:S(2)}, u32[]{:S(2)}) collective-permute-start(bf16[4,160,2688]{2,1,0:T(8,128)(2,1)} %pad_maximum_fusion.2), channel_id=1, source_target_pairs={{0,8},{2,10},{4,12},{6,14},{8,0},{10,2},{12,4},{14,6},{16,24},{18,... | collective-permute-start | bytes 10321928 | tf_op jit(solution)/shard_map/ppermute | solution.py:189
  544.8 77.2 %collective-permute-start.54 = (bf16[4,160,2688]{2,1,0:T(8,128)(2,1)}, bf16[4,160,2688]{2,1,0:T(8,128)(2,1)}, u32[]{:S(2)}, u32[]{:S(2)}) collective-permute-start(bf16[4,160,2688]{2,1,0:T(8,128)(2,1)} %pad_maximum_fusion.1), channel_id=1, source_target_pairs={{0,2},{2,0},{4,6},{6,4},{8,10},{10,8},{12,14},{14,12},{16,18},{18,... | collective-permute-start | bytes 10321928 | tf_op jit(solution)/shard_map/ppermute | solution.py:189
  545.6 38.2 %collective-permute-start.51 = (bf16[4,160,1280]{2,1,0:T(8,128)(2,1)}, bf16[4,160,1280]{2,1,0:T(8,128)(2,1)}, u32[]{:S(2)}, u32[]{:S(2)}) collective-permute-start(bf16[4,160,1280]{2,1,0:T(8,128)(2,1)} %pad_maximum_fusion.10), channel_id=1, source_target_pairs={{0,4},{2,6},{4,0},{6,2},{8,12},{10,14},{12,8},{14,10},{16,20},{18,... | collective-permute-start | bytes 4915208 | tf_op jit(solution)/shard_map/ppermute | solution.py:189
  600.8 30.2 %collective-permute-start.53 = (bf16[128,2560]{1,0:T(8,128)(2,1)S(1)}, bf16[128,2560]{1,0:T(8,128)(2,1)S(1)}, u32[]{:S(2)}, u32[]{:S(2)}) collective-permute-start(bf16[128,2560]{1,0:T(8,128)(2,1)S(1)} %fusion.67), channel_id=1, source_target_pairs={{0,16},{2,18},{4,20},{6,22},{8,24},{10,26},{12,28},{14,30},{16,0},... | collective-permute-start | bytes 1966088 | tf_op jit(solution)/shard_map/ppermute | solution.py:189
  602.3 31.0 %collective-permute-start.55 = (bf16[128,2560]{1,0:T(8,128)(2,1)S(1)}, bf16[128,2560]{1,0:T(8,128)(2,1)S(1)}, u32[]{:S(2)}, u32[]{:S(2)}) collective-permute-start(bf16[128,2560]{1,0:T(8,128)(2,1)S(1)} %copy-done.79), channel_id=1, source_target_pairs={{0,4},{2,6},{4,0},{6,2},{8,12},{10,14},{12,8},{14,10},{16,20},{18,... | collective-permute-start | bytes 1966088 | tf_op jit(solution)/shard_map/ppermute | solution.py:189
  627.3 37.7 %collective-permute-start.61 = (bf16[4,160,1280]{2,1,0:T(8,128)(2,1)}, bf16[4,160,1280]{2,1,0:T(8,128)(2,1)}, u32[]{:S(2)}, u32[]{:S(2)}) collective-permute-start(bf16[4,160,1280]{2,1,0:T(8,128)(2,1)} %pad_maximum_fusion.11), channel_id=1, source_target_pairs={{0,2},{2,0},{4,6},{6,4},{8,10},{10,8},{12,14},{14,12},{16,18},{18,... | collective-permute-start | bytes 4915208 | tf_op jit(solution)/shard_map/ppermute | solution.py:189
  634.3 39.1 %collective-permute-start.74 = (bf16[160,2688]{1,0:T(8,128)(2,1)}, bf16[160,2688]{1,0:T(8,128)(2,1)}, u32[]{:S(2)}, u32[]{:S(2)}) collective-permute-start(bf16[160,2688]{1,0:T(8,128)(2,1)} %get-tuple-element.193), channel_id=1, source_target_pairs={{0,16},{2,18},{4,20},{6,22},{8,24},{10,26},{12,28},{14,30},{16,0},... | collective-permute-start | bytes 2580488 | tf_op jit(solution)/shard_map/ppermute | solution.py:189
  634.4 37.5 %collective-permute-start.59 = (bf16[2,160,2688]{2,1,0:T(8,128)(2,1)}, bf16[2,160,2688]{2,1,0:T(8,128)(2,1)}, u32[]{:S(2)}, u32[]{:S(2)}) collective-permute-start(bf16[2,160,2688]{2,1,0:T(8,128)(2,1)} %pad_maximum_fusion.6), channel_id=1, source_target_pairs={{0,4},{2,6},{4,0},{6,2},{8,12},{10,14},{12,8},{14,10},{16,20},{18,... | collective-permute-start | bytes 5160968 | tf_op jit(solution)/shard_map/ppermute | solution.py:189
  641.5 74.1 %collective-permute-start.57 = (bf16[16,80,1152]{2,1,0:T(8,128)(2,1)}, bf16[16,80,1152]{2,1,0:T(8,128)(2,1)}, u32[]{:S(2)}, u32[]{:S(2)}) collective-permute-start(bf16[16,80,1152]{2,1,0:T(8,128)(2,1)} %fusion.32), channel_id=1, source_target_pairs={{0,1},{1,0},{2,3},{3,2},{4,5},{5,4},{6,7},{7,6},{8,9},{9,8},{10,11... | collective-permute-start | bytes 8847368 | tf_op jit(solution)/shard_map/ppermute | solution.py:77
  673.5 39.1 %collective-permute-start.75 = (bf16[160,2688]{1,0:T(8,128)(2,1)S(1)}, bf16[160,2688]{1,0:T(8,128)(2,1)S(1)}, u32[]{:S(2)}, u32[]{:S(2)}) collective-permute-start(bf16[160,2688]{1,0:T(8,128)(2,1)S(1)} %get-tuple-element.194), channel_id=1, source_target_pairs={{0,16},{2,18},{4,20},{6,22},{8,24},{10,26},{12,28},{14,30},{16,0},... | collective-permute-start | bytes 2580488 | tf_op jit(solution)/shard_map/ppermute | solution.py:189
  684.8 43.5 %collective-permute-start.72 = (bf16[160,1280]{1,0:T(8,128)(2,1)}, bf16[160,1280]{1,0:T(8,128)(2,1)}, u32[]{:S(2)}, u32[]{:S(2)}) collective-permute-start(bf16[160,1280]{1,0:T(8,128)(2,1)} %get-tuple-element.191), channel_id=1, source_target_pairs={{0,8},{2,10},{4,12},{6,14},{8,0},{10,2},{12,4},{14,6},{16,24},{18,... | collective-permute-start | bytes 1228808 | tf_op jit(solution)/shard_map/ppermute | solution.py:189
  690.3 35.5 %collective-permute-start.63 = (bf16[4,64,2560]{2,1,0:T(8,128)(2,1)}, bf16[4,64,2560]{2,1,0:T(8,128)(2,1)}, u32[]{:S(2)}, u32[]{:S(2)}) collective-permute-start(bf16[4,64,2560]{2,1,0:T(8,128)(2,1)} %pad_maximum_fusion.14), channel_id=1, source_target_pairs={{0,2},{2,0},{4,6},{6,4},{8,10},{10,8},{12,14},{14,12},{16,18},{18,... | collective-permute-start | bytes 3932168 | tf_op jit(solution)/shard_map/ppermute | solution.py:189
  691.6 34.2 %collective-permute-start.64 = (bf16[4,64,2560]{2,1,0:T(8,128)(2,1)}, bf16[4,64,2560]{2,1,0:T(8,128)(2,1)}, u32[]{:S(2)}, u32[]{:S(2)}) collective-permute-start(bf16[4,64,2560]{2,1,0:T(8,128)(2,1)} %pad_maximum_fusion.15), channel_id=1, source_target_pairs={{0,4},{2,6},{4,0},{6,2},{8,12},{10,14},{12,8},{14,10},{16,20},{18,... | collective-permute-start | bytes 3932168 | tf_op jit(solution)/shard_map/ppermute | solution.py:189
  733.3 31.4 %collective-permute-start.65 = (bf16[4,80,1152]{2,1,0:T(8,128)(2,1)}, bf16[4,80,1152]{2,1,0:T(8,128)(2,1)}, u32[]{:S(2)}, u32[]{:S(2)}) collective-permute-start(bf16[4,80,1152]{2,1,0:T(8,128)(2,1)} %pad_maximum_fusion.21), channel_id=1, source_target_pairs={{0,2},{2,0},{4,6},{6,4},{8,10},{10,8},{12,14},{14,12},{16,18},{18,... | collective-permute-start | bytes 2211848 | tf_op jit(solution)/shard_map/ppermute | solution.py:189
  734.7 34.1 %collective-permute-start.66 = (bf16[4,80,1152]{2,1,0:T(8,128)(2,1)}, bf16[4,80,1152]{2,1,0:T(8,128)(2,1)}, u32[]{:S(2)}, u32[]{:S(2)}) collective-permute-start(bf16[4,80,1152]{2,1,0:T(8,128)(2,1)} %pad_maximum_fusion.22), channel_id=1, source_target_pairs={{0,4},{2,6},{4,0},{6,2},{8,12},{10,14},{12,8},{14,10},{16,20},{18,... | collective-permute-start | bytes 2211848 | tf_op jit(solution)/shard_map/ppermute | solution.py:189
  736.3 32.6 %collective-permute-start.67 = (bf16[4,80,1152]{2,1,0:T(8,128)(2,1)}, bf16[4,80,1152]{2,1,0:T(8,128)(2,1)}, u32[]{:S(2)}, u32[]{:S(2)}) collective-permute-start(bf16[4,80,1152]{2,1,0:T(8,128)(2,1)} %pad_maximum_fusion.23), channel_id=1, source_target_pairs={{0,6},{2,4},{4,2},{6,0},{8,14},{10,12},{12,10},{14,8},{16,22},{18,... | collective-permute-start | bytes 2211848 | tf_op jit(solution)/shard_map/ppermute | solution.py:189
  738.6 36.6 %collective-permute-start.77 = (bf16[64,2560]{1,0:T(8,128)(2,1)}, bf16[64,2560]{1,0:T(8,128)(2,1)}, u32[]{:S(2)}, u32[]{:S(2)}) collective-permute-start(bf16[64,2560]{1,0:T(8,128)(2,1)} %fusion.95), channel_id=1, source_target_pairs={{0,16},{2,18},{4,20},{6,22},{8,24},{10,26},{12,28},{14,30},{16,0},... | collective-permute-start | bytes 983048 | tf_op jit(solution)/shard_map/ppermute | solution.py:189
  739.6 35.6 %collective-permute-start.78 = (bf16[64,2560]{1,0:T(8,128)(2,1)S(1)}, bf16[64,2560]{1,0:T(8,128)(2,1)}, u32[]{:S(2)}, u32[]{:S(2)}) collective-permute-start(bf16[64,2560]{1,0:T(8,128)(2,1)S(1)} %get-tuple-element.197), channel_id=1, source_target_pairs={{0,8},{2,10},{4,12},{6,14},{8,0},{10,2},{12,4},{14,6},{16,24},{18,... | collective-permute-start | bytes 983048 | tf_op jit(solution)/shard_map/ppermute | solution.py:189
  (141 other events, 1986.5 us)

commit v5 on v4

--- a/solution.py
+++ b/solution.py
@@ -455,25 +455,62 @@
     )
 
 
+def bring(pieces, weight_ref, sems, column):
+    copies, start = [], 0
+    for at, piece in enumerate(pieces):
+        rows = piece.shape[0]
+        copies.append(
+            pltpu.make_async_copy(
+                piece.at[:, pl.ds(column, weight_ref.shape[1])],
+                weight_ref.at[pl.ds(start, rows)],
+                sems.at[at],
+            )
+        )
+        start += rows
+    for copy in copies:
+        copy.start()
+    for copy in copies:
+        copy.wait()
+
+
+def units_out_kernel(share, count, act_ref, *refs):
+    pieces, (out_ref, weight_ref, sems) = refs[:count], refs[count:]
+
+    @pl.when(pl.program_id(0) == 0)
+    def _():
+        bring(pieces, weight_ref, sems, 2 * share)
+
+    out_ref[...] = low(mul_trans(act_ref[...], weight_ref[...]))
+
+
+def units_out(act, pieces, share):
+    rows, width = act.shape[0], sum(piece.shape[0] for piece in pieces)
+    block = rows // 4
+    return pl.pallas_call(
+        partial(units_out_kernel, share, len(pieces)),
+        grid=(4,),
+        in_specs=[pl.BlockSpec((block, share), lambda step: (step, 0))]
+        + [pl.BlockSpec(memory_space=pl.ANY)] * len(pieces),
+        out_specs=pl.BlockSpec((block, width), lambda step: (step, 0)),
+        out_shape=jax.ShapeDtypeStruct((rows, width), jnp.bfloat16),
+        scratch_shapes=[
+            pltpu.VMEM((width, share), jnp.bfloat16),
+            pltpu.SemaphoreType.DMA((len(pieces),)),
+        ],
+        compiler_params=pltpu.CompilerParams(vmem_limit_bytes=32 * 2**20),
+        name="units_out",
+    )(act, *pieces)
+
+
 def units_kernel(
     share, count, own_ref, other_ref, own_back_ref, other_back_ref, *refs
 ):
-    pieces, (act_ref, d_units_ref, d_in_ref, out_ref, weight_ref, sems) = refs[:count], refs[count:]
+    pieces, (act_ref, d_units_ref, d_in_ref, weight_ref, sems) = refs[:count], refs[count:]
     step = pl.program_id(0)
 
     @pl.when(step == 0)
     def _():
-        copies, start = [], 0
-        for at, piece in enumerate(pieces):
-            rows = piece.shape[0]
-            copies.append(
-                pltpu.make_async_copy(piece, weight_ref.at[pl.ds(start, rows)], sems.at[at])
-            )
-            start += rows
-        for copy in copies:
-            copy.start()
-        for copy in copies:
-            copy.wait()
+        bring(pieces, weight_ref, sems, 0)
 
     is_own = step < pl.num_programs(0) // 2
     tokens = jnp.where(is_own, own_ref[...], other_ref[...])
@@ -490,7 +527,6 @@
     d_units_ref[:, gate_cut] = low(d_act * upper * (slope + swished * (1.0 - slope)))
     d_units_ref[:, up_cut] = low(d_act * swished)
     d_in_ref[...] = low(mul_trans(d_units_ref[...], weight_ref[:, : 2 * share]))
-    out_ref[...] = low(mul_trans(act, weight_ref[:, down_cut]))
 
 
 def run_units(tokens, back, pieces, share):
@@ -506,7 +542,7 @@
     def out_spec(columns):
         return pl.BlockSpec((block, columns), lambda step: (step, 0))
 
-    columns = (share, 2 * share, width, width)
+    columns = (share, 2 * share, width)
     return pl.pallas_call(
         partial(units_kernel, share, len(pieces)),
         grid=(steps,),
@@ -901,7 +937,7 @@
     ]
     if any(piece.shape[0] % 16 for piece in unit_pieces):
         unit_pieces = [jnp.concatenate(unit_pieces)]
-    act_low, d_units, d_mlp_terms, mlp_terms = run_units(mlp_seq, mlp_back, unit_pieces, share)
+    act_low, d_units, d_mlp_terms = run_units(mlp_seq, mlp_back, unit_pieces, share)
     chip_rows = GROUP * own_rows
     d_mlp_other = core_swap(d_mlp_terms[chip_rows:])
     d_mlp_flow = links.flow("D", return_tokens(d_mlp_terms[:chip_rows], d_mlp_other, own_rows))
@@ -914,11 +950,12 @@
         "R", reduce_bits(lambda mask: unit_grad[masks_of(others).index(mask)], others, "both")
     )
     unit_flow.step(["D1", "D2"]).step()
+    mlp_terms = units_out(tied(act_low, links.named(["D0"])), unit_pieces, share)
     mlp_flow = links.flow(
         "O",
         return_tokens(
             mlp_terms[:chip_rows],
-            core_swap(tied(mlp_terms, [d_mlp_other])[chip_rows:]),
+            core_swap(mlp_terms[chip_rows:]),
             own_rows,
         ),
     )

time: 802 us -> 781 us (0.974)
  waiting for transfers between devices: 356 us -> 328 us
  matrix products: 66.7 us -> 75.8 us
    ppermute x69, waiting for transfers between devices: 351 us -> 323 us  [send(): lax.ppermute(item, 'dp', [(place, place ^ to) for place in range(count)])]
    unnamed x263 -> x329, local copies, waits for them, and re-layouts: 24.8 us -> 30 us
    another operation x11 -> x10, other arithmetic: 26.9 us -> 24.1 us
  transfers between devices with their start and end apart: 79 -> 79, of which waited for: 42 -> 40; matrix products, arithmetic and copies ran while one was open for 29% -> 31% of each run, Pallas kernels for 7% -> 8%
where the time goes in v5:
time: 781 us; the launch traced here: 774 us
  waiting for transfers between devices  328 us (42%)
  local copies, waits for them, and re-layouts  100 us (13%)
  Pallas kernels  97.5 us (12%)
  other arithmetic  88.8 us (11%)
  starting transfers between devices  79.3 us (10%)
  matrix products  75.8 us (10%)
    ppermute x69, waiting for transfers between devices, send(): lax.ppermute(item, 'dp', [(place, place ^ to) for place in range(count)])  323 us
    ppermute x69, starting transfers between devices, send(): lax.ppermute(item, 'dp', [(place, place ^ to) for place in range(count)])  78.8 us
    dot_general x9, matrix products, plain_mul(): return jnp.dot(left, right, preferred_element_type=jnp.float32)  36.8 us
    pallas_call x1, Pallas kernels, run_units(): pl.pallas_call(partial(units_kernel, share, len(pieces)), grid=(steps,),...  36.1 us
    unnamed x329, local copies, waits for them, and re-layouts  30 us
    dot_general x8, matrix products, mul_trans(): lax.dot_general(left, right, (((1,), (1,)), ((), ())), preferred_element_...  25.6 us
    another operation x10, other arithmetic  24.1 us
    pallas_call x1, Pallas kernels, unit_grads(): pl.pallas_call(partial(unit_grads_kernel, share), grid=(CHUNKS,), in_spec...  21.1 us
  transfers between devices with their start and end apart: 79, of which 40 were waited for; matrix products, arithmetic and copies ran while one was open for 31% of the time, Pallas kernels for 8%

profile of v5, /device:TPU:0, one launch (start us, length us, event | category | flops | bytes accessed | tf_op | source)
XLA Modules:
  0.0 773.6 jit_solution(15505450342268023000)
XLA Ops:
  4.1 5.1 collective-permute-start.2
  31.0 11.4 %collective-permute-done.3 = bf16[64,2560]{1,0:T(8,128)(2,1)S(1)} collective-permute-done((bf16[64,2560]{1,0:T(8,128)(2,1)S(1)}, bf16[64,2560]{1,0:T(8,128)(2,1)S(1)}, u32[]{:S(2)}, u32[]{:S(2)}) %collective-permute-start.3) | collective-permute-done | bytes 327712 | tf_op jit(solution)/shard_map/ppermute | solution.py:189
  58.2 11.8 %collective-permute-done.6 = bf16[4,80,1152]{2,1,0:T(8,128)(2,1)S(1)} collective-permute-done((bf16[4,80,1152]{2,1,0:T(8,128)(2,1)S(1)}, bf16[4,80,1152]{2,1,0:T(8,128)(2,1)S(1)}, u32[]{:S(2)}, u32[]{:S(2)}) %collective-permute-start.6) | collective-permute-done | bytes 737312 | tf_op jit(solution)/shard_map/ppermute | solution.py:189
  73.1 14.9 %collective-permute-done.8 = bf16[4,80,1152]{2,1,0:T(8,128)(2,1)S(1)} collective-permute-done((bf16[4,80,1152]{2,1,0:T(8,128)(2,1)S(1)}, bf16[4,80,1152]{2,1,0:T(8,128)(2,1)S(1)}, u32[]{:S(2)}, u32[]{:S(2)}) %collective-permute-start.8) | collective-permute-done | bytes 737312 | tf_op jit(solution)/shard_map/ppermute | solution.py:189
  93.3 5.0 fusion.3
  99.5 5.2 collective-permute-done.14
  107.3 15.3 %collective-permute-done.17 = bf16[4,64,2560]{2,1,0:T(8,128)(2,1)S(1)} collective-permute-done((bf16[4,64,2560]{2,1,0:T(8,128)(2,1)}, bf16[4,64,2560]{2,1,0:T(8,128)(2,1)S(1)}, u32[]{:S(2)}, u32[]{:S(2)}) %collective-permute-start.17) | collective-permute-done | bytes 1310752 | tf_op jit(solution)/shard_map/ppermute | solution.py:189
  123.6 5.1 collective-permute-done.15
  130.2 8.5 %collective-permute-done.23 = bf16[160,2688]{1,0:T(8,128)(2,1)S(1)} collective-permute-done((bf16[160,2688]{1,0:T(8,128)(2,1)S(1)}, bf16[160,2688]{1,0:T(8,128)(2,1)S(1)}, u32[]{:S(2)}, u32[]{:S(2)}) %collective-permute-start.23) | collective-permute-done | bytes 860192 | tf_op jit(solution)/shard_map/ppermute | solution.py:189
  169.7 7.6 collective-permute-done.18
  178.7 17.3 %collective-permute-done.26 = bf16[2,160,2688]{2,1,0:T(8,128)(2,1)} collective-permute-done((bf16[2,160,2688]{2,1,0:T(8,128)(2,1)S(1)}, bf16[2,160,2688]{2,1,0:T(8,128)(2,1)}, u32[]{:S(2)}, u32[]{:S(2)}) %collective-permute-start.26) | collective-permute-done | bytes 1720352 | tf_op jit(solution)/shard_map/ppermute | solution.py:189
  213.0 4.1 convolution_convert_fusion.kv_ref
  217.3 4.5 fusion.276.q_ref
  221.8 10.5 %attend.1 = (bf16[256,1280]{1,0:T(8,128)(2,1)S(1)}, bf16[256,2560]{1,0:T(8,128)(2,1)S(1)}) custom-call(f32[256,2560]{1,0:T(8,128)S(1)} %fusion.276.q_ref, bf16[256,2560]{1,0:T(8,128)(2,1)S(1)} %convolution_convert_fusion.kv_ref, bf16[256,128]{1,0:T(8,128)(2,1)S(1)} %slice.962.rot_ref, f32[256,256]{1,0:T(8,128)S(1)} %copy-done.22, f32[256,128]{1,0:T(8,128)S(1)} %copy-done.30, ...), custom_call_target="tpu_custom_call" | custom-call | tf_op jit(solution)/shard_map/attend/pallas_call | solution.py:727
  232.3 13.3 %collective-permute-done.25 = bf16[128,2560]{1,0:T(8,128)(2,1)S(1)} collective-permute-done((bf16[128,2560]{1,0:T(8,128)(2,1)}, bf16[128,2560]{1,0:T(8,128)(2,1)S(1)}, u32[]{:S(2)}, u32[]{:S(2)}) %collective-permute-start.25) | collective-permute-done | bytes 655392 | tf_op jit(solution)/shard_map/ppermute | solution.py:189
  253.0 14.3 %collective-permute-done.28 = bf16[2,160,1280]{2,1,0:T(8,128)(2,1)S(1)} collective-permute-done((bf16[2,160,1280]{2,1,0:T(8,128)(2,1)S(1)}, bf16[2,160,1280]{2,1,0:T(8,128)(2,1)S(1)}, u32[]{:S(2)}, u32[]{:S(2)}) %collective-permute-start.28) | collective-permute-done | bytes 819232 | tf_op jit(solution)/shard_map/ppermute | solution.py:189
  268.4 7.4 collective-permute-done.30
  285.3 12.9 %collective-permute-done.32.refs_1_ = bf16[128,2560]{1,0:T(8,128)(2,1)S(1)} collective-permute-done((bf16[128,2560]{1,0:T(8,128)(2,1)S(1)}, bf16[128,2560]{1,0:T(8,128)(2,1)S(1)}, u32[]{:S(2)}, u32[]{:S(2)}) %collective-permute-start.32) | collective-permute-done | bytes 655392 | tf_op jit(solution)/shard_map/ppermute | solution.py:189
  298.2 15.3 %collective-permute-done.33.refs_2_ = bf16[128,2560]{1,0:T(8,128)(2,1)S(1)} collective-permute-done((bf16[128,2560]{1,0:T(8,128)(2,1)S(1)}, bf16[128,2560]{1,0:T(8,128)(2,1)S(1)}, u32[]{:S(2)}, u32[]{:S(2)}) %collective-permute-start.33) | collective-permute-done | bytes 655392 | tf_op jit(solution)/shard_map/ppermute | solution.py:189
  313.5 5.7 collective-permute-done.34
  320.6 9.0 %fusion.20.own_back_ref = bf16[512,2560]{1,0:T(8,128)(2,1)S(1)} fusion(s32[2560]{0:T(1024)S(1)} %fusion.188, bf16[128,2560]{1,0:T(8,128)(2,1)S(1)} %collective-permute-done.30, bf16[128,2560]{1,0:T(8,128)(2,1)S(1)} %collective-permute-done.25, bf16[128,2560]{1,0:T(8,128)(2,1)} %collective-permute-done.5, bf16[128,2560]{1,0:T(8,128)(2,1)} %multiply_convert_fusion.5), kind=kOutput, calls=%fused_computation.35 | convolution fusion | flops 6729236480 | bytes 5253120 | tf_op jit(solution)/shard_map/dot_general | solution.py:53
  329.7 5.7 collective-permute-done.35.refs_3_
  339.5 20.0 %collective-permute-done.39 = bf16[1,160,2688]{2,1,0:T(8,128)(2,1)S(1)} collective-permute-done((bf16[1,160,2688]{2,1,0:T(8,128)(2,1)S(1)}, bf16[1,160,2688]{2,1,0:T(8,128)(2,1)S(1)}, u32[]{:S(2)}, u32[]{:S(2)}) %collective-permute-start.39) | collective-permute-done | bytes 860192 | tf_op jit(solution)/shard_map/ppermute | solution.py:189
  361.6 36.1 %run_units.1 = (bf16[1024,896]{1,0:T(8,128)(2,1)}, bf16[1024,1792]{1,0:T(8,128)(2,1)}, bf16[1024,2560]{1,0:T(8,128)(2,1)}) custom-call(bf16[512,2560]{1,0:T(8,128)(2,1)} %bitcast.431, bf16[512,2560]{1,0:T(8,128)(2,1)} %copy-done.46, bf16[512,2560]{1,0:T(8,128)(2,1)} %copy-done.44, bf16[512,2560]{1,0:T(8,128)(2,1)} %copy-done.45, ...), custom_call_target="tpu_custom_call" | custom-call | tf_op jit(solution)/shard_map/run_units/pallas_call | solution.py:546
  399.9 4.9 collective-permute-done.41
  408.0 21.1 %unit_grads.1 = bf16[2560,2688]{1,0:T(8,128)(2,1)} custom-call(bf16[512,2560]{1,0:T(8,128)(2,1)} %bitcast.432, bf16[512,2560]{1,0:T(8,128)(2,1)} %copy-done.46, bf16[512,2560]{1,0:T(8,128)(2,1)} %copy-done.44, bf16[512,2560]{1,0:T(8,128)(2,1)} %copy-done.45, bf16[1024,896]{1,0:T(8,128)(2,1)} %get-tuple-element.153.act_ref, ...), custom_call_target="tpu_custom_call" | custom-call | tf_op jit(solution)/shard_map/unit_grads/pallas_call | solution.py:572
  432.8 7.6 fusion.266
  445.6 7.8 %units_out.1 = bf16[1024,2560]{1,0:T(8,128)(2,1)S(1)} custom-call(bf16[1024,896]{1,0:T(8,128)(2,1)S(1)} %copy-done.11, bf16[320,2688]{1,0:T(8,128)(2,1)S(1)} %bitcast.434, bf16[320,2688]{1,0:T(8,128)(2,1)S(1)} %bitcast.436, bf16[320,2688]{1,0:T(8,128)(2,1)S(1)} %bitcast.442, bf16[320,2688]{1,0:T(8,128)(2,1)S(1)} %bitcast.438, ...), custom_call_target="tpu_custom_call" | custom-call | tf_op jit(solution)/shard_map/units_out/pallas_call | solution.py:489
  455.1 6.4 collective-permute-done.44.refs_0_
  466.1 13.3 %collective-permute-done.48 = bf16[2,160,2688]{2,1,0:T(8,128)(2,1)} collective-permute-done((bf16[2,160,2688]{2,1,0:T(8,128)(2,1)}, bf16[2,160,2688]{2,1,0:T(8,128)(2,1)}, u32[]{:S(2)}, u32[]{:S(2)}) %collective-permute-start.48) | collective-permute-done | bytes 1720352 | tf_op jit(solution)/shard_map/ppermute | solution.py:189
  483.4 6.7 fusion.273
  493.2 5.1 slice_bitcast_fusion.14
  500.2 14.0 %attend_back.1 = (bf16[256,2560]{1,0:T(8,128)(2,1)S(1)}, bf16[256,2560]{1,0:T(8,128)(2,1)S(1)}, f32[256,128]{1,0:T(8,128)S(1)}) custom-call(bf16[256,2560]{1,0:T(8,128)(2,1)S(1)} %copy-done.25, bf16[256,2560]{1,0:T(8,128)(2,1)S(1)} %copy-done.17, bf16[256,128]{1,0:T(8,128)(2,1)S(1)} %slice.962.rot_ref, f32[256,256]{1,0:T(8,128)S(1)} %copy-done.23, ...), custom_call_target="tpu_custom_call" | custom-call | tf_op jit(solution)/shard_map/attend_back/pallas_call | solution.py:744
  534.1 5.0 fusion.255
  544.4 4.9 multiply_reduce_fusion
  554.2 5.3 fusion
  559.6 4.1 collective-permute-done.51
  565.4 14.2 %collective-permute-done.52.refs_0_ = bf16[128,2560]{1,0:T(8,128)(2,1)S(1)} collective-permute-done((bf16[128,2560]{1,0:T(8,128)(2,1)S(1)}, bf16[128,2560]{1,0:T(8,128)(2,1)S(1)}, u32[]{:S(2)}, u32[]{:S(2)}) %collective-permute-start.52) | collective-permute-done | bytes 655392 | tf_op jit(solution)/shard_map/ppermute | solution.py:189
  582.1 19.2 %collective-permute-done.58 = bf16[4,160,2688]{2,1,0:T(8,128)(2,1)} collective-permute-done((bf16[4,160,2688]{2,1,0:T(8,128)(2,1)}, bf16[4,160,2688]{2,1,0:T(8,128)(2,1)}, u32[]{:S(2)}, u32[]{:S(2)}) %collective-permute-start.58) | collective-permute-done | bytes 3440672 | tf_op jit(solution)/shard_map/ppermute | solution.py:189
  601.6 4.3 fusion.13
  620.7 6.7 fusion.24
  627.4 17.3 %collective-permute-done.61 = bf16[4,160,1280]{2,1,0:T(8,128)(2,1)} collective-permute-done((bf16[4,160,1280]{2,1,0:T(8,128)(2,1)}, bf16[4,160,1280]{2,1,0:T(8,128)(2,1)}, u32[]{:S(2)}, u32[]{:S(2)}) %collective-permute-start.61) | collective-permute-done | bytes 1638432 | tf_op jit(solution)/shard_map/ppermute | solution.py:189
  657.6 7.0 collective-permute-done.71
  671.5 20.3 %collective-permute-done.75 = bf16[160,2688]{1,0:T(8,128)(2,1)S(1)} collective-permute-done((bf16[160,2688]{1,0:T(8,128)(2,1)S(1)}, bf16[160,2688]{1,0:T(8,128)(2,1)S(1)}, u32[]{:S(2)}, u32[]{:S(2)}) %collective-permute-start.75) | collective-permute-done | bytes 860192 | tf_op jit(solution)/shard_map/ppermute | solution.py:189
  694.3 6.6 fusion.261
  729.2 4.6 copy.75
  743.5 4.8 collective-permute-done.66
  763.3 6.2 collective-permute-done.69
  (649 shorter events, 286.2 us)
Async XLA Ops:
  11.9 39.4 %collective-permute-start.5 = (bf16[128,2560]{1,0:T(8,128)(2,1)}, bf16[128,2560]{1,0:T(8,128)(2,1)}, u32[]{:S(2)}, u32[]{:S(2)}) collective-permute-start(bf16[128,2560]{1,0:T(8,128)(2,1)} %multiply_convert_fusion.5), channel_id=1, source_target_pairs={{0,4},{2,6},{4,0},{6,2},{8,12},{10,14},{12,8},{14,10},{16,20},{18,... | collective-permute-start | bytes 1966088 | tf_op jit(solution)/shard_map/ppermute | solution.py:189
  43.6 44.9 %collective-permute-start.12 = (bf16[160,1280]{1,0:T(8,128)(2,1)}, bf16[160,1280]{1,0:T(8,128)(2,1)}, u32[]{:S(2)}, u32[]{:S(2)}) collective-permute-start(bf16[160,1280]{1,0:T(8,128)(2,1)} %bitcast.31), channel_id=1, source_target_pairs={{0,16},{2,18},{4,20},{6,22},{8,24},{10,26},{12,28},{14,30},{16,0},... | collective-permute-start | bytes 1228808 | tf_op jit(solution)/shard_map/ppermute | solution.py:189
  55.1 32.8 %collective-permute-start.8 = (bf16[4,80,1152]{2,1,0:T(8,128)(2,1)S(1)}, bf16[4,80,1152]{2,1,0:T(8,128)(2,1)S(1)}, u32[]{:S(2)}, u32[]{:S(2)}) collective-permute-start(bf16[4,80,1152]{2,1,0:T(8,128)(2,1)S(1)} %copy-done.96), channel_id=1, source_target_pairs={{0,6},{2,4},{4,2},{6,0},{8,14},{10,12},{12,10},{14,8},{16,22},{18,... | collective-permute-start | bytes 2211848 | tf_op jit(solution)/shard_map/ppermute | solution.py:189
  58.2 30.4 %collective-permute-start.13 = (bf16[160,1280]{1,0:T(8,128)(2,1)}, bf16[160,1280]{1,0:T(8,128)(2,1)S(1)}, u32[]{:S(2)}, u32[]{:S(2)}) collective-permute-start(bf16[160,1280]{1,0:T(8,128)(2,1)} %bitcast.31), channel_id=1, source_target_pairs={{0,8},{2,10},{4,12},{6,14},{8,0},{10,2},{12,4},{14,6},{16,24},{18,... | collective-permute-start | bytes 1228808 | tf_op jit(solution)/shard_map/ppermute | solution.py:189
  88.3 53.1 %collective-permute-start.9 = (bf16[16,80,1152]{2,1,0:T(8,128)(2,1)S(1)}, bf16[16,80,1152]{2,1,0:T(8,128)(2,1)S(1)}, u32[]{:S(2)}, u32[]{:S(2)}) collective-permute-start(bf16[16,80,1152]{2,1,0:T(8,128)(2,1)S(1)} %bitcast.462), channel_id=1, source_target_pairs={{0,1},{1,0},{2,3},{3,2},{4,5},{5,4},{6,7},{7,6},{8,9},{9,8},{10,11... | collective-permute-start | bytes 8847368 | tf_op jit(solution)/shard_map/ppermute | solution.py:77
  88.6 40.0 %collective-permute-start.15 = (bf16[2,160,2688]{2,1,0:T(8,128)(2,1)S(1)}, bf16[2,160,2688]{2,1,0:T(8,128)(2,1)S(1)}, u32[]{:S(2)}, u32[]{:S(2)}) collective-permute-start(bf16[2,160,2688]{2,1,0:T(8,128)(2,1)S(1)} %pad_maximum_fusion.3), channel_id=1, source_target_pairs={{0,4},{2,6},{4,0},{6,2},{8,12},{10,14},{12,8},{14,10},{16,20},{18,... | collective-permute-start | bytes 5160968 | tf_op jit(solution)/shard_map/ppermute | solution.py:189
  91.8 30.8 %collective-permute-start.17 = (bf16[4,64,2560]{2,1,0:T(8,128)(2,1)}, bf16[4,64,2560]{2,1,0:T(8,128)(2,1)S(1)}, u32[]{:S(2)}, u32[]{:S(2)}) collective-permute-start(bf16[4,64,2560]{2,1,0:T(8,128)(2,1)} %pad_maximum_fusion.12), channel_id=1, source_target_pairs={{0,2},{2,0},{4,6},{6,4},{8,10},{10,8},{12,14},{14,12},{16,18},{18,... | collective-permute-start | bytes 3932168 | tf_op jit(solution)/shard_map/ppermute | solution.py:189
  98.5 40.1 %collective-permute-start.23 = (bf16[160,2688]{1,0:T(8,128)(2,1)S(1)}, bf16[160,2688]{1,0:T(8,128)(2,1)S(1)}, u32[]{:S(2)}, u32[]{:S(2)}) collective-permute-start(bf16[160,2688]{1,0:T(8,128)(2,1)S(1)} %get-tuple-element.132), channel_id=1, source_target_pairs={{0,16},{2,18},{4,20},{6,22},{8,24},{10,26},{12,28},{14,30},{16,0},... | collective-permute-start | bytes 2580488 | tf_op jit(solution)/shard_map/ppermute | solution.py:189
  128.6 32.9 %collective-permute-start.16 = (bf16[4,64,2560]{2,1,0:T(8,128)(2,1)}, bf16[4,64,2560]{2,1,0:T(8,128)(2,1)}, u32[]{:S(2)}, u32[]{:S(2)}) collective-permute-start(bf16[4,64,2560]{2,1,0:T(8,128)(2,1)} %pad_maximum_fusion.12), channel_id=1, source_target_pairs={{0,4},{2,6},{4,0},{6,2},{8,12},{10,14},{12,8},{14,10},{16,20},{18,... | collective-permute-start | bytes 3932168 | tf_op jit(solution)/shard_map/ppermute | solution.py:189
  138.8 59.0 %collective-permute-start.24 = (bf16[160,2688]{1,0:T(8,128)(2,1)}, bf16[160,2688]{1,0:T(8,128)(2,1)}, u32[]{:S(2)}, u32[]{:S(2)}) collective-permute-start(bf16[160,2688]{1,0:T(8,128)(2,1)} %get-tuple-element.133), channel_id=1, source_target_pairs={{0,16},{2,18},{4,20},{6,22},{8,24},{10,26},{12,28},{14,30},{16,0},... | collective-permute-start | bytes 2580488 | tf_op jit(solution)/shard_map/ppermute | solution.py:189
  138.9 38.4 %collective-permute-start.18 = (bf16[2,160,2688]{2,1,0:T(8,128)(2,1)S(1)}, bf16[2,160,2688]{2,1,0:T(8,128)(2,1)S(1)}, u32[]{:S(2)}, u32[]{:S(2)}) collective-permute-start(bf16[2,160,2688]{2,1,0:T(8,128)(2,1)S(1)} %pad_maximum_fusion.4), channel_id=1, source_target_pairs={{0,2},{2,0},{4,6},{6,4},{8,10},{10,8},{12,14},{14,12},{16,18},{18,... | collective-permute-start | bytes 5160968 | tf_op jit(solution)/shard_map/ppermute | solution.py:189
  139.5 56.5 %collective-permute-start.26 = (bf16[2,160,2688]{2,1,0:T(8,128)(2,1)S(1)}, bf16[2,160,2688]{2,1,0:T(8,128)(2,1)}, u32[]{:S(2)}, u32[]{:S(2)}) collective-permute-start(bf16[2,160,2688]{2,1,0:T(8,128)(2,1)S(1)} %pad_maximum_fusion.4), channel_id=1, source_target_pairs={{0,8},{2,10},{4,12},{6,14},{8,0},{10,2},{12,4},{14,6},{16,24},{18,... | collective-permute-start | bytes 5160968 | tf_op jit(solution)/shard_map/ppermute | solution.py:189
  168.1 28.1 %collective-permute-start.20 = (bf16[2,64,2560]{2,1,0:T(8,128)(2,1)S(1)}, bf16[2,64,2560]{2,1,0:T(8,128)(2,1)S(1)}, u32[]{:S(2)}, u32[]{:S(2)}) collective-permute-start(bf16[2,64,2560]{2,1,0:T(8,128)(2,1)S(1)} %copy-done.110), channel_id=1, source_target_pairs={{0,4},{2,6},{4,0},{6,2},{8,12},{10,14},{12,8},{14,10},{16,20},{18,... | collective-permute-start | bytes 1966088 | tf_op jit(solution)/shard_map/ppermute | solution.py:189
  196.0 54.1 %collective-permute-start.27 = (bf16[2,160,2688]{2,1,0:T(8,128)(2,1)S(1)}, bf16[2,160,2688]{2,1,0:T(8,128)(2,1)S(1)}, u32[]{:S(2)}, u32[]{:S(2)}) collective-permute-start(bf16[2,160,2688]{2,1,0:T(8,128)(2,1)S(1)} %collective-permute-done.18), channel_id=1, source_target_pairs={{0,8},{2,10},{4,12},{6,14},{8,0},{10,2},{12,4},{14,6},{16,24},{18,... | collective-permute-start | bytes 5160968 | tf_op jit(solution)/shard_map/ppermute | solution.py:189
  196.2 52.7 %collective-permute-start.21 = (bf16[4,160,1280]{2,1,0:T(8,128)(2,1)S(1)}, bf16[4,160,1280]{2,1,0:T(8,128)(2,1)S(1)}, u32[]{:S(2)}, u32[]{:S(2)}) collective-permute-start(bf16[4,160,1280]{2,1,0:T(8,128)(2,1)S(1)} %copy-done.81), channel_id=1, source_target_pairs={{0,4},{2,6},{4,0},{6,2},{8,12},{10,14},{12,8},{14,10},{16,20},{18,... | collective-permute-start | bytes 4915208 | tf_op jit(solution)/shard_map/ppermute | solution.py:189
  197.8 47.8 %collective-permute-start.25 = (bf16[128,2560]{1,0:T(8,128)(2,1)}, bf16[128,2560]{1,0:T(8,128)(2,1)S(1)}, u32[]{:S(2)}, u32[]{:S(2)}) collective-permute-start(bf16[128,2560]{1,0:T(8,128)(2,1)} %multiply_convert_fusion.5), channel_id=1, source_target_pairs={{0,16},{2,18},{4,20},{6,22},{8,24},{10,26},{12,28},{14,30},{16,0},... | collective-permute-start | bytes 1966088 | tf_op jit(solution)/shard_map/ppermute | solution.py:189
  200.3 49.9 %collective-permute-start.22 = (bf16[4,160,1280]{2,1,0:T(8,128)(2,1)S(1)}, bf16[4,160,1280]{2,1,0:T(8,128)(2,1)S(1)}, u32[]{:S(2)}, u32[]{:S(2)}) collective-permute-start(bf16[4,160,1280]{2,1,0:T(8,128)(2,1)S(1)} %copy-done.81), channel_id=1, source_target_pairs={{0,2},{2,0},{4,6},{6,4},{8,10},{10,8},{12,14},{14,12},{16,18},{18,... | collective-permute-start | bytes 4915208 | tf_op jit(solution)/shard_map/ppermute | solution.py:189
  245.6 30.2 %collective-permute-start.30 = (bf16[128,2560]{1,0:T(8,128)(2,1)}, bf16[128,2560]{1,0:T(8,128)(2,1)S(1)}, u32[]{:S(2)}, u32[]{:S(2)}) collective-permute-start(bf16[128,2560]{1,0:T(8,128)(2,1)} %collective-permute-done.5), channel_id=1, source_target_pairs={{0,16},{2,18},{4,20},{6,22},{8,24},{10,26},{12,28},{14,30},{16,0},... | collective-permute-start | bytes 1966088 | tf_op jit(solution)/shard_map/ppermute | solution.py:189
  279.4 39.9 %collective-permute-start.34 = (bf16[2,160,2688]{2,1,0:T(8,128)(2,1)S(1)}, bf16[2,160,2688]{2,1,0:T(8,128)(2,1)S(1)}, u32[]{:S(2)}, u32[]{:S(2)}) collective-permute-start(bf16[2,160,2688]{2,1,0:T(8,128)(2,1)S(1)} %pad_maximum_fusion.5), channel_id=1, source_target_pairs={{0,2},{2,0},{4,6},{6,4},{8,10},{10,8},{12,14},{14,12},{16,18},{18,... | collective-permute-start | bytes 5160968 | tf_op jit(solution)/shard_map/ppermute | solution.py:189
  283.0 30.5 %collective-permute-start.33 = (bf16[128,2560]{1,0:T(8,128)(2,1)S(1)}, bf16[128,2560]{1,0:T(8,128)(2,1)S(1)}, u32[]{:S(2)}, u32[]{:S(2)}) collective-permute-start(bf16[128,2560]{1,0:T(8,128)(2,1)S(1)} %multiply_convert_fusion.3.refs_0_), channel_id=1, source_target_pairs={{0,16},{2,18},{4,20},{6,22},{8,24},{10,26},{12,28},{14,30},{16,0},... | collective-permute-start | bytes 1966088 | tf_op jit(solution)/shard_map/ppermute | solution.py:189
  283.0 54.7 %collective-permute-start.36 = (bf16[2,160,2688]{2,1,0:T(8,128)(2,1)S(1)}, bf16[2,160,2688]{2,1,0:T(8,128)(2,1)S(1)}, u32[]{:S(2)}, u32[]{:S(2)}) collective-permute-start(bf16[2,160,2688]{2,1,0:T(8,128)(2,1)S(1)} %pad_maximum_fusion.5), channel_id=1, source_target_pairs={{0,8},{2,10},{4,12},{6,14},{8,0},{10,2},{12,4},{14,6},{16,24},{18,... | collective-permute-start | bytes 5160968 | tf_op jit(solution)/shard_map/ppermute | solution.py:189
  337.7 21.9 %collective-permute-start.37 = (bf16[512,2560]{1,0:T(8,128)(2,1)S(1)}, bf16[512,2560]{1,0:T(8,128)(2,1)S(1)}, u32[]{:S(2)}, u32[]{:S(2)}) collective-permute-start(bf16[512,2560]{1,0:T(8,128)(2,1)S(1)} %bitcast.430), channel_id=1, source_target_pairs={{0,1},{1,0},{2,3},{3,2},{4,5},{5,4},{6,7},{7,6},{8,9},{9,8},{10,11... | collective-permute-start | bytes 7864328 | tf_op jit(solution)/shard_map/ppermute | solution.py:77
  406.6 22.5 %collective-permute-start.42 = (bf16[128,2560]{1,0:T(8,128)(2,1)S(1)}, bf16[128,2560]{1,0:T(8,128)(2,1)S(1)}, u32[]{:S(2)}, u32[]{:S(2)}) collective-permute-start(bf16[128,2560]{1,0:T(8,128)(2,1)S(1)} %get-tuple-element.151), channel_id=1, source_target_pairs={{0,4},{2,6},{4,0},{6,2},{8,12},{10,14},{12,8},{14,10},{16,20},{18,... | collective-permute-start | bytes 1966088 | tf_op jit(solution)/shard_map/ppermute | solution.py:189
  430.1 31.5 %collective-permute-start.44 = (bf16[128,2560]{1,0:T(8,128)(2,1)S(1)}, bf16[128,2560]{1,0:T(8,128)(2,1)S(1)}, u32[]{:S(2)}, u32[]{:S(2)}) collective-permute-start(bf16[128,2560]{1,0:T(8,128)(2,1)S(1)} %fusion.66), channel_id=1, source_target_pairs={{0,16},{2,18},{4,20},{6,22},{8,24},{10,26},{12,28},{14,30},{16,0},... | collective-permute-start | bytes 1966088 | tf_op jit(solution)/shard_map/ppermute | solution.py:189
  432.3 30.1 %collective-permute-start.46 = (bf16[128,2560]{1,0:T(8,128)(2,1)}, bf16[128,2560]{1,0:T(8,128)(2,1)S(1)}, u32[]{:S(2)}, u32[]{:S(2)}) collective-permute-start(bf16[128,2560]{1,0:T(8,128)(2,1)} %get-tuple-element.157), channel_id=1, source_target_pairs={{0,4},{2,6},{4,0},{6,2},{8,12},{10,14},{12,8},{14,10},{16,20},{18,... | collective-permute-start | bytes 1966088 | tf_op jit(solution)/shard_map/ppermute | solution.py:189
  440.4 39.1 %collective-permute-start.48 = (bf16[2,160,2688]{2,1,0:T(8,128)(2,1)}, bf16[2,160,2688]{2,1,0:T(8,128)(2,1)}, u32[]{:S(2)}, u32[]{:S(2)}) collective-permute-start(bf16[2,160,2688]{2,1,0:T(8,128)(2,1)} %bitcast.90), channel_id=1, source_target_pairs={{0,2},{2,0},{4,6},{6,4},{8,10},{10,8},{12,14},{14,12},{16,18},{18,... | collective-permute-start | bytes 5160968 | tf_op jit(solution)/shard_map/ppermute | solution.py:189
  455.1 78.9 %collective-permute-start.43 = (bf16[512,2560]{1,0:T(8,128)(2,1)}, bf16[512,2560]{1,0:T(8,128)(2,1)}, u32[]{:S(2)}, u32[]{:S(2)}) collective-permute-start(bf16[512,2560]{1,0:T(8,128)(2,1)} %slice.985), channel_id=1, source_target_pairs={{0,1},{1,0},{2,3},{3,2},{4,5},{5,4},{6,7},{7,6},{8,9},{9,8},{10,11... | collective-permute-start | bytes 7864328 | tf_op jit(solution)/shard_map/ppermute | solution.py:77
  466.1 51.2 %collective-permute-start.45 = (bf16[2,160,2688]{2,1,0:T(8,128)(2,1)S(1)}, bf16[2,160,2688]{2,1,0:T(8,128)(2,1)S(1)}, u32[]{:S(2)}, u32[]{:S(2)}) collective-permute-start(bf16[2,160,2688]{2,1,0:T(8,128)(2,1)S(1)} %bitcast.466), channel_id=1, source_target_pairs={{0,8},{2,10},{4,12},{6,14},{8,0},{10,2},{12,4},{14,6},{16,24},{18,... | collective-permute-start | bytes 5160968 | tf_op jit(solution)/shard_map/ppermute | solution.py:189
  490.5 23.7 %collective-permute-start.49 = (bf16[2,160,1280]{2,1,0:T(8,128)(2,1)S(1)}, bf16[2,160,1280]{2,1,0:T(8,128)(2,1)S(1)}, u32[]{:S(2)}, u32[]{:S(2)}) collective-permute-start(bf16[2,160,1280]{2,1,0:T(8,128)(2,1)S(1)} %pad_maximum_fusion.18), channel_id=1, source_target_pairs={{0,2},{2,0},{4,6},{6,4},{8,10},{10,8},{12,14},{14,12},{16,18},{18,... | collective-permute-start | bytes 2457608 | tf_op jit(solution)/shard_map/ppermute | solution.py:189
  491.6 24.1 %collective-permute-start.50 = (bf16[2,160,1280]{2,1,0:T(8,128)(2,1)S(1)}, bf16[2,160,1280]{2,1,0:T(8,128)(2,1)S(1)}, u32[]{:S(2)}, u32[]{:S(2)}) collective-permute-start(bf16[2,160,1280]{2,1,0:T(8,128)(2,1)S(1)} %pad_maximum_fusion.19), channel_id=1, source_target_pairs={{0,4},{2,6},{4,0},{6,2},{8,12},{10,14},{12,8},{14,10},{16,20},{18,... | collective-permute-start | bytes 2457608 | tf_op jit(solution)/shard_map/ppermute | solution.py:189
  517.2 84.1 %collective-permute-start.58 = (bf16[4,160,2688]{2,1,0:T(8,128)(2,1)}, bf16[4,160,2688]{2,1,0:T(8,128)(2,1)}, u32[]{:S(2)}, u32[]{:S(2)}) collective-permute-start(bf16[4,160,2688]{2,1,0:T(8,128)(2,1)} %pad_maximum_fusion.2), channel_id=1, source_target_pairs={{0,8},{2,10},{4,12},{6,14},{8,0},{10,2},{12,4},{14,6},{16,24},{18,... | collective-permute-start | bytes 10321928 | tf_op jit(solution)/shard_map/ppermute | solution.py:189
  524.4 77.2 %collective-permute-start.54 = (bf16[4,160,2688]{2,1,0:T(8,128)(2,1)}, bf16[4,160,2688]{2,1,0:T(8,128)(2,1)}, u32[]{:S(2)}, u32[]{:S(2)}) collective-permute-start(bf16[4,160,2688]{2,1,0:T(8,128)(2,1)} %pad_maximum_fusion.1), channel_id=1, source_target_pairs={{0,2},{2,0},{4,6},{6,4},{8,10},{10,8},{12,14},{14,12},{16,18},{18,... | collective-permute-start | bytes 10321928 | tf_op jit(solution)/shard_map/ppermute | solution.py:189
  525.5 38.2 %collective-permute-start.51 = (bf16[4,160,1280]{2,1,0:T(8,128)(2,1)}, bf16[4,160,1280]{2,1,0:T(8,128)(2,1)}, u32[]{:S(2)}, u32[]{:S(2)}) collective-permute-start(bf16[4,160,1280]{2,1,0:T(8,128)(2,1)} %pad_maximum_fusion.10), channel_id=1, source_target_pairs={{0,4},{2,6},{4,0},{6,2},{8,12},{10,14},{12,8},{14,10},{16,20},{18,... | collective-permute-start | bytes 4915208 | tf_op jit(solution)/shard_map/ppermute | solution.py:189
  580.6 30.2 %collective-permute-start.53 = (bf16[128,2560]{1,0:T(8,128)(2,1)S(1)}, bf16[128,2560]{1,0:T(8,128)(2,1)S(1)}, u32[]{:S(2)}, u32[]{:S(2)}) collective-permute-start(bf16[128,2560]{1,0:T(8,128)(2,1)S(1)} %fusion.67), channel_id=1, source_target_pairs={{0,16},{2,18},{4,20},{6,22},{8,24},{10,26},{12,28},{14,30},{16,0},... | collective-permute-start | bytes 1966088 | tf_op jit(solution)/shard_map/ppermute | solution.py:189
  581.5 31.6 %collective-permute-start.55 = (bf16[128,2560]{1,0:T(8,128)(2,1)S(1)}, bf16[128,2560]{1,0:T(8,128)(2,1)S(1)}, u32[]{:S(2)}, u32[]{:S(2)}) collective-permute-start(bf16[128,2560]{1,0:T(8,128)(2,1)S(1)} %copy-done.104), channel_id=1, source_target_pairs={{0,4},{2,6},{4,0},{6,2},{8,12},{10,14},{12,8},{14,10},{16,20},{18,... | collective-permute-start | bytes 1966088 | tf_op jit(solution)/shard_map/ppermute | solution.py:189
  607.0 37.7 %collective-permute-start.61 = (bf16[4,160,1280]{2,1,0:T(8,128)(2,1)}, bf16[4,160,1280]{2,1,0:T(8,128)(2,1)}, u32[]{:S(2)}, u32[]{:S(2)}) collective-permute-start(bf16[4,160,1280]{2,1,0:T(8,128)(2,1)} %pad_maximum_fusion.11), channel_id=1, source_target_pairs={{0,2},{2,0},{4,6},{6,4},{8,10},{10,8},{12,14},{14,12},{16,18},{18,... | collective-permute-start | bytes 4915208 | tf_op jit(solution)/shard_map/ppermute | solution.py:189
  614.0 39.1 %collective-permute-start.74 = (bf16[160,2688]{1,0:T(8,128)(2,1)}, bf16[160,2688]{1,0:T(8,128)(2,1)}, u32[]{:S(2)}, u32[]{:S(2)}) collective-permute-start(bf16[160,2688]{1,0:T(8,128)(2,1)} %get-tuple-element.191), channel_id=1, source_target_pairs={{0,16},{2,18},{4,20},{6,22},{8,24},{10,26},{12,28},{14,30},{16,0},... | collective-permute-start | bytes 2580488 | tf_op jit(solution)/shard_map/ppermute | solution.py:189
  614.1 37.5 %collective-permute-start.59 = (bf16[2,160,2688]{2,1,0:T(8,128)(2,1)}, bf16[2,160,2688]{2,1,0:T(8,128)(2,1)}, u32[]{:S(2)}, u32[]{:S(2)}) collective-permute-start(bf16[2,160,2688]{2,1,0:T(8,128)(2,1)} %pad_maximum_fusion.6), channel_id=1, source_target_pairs={{0,4},{2,6},{4,0},{6,2},{8,12},{10,14},{12,8},{14,10},{16,20},{18,... | collective-permute-start | bytes 5160968 | tf_op jit(solution)/shard_map/ppermute | solution.py:189
  620.6 73.7 %collective-permute-start.57 = (bf16[16,80,1152]{2,1,0:T(8,128)(2,1)}, bf16[16,80,1152]{2,1,0:T(8,128)(2,1)}, u32[]{:S(2)}, u32[]{:S(2)}) collective-permute-start(bf16[16,80,1152]{2,1,0:T(8,128)(2,1)} %fusion.32), channel_id=1, source_target_pairs={{0,1},{1,0},{2,3},{3,2},{4,5},{5,4},{6,7},{7,6},{8,9},{9,8},{10,11... | collective-permute-start | bytes 8847368 | tf_op jit(solution)/shard_map/ppermute | solution.py:77
  653.1 38.7 %collective-permute-start.75 = (bf16[160,2688]{1,0:T(8,128)(2,1)S(1)}, bf16[160,2688]{1,0:T(8,128)(2,1)S(1)}, u32[]{:S(2)}, u32[]{:S(2)}) collective-permute-start(bf16[160,2688]{1,0:T(8,128)(2,1)S(1)} %get-tuple-element.192), channel_id=1, source_target_pairs={{0,16},{2,18},{4,20},{6,22},{8,24},{10,26},{12,28},{14,30},{16,0},... | collective-permute-start | bytes 2580488 | tf_op jit(solution)/shard_map/ppermute | solution.py:189
  664.6 43.5 %collective-permute-start.72 = (bf16[160,1280]{1,0:T(8,128)(2,1)}, bf16[160,1280]{1,0:T(8,128)(2,1)}, u32[]{:S(2)}, u32[]{:S(2)}) collective-permute-start(bf16[160,1280]{1,0:T(8,128)(2,1)} %get-tuple-element.189), channel_id=1, source_target_pairs={{0,8},{2,10},{4,12},{6,14},{8,0},{10,2},{12,4},{14,6},{16,24},{18,... | collective-permute-start | bytes 1228808 | tf_op jit(solution)/shard_map/ppermute | solution.py:189
  669.9 35.0 %collective-permute-start.63 = (bf16[4,64,2560]{2,1,0:T(8,128)(2,1)}, bf16[4,64,2560]{2,1,0:T(8,128)(2,1)}, u32[]{:S(2)}, u32[]{:S(2)}) collective-permute-start(bf16[4,64,2560]{2,1,0:T(8,128)(2,1)} %pad_maximum_fusion.14), channel_id=1, source_target_pairs={{0,2},{2,0},{4,6},{6,4},{8,10},{10,8},{12,14},{14,12},{16,18},{18,... | collective-permute-start | bytes 3932168 | tf_op jit(solution)/shard_map/ppermute | solution.py:189
  671.0 34.0 %collective-permute-start.64 = (bf16[4,64,2560]{2,1,0:T(8,128)(2,1)}, bf16[4,64,2560]{2,1,0:T(8,128)(2,1)}, u32[]{:S(2)}, u32[]{:S(2)}) collective-permute-start(bf16[4,64,2560]{2,1,0:T(8,128)(2,1)} %pad_maximum_fusion.15), channel_id=1, source_target_pairs={{0,4},{2,6},{4,0},{6,2},{8,12},{10,14},{12,8},{14,10},{16,20},{18,... | collective-permute-start | bytes 3932168 | tf_op jit(solution)/shard_map/ppermute | solution.py:189
  713.2 30.3 %collective-permute-start.65 = (bf16[4,80,1152]{2,1,0:T(8,128)(2,1)}, bf16[4,80,1152]{2,1,0:T(8,128)(2,1)}, u32[]{:S(2)}, u32[]{:S(2)}) collective-permute-start(bf16[4,80,1152]{2,1,0:T(8,128)(2,1)} %pad_maximum_fusion.21), channel_id=1, source_target_pairs={{0,2},{2,0},{4,6},{6,4},{8,10},{10,8},{12,14},{14,12},{16,18},{18,... | collective-permute-start | bytes 2211848 | tf_op jit(solution)/shard_map/ppermute | solution.py:189
  714.3 34.1 %collective-permute-start.66 = (bf16[4,80,1152]{2,1,0:T(8,128)(2,1)}, bf16[4,80,1152]{2,1,0:T(8,128)(2,1)}, u32[]{:S(2)}, u32[]{:S(2)}) collective-permute-start(bf16[4,80,1152]{2,1,0:T(8,128)(2,1)} %pad_maximum_fusion.22), channel_id=1, source_target_pairs={{0,4},{2,6},{4,0},{6,2},{8,12},{10,14},{12,8},{14,10},{16,20},{18,... | collective-permute-start | bytes 2211848 | tf_op jit(solution)/shard_map/ppermute | solution.py:189
  714.8 33.6 %collective-permute-start.67 = (bf16[4,80,1152]{2,1,0:T(8,128)(2,1)}, bf16[4,80,1152]{2,1,0:T(8,128)(2,1)}, u32[]{:S(2)}, u32[]{:S(2)}) collective-permute-start(bf16[4,80,1152]{2,1,0:T(8,128)(2,1)} %pad_maximum_fusion.23), channel_id=1, source_target_pairs={{0,6},{2,4},{4,2},{6,0},{8,14},{10,12},{12,10},{14,8},{16,22},{18,... | collective-permute-start | bytes 2211848 | tf_op jit(solution)/shard_map/ppermute | solution.py:189
  718.6 35.9 %collective-permute-start.77 = (bf16[64,2560]{1,0:T(8,128)(2,1)}, bf16[64,2560]{1,0:T(8,128)(2,1)}, u32[]{:S(2)}, u32[]{:S(2)}) collective-permute-start(bf16[64,2560]{1,0:T(8,128)(2,1)} %fusion.95), channel_id=1, source_target_pairs={{0,16},{2,18},{4,20},{6,22},{8,24},{10,26},{12,28},{14,30},{16,0},... | collective-permute-start | bytes 983048 | tf_op jit(solution)/shard_map/ppermute | solution.py:189
  719.0 35.5 %collective-permute-start.78 = (bf16[64,2560]{1,0:T(8,128)(2,1)}, bf16[64,2560]{1,0:T(8,128)(2,1)}, u32[]{:S(2)}, u32[]{:S(2)}) collective-permute-start(bf16[64,2560]{1,0:T(8,128)(2,1)} %get-tuple-element.195), channel_id=1, source_target_pairs={{0,8},{2,10},{4,12},{6,14},{8,0},{10,2},{12,4},{14,6},{16,24},{18,... | collective-permute-start | bytes 983048 | tf_op jit(solution)/shard_map/ppermute | solution.py:189
  (174 other events, 2262.1 us)

commit v6 on v5

--- a/solution.py
+++ b/solution.py
@@ -565,17 +565,17 @@
     out_ref[:, 2 * share :] = low(trans_mul(back, act_ref[...]))
 
 
-def unit_grads(tokens, back, act, d_units, share):
+def unit_grads(tokens, back, act, d_units, share, first, count):
     rows, width = tokens[0].shape
     chunk = width // CHUNKS
-    part = pl.BlockSpec((rows, chunk), lambda step: (0, step))
+    part = pl.BlockSpec((rows, chunk), lambda step: (0, first + step))
     return pl.pallas_call(
         partial(unit_grads_kernel, share),
-        grid=(CHUNKS,),
+        grid=(count,),
         in_specs=[part] * 4
         + [pl.BlockSpec(act.shape, lambda step: (0, 0)), pl.BlockSpec(d_units.shape, lambda step: (0, 0))],
         out_specs=pl.BlockSpec((chunk, 3 * share), lambda step: (step, 0)),
-        out_shape=jax.ShapeDtypeStruct((width, 3 * share), jnp.bfloat16),
+        out_shape=jax.ShapeDtypeStruct((count * chunk, 3 * share), jnp.bfloat16),
         compiler_params=pltpu.CompilerParams(vmem_limit_bytes=56 * 2**20),
         name="unit_grads",
     )(*tokens, *back, act, d_units)
@@ -943,11 +943,21 @@
     d_mlp_flow = links.flow("D", return_tokens(d_mlp_terms[:chip_rows], d_mlp_other, own_rows))
     d_mlp_flow.step().step().step()
     d_mlp_own = d_mlp_flow.end()
-    unit_grad = unit_grads(
-        mlp_seq, mlp_back, tied(act_low, [d_mlp_other]), d_units, share
-    ).reshape(len(masks_of(others)), GROUP, -1, 3 * share)
+    other_masks = masks_of(others)
+
+    def some_grads(act, first, count):
+        grads = unit_grads(mlp_seq, mlp_back, act, d_units, share, first, count)
+        return grads.reshape(count * len(other_masks) // CHUNKS, GROUP, -1, 3 * share)
+
+    late_grads = some_grads(tied(act_low, [d_mlp_other]), CHUNKS // 2, CHUNKS // 2)
+    early_grads = some_grads(tied(act_low, links.named(["D0"])), 0, CHUNKS // 2)
+
+    def unit_block(mask):
+        at = other_masks.index(mask)
+        return early_grads[at] if at < early_grads.shape[0] else late_grads[at - early_grads.shape[0]]
+
     unit_flow = links.flow(
-        "R", reduce_bits(lambda mask: unit_grad[masks_of(others).index(mask)], others, "both")
+        "R", reduce_bits(unit_block, others, "both")
     )
     unit_flow.step(["D1", "D2"]).step()
     mlp_terms = units_out(tied(act_low, links.named(["D0"])), unit_pieces, share)

time: 781 us -> 778 us (level)
  waiting for transfers between devices: 328 us -> 310 us
  Pallas kernels: 97.5 us -> 106 us
    ppermute x69, waiting for transfers between devices: 323 us -> 306 us  [send(): lax.ppermute(item, 'dp', [(place, place ^ to) for place in range(count)])]
    pallas_call x1 -> x2, Pallas kernels: 21.1 us -> 26.8 us  [unit_grads(): pl.pallas_call(partial(unit_grads_kernel, share), grid=(count,), in_specs...]
    unnamed x329 -> x331, local copies, waits for them, and re-layouts: 30 us -> 26.3 us
  transfers between devices with their start and end apart: 79 -> 79, of which waited for: 40 -> 37; matrix products, arithmetic and copies ran while one was open for 31% -> 32% of each run, Pallas kernels for 8% -> 9%
where the time goes in v6:
time: 778 us; the launch traced here: 771 us
  waiting for transfers between devices  310 us (40%)
  Pallas kernels  106 us (14%)
  local copies, waits for them, and re-layouts  98.4 us (13%)
  other arithmetic  92.8 us (12%)
  starting transfers between devices  83.7 us (11%)
  matrix products  75.6 us (10%)
    ppermute x69, waiting for transfers between devices, send(): lax.ppermute(item, 'dp', [(place, place ^ to) for place in range(count)])  306 us
    ppermute x69, starting transfers between devices, send(): lax.ppermute(item, 'dp', [(place, place ^ to) for place in range(count)])  83.2 us
    dot_general x9, matrix products, plain_mul(): return jnp.dot(left, right, preferred_element_type=jnp.float32)  36.7 us
    pallas_call x1, Pallas kernels, run_units(): pl.pallas_call(partial(units_kernel, share, len(pieces)), grid=(steps,),...  36 us
    pallas_call x2, Pallas kernels, unit_grads(): pl.pallas_call(partial(unit_grads_kernel, share), grid=(count,), in_specs...  26.8 us
    unnamed x331, local copies, waits for them, and re-layouts  26.3 us
    dot_general x8, matrix products, mul_trans(): lax.dot_general(left, right, (((1,), (1,)), ((), ())), preferred_element_...  25.6 us
    another operation x10, other arithmetic  24.1 us
  transfers between devices with their start and end apart: 79, of which 37 were waited for; matrix products, arithmetic and copies ran while one was open for 32% of the time, Pallas kernels for 9%

profile of v6, /device:TPU:0, one launch (start us, length us, event | category | flops | bytes accessed | tf_op | source)
XLA Modules:
  0.0 770.5 jit_solution(13344105124755031654)
XLA Ops:
  4.1 5.1 collective-permute-start.2
  16.4 4.0 constant_dynamic-update-slice_fusion.8
  31.1 11.4 %collective-permute-done.3 = bf16[64,2560]{1,0:T(8,128)(2,1)S(1)} collective-permute-done((bf16[64,2560]{1,0:T(8,128)(2,1)S(1)}, bf16[64,2560]{1,0:T(8,128)(2,1)S(1)}, u32[]{:S(2)}, u32[]{:S(2)}) %collective-permute-start.3) | collective-permute-done | bytes 327712 | tf_op jit(solution)/shard_map/ppermute | solution.py:189
  58.3 11.8 %collective-permute-done.6 = bf16[4,80,1152]{2,1,0:T(8,128)(2,1)S(1)} collective-permute-done((bf16[4,80,1152]{2,1,0:T(8,128)(2,1)S(1)}, bf16[4,80,1152]{2,1,0:T(8,128)(2,1)S(1)}, u32[]{:S(2)}, u32[]{:S(2)}) %collective-permute-start.6) | collective-permute-done | bytes 737312 | tf_op jit(solution)/shard_map/ppermute | solution.py:189
  73.2 14.9 %collective-permute-done.8 = bf16[4,80,1152]{2,1,0:T(8,128)(2,1)S(1)} collective-permute-done((bf16[4,80,1152]{2,1,0:T(8,128)(2,1)S(1)}, bf16[4,80,1152]{2,1,0:T(8,128)(2,1)S(1)}, u32[]{:S(2)}, u32[]{:S(2)}) %collective-permute-start.8) | collective-permute-done | bytes 737312 | tf_op jit(solution)/shard_map/ppermute | solution.py:189
  93.4 5.0 fusion.3
  99.4 5.4 collective-permute-done.14
  107.4 15.3 %collective-permute-done.17 = bf16[4,64,2560]{2,1,0:T(8,128)(2,1)S(1)} collective-permute-done((bf16[4,64,2560]{2,1,0:T(8,128)(2,1)}, bf16[4,64,2560]{2,1,0:T(8,128)(2,1)S(1)}, u32[]{:S(2)}, u32[]{:S(2)}) %collective-permute-start.17) | collective-permute-done | bytes 1310752 | tf_op jit(solution)/shard_map/ppermute | solution.py:189
  123.6 5.1 collective-permute-done.15
  130.2 8.4 %collective-permute-done.23 = bf16[160,2688]{1,0:T(8,128)(2,1)S(1)} collective-permute-done((bf16[160,2688]{1,0:T(8,128)(2,1)S(1)}, bf16[160,2688]{1,0:T(8,128)(2,1)S(1)}, u32[]{:S(2)}, u32[]{:S(2)}) %collective-permute-start.23) | collective-permute-done | bytes 860192 | tf_op jit(solution)/shard_map/ppermute | solution.py:189
  148.5 3.9 fusion.276
  169.7 7.6 collective-permute-done.18
  178.7 17.4 %collective-permute-done.26 = bf16[2,160,2688]{2,1,0:T(8,128)(2,1)} collective-permute-done((bf16[2,160,2688]{2,1,0:T(8,128)(2,1)S(1)}, bf16[2,160,2688]{2,1,0:T(8,128)(2,1)}, u32[]{:S(2)}, u32[]{:S(2)}) %collective-permute-start.26) | collective-permute-done | bytes 1720352 | tf_op jit(solution)/shard_map/ppermute | solution.py:189
  213.1 4.2 convolution_convert_fusion.kv_ref
  217.3 4.5 fusion.277.q_ref
  221.9 10.5 %attend.1 = (bf16[256,1280]{1,0:T(8,128)(2,1)S(1)}, bf16[256,2560]{1,0:T(8,128)(2,1)S(1)}) custom-call(f32[256,2560]{1,0:T(8,128)S(1)} %fusion.277.q_ref, bf16[256,2560]{1,0:T(8,128)(2,1)S(1)} %convolution_convert_fusion.kv_ref, bf16[256,128]{1,0:T(8,128)(2,1)S(1)} %slice.962.rot_ref, f32[256,256]{1,0:T(8,128)S(1)} %copy-done.22, f32[256,128]{1,0:T(8,128)S(1)} %copy-done.30, ...), custom_call_target="tpu_custom_call" | custom-call | tf_op jit(solution)/shard_map/attend/pallas_call | solution.py:727
  232.4 13.3 %collective-permute-done.25 = bf16[128,2560]{1,0:T(8,128)(2,1)S(1)} collective-permute-done((bf16[128,2560]{1,0:T(8,128)(2,1)}, bf16[128,2560]{1,0:T(8,128)(2,1)S(1)}, u32[]{:S(2)}, u32[]{:S(2)}) %collective-permute-start.25) | collective-permute-done | bytes 655392 | tf_op jit(solution)/shard_map/ppermute | solution.py:189
  253.0 14.3 %collective-permute-done.28 = bf16[2,160,1280]{2,1,0:T(8,128)(2,1)S(1)} collective-permute-done((bf16[2,160,1280]{2,1,0:T(8,128)(2,1)S(1)}, bf16[2,160,1280]{2,1,0:T(8,128)(2,1)S(1)}, u32[]{:S(2)}, u32[]{:S(2)}) %collective-permute-start.28) | collective-permute-done | bytes 819232 | tf_op jit(solution)/shard_map/ppermute | solution.py:189
  268.4 7.5 collective-permute-done.30
  285.3 13.0 %collective-permute-done.32.refs_1_ = bf16[128,2560]{1,0:T(8,128)(2,1)S(1)} collective-permute-done((bf16[128,2560]{1,0:T(8,128)(2,1)S(1)}, bf16[128,2560]{1,0:T(8,128)(2,1)S(1)}, u32[]{:S(2)}, u32[]{:S(2)}) %collective-permute-start.32) | collective-permute-done | bytes 655392 | tf_op jit(solution)/shard_map/ppermute | solution.py:189
  298.3 15.3 %collective-permute-done.33.refs_2_ = bf16[128,2560]{1,0:T(8,128)(2,1)S(1)} collective-permute-done((bf16[128,2560]{1,0:T(8,128)(2,1)S(1)}, bf16[128,2560]{1,0:T(8,128)(2,1)S(1)}, u32[]{:S(2)}, u32[]{:S(2)}) %collective-permute-start.33) | collective-permute-done | bytes 655392 | tf_op jit(solution)/shard_map/ppermute | solution.py:189
  313.5 5.8 collective-permute-done.34
  320.8 9.0 %fusion.20.own_back_ref = bf16[512,2560]{1,0:T(8,128)(2,1)S(1)} fusion(s32[2560]{0:T(1024)S(1)} %fusion.188, bf16[128,2560]{1,0:T(8,128)(2,1)S(1)} %collective-permute-done.30, bf16[128,2560]{1,0:T(8,128)(2,1)S(1)} %collective-permute-done.25, bf16[128,2560]{1,0:T(8,128)(2,1)} %collective-permute-done.5, bf16[128,2560]{1,0:T(8,128)(2,1)} %multiply_convert_fusion.5), kind=kOutput, calls=%fused_computation.35 | convolution fusion | flops 6729236480 | bytes 5253120 | tf_op jit(solution)/shard_map/dot_general | solution.py:53
  329.9 5.6 collective-permute-done.35.refs_3_
  339.6 20.1 %collective-permute-done.39 = bf16[1,160,2688]{2,1,0:T(8,128)(2,1)S(1)} collective-permute-done((bf16[1,160,2688]{2,1,0:T(8,128)(2,1)S(1)}, bf16[1,160,2688]{2,1,0:T(8,128)(2,1)S(1)}, u32[]{:S(2)}, u32[]{:S(2)}) %collective-permute-start.39) | collective-permute-done | bytes 860192 | tf_op jit(solution)/shard_map/ppermute | solution.py:189
  361.7 36.0 %run_units.1 = (bf16[1024,896]{1,0:T(8,128)(2,1)}, bf16[1024,1792]{1,0:T(8,128)(2,1)}, bf16[1024,2560]{1,0:T(8,128)(2,1)}) custom-call(bf16[512,2560]{1,0:T(8,128)(2,1)} %bitcast.431, bf16[512,2560]{1,0:T(8,128)(2,1)} %copy-done.41, bf16[512,2560]{1,0:T(8,128)(2,1)} %copy-done.39, bf16[512,2560]{1,0:T(8,128)(2,1)} %copy-done.40, ...), custom_call_target="tpu_custom_call" | custom-call | tf_op jit(solution)/shard_map/run_units/pallas_call | solution.py:546
  408.2 13.4 %unit_grads.2 = bf16[1280,2688]{1,0:T(8,128)(2,1)} custom-call(bf16[512,2560]{1,0:T(8,128)(2,1)} %bitcast.432, bf16[512,2560]{1,0:T(8,128)(2,1)} %copy-done.41, bf16[512,2560]{1,0:T(8,128)(2,1)} %copy-done.39, bf16[512,2560]{1,0:T(8,128)(2,1)} %copy-done.40, bf16[1024,896]{1,0:T(8,128)(2,1)} %get-tuple-element.153.act_ref, ...), custom_call_target="tpu_custom_call" | custom-call | tf_op jit(solution)/shard_map/unit_grads/pallas_call | solution.py:572
  421.6 5.9 fusion.266
  433.3 13.5 %unit_grads.3 = bf16[1280,2688]{1,0:T(8,128)(2,1)} custom-call(bf16[512,2560]{1,0:T(8,128)(2,1)} %bitcast.433, bf16[512,2560]{1,0:T(8,128)(2,1)} %copy-done.41, bf16[512,2560]{1,0:T(8,128)(2,1)} %copy-done.39, bf16[512,2560]{1,0:T(8,128)(2,1)} %copy-done.40, bf16[1024,896]{1,0:T(8,128)(2,1)} %get-tuple-element.153.act_ref, ...), custom_call_target="tpu_custom_call" | custom-call | tf_op jit(solution)/shard_map/unit_grads/pallas_call | solution.py:572
  451.1 7.8 %units_out.1 = bf16[1024,2560]{1,0:T(8,128)(2,1)S(1)} custom-call(bf16[1024,896]{1,0:T(8,128)(2,1)S(1)} %copy-done.3, bf16[320,2688]{1,0:T(8,128)(2,1)S(1)} %bitcast.435, bf16[320,2688]{1,0:T(8,128)(2,1)S(1)} %bitcast.437, bf16[320,2688]{1,0:T(8,128)(2,1)S(1)} %bitcast.443, bf16[320,2688]{1,0:T(8,128)(2,1)S(1)} %bitcast.439, ...), custom_call_target="tpu_custom_call" | custom-call | tf_op jit(solution)/shard_map/units_out/pallas_call | solution.py:489
  475.5 6.6 fusion.274
  484.5 5.1 slice_bitcast_fusion.14
  491.5 14.0 %attend_back.1 = (bf16[256,2560]{1,0:T(8,128)(2,1)S(1)}, bf16[256,2560]{1,0:T(8,128)(2,1)S(1)}, f32[256,128]{1,0:T(8,128)S(1)}) custom-call(bf16[256,2560]{1,0:T(8,128)(2,1)S(1)} %copy-done.25, bf16[256,2560]{1,0:T(8,128)(2,1)S(1)} %copy-done.17, bf16[256,128]{1,0:T(8,128)(2,1)S(1)} %slice.962.rot_ref, f32[256,256]{1,0:T(8,128)S(1)} %copy-done.23, ...), custom_call_target="tpu_custom_call" | custom-call | tf_op jit(solution)/shard_map/attend_back/pallas_call | solution.py:744
  527.5 5.0 fusion.255
  537.8 4.9 multiply_reduce_fusion
  547.7 5.3 fusion
  558.7 13.5 %collective-permute-done.52.refs_0_ = bf16[128,2560]{1,0:T(8,128)(2,1)S(1)} collective-permute-done((bf16[128,2560]{1,0:T(8,128)(2,1)S(1)}, bf16[128,2560]{1,0:T(8,128)(2,1)S(1)}, u32[]{:S(2)}, u32[]{:S(2)}) %collective-permute-start.52) | collective-permute-done | bytes 655392 | tf_op jit(solution)/shard_map/ppermute | solution.py:189
  576.8 23.2 %collective-permute-done.58 = bf16[4,160,2688]{2,1,0:T(8,128)(2,1)} collective-permute-done((bf16[4,160,2688]{2,1,0:T(8,128)(2,1)}, bf16[4,160,2688]{2,1,0:T(8,128)(2,1)}, u32[]{:S(2)}, u32[]{:S(2)}) %collective-permute-start.58) | collective-permute-done | bytes 3440672 | tf_op jit(solution)/shard_map/ppermute | solution.py:189
  600.0 4.3 fusion.13
  610.3 3.8 fusion.40
  616.4 6.7 fusion.24
  623.1 19.0 %collective-permute-done.61 = bf16[4,160,1280]{2,1,0:T(8,128)(2,1)} collective-permute-done((bf16[4,160,1280]{2,1,0:T(8,128)(2,1)}, bf16[4,160,1280]{2,1,0:T(8,128)(2,1)}, u32[]{:S(2)}, u32[]{:S(2)}) %collective-permute-start.61) | collective-permute-done | bytes 1638432 | tf_op jit(solution)/shard_map/ppermute | solution.py:189
  654.0 6.4 collective-permute-done.71
  669.4 18.5 %collective-permute-done.75 = bf16[160,2688]{1,0:T(8,128)(2,1)S(1)} collective-permute-done((bf16[160,2688]{1,0:T(8,128)(2,1)S(1)}, bf16[160,2688]{1,0:T(8,128)(2,1)S(1)}, u32[]{:S(2)}, u32[]{:S(2)}) %collective-permute-start.75) | collective-permute-done | bytes 860192 | tf_op jit(solution)/shard_map/ppermute | solution.py:189
  690.4 6.6 fusion.261
  725.9 4.6 copy.75
  740.1 5.2 collective-permute-done.66
  759.2 7.3 collective-permute-done.69
  (653 shorter events, 291.6 us)
Async XLA Ops:
  12.0 39.5 %collective-permute-start.5 = (bf16[128,2560]{1,0:T(8,128)(2,1)}, bf16[128,2560]{1,0:T(8,128)(2,1)}, u32[]{:S(2)}, u32[]{:S(2)}) collective-permute-start(bf16[128,2560]{1,0:T(8,128)(2,1)} %multiply_convert_fusion.5), channel_id=1, source_target_pairs={{0,4},{2,6},{4,0},{6,2},{8,12},{10,14},{12,8},{14,10},{16,20},{18,... | collective-permute-start | bytes 1966088 | tf_op jit(solution)/shard_map/ppermute | solution.py:189
  43.7 44.9 %collective-permute-start.12 = (bf16[160,1280]{1,0:T(8,128)(2,1)}, bf16[160,1280]{1,0:T(8,128)(2,1)}, u32[]{:S(2)}, u32[]{:S(2)}) collective-permute-start(bf16[160,1280]{1,0:T(8,128)(2,1)} %bitcast.31), channel_id=1, source_target_pairs={{0,16},{2,18},{4,20},{6,22},{8,24},{10,26},{12,28},{14,30},{16,0},... | collective-permute-start | bytes 1228808 | tf_op jit(solution)/shard_map/ppermute | solution.py:189
  55.2 32.8 %collective-permute-start.8 = (bf16[4,80,1152]{2,1,0:T(8,128)(2,1)S(1)}, bf16[4,80,1152]{2,1,0:T(8,128)(2,1)S(1)}, u32[]{:S(2)}, u32[]{:S(2)}) collective-permute-start(bf16[4,80,1152]{2,1,0:T(8,128)(2,1)S(1)} %copy-done.97), channel_id=1, source_target_pairs={{0,6},{2,4},{4,2},{6,0},{8,14},{10,12},{12,10},{14,8},{16,22},{18,... | collective-permute-start | bytes 2211848 | tf_op jit(solution)/shard_map/ppermute | solution.py:189
  58.3 30.4 %collective-permute-start.13 = (bf16[160,1280]{1,0:T(8,128)(2,1)}, bf16[160,1280]{1,0:T(8,128)(2,1)S(1)}, u32[]{:S(2)}, u32[]{:S(2)}) collective-permute-start(bf16[160,1280]{1,0:T(8,128)(2,1)} %bitcast.31), channel_id=1, source_target_pairs={{0,8},{2,10},{4,12},{6,14},{8,0},{10,2},{12,4},{14,6},{16,24},{18,... | collective-permute-start | bytes 1228808 | tf_op jit(solution)/shard_map/ppermute | solution.py:189
  88.4 53.1 %collective-permute-start.9 = (bf16[16,80,1152]{2,1,0:T(8,128)(2,1)S(1)}, bf16[16,80,1152]{2,1,0:T(8,128)(2,1)S(1)}, u32[]{:S(2)}, u32[]{:S(2)}) collective-permute-start(bf16[16,80,1152]{2,1,0:T(8,128)(2,1)S(1)} %bitcast.463), channel_id=1, source_target_pairs={{0,1},{1,0},{2,3},{3,2},{4,5},{5,4},{6,7},{7,6},{8,9},{9,8},{10,11... | collective-permute-start | bytes 8847368 | tf_op jit(solution)/shard_map/ppermute | solution.py:77
  88.7 40.0 %collective-permute-start.15 = (bf16[2,160,2688]{2,1,0:T(8,128)(2,1)S(1)}, bf16[2,160,2688]{2,1,0:T(8,128)(2,1)S(1)}, u32[]{:S(2)}, u32[]{:S(2)}) collective-permute-start(bf16[2,160,2688]{2,1,0:T(8,128)(2,1)S(1)} %pad_maximum_fusion.3), channel_id=1, source_target_pairs={{0,4},{2,6},{4,0},{6,2},{8,12},{10,14},{12,8},{14,10},{16,20},{18,... | collective-permute-start | bytes 5160968 | tf_op jit(solution)/shard_map/ppermute | solution.py:189
  91.9 30.8 %collective-permute-start.17 = (bf16[4,64,2560]{2,1,0:T(8,128)(2,1)}, bf16[4,64,2560]{2,1,0:T(8,128)(2,1)S(1)}, u32[]{:S(2)}, u32[]{:S(2)}) collective-permute-start(bf16[4,64,2560]{2,1,0:T(8,128)(2,1)} %pad_maximum_fusion.12), channel_id=1, source_target_pairs={{0,2},{2,0},{4,6},{6,4},{8,10},{10,8},{12,14},{14,12},{16,18},{18,... | collective-permute-start | bytes 3932168 | tf_op jit(solution)/shard_map/ppermute | solution.py:189
  98.6 40.1 %collective-permute-start.23 = (bf16[160,2688]{1,0:T(8,128)(2,1)S(1)}, bf16[160,2688]{1,0:T(8,128)(2,1)S(1)}, u32[]{:S(2)}, u32[]{:S(2)}) collective-permute-start(bf16[160,2688]{1,0:T(8,128)(2,1)S(1)} %get-tuple-element.132), channel_id=1, source_target_pairs={{0,16},{2,18},{4,20},{6,22},{8,24},{10,26},{12,28},{14,30},{16,0},... | collective-permute-start | bytes 2580488 | tf_op jit(solution)/shard_map/ppermute | solution.py:189
  128.7 32.9 %collective-permute-start.16 = (bf16[4,64,2560]{2,1,0:T(8,128)(2,1)}, bf16[4,64,2560]{2,1,0:T(8,128)(2,1)}, u32[]{:S(2)}, u32[]{:S(2)}) collective-permute-start(bf16[4,64,2560]{2,1,0:T(8,128)(2,1)} %pad_maximum_fusion.12), channel_id=1, source_target_pairs={{0,4},{2,6},{4,0},{6,2},{8,12},{10,14},{12,8},{14,10},{16,20},{18,... | collective-permute-start | bytes 3932168 | tf_op jit(solution)/shard_map/ppermute | solution.py:189
  138.9 58.9 %collective-permute-start.24 = (bf16[160,2688]{1,0:T(8,128)(2,1)}, bf16[160,2688]{1,0:T(8,128)(2,1)}, u32[]{:S(2)}, u32[]{:S(2)}) collective-permute-start(bf16[160,2688]{1,0:T(8,128)(2,1)} %get-tuple-element.133), channel_id=1, source_target_pairs={{0,16},{2,18},{4,20},{6,22},{8,24},{10,26},{12,28},{14,30},{16,0},... | collective-permute-start | bytes 2580488 | tf_op jit(solution)/shard_map/ppermute | solution.py:189
  139.0 38.4 %collective-permute-start.18 = (bf16[2,160,2688]{2,1,0:T(8,128)(2,1)S(1)}, bf16[2,160,2688]{2,1,0:T(8,128)(2,1)S(1)}, u32[]{:S(2)}, u32[]{:S(2)}) collective-permute-start(bf16[2,160,2688]{2,1,0:T(8,128)(2,1)S(1)} %pad_maximum_fusion.4), channel_id=1, source_target_pairs={{0,2},{2,0},{4,6},{6,4},{8,10},{10,8},{12,14},{14,12},{16,18},{18,... | collective-permute-start | bytes 5160968 | tf_op jit(solution)/shard_map/ppermute | solution.py:189
  139.6 56.5 %collective-permute-start.26 = (bf16[2,160,2688]{2,1,0:T(8,128)(2,1)S(1)}, bf16[2,160,2688]{2,1,0:T(8,128)(2,1)}, u32[]{:S(2)}, u32[]{:S(2)}) collective-permute-start(bf16[2,160,2688]{2,1,0:T(8,128)(2,1)S(1)} %pad_maximum_fusion.4), channel_id=1, source_target_pairs={{0,8},{2,10},{4,12},{6,14},{8,0},{10,2},{12,4},{14,6},{16,24},{18,... | collective-permute-start | bytes 5160968 | tf_op jit(solution)/shard_map/ppermute | solution.py:189
  168.2 28.1 %collective-permute-start.20 = (bf16[2,64,2560]{2,1,0:T(8,128)(2,1)S(1)}, bf16[2,64,2560]{2,1,0:T(8,128)(2,1)S(1)}, u32[]{:S(2)}, u32[]{:S(2)}) collective-permute-start(bf16[2,64,2560]{2,1,0:T(8,128)(2,1)S(1)} %copy-done.111), channel_id=1, source_target_pairs={{0,4},{2,6},{4,0},{6,2},{8,12},{10,14},{12,8},{14,10},{16,20},{18,... | collective-permute-start | bytes 1966088 | tf_op jit(solution)/shard_map/ppermute | solution.py:189
  196.1 54.1 %collective-permute-start.27 = (bf16[2,160,2688]{2,1,0:T(8,128)(2,1)S(1)}, bf16[2,160,2688]{2,1,0:T(8,128)(2,1)S(1)}, u32[]{:S(2)}, u32[]{:S(2)}) collective-permute-start(bf16[2,160,2688]{2,1,0:T(8,128)(2,1)S(1)} %collective-permute-done.18), channel_id=1, source_target_pairs={{0,8},{2,10},{4,12},{6,14},{8,0},{10,2},{12,4},{14,6},{16,24},{18,... | collective-permute-start | bytes 5160968 | tf_op jit(solution)/shard_map/ppermute | solution.py:189
  196.3 52.7 %collective-permute-start.21 = (bf16[4,160,1280]{2,1,0:T(8,128)(2,1)S(1)}, bf16[4,160,1280]{2,1,0:T(8,128)(2,1)S(1)}, u32[]{:S(2)}, u32[]{:S(2)}) collective-permute-start(bf16[4,160,1280]{2,1,0:T(8,128)(2,1)S(1)} %copy-done.82), channel_id=1, source_target_pairs={{0,4},{2,6},{4,0},{6,2},{8,12},{10,14},{12,8},{14,10},{16,20},{18,... | collective-permute-start | bytes 4915208 | tf_op jit(solution)/shard_map/ppermute | solution.py:189
  197.8 47.8 %collective-permute-start.25 = (bf16[128,2560]{1,0:T(8,128)(2,1)}, bf16[128,2560]{1,0:T(8,128)(2,1)S(1)}, u32[]{:S(2)}, u32[]{:S(2)}) collective-permute-start(bf16[128,2560]{1,0:T(8,128)(2,1)} %multiply_convert_fusion.5), channel_id=1, source_target_pairs={{0,16},{2,18},{4,20},{6,22},{8,24},{10,26},{12,28},{14,30},{16,0},... | collective-permute-start | bytes 1966088 | tf_op jit(solution)/shard_map/ppermute | solution.py:189
  200.4 49.8 %collective-permute-start.22 = (bf16[4,160,1280]{2,1,0:T(8,128)(2,1)S(1)}, bf16[4,160,1280]{2,1,0:T(8,128)(2,1)S(1)}, u32[]{:S(2)}, u32[]{:S(2)}) collective-permute-start(bf16[4,160,1280]{2,1,0:T(8,128)(2,1)S(1)} %copy-done.82), channel_id=1, source_target_pairs={{0,2},{2,0},{4,6},{6,4},{8,10},{10,8},{12,14},{14,12},{16,18},{18,... | collective-permute-start | bytes 4915208 | tf_op jit(solution)/shard_map/ppermute | solution.py:189
  245.6 30.2 %collective-permute-start.30 = (bf16[128,2560]{1,0:T(8,128)(2,1)}, bf16[128,2560]{1,0:T(8,128)(2,1)S(1)}, u32[]{:S(2)}, u32[]{:S(2)}) collective-permute-start(bf16[128,2560]{1,0:T(8,128)(2,1)} %collective-permute-done.5), channel_id=1, source_target_pairs={{0,16},{2,18},{4,20},{6,22},{8,24},{10,26},{12,28},{14,30},{16,0},... | collective-permute-start | bytes 1966088 | tf_op jit(solution)/shard_map/ppermute | solution.py:189
  279.5 39.9 %collective-permute-start.34 = (bf16[2,160,2688]{2,1,0:T(8,128)(2,1)S(1)}, bf16[2,160,2688]{2,1,0:T(8,128)(2,1)S(1)}, u32[]{:S(2)}, u32[]{:S(2)}) collective-permute-start(bf16[2,160,2688]{2,1,0:T(8,128)(2,1)S(1)} %pad_maximum_fusion.5), channel_id=1, source_target_pairs={{0,2},{2,0},{4,6},{6,4},{8,10},{10,8},{12,14},{14,12},{16,18},{18,... | collective-permute-start | bytes 5160968 | tf_op jit(solution)/shard_map/ppermute | solution.py:189
  283.0 30.5 %collective-permute-start.33 = (bf16[128,2560]{1,0:T(8,128)(2,1)S(1)}, bf16[128,2560]{1,0:T(8,128)(2,1)S(1)}, u32[]{:S(2)}, u32[]{:S(2)}) collective-permute-start(bf16[128,2560]{1,0:T(8,128)(2,1)S(1)} %multiply_convert_fusion.3.refs_0_), channel_id=1, source_target_pairs={{0,16},{2,18},{4,20},{6,22},{8,24},{10,26},{12,28},{14,30},{16,0},... | collective-permute-start | bytes 1966088 | tf_op jit(solution)/shard_map/ppermute | solution.py:189
  283.0 54.8 %collective-permute-start.36 = (bf16[2,160,2688]{2,1,0:T(8,128)(2,1)S(1)}, bf16[2,160,2688]{2,1,0:T(8,128)(2,1)S(1)}, u32[]{:S(2)}, u32[]{:S(2)}) collective-permute-start(bf16[2,160,2688]{2,1,0:T(8,128)(2,1)S(1)} %pad_maximum_fusion.5), channel_id=1, source_target_pairs={{0,8},{2,10},{4,12},{6,14},{8,0},{10,2},{12,4},{14,6},{16,24},{18,... | collective-permute-start | bytes 5160968 | tf_op jit(solution)/shard_map/ppermute | solution.py:189
  337.8 21.9 %collective-permute-start.37 = (bf16[512,2560]{1,0:T(8,128)(2,1)S(1)}, bf16[512,2560]{1,0:T(8,128)(2,1)S(1)}, u32[]{:S(2)}, u32[]{:S(2)}) collective-permute-start(bf16[512,2560]{1,0:T(8,128)(2,1)S(1)} %bitcast.430), channel_id=1, source_target_pairs={{0,1},{1,0},{2,3},{3,2},{4,5},{5,4},{6,7},{7,6},{8,9},{9,8},{10,11... | collective-permute-start | bytes 7864328 | tf_op jit(solution)/shard_map/ppermute | solution.py:77
  406.8 22.1 %collective-permute-start.42 = (bf16[128,2560]{1,0:T(8,128)(2,1)S(1)}, bf16[128,2560]{1,0:T(8,128)(2,1)S(1)}, u32[]{:S(2)}, u32[]{:S(2)}) collective-permute-start(bf16[128,2560]{1,0:T(8,128)(2,1)S(1)} %get-tuple-element.151), channel_id=1, source_target_pairs={{0,4},{2,6},{4,0},{6,2},{8,12},{10,14},{12,8},{14,10},{16,20},{18,... | collective-permute-start | bytes 1966088 | tf_op jit(solution)/shard_map/ppermute | solution.py:189
  427.5 43.9 %collective-permute-start.48 = (bf16[2,160,2688]{2,1,0:T(8,128)(2,1)}, bf16[2,160,2688]{2,1,0:T(8,128)(2,1)}, u32[]{:S(2)}, u32[]{:S(2)}) collective-permute-start(bf16[2,160,2688]{2,1,0:T(8,128)(2,1)} %bitcast.90), channel_id=1, source_target_pairs={{0,2},{2,0},{4,6},{6,4},{8,10},{10,8},{12,14},{14,12},{16,18},{18,... | collective-permute-start | bytes 5160968 | tf_op jit(solution)/shard_map/ppermute | solution.py:189
  430.7 31.5 %collective-permute-start.44 = (bf16[128,2560]{1,0:T(8,128)(2,1)}, bf16[128,2560]{1,0:T(8,128)(2,1)}, u32[]{:S(2)}, u32[]{:S(2)}) collective-permute-start(bf16[128,2560]{1,0:T(8,128)(2,1)} %fusion.66), channel_id=1, source_target_pairs={{0,16},{2,18},{4,20},{6,22},{8,24},{10,26},{12,28},{14,30},{16,0},... | collective-permute-start | bytes 1966088 | tf_op jit(solution)/shard_map/ppermute | solution.py:189
  432.3 31.8 %collective-permute-start.46 = (bf16[128,2560]{1,0:T(8,128)(2,1)}, bf16[128,2560]{1,0:T(8,128)(2,1)}, u32[]{:S(2)}, u32[]{:S(2)}) collective-permute-start(bf16[128,2560]{1,0:T(8,128)(2,1)} %get-tuple-element.157), channel_id=1, source_target_pairs={{0,4},{2,6},{4,0},{6,2},{8,12},{10,14},{12,8},{14,10},{16,20},{18,... | collective-permute-start | bytes 1966088 | tf_op jit(solution)/shard_map/ppermute | solution.py:189
  460.6 66.9 %collective-permute-start.43 = (bf16[512,2560]{1,0:T(8,128)(2,1)}, bf16[512,2560]{1,0:T(8,128)(2,1)}, u32[]{:S(2)}, u32[]{:S(2)}) collective-permute-start(bf16[512,2560]{1,0:T(8,128)(2,1)} %slice.985), channel_id=1, source_target_pairs={{0,1},{1,0},{2,3},{3,2},{4,5},{5,4},{6,7},{7,6},{8,9},{9,8},{10,11... | collective-permute-start | bytes 7864328 | tf_op jit(solution)/shard_map/ppermute | solution.py:77
  471.3 40.0 %collective-permute-start.45 = (bf16[2,160,2688]{2,1,0:T(8,128)(2,1)S(1)}, bf16[2,160,2688]{2,1,0:T(8,128)(2,1)S(1)}, u32[]{:S(2)}, u32[]{:S(2)}) collective-permute-start(bf16[2,160,2688]{2,1,0:T(8,128)(2,1)S(1)} %bitcast.467), channel_id=1, source_target_pairs={{0,8},{2,10},{4,12},{6,14},{8,0},{10,2},{12,4},{14,6},{16,24},{18,... | collective-permute-start | bytes 5160968 | tf_op jit(solution)/shard_map/ppermute | solution.py:189
  482.5 23.0 %collective-permute-start.49 = (bf16[2,160,1280]{2,1,0:T(8,128)(2,1)S(1)}, bf16[2,160,1280]{2,1,0:T(8,128)(2,1)S(1)}, u32[]{:S(2)}, u32[]{:S(2)}) collective-permute-start(bf16[2,160,1280]{2,1,0:T(8,128)(2,1)S(1)} %pad_maximum_fusion.18), channel_id=1, source_target_pairs={{0,2},{2,0},{4,6},{6,4},{8,10},{10,8},{12,14},{14,12},{16,18},{18,... | collective-permute-start | bytes 2457608 | tf_op jit(solution)/shard_map/ppermute | solution.py:189
  483.2 23.8 %collective-permute-start.50 = (bf16[2,160,1280]{2,1,0:T(8,128)(2,1)S(1)}, bf16[2,160,1280]{2,1,0:T(8,128)(2,1)S(1)}, u32[]{:S(2)}, u32[]{:S(2)}) collective-permute-start(bf16[2,160,1280]{2,1,0:T(8,128)(2,1)S(1)} %pad_maximum_fusion.19), channel_id=1, source_target_pairs={{0,4},{2,6},{4,0},{6,2},{8,12},{10,14},{12,8},{14,10},{16,20},{18,... | collective-permute-start | bytes 2457608 | tf_op jit(solution)/shard_map/ppermute | solution.py:189
  511.3 88.7 %collective-permute-start.58 = (bf16[4,160,2688]{2,1,0:T(8,128)(2,1)}, bf16[4,160,2688]{2,1,0:T(8,128)(2,1)}, u32[]{:S(2)}, u32[]{:S(2)}) collective-permute-start(bf16[4,160,2688]{2,1,0:T(8,128)(2,1)} %pad_maximum_fusion.2), channel_id=1, source_target_pairs={{0,8},{2,10},{4,12},{6,14},{8,0},{10,2},{12,4},{14,6},{16,24},{18,... | collective-permute-start | bytes 10321928 | tf_op jit(solution)/shard_map/ppermute | solution.py:189
  517.3 82.6 %collective-permute-start.54 = (bf16[4,160,2688]{2,1,0:T(8,128)(2,1)}, bf16[4,160,2688]{2,1,0:T(8,128)(2,1)}, u32[]{:S(2)}, u32[]{:S(2)}) collective-permute-start(bf16[4,160,2688]{2,1,0:T(8,128)(2,1)} %pad_maximum_fusion.1), channel_id=1, source_target_pairs={{0,2},{2,0},{4,6},{6,4},{8,10},{10,8},{12,14},{14,12},{16,18},{18,... | collective-permute-start | bytes 10321928 | tf_op jit(solution)/shard_map/ppermute | solution.py:189
  518.0 38.2 %collective-permute-start.51 = (bf16[4,160,1280]{2,1,0:T(8,128)(2,1)}, bf16[4,160,1280]{2,1,0:T(8,128)(2,1)}, u32[]{:S(2)}, u32[]{:S(2)}) collective-permute-start(bf16[4,160,1280]{2,1,0:T(8,128)(2,1)} %pad_maximum_fusion.10), channel_id=1, source_target_pairs={{0,4},{2,6},{4,0},{6,2},{8,12},{10,14},{12,8},{14,10},{16,20},{18,... | collective-permute-start | bytes 4915208 | tf_op jit(solution)/shard_map/ppermute | solution.py:189
  573.2 32.5 %collective-permute-start.53 = (bf16[128,2560]{1,0:T(8,128)(2,1)S(1)}, bf16[128,2560]{1,0:T(8,128)(2,1)S(1)}, u32[]{:S(2)}, u32[]{:S(2)}) collective-permute-start(bf16[128,2560]{1,0:T(8,128)(2,1)S(1)} %fusion.67), channel_id=1, source_target_pairs={{0,16},{2,18},{4,20},{6,22},{8,24},{10,26},{12,28},{14,30},{16,0},... | collective-permute-start | bytes 1966088 | tf_op jit(solution)/shard_map/ppermute | solution.py:189
  575.6 32.4 %collective-permute-start.55 = (bf16[128,2560]{1,0:T(8,128)(2,1)S(1)}, bf16[128,2560]{1,0:T(8,128)(2,1)S(1)}, u32[]{:S(2)}, u32[]{:S(2)}) collective-permute-start(bf16[128,2560]{1,0:T(8,128)(2,1)S(1)} %copy-done.105), channel_id=1, source_target_pairs={{0,4},{2,6},{4,0},{6,2},{8,12},{10,14},{12,8},{14,10},{16,20},{18,... | collective-permute-start | bytes 1966088 | tf_op jit(solution)/shard_map/ppermute | solution.py:189
  605.4 36.8 %collective-permute-start.61 = (bf16[4,160,1280]{2,1,0:T(8,128)(2,1)}, bf16[4,160,1280]{2,1,0:T(8,128)(2,1)}, u32[]{:S(2)}, u32[]{:S(2)}) collective-permute-start(bf16[4,160,1280]{2,1,0:T(8,128)(2,1)} %pad_maximum_fusion.11), channel_id=1, source_target_pairs={{0,2},{2,0},{4,6},{6,4},{8,10},{10,8},{12,14},{14,12},{16,18},{18,... | collective-permute-start | bytes 4915208 | tf_op jit(solution)/shard_map/ppermute | solution.py:189
  608.8 40.0 %collective-permute-start.74 = (bf16[160,2688]{1,0:T(8,128)(2,1)}, bf16[160,2688]{1,0:T(8,128)(2,1)}, u32[]{:S(2)}, u32[]{:S(2)}) collective-permute-start(bf16[160,2688]{1,0:T(8,128)(2,1)} %get-tuple-element.191), channel_id=1, source_target_pairs={{0,16},{2,18},{4,20},{6,22},{8,24},{10,26},{12,28},{14,30},{16,0},... | collective-permute-start | bytes 2580488 | tf_op jit(solution)/shard_map/ppermute | solution.py:189
  609.1 38.1 %collective-permute-start.59 = (bf16[2,160,2688]{2,1,0:T(8,128)(2,1)}, bf16[2,160,2688]{2,1,0:T(8,128)(2,1)}, u32[]{:S(2)}, u32[]{:S(2)}) collective-permute-start(bf16[2,160,2688]{2,1,0:T(8,128)(2,1)} %pad_maximum_fusion.6), channel_id=1, source_target_pairs={{0,4},{2,6},{4,0},{6,2},{8,12},{10,14},{12,8},{14,10},{16,20},{18,... | collective-permute-start | bytes 5160968 | tf_op jit(solution)/shard_map/ppermute | solution.py:189
  616.4 74.0 %collective-permute-start.57 = (bf16[16,80,1152]{2,1,0:T(8,128)(2,1)}, bf16[16,80,1152]{2,1,0:T(8,128)(2,1)}, u32[]{:S(2)}, u32[]{:S(2)}) collective-permute-start(bf16[16,80,1152]{2,1,0:T(8,128)(2,1)} %fusion.32), channel_id=1, source_target_pairs={{0,1},{1,0},{2,3},{3,2},{4,5},{5,4},{6,7},{7,6},{8,9},{9,8},{10,11... | collective-permute-start | bytes 8847368 | tf_op jit(solution)/shard_map/ppermute | solution.py:77
  648.8 39.1 %collective-permute-start.75 = (bf16[160,2688]{1,0:T(8,128)(2,1)S(1)}, bf16[160,2688]{1,0:T(8,128)(2,1)S(1)}, u32[]{:S(2)}, u32[]{:S(2)}) collective-permute-start(bf16[160,2688]{1,0:T(8,128)(2,1)S(1)} %get-tuple-element.192), channel_id=1, source_target_pairs={{0,16},{2,18},{4,20},{6,22},{8,24},{10,26},{12,28},{14,30},{16,0},... | collective-permute-start | bytes 2580488 | tf_op jit(solution)/shard_map/ppermute | solution.py:189
  660.4 43.8 %collective-permute-start.72 = (bf16[160,1280]{1,0:T(8,128)(2,1)}, bf16[160,1280]{1,0:T(8,128)(2,1)}, u32[]{:S(2)}, u32[]{:S(2)}) collective-permute-start(bf16[160,1280]{1,0:T(8,128)(2,1)} %get-tuple-element.189), channel_id=1, source_target_pairs={{0,8},{2,10},{4,12},{6,14},{8,0},{10,2},{12,4},{14,6},{16,24},{18,... | collective-permute-start | bytes 1228808 | tf_op jit(solution)/shard_map/ppermute | solution.py:189
  666.4 34.7 %collective-permute-start.63 = (bf16[4,64,2560]{2,1,0:T(8,128)(2,1)}, bf16[4,64,2560]{2,1,0:T(8,128)(2,1)}, u32[]{:S(2)}, u32[]{:S(2)}) collective-permute-start(bf16[4,64,2560]{2,1,0:T(8,128)(2,1)} %pad_maximum_fusion.14), channel_id=1, source_target_pairs={{0,2},{2,0},{4,6},{6,4},{8,10},{10,8},{12,14},{14,12},{16,18},{18,... | collective-permute-start | bytes 3932168 | tf_op jit(solution)/shard_map/ppermute | solution.py:189
  668.1 33.0 %collective-permute-start.64 = (bf16[4,64,2560]{2,1,0:T(8,128)(2,1)}, bf16[4,64,2560]{2,1,0:T(8,128)(2,1)}, u32[]{:S(2)}, u32[]{:S(2)}) collective-permute-start(bf16[4,64,2560]{2,1,0:T(8,128)(2,1)} %pad_maximum_fusion.15), channel_id=1, source_target_pairs={{0,4},{2,6},{4,0},{6,2},{8,12},{10,14},{12,8},{14,10},{16,20},{18,... | collective-permute-start | bytes 3932168 | tf_op jit(solution)/shard_map/ppermute | solution.py:189
  708.9 31.2 %collective-permute-start.65 = (bf16[4,80,1152]{2,1,0:T(8,128)(2,1)}, bf16[4,80,1152]{2,1,0:T(8,128)(2,1)}, u32[]{:S(2)}, u32[]{:S(2)}) collective-permute-start(bf16[4,80,1152]{2,1,0:T(8,128)(2,1)} %pad_maximum_fusion.21), channel_id=1, source_target_pairs={{0,2},{2,0},{4,6},{6,4},{8,10},{10,8},{12,14},{14,12},{16,18},{18,... | collective-permute-start | bytes 2211848 | tf_op jit(solution)/shard_map/ppermute | solution.py:189
  711.2 34.1 %collective-permute-start.66 = (bf16[4,80,1152]{2,1,0:T(8,128)(2,1)}, bf16[4,80,1152]{2,1,0:T(8,128)(2,1)}, u32[]{:S(2)}, u32[]{:S(2)}) collective-permute-start(bf16[4,80,1152]{2,1,0:T(8,128)(2,1)} %pad_maximum_fusion.22), channel_id=1, source_target_pairs={{0,4},{2,6},{4,0},{6,2},{8,12},{10,14},{12,8},{14,10},{16,20},{18,... | collective-permute-start | bytes 2211848 | tf_op jit(solution)/shard_map/ppermute | solution.py:189
  712.5 32.9 %collective-permute-start.67 = (bf16[4,80,1152]{2,1,0:T(8,128)(2,1)}, bf16[4,80,1152]{2,1,0:T(8,128)(2,1)}, u32[]{:S(2)}, u32[]{:S(2)}) collective-permute-start(bf16[4,80,1152]{2,1,0:T(8,128)(2,1)} %pad_maximum_fusion.23), channel_id=1, source_target_pairs={{0,6},{2,4},{4,2},{6,0},{8,14},{10,12},{12,10},{14,8},{16,22},{18,... | collective-permute-start | bytes 2211848 | tf_op jit(solution)/shard_map/ppermute | solution.py:189
  714.1 37.4 %collective-permute-start.77 = (bf16[64,2560]{1,0:T(8,128)(2,1)}, bf16[64,2560]{1,0:T(8,128)(2,1)}, u32[]{:S(2)}, u32[]{:S(2)}) collective-permute-start(bf16[64,2560]{1,0:T(8,128)(2,1)} %fusion.95), channel_id=1, source_target_pairs={{0,16},{2,18},{4,20},{6,22},{8,24},{10,26},{12,28},{14,30},{16,0},... | collective-permute-start | bytes 983048 | tf_op jit(solution)/shard_map/ppermute | solution.py:189
  715.7 35.8 %collective-permute-start.78 = (bf16[64,2560]{1,0:T(8,128)(2,1)}, bf16[64,2560]{1,0:T(8,128)(2,1)}, u32[]{:S(2)}, u32[]{:S(2)}) collective-permute-start(bf16[64,2560]{1,0:T(8,128)(2,1)} %get-tuple-element.195), channel_id=1, source_target_pairs={{0,8},{2,10},{4,12},{6,14},{8,0},{10,2},{12,4},{14,6},{16,24},{18,... | collective-permute-start | bytes 983048 | tf_op jit(solution)/shard_map/ppermute | solution.py:189
  (175 other events, 2310.5 us)
